TPU v7x, 32 devices: a whole 2x2x4 slice. The times are simulated.
32 devices in a mesh: section: 2 (over x), dp: 4 (over y, core), tensor: 4 (over z).
Axes of the slice: x: 2, y: 2, z: 4, core: 2. Of those that a mesh axis runs over, the one named last changes fastest.
Arguments:
- tokens: bfloat16 [8, 1024, 768], P('dp', 'tensor'), may hold values from -6 to 6
- cotangent: bfloat16 [8, 1024, 768], P('dp', 'tensor'), may hold values from -6 to 6
- lengths: int32 [8, 8], P('dp'), may hold values from 1 to 896, 1024 in all within a row
- w_qkv: bfloat16 [2, 768, 3, 768], P('section', 'dp', None, 'tensor'), may hold values from -0.21875 to 0.21875
- w_out: bfloat16 [2, 768, 768], P('section', 'tensor', 'dp'), may hold values from -0.625 to 0.625
- w_gate_up: bfloat16 [2, 768, 2, 3072], P('section', 'dp', None, 'tensor'), may hold values from -0.21875 to 0.21875
- w_down: bfloat16 [2, 3072, 768], P('section', 'tensor', 'dp'), may hold values from -0.109375 to 0.109375
- norm_gains: bfloat16 [2, 1536], P('section', 'dp'), may hold values from 0.5 to 1.5
- norm_biases: bfloat16 [2, 1536], P('section', 'dp'), may hold values from -1.796875 to 1.796875
Outputs:
- ends: bfloat16 [2, 8, 1024, 768], P('section', 'dp', 'tensor')
- grad_qkv: float32 [2, 768, 3, 768], P('section', 'dp', None, 'tensor')
- grad_out: float32 [2, 768, 768], P('section', 'tensor', 'dp')
- grad_gate_up: float32 [2, 768, 2, 3072], P('section', 'dp', None, 'tensor')
- grad_down: float32 [2, 3072, 768], P('section', 'tensor', 'dp')
- grad_gains: float32 [2, 1536], P('section', ('dp', 'tensor'))
- grad_biases: float32 [2, 1536], P('section', ('dp', 'tensor'))
Inputs may be any that keep to these rules, and one draw needn't show every extreme that they name: `lengths`: each row sums to 1024 and its largest length is exactly 896.
All inputs are finite; a program needn't handle non-finite values.
Results may differ from a plain program's by a relative error of at most 0.02.
Values may be sent and summed in bfloat16 or wider, within the bound.
A program may use at most 256 MiB of HBM per device.

v0:
```python
import jax
import jax.numpy as jnp
from jax import lax
from jax.sharding import PartitionSpec as P

HD = 64


eps = 1e-05
neg_fill = -1e30


def from_behind(value, axis, steps):
    count = lax.axis_size(axis)
    first, last = (max(0, -steps), min(count, count - steps))
    return lax.ppermute(value, axis, [(source, source + steps) for source in range(first, last)])


def layer_norm(resid, gain, shift):
    center = resid - jnp.mean(resid, axis=-1, keepdims=True)
    spread = jnp.mean(center * center, axis=-1, keepdims=True)
    return center * lax.rsqrt(spread + eps) * gain + shift


def gate_act(joined):
    halfway = joined.shape[-1] // 2
    return jax.nn.silu(joined[:, :halfway]) * joined[:, halfway:]


def rope_tables(length, head_size):
    halfway = head_size // 2
    freqs = 1000.0 ** (-jnp.arange(halfway, dtype=jnp.float32) / halfway)
    angles = jnp.arange(length, dtype=jnp.float32)[:, None] * freqs[None, :]
    return (jnp.cos(angles), jnp.sin(angles))


def rotate(values, cosine, sine, direction):
    halfway = values.shape[-1] // 2
    leading = values[..., :halfway]
    trailing = values[..., halfway:]
    cos_table = cosine[:, None, :]
    sin_table = sine[:, None, :] * direction
    return jnp.concatenate(
        [leading * cos_table - trailing * sin_table, trailing * cos_table + leading * sin_table],
        axis=-1,
    )


def gather_weights(stored):
    return (
        lax.all_gather(stored[0], "dp", axis=0, tiled=True),
        lax.all_gather(stored[1], "dp", axis=1, tiled=True),
        lax.all_gather(stored[2], "dp", axis=0, tiled=True),
        lax.all_gather(stored[3], "dp", axis=1, tiled=True),
        lax.all_gather(stored[4], "dp", axis=0, tiled=True),
        lax.all_gather(stored[5], "dp", axis=0, tiled=True),
    )


def reduce_grads(grads):
    shared = (
        lax.psum_scatter(grads[0], "dp", scatter_dimension=0, tiled=True),
        lax.psum_scatter(grads[1], "dp", scatter_dimension=1, tiled=True),
        lax.psum_scatter(grads[2], "dp", scatter_dimension=0, tiled=True),
        lax.psum_scatter(grads[3], "dp", scatter_dimension=1, tiled=True),
    )
    norms = (
        lax.psum_scatter(grads[4], ("dp", "tensor"), scatter_dimension=0, tiled=True),
        lax.psum_scatter(grads[5], ("dp", "tensor"), scatter_dimension=0, tiled=True),
    )
    return (shared[0], shared[1], shared[2], shared[3], norms[0], norms[1])


def add_all(first_set, second_set):
    return jax.tree.map(jnp.add, first_set, second_set)


def project_in(rows_low, weight_flat):
    return jnp.dot(
        lax.all_gather(rows_low, "tensor", axis=0, tiled=True),
        weight_flat,
        preferred_element_type=jnp.float32,
    )


def combine_out(full_low, weight):
    return lax.psum_scatter(
        jnp.dot(full_low, weight, preferred_element_type=jnp.float32),
        "tensor",
        scatter_dimension=0,
        tiled=True,
    )


def spread_back(grads_low, weight, kept_low):
    shard_rows = lax.all_gather(grads_low, "tensor", axis=0, tiled=True)
    product = lax.dot_general(
        shard_rows, weight, (((1,), (1,)), ((), ())), preferred_element_type=jnp.float32
    )
    grad_weight = lax.dot_general(
        kept_low, shard_rows, (((0,), (0,)), ((), ())), preferred_element_type=jnp.float32
    )
    return (product, grad_weight)


def return_rows(grads_low, weight_flat):
    return lax.psum_scatter(
        lax.dot_general(
            grads_low, weight_flat, (((1,), (1,)), ((), ())), preferred_element_type=jnp.float32
        ),
        "tensor",
        scatter_dimension=0,
        tiled=True,
    )


def weight_grad(rows_low, grads_low):
    return lax.dot_general(
        lax.all_gather(rows_low, "tensor", axis=0, tiled=True),
        grads_low,
        (((0,), (0,)), ((), ())),
        preferred_element_type=jnp.float32,
    )


def block_scores(query_rows, keys, query_seg, key_seg, scale):
    scores = (
        jnp.einsum("qhd,khd->hqk", query_rows, keys, preferred_element_type=jnp.float32) * scale
    )
    return jnp.where((query_seg[:, None] == key_seg[None, :])[None], scores, neg_fill)


def attend(queries, keys, values, segment):
    length = queries.shape[0]
    block_rows = min(512, length)
    scale = queries.shape[2] ** (-0.5)
    outputs = []
    log_totals = []
    for offset in range(0, length, block_rows):
        scores = block_scores(
            queries[offset : offset + block_rows],
            keys,
            segment[offset : offset + block_rows],
            segment,
            scale,
        )
        highest = jnp.max(scores, axis=-1, keepdims=True)
        exps = jnp.exp(scores - highest)
        totals = jnp.sum(exps, axis=-1, keepdims=True)
        probs = exps / totals
        outputs.append(
            jnp.einsum(
                "hqk,khd->qhd",
                probs.astype(jnp.bfloat16),
                values,
                preferred_element_type=jnp.float32,
            )
        )
        log_totals.append(highest + jnp.log(totals))
    mixed = jnp.concatenate(outputs, axis=0)
    return (mixed.reshape(length, -1).astype(jnp.bfloat16), jnp.concatenate(log_totals, axis=1))


def attend_back(queries, keys, values, grad_mixed, log_totals, segment):
    length, heads_here, head_size = queries.shape
    grad_mixed = grad_mixed.reshape(length, heads_here, head_size)
    block_rows = min(512, length)
    scale = head_size ** (-0.5)
    grad_queries = []
    grad_keys = jnp.zeros(keys.shape, jnp.float32)
    grad_values = jnp.zeros(values.shape, jnp.float32)
    for offset in range(0, length, block_rows):
        query_rows = queries[offset : offset + block_rows]
        grad_block = grad_mixed[offset : offset + block_rows]
        scores = block_scores(
            query_rows, keys, segment[offset : offset + block_rows], segment, scale
        )
        probs = jnp.exp(scores - log_totals[:, offset : offset + block_rows])
        grad_probs = jnp.einsum(
            "qhd,khd->hqk", grad_block, values, preferred_element_type=jnp.float32
        )
        inner = jnp.sum(probs * grad_probs, axis=-1, keepdims=True)
        grad_scores = (probs * (grad_probs - inner)).astype(jnp.bfloat16)
        grad_queries.append(
            jnp.einsum("hqk,khd->qhd", grad_scores, keys, preferred_element_type=jnp.float32)
            * scale
        )
        grad_keys = (
            grad_keys
            + jnp.einsum(
                "hqk,qhd->khd", grad_scores, query_rows, preferred_element_type=jnp.float32
            )
            * scale
        )
        grad_values = grad_values + jnp.einsum(
            "hqk,qhd->khd",
            probs.astype(jnp.bfloat16),
            grad_block,
            preferred_element_type=jnp.float32,
        )
    return (jnp.concatenate(grad_queries, axis=0), grad_keys, grad_values)


def layer_forward(inputs_low, weights, segment, tables):
    w_joint, w_mix, w_pair, w_back, gains, shifts = weights
    width = inputs_low.shape[1]
    joined = project_in(inputs_low, w_joint.reshape(width, -1))
    length = joined.shape[0]
    heads_view = joined.reshape(length, 3, -1, HD)
    queries = rotate(heads_view[:, 0], tables[0], tables[1], 1.0).astype(jnp.bfloat16)
    keys = rotate(heads_view[:, 1], tables[0], tables[1], 1.0).astype(jnp.bfloat16)
    values = heads_view[:, 2].astype(jnp.bfloat16)
    mixed_low, log_totals = attend(queries, keys, values, segment)
    attn_rows = combine_out(mixed_low, w_mix)
    gain_values = gains.astype(jnp.float32).reshape(2, width)
    shift_values = shifts.astype(jnp.float32).reshape(2, width)
    first_sum = inputs_low.astype(jnp.float32) + attn_rows
    hidden = layer_norm(first_sum, gain_values[0], shift_values[0])
    hidden_low = hidden.astype(jnp.bfloat16)
    gate_up = project_in(hidden_low, w_pair.reshape(width, -1))
    active_low = gate_act(gate_up).astype(jnp.bfloat16)
    ffn_rows = combine_out(active_low, w_back)
    second_sum = hidden + ffn_rows
    result = layer_norm(second_sum, gain_values[1], shift_values[1])
    kept = (
        queries,
        keys,
        values,
        mixed_low,
        log_totals,
        first_sum,
        hidden_low,
        gate_up,
        active_low,
        second_sum,
        gain_values,
        shift_values,
    )
    return (result, kept)


def layer_backward(inputs_low, grad_result, weights, segment, tables):
    w_joint, w_mix, w_pair, w_back, gains, shifts = weights
    width = inputs_low.shape[1]
    unused, kept = layer_forward(inputs_low, weights, segment, tables)
    (
        queries,
        keys,
        values,
        mixed_low,
        log_totals,
        first_sum,
        hidden_low,
        gate_up,
        active_low,
        second_sum,
        gain_values,
        shift_values,
    ) = kept
    unused_out, norm_second = jax.vjp(layer_norm, second_sum, gain_values[1], shift_values[1])
    grad_second, grad_gain_two, grad_shift_two = norm_second(grad_result)
    grad_ffn_low = grad_second.astype(jnp.bfloat16)
    grad_active, grad_w_back = spread_back(grad_ffn_low, w_back, active_low)
    unused_act, act_back = jax.vjp(gate_act, gate_up)
    grad_pair_low = act_back(grad_active)[0].astype(jnp.bfloat16)
    grad_hidden = grad_second + return_rows(grad_pair_low, w_pair.reshape(width, -1))
    grad_w_pair = weight_grad(hidden_low, grad_pair_low)
    unused_first, norm_first = jax.vjp(layer_norm, first_sum, gain_values[0], shift_values[0])
    grad_first, grad_gain_one, grad_shift_one = norm_first(grad_hidden)
    grad_attn_low = grad_first.astype(jnp.bfloat16)
    grad_mixed, grad_w_mix = spread_back(grad_attn_low, w_mix, mixed_low)
    grad_queries, grad_keys, grad_values = attend_back(
        queries, keys, values, grad_mixed.astype(jnp.bfloat16), log_totals, segment
    )
    grad_queries = rotate(grad_queries, tables[0], tables[1], -1.0)
    grad_keys = rotate(grad_keys, tables[0], tables[1], -1.0)
    length = queries.shape[0]
    grad_joint_low = (
        jnp.stack([grad_queries, grad_keys, grad_values], axis=1)
        .reshape(length, -1)
        .astype(jnp.bfloat16)
    )
    grad_inputs = grad_first + return_rows(grad_joint_low, w_joint.reshape(width, -1))
    grad_w_joint = weight_grad(inputs_low, grad_joint_low)
    grads = (
        grad_w_joint.reshape(w_joint.shape),
        grad_w_mix,
        grad_w_pair.reshape(w_pair.shape),
        grad_w_back,
        jnp.concatenate([grad_gain_one, grad_gain_two]),
        jnp.concatenate([grad_shift_one, grad_shift_two]),
    )
    return (grad_inputs, grads)


def on_device(tokens, cotangent, lengths, w_qkv, w_out, w_gate_up, w_down, norm_gains, norm_biases):
    section = lax.axis_index("section")
    micro, own_rows, width = tokens.shape
    length = own_rows * lax.axis_size("tensor")
    positions = jnp.arange(length, dtype=jnp.int32)
    doc_ends = jnp.cumsum(lengths, axis=1)
    segments = jnp.sum(
        (doc_ends[:, None, :] <= positions[None, :, None]).astype(jnp.int32), axis=-1
    )
    tables = rope_tables(length, HD)
    stored = (w_qkv[0], w_out[0], w_gate_up[0], w_down[0], norm_gains[0], norm_biases[0])
    received = jnp.zeros((own_rows, width), jnp.bfloat16)
    seen = []
    results = []
    for tick in range(micro + 1):
        weights = gather_weights(stored)
        fresh = tokens[min(tick, micro - 1)]
        inputs_low = jnp.where(section == 0, fresh, received)
        segment = jnp.where(
            section == 0, segments[min(tick, micro - 1)], segments[max(tick - 1, 0)]
        )
        result, unused = layer_forward(inputs_low, weights, segment, tables)
        seen.append(inputs_low)
        results.append(result)
        if tick < micro:
            received = from_behind(result.astype(jnp.bfloat16), "section", 1)
    back_received = jnp.zeros((own_rows, width), jnp.float32)
    totals = None
    grad_list = []
    for tick in range(micro + 1):
        weights = gather_weights(stored)
        if tick < micro:
            start_grad = cotangent[tick].astype(jnp.float32)
        else:
            start_grad = jnp.zeros((own_rows, width), jnp.float32)
        grad_result = jnp.where(section == 1, start_grad, back_received)
        inputs_low = jnp.where(section == 1, seen[min(tick + 1, micro)], seen[max(tick - 1, 0)])
        segment = jnp.where(
            section == 1, segments[min(tick, micro - 1)], segments[max(tick - 1, 0)]
        )
        grad_inputs, grads = layer_backward(inputs_low, grad_result, weights, segment, tables)
        grad_list.append(grad_inputs)
        if tick < micro:
            back_received = from_behind(grad_inputs, "section", -1)
        reduced = reduce_grads(grads)
        totals = reduced if totals is None else add_all(totals, reduced)
    forward_rows = jnp.stack(results[1:], axis=0)
    backward_rows = jnp.stack(grad_list[1:], axis=0)
    ends = jnp.where(section == 0, backward_rows, forward_rows).astype(jnp.bfloat16)[None]
    return (
        ends,
        totals[0][None],
        totals[1][None],
        totals[2][None],
        totals[3][None],
        totals[4][None],
        totals[5][None],
    )


def solution(mesh):
    in_specs = (
        P("dp", "tensor", None),
        P("dp", "tensor", None),
        P("dp", None),
        P("section", "dp", None, "tensor"),
        P("section", "tensor", "dp"),
        P("section", "dp", None, "tensor"),
        P("section", "tensor", "dp"),
        P("section", "dp"),
        P("section", "dp"),
    )
    out_specs = (
        P("section", "dp", "tensor", None),
        P("section", "dp", None, "tensor"),
        P("section", "tensor", "dp"),
        P("section", "dp", None, "tensor"),
        P("section", "tensor", "dp"),
        P("section", ("dp", "tensor")),
        P("section", ("dp", "tensor")),
    )
    return jax.shard_map(
        on_device, mesh=mesh, in_specs=in_specs, out_specs=out_specs, check_vma=False
    )
```

profile of v0, /device:TPU:0, one launch (start us, length us, event | category | flops | bytes accessed | tf_op | source)
XLA Modules:
  0.0 2261.2 jit_solution(15844959841748065590)
XLA Ops:
  13.0 10.1 all-gather.3
  23.6 13.0 all-gather.2
  41.8 9.0 all-gather.62.cloned.1.call-done
  86.2 48.0 %reduce-scatter.24.cloned.1.call-done = f32[256,768]{1,0:T(8,128)} async-done(((f32[1024,768]{1,0:T(8,128)}), f32[256,768]{1,0:T(8,128)}) %reduce-scatter.24.cloned.1.call-update) | async-done | bytes 786448 | tf_op jit(solution)/shard_map/reduce_scatter | solution.py:87
  143.3 32.8 %all-gather.28.cloned.1.call-done = bf16[1024,768]{1,0:T(8,128)(2,1)} async-done(((bf16[256,768]{1,0:T(8,128)(2,1)}), bf16[1024,768]{1,0:T(8,128)(2,1)}) %all-gather.28.cloned.1.call-update) | async-done | bytes 1572880 | tf_op jit(solution)/shard_map/all_gather | solution.py:80
  176.1 7.4 fusion.392
  183.5 10.3 all-gather.66.cloned.1.call-done
  200.5 60.3 %reduce-scatter.26.cloned.1.call-done = f32[256,768]{1,0:T(8,128)} async-done(((f32[1024,768]{1,0:T(8,128)}), f32[256,768]{1,0:T(8,128)}) %reduce-scatter.26.cloned.1.call-update) | async-done | bytes 786448 | tf_op jit(solution)/shard_map/reduce_scatter | solution.py:87
  266.2 8.0 collective-permute-done
  276.8 36.8 %all-gather.38.cloned.1.call-done = bf16[1024,768]{1,0:T(8,128)(2,1)} async-done(((bf16[256,768]{1,0:T(8,128)(2,1)}), bf16[1024,768]{1,0:T(8,128)(2,1)}) %all-gather.38.cloned.1.call-update) | async-done | bytes 1572880 | tf_op jit(solution)/shard_map/all_gather | solution.py:80
  338.6 59.2 %reduce-scatter.36.cloned.1.call-done = f32[256,768]{1,0:T(8,128)} async-done(((f32[1024,768]{1,0:T(8,128)}), f32[256,768]{1,0:T(8,128)}) %reduce-scatter.36.cloned.1.call-update) | async-done | bytes 786448 | tf_op jit(solution)/shard_map/reduce_scatter | solution.py:87
  402.7 37.0 %all-gather.40.cloned.1.call-done = bf16[1024,768]{1,0:T(8,128)(2,1)} async-done(((bf16[256,768]{1,0:T(8,128)(2,1)}), bf16[1024,768]{1,0:T(8,128)(2,1)}) %all-gather.40.cloned.1.call-update) | async-done | bytes 1572880 | tf_op jit(solution)/shard_map/all_gather | solution.py:80
  448.6 76.4 %reduce-scatter.38.cloned.1.call-done = f32[256,768]{1,0:T(8,128)} async-done(((f32[1024,768]{1,0:T(8,128)}), f32[256,768]{1,0:T(8,128)}) %reduce-scatter.38.cloned.1.call-update) | async-done | bytes 786448 | tf_op jit(solution)/shard_map/reduce_scatter | solution.py:87
  529.3 7.9 collective-permute-done.2
  539.9 8.8 reduce-scatter.56.cloned.1.call-start
  555.8 21.0 all-gather.58.cloned.1.call-done
  582.0 32.4 %all-gather.42.cloned.1.call-done = bf16[1024,768]{1,0:T(8,128)(2,1)} async-done(((bf16[256,768]{1,0:T(8,128)(2,1)}), bf16[1024,768]{1,0:T(8,128)(2,1)}) %all-gather.42.cloned.1.call-update) | async-done | bytes 1572880 | tf_op jit(solution)/shard_map/all_gather | solution.py:80
  619.6 32.3 %all-gather.50.cloned.1.call-done = bf16[1024,768]{1,0:T(8,128)(2,1)} async-done(((bf16[256,768]{1,0:T(8,128)(2,1)}), bf16[1024,768]{1,0:T(8,128)(2,1)}) %all-gather.50.cloned.1.call-update) | async-done | bytes 1572880 | tf_op jit(solution)/shard_map/all_gather | solution.py:80
  693.0 49.1 %reduce-scatter.56.cloned.1.call-done = f32[256,768]{1,0:T(8,128)} async-done(((f32[1024,768]{1,0:T(8,128)}), f32[256,768]{1,0:T(8,128)}) %reduce-scatter.56.cloned.1.call-update) | async-done | bytes 786448 | tf_op jit(solution)/shard_map/reduce_scatter | solution.py:87
  791.1 23.4 %all-gather.60.cloned.1.call-done = bf16[1024,768]{1,0:T(8,128)(2,1)} async-done(((bf16[256,768]{1,0:T(8,128)(2,1)}), bf16[1024,768]{1,0:T(8,128)(2,1)}) %all-gather.60.cloned.1.call-update) | async-done | bytes 1572880 | tf_op jit(solution)/shard_map/all_gather | solution.py:80
  822.6 12.1 reduce-scatter.40.cloned.1.call-done
  836.2 61.0 %reduce-scatter.28.cloned.1.call-done = f32[256,768]{1,0:T(8,128)} async-done(((f32[1024,768]{1,0:T(8,128)}), f32[256,768]{1,0:T(8,128)}) %reduce-scatter.28.cloned.1.call-update) | async-done | bytes 786448 | tf_op jit(solution)/shard_map/reduce_scatter | solution.py:87
  898.7 61.0 %reduce-scatter.48.cloned.1.call-done = f32[256,768]{1,0:T(8,128)} async-done(((f32[1024,768]{1,0:T(8,128)}), f32[256,768]{1,0:T(8,128)}) %reduce-scatter.48.cloned.1.call-update) | async-done | bytes 786448 | tf_op jit(solution)/shard_map/reduce_scatter | solution.py:87
  961.3 60.8 %reduce-scatter.58.cloned.1.call-done = f32[256,768]{1,0:T(8,128)} async-done(((f32[1024,768]{1,0:T(8,128)}), f32[256,768]{1,0:T(8,128)}) %reduce-scatter.58.cloned.1.call-update) | async-done | bytes 786448 | tf_op jit(solution)/shard_map/reduce_scatter | solution.py:87
  1027.2 35.8 %all-gather.52.cloned.1.call-done = bf16[1024,768]{1,0:T(8,128)(2,1)} async-done(((bf16[256,768]{1,0:T(8,128)(2,1)}), bf16[1024,768]{1,0:T(8,128)(2,1)}) %all-gather.52.cloned.1.call-update) | async-done | bytes 1572880 | tf_op jit(solution)/shard_map/all_gather | solution.py:80
  1074.8 26.3 %all-gather.44.cloned.1.call-done = bf16[1024,768]{1,0:T(8,128)(2,1)} async-done(((bf16[256,768]{1,0:T(8,128)(2,1)}), bf16[1024,768]{1,0:T(8,128)(2,1)}) %all-gather.44.cloned.1.call-update) | async-done | bytes 1572880 | tf_op jit(solution)/shard_map/all_gather | solution.py:80
  1113.0 26.1 %all-gather.32.cloned.1.call-done = bf16[1024,768]{1,0:T(8,128)(2,1)} async-done(((bf16[256,768]{1,0:T(8,128)(2,1)}), bf16[1024,768]{1,0:T(8,128)(2,1)}) %all-gather.32.cloned.1.call-update) | async-done | bytes 1572880 | tf_op jit(solution)/shard_map/all_gather | solution.py:80
  1151.6 49.1 %reduce-scatter.50.cloned.1.call-done = f32[256,768]{1,0:T(8,128)} async-done(((f32[1024,768]{1,0:T(8,128)}), f32[256,768]{1,0:T(8,128)}) %reduce-scatter.50.cloned.1.call-update) | async-done | bytes 786448 | tf_op jit(solution)/shard_map/reduce_scatter | solution.py:87
  1200.6 62.5 %reduce-scatter.42.cloned.1.call-done = f32[256,768]{1,0:T(8,128)} async-done(((f32[1024,768]{1,0:T(8,128)}), f32[256,768]{1,0:T(8,128)}) %reduce-scatter.42.cloned.1.call-update) | async-done | bytes 786448 | tf_op jit(solution)/shard_map/reduce_scatter | solution.py:87
  1263.1 62.5 %reduce-scatter.30.cloned.1.call-done = f32[256,768]{1,0:T(8,128)} async-done(((f32[1024,768]{1,0:T(8,128)}), f32[256,768]{1,0:T(8,128)}) %reduce-scatter.30.cloned.1.call-update) | async-done | bytes 786448 | tf_op jit(solution)/shard_map/reduce_scatter | solution.py:87
  1334.3 37.0 %all-gather.34.cloned.1.call-done = bf16[1024,768]{1,0:T(8,128)(2,1)} async-done(((bf16[256,768]{1,0:T(8,128)(2,1)}), bf16[1024,768]{1,0:T(8,128)(2,1)}) %all-gather.34.cloned.1.call-update) | async-done | bytes 1572880 | tf_op jit(solution)/shard_map/all_gather | solution.py:96
  1384.4 59.2 %reduce-scatter.32.cloned.1.call-done = f32[256,768]{1,0:T(8,128)} async-done(((f32[1024,768]{1,0:T(8,128)}), f32[256,768]{1,0:T(8,128)}) %reduce-scatter.32.cloned.1.call-update) | async-done | bytes 786448 | tf_op jit(solution)/shard_map/reduce_scatter | solution.py:107
  1448.2 37.0 %all-gather.36.cloned.1.call-done = bf16[1024,768]{1,0:T(8,128)(2,1)} async-done(((bf16[256,768]{1,0:T(8,128)(2,1)}), bf16[1024,768]{1,0:T(8,128)(2,1)}) %all-gather.36.cloned.1.call-update) | async-done | bytes 1572880 | tf_op jit(solution)/shard_map/all_gather | solution.py:96
  1507.7 59.2 %reduce-scatter.34.cloned.1.call-done = f32[256,768]{1,0:T(8,128)} async-done(((f32[1024,768]{1,0:T(8,128)}), f32[256,768]{1,0:T(8,128)}) %reduce-scatter.34.cloned.1.call-update) | async-done | bytes 786448 | tf_op jit(solution)/shard_map/reduce_scatter | solution.py:107
  1570.1 19.2 collective-permute-done.1
  1592.9 36.2 %all-gather.46.cloned.1.call-done = bf16[1024,768]{1,0:T(8,128)(2,1)} async-done(((bf16[256,768]{1,0:T(8,128)(2,1)}), bf16[1024,768]{1,0:T(8,128)(2,1)}) %all-gather.46.cloned.1.call-update) | async-done | bytes 1572880 | tf_op jit(solution)/shard_map/all_gather | solution.py:96
  1642.1 59.2 %reduce-scatter.44.cloned.1.call-done = f32[256,768]{1,0:T(8,128)} async-done(((f32[1024,768]{1,0:T(8,128)}), f32[256,768]{1,0:T(8,128)}) %reduce-scatter.44.cloned.1.call-update) | async-done | bytes 786448 | tf_op jit(solution)/shard_map/reduce_scatter | solution.py:107
  1704.8 36.9 %all-gather.48.cloned.1.call-done = bf16[1024,768]{1,0:T(8,128)(2,1)} async-done(((bf16[256,768]{1,0:T(8,128)(2,1)}), bf16[1024,768]{1,0:T(8,128)(2,1)}) %all-gather.48.cloned.1.call-update) | async-done | bytes 1572880 | tf_op jit(solution)/shard_map/all_gather | solution.py:96
  1764.0 59.2 %reduce-scatter.46.cloned.1.call-done = f32[256,768]{1,0:T(8,128)} async-done(((f32[1024,768]{1,0:T(8,128)}), f32[256,768]{1,0:T(8,128)}) %reduce-scatter.46.cloned.1.call-update) | async-done | bytes 786448 | tf_op jit(solution)/shard_map/reduce_scatter | solution.py:107
  1826.0 19.3 collective-permute-done.3
  1847.7 36.4 %all-gather.54.cloned.1.call-done = bf16[1024,768]{1,0:T(8,128)(2,1)} async-done(((bf16[256,768]{1,0:T(8,128)(2,1)}), bf16[1024,768]{1,0:T(8,128)(2,1)}) %all-gather.54.cloned.1.call-update) | async-done | bytes 1572880 | tf_op jit(solution)/shard_map/all_gather | solution.py:96
  1897.6 58.5 %reduce-scatter.52.cloned.1.call-done = f32[256,768]{1,0:T(8,128)} async-done(((f32[1024,768]{1,0:T(8,128)}), f32[256,768]{1,0:T(8,128)}) %reduce-scatter.52.cloned.1.call-update) | async-done | bytes 786448 | tf_op jit(solution)/shard_map/reduce_scatter | solution.py:107
  1983.0 13.7 all-gather.56.cloned.1.call-done
  2053.6 38.1 %all-reduce.12.cloned.1.call-done = f32[768,2,768]{2,1,0:T(2,128)} async-done(((f32[768,2,768]{2,1,0:T(2,128)}), f32[768,2,768]{2,1,0:T(2,128)}) %all-reduce.12.cloned.1.call-update) | async-done | bytes 4718608
  2095.9 62.9 %all-reduce.9 = (f32[1536]{0:T(1024)S(1)}, f32[1536]{0:T(1024)S(1)}) all-reduce(f32[1536]{0:T(1024)S(1)} %fusion.260, f32[1536]{0:T(1024)S(1)} %fusion.261), channel_id=43, replica_groups=mesh['section'=2,'dp'=4,'tensor'=4] {'dp','tensor'}, use_global_device_ids=true, to_apply=%region_100.101.clone | all-reduce | flops 3072 | bytes 24576
  2161.7 19.6 reduce-scatter.54.cloned.1.call-done
  2183.7 33.7 %reduce-scatter.62.cloned.1.call-done = f32[768,192]{0,1:T(8,128)} async-done(((f32[768,768]{0,1:T(8,128)}), f32[768,192]{0,1:T(8,128)}) %reduce-scatter.62.cloned.1.call-update) | async-done | bytes 589840 | tf_op jit(solution)/shard_map/reduce_scatter | solution.py:65
  2217.3 36.0 %reduce-scatter.60.cloned.1.call-done = f32[192,3,192]{2,0,1:T(8,128)} async-done(((f32[768,3,192]{2,0,1:T(8,128)}), f32[192,3,192]{2,0,1:T(8,128)}) %reduce-scatter.60.cloned.1.call-update) | async-done | bytes 442384 | tf_op jit(solution)/shard_map/reduce_scatter | solution.py:62
  (744 shorter events, 479.0 us)
Async XLA Ops:
  8.0 42.8 %all-gather.62.cloned.1.call-start = ((), (), s32[]{:S(2)}) async-start(), calls=%async_computation.56 | async-start | bytes 1966080 | tf_op jit(solution)/shard_map/all_gather | solution.py:80
  9.8 124.4 %reduce-scatter.24.cloned.1.call-start = ((), (), s32[]{:S(2)}) async-start(), calls=%async_computation.21 | async-start | bytes 3932160 | tf_op jit(solution)/shard_map/reduce_scatter | solution.py:87
  40.1 618.8 %copy-start.15 = (f32[1024,32]{0,1:T(8,128)}, f32[1024,32]{0,1:T(8,128)S(1)}, u32[]{:S(2)}) copy-start(f32[1024,32]{0,1:T(8,128)S(1)} %get-tuple-element.182) | copy-start | bytes 393220
  74.9 64.8 %all-gather.64.cloned.1.call-start = ((), (), s32[]{:S(2)}) async-start(), calls=%async_computation.57 | async-start | bytes 2949120 | tf_op jit(solution)/shard_map/all_gather | solution.py:53
  75.5 100.6 %all-gather.28.cloned.1.call-start = ((), (), s32[]{:S(2)}) async-start(), calls=%async_computation.22 | async-start | bytes 1966080 | tf_op jit(solution)/shard_map/all_gather | solution.py:80
  86.2 440.6 %copy-start.116 = (f32[768]{0:T(1024)}, f32[768]{0:T(1024)S(1)}, u32[]{:S(2)}) copy-start(f32[768]{0:T(1024)S(1)} %get-tuple-element.24) | copy-start | bytes 9220
  139.0 54.7 %all-gather.66.cloned.1.call-start = ((), (), s32[]{:S(2)}) async-start(), calls=%async_computation.58 | async-start | bytes 1474560 | tf_op jit(solution)/shard_map/all_gather | solution.py:54
  139.6 121.2 %reduce-scatter.26.cloned.1.call-start = ((), (), s32[]{:S(2)}) async-start(), calls=%async_computation.23 | async-start | bytes 3932160 | tf_op jit(solution)/shard_map/reduce_scatter | solution.py:87
  200.4 113.2 %all-gather.38.cloned.1.call-start = ((), (), s32[]{:S(2)}) async-start(), calls=%async_computation.32 | async-start | bytes 1966080 | tf_op jit(solution)/shard_map/all_gather | solution.py:80
  262.8 11.4 collective-permute-start
  275.1 122.7 %reduce-scatter.36.cloned.1.call-start = ((), (), s32[]{:S(2)}) async-start(), calls=%async_computation.33 | async-start | bytes 3932160 | tf_op jit(solution)/shard_map/reduce_scatter | solution.py:87
  338.5 101.1 %all-gather.40.cloned.1.call-start = ((), (), s32[]{:S(2)}) async-start(), calls=%async_computation.34 | async-start | bytes 1966080 | tf_op jit(solution)/shard_map/all_gather | solution.py:80
  402.6 122.4 %reduce-scatter.38.cloned.1.call-start = ((), (), s32[]{:S(2)}) async-start(), calls=%async_computation.35 | async-start | bytes 3932160 | tf_op jit(solution)/shard_map/reduce_scatter | solution.py:87
  447.9 102.4 %all-gather.30.cloned.1.call-start = ((), (), s32[]{:S(2)}) async-start(), calls=%async_computation.24 | async-start | bytes 1966080 | tf_op jit(solution)/shard_map/all_gather | solution.py:80
  448.5 128.3 %all-gather.58.cloned.1.call-start = ((), (), s32[]{:S(2)}) async-start(), calls=%async_computation.52 | async-start | bytes 1966080 | tf_op jit(solution)/shard_map/all_gather | solution.py:80
  527.0 10.3 collective-permute-start.2
  538.3 76.1 %all-gather.42.cloned.1.call-start = ((), (), s32[]{:S(2)}) async-start(), calls=%async_computation.36 | async-start | bytes 1966080 | tf_op jit(solution)/shard_map/all_gather | solution.py:80
  539.1 112.9 %all-gather.50.cloned.1.call-start = ((), (), s32[]{:S(2)}) async-start(), calls=%async_computation.44 | async-start | bytes 1966080 | tf_op jit(solution)/shard_map/all_gather | solution.py:80
  539.9 202.1 %reduce-scatter.56.cloned.1.call-start = ((), (), s32[]{:S(2)}) async-start(), calls=%async_computation.53 | async-start | bytes 3932160 | tf_op jit(solution)/shard_map/reduce_scatter | solution.py:87
  682.8 131.6 %all-gather.60.cloned.1.call-start = ((), (), s32[]{:S(2)}) async-start(), calls=%async_computation.54 | async-start | bytes 1966080 | tf_op jit(solution)/shard_map/all_gather | solution.py:80
  746.9 87.8 %reduce-scatter.40.cloned.1.call-start = ((), (), s32[]{:S(2)}) async-start(), calls=%async_computation.37 | async-start | bytes 3932160 | tf_op jit(solution)/shard_map/reduce_scatter | solution.py:87
  760.1 137.1 %reduce-scatter.28.cloned.1.call-start = ((), (), s32[]{:S(2)}) async-start(), calls=%async_computation.25 | async-start | bytes 3932160 | tf_op jit(solution)/shard_map/reduce_scatter | solution.py:87
  776.9 182.9 %reduce-scatter.48.cloned.1.call-start = ((), (), s32[]{:S(2)}) async-start(), calls=%async_computation.45 | async-start | bytes 3932160 | tf_op jit(solution)/shard_map/reduce_scatter | solution.py:87
  791.0 231.1 %reduce-scatter.58.cloned.1.call-start = ((), (), s32[]{:S(2)}) async-start(), calls=%async_computation.55 | async-start | bytes 3932160 | tf_op jit(solution)/shard_map/reduce_scatter | solution.py:87
  822.2 240.9 %all-gather.52.cloned.1.call-start = ((), (), s32[]{:S(2)}) async-start(), calls=%async_computation.46 | async-start | bytes 1966080 | tf_op jit(solution)/shard_map/all_gather | solution.py:80
  1025.9 75.3 %all-gather.44.cloned.1.call-start = ((), (), s32[]{:S(2)}) async-start(), calls=%async_computation.38 | async-start | bytes 1966080 | tf_op jit(solution)/shard_map/all_gather | solution.py:80
  1026.6 112.6 %all-gather.32.cloned.1.call-start = ((), (), s32[]{:S(2)}) async-start(), calls=%async_computation.26 | async-start | bytes 1966080 | tf_op jit(solution)/shard_map/all_gather | solution.py:80
  1027.2 173.4 %reduce-scatter.50.cloned.1.call-start = ((), (), s32[]{:S(2)}) async-start(), calls=%async_computation.47 | async-start | bytes 3932160 | tf_op jit(solution)/shard_map/reduce_scatter | solution.py:87
  1074.8 188.3 %reduce-scatter.42.cloned.1.call-start = ((), (), s32[]{:S(2)}) async-start(), calls=%async_computation.39 | async-start | bytes 3932160 | tf_op jit(solution)/shard_map/reduce_scatter | solution.py:87
  1113.0 212.6 %reduce-scatter.30.cloned.1.call-start = ((), (), s32[]{:S(2)}) async-start(), calls=%async_computation.27 | async-start | bytes 3932160 | tf_op jit(solution)/shard_map/reduce_scatter | solution.py:87
  1151.3 220.0 %all-gather.34.cloned.1.call-start = ((), (), s32[]{:S(2)}) async-start(), calls=%async_computation.28 | async-start | bytes 1966080 | tf_op jit(solution)/shard_map/all_gather | solution.py:96
  1334.3 109.3 %reduce-scatter.32.cloned.1.call-start = ((), (), s32[]{:S(2)}) async-start(), calls=%async_computation.29 | async-start | bytes 3932160 | tf_op jit(solution)/shard_map/reduce_scatter | solution.py:107
  1384.3 100.8 %all-gather.36.cloned.1.call-start = ((), (), s32[]{:S(2)}) async-start(), calls=%async_computation.30 | async-start | bytes 1966080 | tf_op jit(solution)/shard_map/all_gather | solution.py:96
  1448.1 118.8 %reduce-scatter.34.cloned.1.call-start = ((), (), s32[]{:S(2)}) async-start(), calls=%async_computation.31 | async-start | bytes 3932160 | tf_op jit(solution)/shard_map/reduce_scatter | solution.py:107
  1507.7 121.4 %all-gather.46.cloned.1.call-start = ((), (), s32[]{:S(2)}) async-start(), calls=%async_computation.40 | async-start | bytes 1966080 | tf_op jit(solution)/shard_map/all_gather | solution.py:96
  1568.5 20.8 collective-permute-start.1
  1592.4 108.8 %reduce-scatter.44.cloned.1.call-start = ((), (), s32[]{:S(2)}) async-start(), calls=%async_computation.41 | async-start | bytes 3932160 | tf_op jit(solution)/shard_map/reduce_scatter | solution.py:107
  1642.0 99.7 %all-gather.48.cloned.1.call-start = ((), (), s32[]{:S(2)}) async-start(), calls=%async_computation.42 | async-start | bytes 1966080 | tf_op jit(solution)/shard_map/all_gather | solution.py:96
  1704.6 118.5 %reduce-scatter.46.cloned.1.call-start = ((), (), s32[]{:S(2)}) async-start(), calls=%async_computation.43 | async-start | bytes 3932160 | tf_op jit(solution)/shard_map/reduce_scatter | solution.py:107
  1764.0 120.1 %all-gather.54.cloned.1.call-start = ((), (), s32[]{:S(2)}) async-start(), calls=%async_computation.48 | async-start | bytes 1966080 | tf_op jit(solution)/shard_map/all_gather | solution.py:96
  1824.5 20.8 collective-permute-start.3
  1847.4 108.8 %reduce-scatter.52.cloned.1.call-start = ((), (), s32[]{:S(2)}) async-start(), calls=%async_computation.49 | async-start | bytes 3932160 | tf_op jit(solution)/shard_map/reduce_scatter | solution.py:107
  1896.9 99.8 %all-gather.56.cloned.1.call-start = ((), (), s32[]{:S(2)}) async-start(), calls=%async_computation.50 | async-start | bytes 1966080 | tf_op jit(solution)/shard_map/all_gather | solution.py:96
  1959.6 132.1 %all-reduce.12.cloned.1.call-start = ((), (), s32[]{:S(2)}) async-start(), calls=%async_computation.62 | async-start | bytes 9437184
  1982.7 177.3 %reduce-scatter.64.cloned.1.call-start = ((), (), s32[]{:S(2)}) async-start(), calls=%async_computation.61 | async-start | bytes 983040
  2017.3 164.1 %reduce-scatter.54.cloned.1.call-start = ((), (), s32[]{:S(2)}) async-start(), calls=%async_computation.51 | async-start | bytes 3932160 | tf_op jit(solution)/shard_map/reduce_scatter | solution.py:107
  2031.5 185.8 %reduce-scatter.62.cloned.1.call-start = ((), (), s32[]{:S(2)}) async-start(), calls=%async_computation.60 | async-start | bytes 2949120 | tf_op jit(solution)/shard_map/reduce_scatter | solution.py:65
  2040.4 212.9 %reduce-scatter.60.cloned.1.call-start = ((), (), s32[]{:S(2)}) async-start(), calls=%async_computation.59 | async-start | bytes 2949120 | tf_op jit(solution)/shard_map/reduce_scatter | solution.py:62
  (186 other events, 3376.2 us)
Sparse Core Ops, SparseCore 0:
  11.0 39.7 all-gather.61
  75.1 59.1 reduce-scatter.23
  275.2 38.3 all-gather.37
  338.6 59.1 reduce-scatter.35
  450.0 81.0 all-gather.29
  538.4 38.3 all-gather.57
  578.4 35.9 all-gather.41
  615.9 35.9 all-gather.49
  747.0 67.4 all-gather.59
  1026.0 36.9 all-gather.51
  1065.2 35.9 all-gather.43
  1103.2 35.9 all-gather.31
  1141.5 59.1 reduce-scatter.49
  1202.8 60.2 reduce-scatter.41
  1265.3 60.2 reduce-scatter.29
  1384.4 59.0 reduce-scatter.31
  1592.5 36.4 all-gather.45
  1642.1 59.0 reduce-scatter.43
  1847.6 36.4 all-gather.53
  1897.1 59.0 reduce-scatter.51
Sparse Core Ops, SparseCore 1:
  77.0 22.8 all-gather.63
  139.1 36.9 all-gather.27
  177.5 16.1 all-gather.65
  200.5 60.2 reduce-scatter.25
  402.7 36.9 all-gather.39
  448.0 76.9 reduce-scatter.37
  682.9 59.1 reduce-scatter.55
  760.2 74.4 reduce-scatter.39
  836.9 60.3 reduce-scatter.27
  899.5 60.1 reduce-scatter.47
  961.9 60.1 reduce-scatter.57
  1334.3 36.9 all-gather.33
  1448.2 36.9 all-gather.35
  1507.7 59.1 reduce-scatter.33
  1704.7 36.9 all-gather.47
  1764.0 59.1 reduce-scatter.45
  1959.7 36.9 all-gather.55
  1999.1 92.6 all-reduce.11
  2094.2 23.4 reduce-scatter.63
  2120.0 61.3 reduce-scatter.53
  2184.5 32.8 reduce-scatter.61
  2220.3 33.0 reduce-scatter.59
where the time goes:
time: 2270 us; the launch traced here: 2260 us
  waiting for transfers between devices  1660 us (73%)
  matrix products  285 us (13%)
  other arithmetic  102 us (4%)
  blocking collectives  96.5 us (4%)
  local copies, waits for them, and re-layouts  72.2 us (3%)
    reduce_scatter x12, waiting for transfers between devices, combine_out(): lax.psum_scatter(jnp.dot(full_low, weight, preferred_element_type=jnp.flo...  662 us
    reduce_scatter x6, waiting for transfers between devices, return_rows(): lax.psum_scatter(lax.dot_general(grads_low, weight_flat, (((1,), (1,)), (...  315 us
    all_gather x12, waiting for transfers between devices, project_in(): lax.all_gather(rows_low, 'tensor', axis=0, tiled=True)  313 us
    all_gather x6, waiting for transfers between devices, spread_back(): shard_rows = lax.all_gather(grads_low, 'tensor', axis=0, tiled=True)  197 us
    unnamed x1, blocking collectives  62.9 us
    unnamed x383, local copies, waits for them, and re-layouts  54.7 us
    ppermute x4, waiting for transfers between devices, from_behind(): lax.ppermute(value, axis, [(source, source + steps) for source in range(f...  54.4 us
    dot_general x12, matrix products, project_in(): jnp.dot(lax.all_gather(rows_low, 'tensor', axis=0, tiled=True), weight_fl...  46.4 us
  transfers between devices with their start and end apart: 46, of which 43 were waited for; matrix products, arithmetic and copies ran while one was open for 9% of the time, Pallas kernels for 0%

commit v1 on v0

v1 whole, which is shorter than its diff:
```python
import functools

import jax
import jax.numpy as jnp
from jax import lax
from jax.sharding import Mesh, PartitionSpec as P

HD = 64
eps = 1e-05
neg_fill = -1e30
ALL = ("y", "core", "tensor")
BF = jnp.bfloat16
F32 = jnp.float32


def layer_norm(resid, gain, shift):
    center = resid - jnp.mean(resid, axis=-1, keepdims=True)
    spread = jnp.mean(center * center, axis=-1, keepdims=True)
    return center * lax.rsqrt(spread + eps) * gain + shift


def gate_act(joined):
    return jax.nn.silu(joined[:, 0]) * joined[:, 1]


def rope_tables(positions, head_size):
    halfway = head_size // 2
    freqs = 1000.0 ** (-jnp.arange(halfway, dtype=F32) / halfway)
    angles = positions.astype(F32)[:, None] * freqs[None, :]
    return (jnp.cos(angles), jnp.sin(angles))


def rotate(values, tables, direction):
    halfway = values.shape[-1] // 2
    leading = values[..., :halfway]
    trailing = values[..., halfway:]
    cos_table = tables[0][:, None, :]
    sin_table = tables[1][:, None, :] * direction
    return jnp.concatenate(
        [leading * cos_table - trailing * sin_table, trailing * cos_table + leading * sin_table],
        axis=-1,
    )


def dot(a, b, dims=((1,), (0,))):
    return lax.dot_general(a, b, (dims, ((), ())), preferred_element_type=F32)


def gather_weights(w_qkv, w_out, w_gate_up, w_down, gains, biases, dp, tp):
    def whole(shard):
        return lax.all_gather(shard, ALL, axis=0, tiled=False).reshape((dp, tp) + shard.shape)

    joint = whole(w_qkv).transpose(0, 2, 3, 1, 4)
    joint = joint.reshape(joint.shape[0] * joint.shape[1], 3, -1)
    mix = whole(w_out).transpose(1, 2, 0, 3)
    mix = mix.reshape(mix.shape[0] * mix.shape[1], -1)
    pair = whole(w_gate_up).transpose(0, 2, 3, 1, 4)
    pair = pair.reshape(pair.shape[0] * pair.shape[1], 2, -1)
    back = whole(w_down).transpose(1, 2, 0, 3)
    back = back.reshape(back.shape[0] * back.shape[1], -1)
    gains = lax.all_gather(gains, ("y", "core"), axis=0, tiled=True).astype(F32).reshape(2, -1)
    biases = lax.all_gather(biases, ("y", "core"), axis=0, tiled=True).astype(F32).reshape(2, -1)
    return (joint, mix, pair, back, gains, biases)


def spread_grads(grads, dp, tp):
    joint, mix, pair, back, gains, biases = grads
    width = joint.shape[0]
    joint = joint.reshape(dp, width // dp, 3, tp, -1).transpose(0, 3, 1, 2, 4)
    mix = mix.reshape(tp, -1, dp, width // dp).transpose(2, 0, 1, 3)
    pair = pair.reshape(dp, width // dp, 2, tp, -1).transpose(0, 3, 1, 2, 4)
    back = back.reshape(tp, -1, dp, width // dp).transpose(2, 0, 1, 3)

    def scatter(parts, kind):
        shape = parts.shape[2:]
        flat = parts.reshape((dp * tp,) + shape).astype(kind)
        return lax.psum_scatter(flat, ALL, scatter_dimension=0, tiled=True).reshape(shape).astype(F32)

    def norm(parts):
        return lax.psum_scatter(parts, ALL, scatter_dimension=0, tiled=True)

    return (
        scatter(joint, BF),
        scatter(mix, BF),
        scatter(pair, BF),
        scatter(back, BF),
        norm(gains),
        norm(biases),
    )


def attend(queries, keys, values, allowed):
    scale = HD ** (-0.5)
    scores = jnp.einsum("qhd,khd->hqk", queries, keys, preferred_element_type=F32) * scale
    scores = jnp.where(allowed[None], scores, neg_fill)
    exps = jnp.exp(scores - jnp.max(scores, axis=-1, keepdims=True))
    probs = exps / jnp.sum(exps, axis=-1, keepdims=True)
    probs_low = probs.astype(BF)
    mixed = jnp.einsum("hqk,khd->qhd", probs_low, values, preferred_element_type=F32)
    return mixed.reshape(mixed.shape[0], -1).astype(BF), probs_low


def attend_back(queries, keys, values, probs, grad_mixed):
    scale = HD ** (-0.5)
    grad_mixed = grad_mixed.reshape(queries.shape)
    grad_probs = jnp.einsum("qhd,khd->hqk", grad_mixed, values, preferred_element_type=F32)
    wide = probs.astype(F32)
    inner = jnp.sum(wide * grad_probs, axis=-1, keepdims=True)
    grad_scores = (wide * (grad_probs - inner) * scale).astype(BF)
    grad_queries = jnp.einsum("hqk,khd->qhd", grad_scores, keys, preferred_element_type=F32)
    grad_keys = jnp.einsum("hqk,qhd->khd", grad_scores, queries, preferred_element_type=F32)
    grad_values = jnp.einsum("hqk,qhd->khd", probs, grad_mixed, preferred_element_type=F32)
    return (grad_queries, grad_keys, grad_values)


def layer_forward(inputs_low, weights, allowed, tables):
    w_joint, w_mix, w_pair, w_back, gains, shifts = weights
    rows, width = inputs_low.shape
    joined = dot(inputs_low, w_joint.reshape(width, -1)).reshape(rows, 3, -1, HD)
    queries = rotate(joined[:, 0], tables, 1.0).astype(BF)
    keys = rotate(joined[:, 1], tables, 1.0).astype(BF)
    values = joined[:, 2].astype(BF)
    keys, values = lax.all_gather(jnp.stack([keys, values]), "core", axis=1, tiled=True)
    mixed_low, probs = attend(queries, keys, values, allowed)
    first_sum = inputs_low.astype(F32) + dot(mixed_low, w_mix)
    hidden = layer_norm(first_sum, gains[0], shifts[0])
    hidden_low = hidden.astype(BF)
    gate_up = dot(hidden_low, w_pair.reshape(width, -1)).reshape(rows, 2, -1)
    active_low = gate_act(gate_up).astype(BF)
    second_sum = hidden + dot(active_low, w_back)
    result = layer_norm(second_sum, gains[1], shifts[1])
    kept = (
        inputs_low,
        queries,
        keys,
        values,
        mixed_low,
        probs,
        first_sum,
        hidden_low,
        gate_up,
        active_low,
        second_sum,
    )
    return (result, kept)


def layer_backward(grad_result, kept, weights, tables):
    w_joint, w_mix, w_pair, w_back, gains, shifts = weights
    inputs_low, queries, keys, values, mixed_low, probs, first_sum, hidden_low, gate_up, active_low, second_sum = kept
    rows, width = inputs_low.shape
    unused_out, norm_second = jax.vjp(layer_norm, second_sum, gains[1], shifts[1])
    grad_second, grad_gain_two, grad_shift_two = norm_second(grad_result)
    grad_ffn_low = grad_second.astype(BF)
    grad_active = dot(grad_ffn_low, w_back, ((1,), (1,)))
    grad_w_back = dot(active_low, grad_ffn_low, ((0,), (0,)))
    unused_act, act_back = jax.vjp(gate_act, gate_up)
    grad_pair_low = act_back(grad_active)[0].astype(BF).reshape(rows, -1)
    grad_hidden = grad_second + dot(grad_pair_low, w_pair.reshape(width, -1), ((1,), (1,)))
    grad_w_pair = dot(hidden_low, grad_pair_low, ((0,), (0,)))
    unused_first, norm_first = jax.vjp(layer_norm, first_sum, gains[0], shifts[0])
    grad_first, grad_gain_one, grad_shift_one = norm_first(grad_hidden)
    grad_attn_low = grad_first.astype(BF)
    grad_mixed = dot(grad_attn_low, w_mix, ((1,), (1,))).astype(BF)
    grad_w_mix = dot(mixed_low, grad_attn_low, ((0,), (0,)))
    grad_queries, grad_keys, grad_values = attend_back(queries, keys, values, probs, grad_mixed)
    both = jnp.stack([grad_keys, grad_values]).astype(BF)
    grad_keys, grad_values = lax.psum_scatter(both, "core", scatter_dimension=1, tiled=True).astype(F32)
    grad_queries = rotate(grad_queries, tables, -1.0)
    grad_keys = rotate(grad_keys, tables, -1.0)
    grad_joint_low = jnp.stack([grad_queries, grad_keys, grad_values], axis=1).reshape(rows, -1).astype(BF)
    grad_inputs = grad_first + dot(grad_joint_low, w_joint.reshape(width, -1), ((1,), (1,)))
    grad_w_joint = dot(inputs_low, grad_joint_low, ((0,), (0,)))
    grads = (
        grad_w_joint.reshape(w_joint.shape),
        grad_w_mix,
        grad_w_pair.reshape(w_pair.shape),
        grad_w_back,
        jnp.concatenate([grad_gain_one, grad_gain_two]),
        jnp.concatenate([grad_shift_one, grad_shift_two]),
    )
    return (grad_inputs, grads)


def swap_pairs(tp, step, dp_axes):
    pairs = []
    half = tp // 2
    for core in range(2):
        for at in range(tp):
            source = core * tp + at
            target = (at // half) * tp + half * core + (at + step) % half
            pairs.append((source, target))
    return pairs


def to_sequences(rows, tp):
    half = tp // 2
    at = lax.axis_index("tensor")
    pieces = [None] * half
    got = []
    for step in range(half):
        piece = lax.dynamic_index_in_dim(rows, (at + step) % half, 0, keepdims=False)
        got.append(lax.ppermute(piece, ("core", "tensor"), swap_pairs(tp, step, None)))
    stacked = jnp.stack(got)
    order = (at - jnp.arange(half)) % half
    return jnp.take(stacked, order, axis=0).reshape(-1, rows.shape[-1])


def to_positions(rows, tp):
    half = tp // 2
    at = lax.axis_index("tensor")
    parts = rows.reshape(half, -1, rows.shape[-1])
    got = []
    for step in range(half):
        piece = lax.dynamic_index_in_dim(parts, (at - step) % half, 0, keepdims=False)
        back = [(target, source) for source, target in swap_pairs(tp, step, None)]
        got.append(lax.ppermute(piece, ("core", "tensor"), back))
    stacked = jnp.stack(got)
    order = (at + jnp.arange(half)) % half
    return jnp.take(stacked, (jnp.arange(half) - at) % half, axis=0)


def on_device(dp, tp, tokens, cotangent, lengths, w_qkv, w_out, w_gate_up, w_down, norm_gains, norm_biases):
    section = lax.axis_index("section")
    core = lax.axis_index("core")
    at = lax.axis_index("tensor")
    micro, own, width = tokens.shape
    assert micro * 2 == tp
    length = own * tp
    rows = length // 2
    weights = gather_weights(
        w_qkv[0], w_out[0], w_gate_up[0], w_down[0], norm_gains[0], norm_biases[0], dp, tp
    )
    inputs = to_sequences(tokens, tp)
    grad_top = to_sequences(cotangent, tp)
    chip_lengths = lax.all_gather(lengths, "core", axis=0, tiled=True)
    my_lengths = lax.dynamic_index_in_dim(chip_lengths, at, 0, keepdims=False)
    positions = jnp.arange(length, dtype=jnp.int32)
    segment = jnp.sum((jnp.cumsum(my_lengths)[None, :] <= positions[:, None]).astype(jnp.int32), axis=-1)
    own_positions = core * rows + jnp.arange(rows, dtype=jnp.int32)
    own_segment = lax.dynamic_slice_in_dim(segment, core * rows, rows, 0)
    allowed = own_segment[:, None] == segment[None, :]
    tables = rope_tables(own_positions, HD)

    result, kept = layer_forward(inputs, weights, allowed, tables)
    received = lax.ppermute(result.astype(BF), "section", [(0, 1)])
    inputs = jnp.where(section == 0, inputs, received)
    result, kept = layer_forward(inputs, weights, allowed, tables)
    grad_in, grads = layer_backward(grad_top.astype(F32), kept, weights, tables)
    received = lax.ppermute(grad_in, "section", [(1, 0)])
    grad_top = jnp.where(section == 0, received, grad_top.astype(F32))
    grad_in, grads = layer_backward(grad_top, kept, weights, tables)
    ends = to_positions(jnp.where(section == 0, grad_in, result).astype(BF), tp)
    outs = spread_grads(grads, dp, tp)
    return (ends[None],) + tuple(o[None] for o in outs)


def solution(mesh):
    sections, dp, tp = mesh.devices.shape
    fine = Mesh(mesh.devices.reshape(sections, dp // 2, 2, tp), ("section", "y", "core", "tensor"))
    both = ("y", "core")
    in_specs = (
        P(both, "tensor", None),
        P(both, "tensor", None),
        P(both, None),
        P("section", both, None, "tensor"),
        P("section", "tensor", both),
        P("section", both, None, "tensor"),
        P("section", "tensor", both),
        P("section", both),
        P("section", both),
    )
    out_specs = (
        P("section", both, "tensor", None),
        P("section", both, None, "tensor"),
        P("section", "tensor", both),
        P("section", both, None, "tensor"),
        P("section", "tensor", both),
        P("section", ALL),
        P("section", ALL),
    )
    return jax.shard_map(
        functools.partial(on_device, dp, tp), mesh=fine, in_specs=in_specs, out_specs=out_specs, check_vma=False
    )
```

time: 2270 us -> 1110 us (0.49)
  waiting for transfers between devices: 1660 us -> 348 us
  local copies, waits for them, and re-layouts: 72.2 us -> 149 us
  other arithmetic: 102 us -> 145 us
  matrix products: 285 us -> 321 us
    reduce_scatter x20 -> x6, waiting for transfers between devices: 1050 us -> 154 us  [the longest x4 154 us: scatter(): lax.psum_scatter(flat, ALL, scatter_dimension=0, tiled=True).reshape(shape)]
    all_gather x20 -> x6, waiting for transfers between devices: 520 us -> 116 us  [the longest x4 101 us: whole(): lax.all_gather(shard, ALL, axis=0, tiled=False)]
    dot_general x90 -> x32, matrix products: 249 us -> 321 us  [the longest x20 120 us: dot(): return lax.dot_general(a, b, (dims, ((), ())), preferred_element_type=F32)]
    sub x0 -> x2, other arithmetic: none -> 69.1 us  [attend(): exps = jnp.exp(scores - jnp.max(scores, axis=-1, keepdims=True))]
    unnamed x44 -> x12, waiting for transfers between devices: 42.2 us -> 2.2 us
    convert_element_type x0 -> x10, local copies, waits for them, and re-layouts: none -> 36.9 us  [the longest x2 17.3 us: layer_backward(): grad_pair_low = act_back(grad_active)[0].astype(BF).reshape(rows, -1)]
    sub x6 -> x0, matrix products: 36 us -> none  [attend(): exps = jnp.exp(scores - highest)]
    unnamed x383 -> x154, local copies, waits for them, and re-layouts: 54.7 us -> 21 us
  transfers between devices with their start and end apart: 46 -> 20, of which waited for: 43 -> 11; matrix products, arithmetic and copies ran while one was open for 9% -> 22% of each run, Pallas kernels for 0% -> 0%
where the time goes in v1:
time: 1110 us; the launch traced here: 1100 us
  waiting for transfers between devices  348 us (31%)
  matrix products  321 us (29%)
  local copies, waits for them, and re-layouts  149 us (13%)
  other arithmetic  145 us (13%)
  blocking collectives  105 us (9%)
  between operations  16.4 us (1%)
  starting transfers between devices  13.2 us (1%)
    reduce_scatter x4, waiting for transfers between devices, scatter(): lax.psum_scatter(flat, ALL, scatter_dimension=0, tiled=True).reshape(shape)  154 us
    dot_general x20, matrix products, dot(): return lax.dot_general(a, b, (dims, ((), ())), preferred_element_type=F32)  120 us
    all_gather x4, waiting for transfers between devices, whole(): lax.all_gather(shard, ALL, axis=0, tiled=False)  101 us
    unnamed x1, blocking collectives  91.8 us
    sub x2, other arithmetic, attend(): exps = jnp.exp(scores - jnp.max(scores, axis=-1, keepdims=True))  69.1 us
    dot_general x2, matrix products, attend_back(): jnp.einsum('hqk,qhd->khd', grad_scores, queries, preferred_element_type=F32)  59.3 us
    dot_general x2, matrix products, attend_back(): jnp.einsum('hqk,khd->qhd', grad_scores, keys, preferred_element_type=F32)  58.7 us
    ppermute x1, waiting for transfers between devices, on_device(): received = lax.ppermute(grad_in, 'section', [(1, 0)])  37.1 us
  transfers between devices with their start and end apart: 20, of which 11 were waited for; matrix products, arithmetic and copies ran while one was open for 22% of the time, Pallas kernels for 0%

profile of v1, /device:TPU:0, one launch (start us, length us, event | category | flops | bytes accessed | tf_op | source)
XLA Modules:
  0.0 1097.8 jit_solution(5728554367222828150)
XLA Ops:
  16.3 6.9 collective-permute-done.1
  23.9 16.0 %collective-permute-done.3 = bf16[256,768]{1,0:T(8,128)(2,1)} collective-permute-done((bf16[256,768]{1,0:T(8,128)(2,1)S(1)}, bf16[256,768]{1,0:T(8,128)(2,1)}, u32[]{:S(2)}, u32[]{:S(2)}) %collective-permute-start.3) | collective-permute-done | bytes 393248 | tf_op jit(solution)/shard_map/ppermute | solution.py:203
  43.0 34.7 %all-gather.10.cloned.1.call-done = bf16[16,192,3,192]{3,1,2,0:T(8,128)(2,1)} async-done(((bf16[1,192,3,192]{3,1,2,0:T(8,128)(2,1)}), bf16[16,192,3,192]{3,1,2,0:T(8,128)(2,1)}) %all-gather.10.cloned.1.call-update) | async-done | bytes 3538960 | tf_op jit(solution)/shard_map/all_gather | solution.py:51
  77.6 9.7 copy.66
  87.3 7.7 reshape_reshape.4
  113.8 5.3 all-gather.1
  130.2 44.3 %all-gather.18.cloned.1.call-done = bf16[16,768,192]{1,2,0:T(8,128)(2,1)} async-done(((bf16[1,768,192]{1,2,0:T(8,128)(2,1)}), bf16[16,768,192]{1,2,0:T(8,128)(2,1)}) %all-gather.18.cloned.1.call-update) | async-done | bytes 4718608 | tf_op jit(solution)/shard_map/all_gather | solution.py:51
  174.4 6.0 copy.71
  186.5 14.0 %fusion.45 = f32[12,512,1024]{2,1,0:T(8,128)} fusion(bf16[2,1024,12,64]{1,3,2,0:T(8,128)(2,1)} %all-gather.12.cloned.1.call-done, bf16[512,12,32]{0,2,1:T(8,128)(2,1)} %get-tuple-element.75, bf16[512,12,32]{0,2,1:T(8,128)(2,1)} %get-tuple-element.74), kind=kOutput, calls=%fused_computation.96 | convolution fusion | flops 806879232 | bytes 27525120 | tf_op jit(solution)/shard_map/qhd,khd->hqk/dot_general | solution.py:94
  200.6 35.1 %fusion.125 = (f32[12,512]{1,0:T(8,128)}, f32[12,512,1024]{2,1,0:T(8,128)}) fusion(f32[12,512,1024]{2,1,0:T(8,128)} %fusion.45, pred[512,1024]{1,0:T(8,128)(4,1)} %broadcast_compare_fusion), kind=kOutput, calls=%fused_computation.284 | output fusion | flops 37749760 | bytes 50880512 | tf_op jit(solution)/shard_map/sub | solution.py:96
  235.7 11.1 %fusion.59 = bf16[12,64,512]{2,1,0:T(8,128)(2,1)S(1)} fusion(f32[12,512,1024]{2,1,0:T(8,128)} %get-tuple-element.103, f32[12,512]{1,0:T(8,128)} %get-tuple-element.102, bf16[2,1024,12,64]{1,3,2,0:T(8,128)(2,1)} %all-gather.12.cloned.1.call-done), kind=kOutput, calls=%fused_computation.137 | convolution fusion | flops 818282496 | bytes 27557888 | tf_op jit(solution)/shard_map/hqk,khd->qhd/dot_general | solution.py:99
  249.7 22.2 %all-gather.16.cloned.1.call-done = bf16[16,192,2,768]{3,1,2,0:T(8,128)(2,1)} async-done(((bf16[1,192,2,768]{3,1,2,0:T(8,128)(2,1)}), bf16[16,192,2,768]{3,1,2,0:T(8,128)(2,1)}) %all-gather.16.cloned.1.call-update) | async-done | bytes 9437200 | tf_op jit(solution)/shard_map/all_gather | solution.py:51
  271.9 12.4 %copy.96 = bf16[4,4,192,2,768]{4,1,3,2,0:T(4,128)(2,1)} copy(bf16[4,4,192,2,768]{4,2,3,1,0:T(8,128)(2,1)} %bitcast.363) | data formatting | bytes 18874368 | tf_op jit(solution)/shard_map/reshape | solution.py:51
  284.3 15.2 %reshape_reshape.5 = bf16[768,6144]{1,0:T(8,128)(2,1)} reshape(bf16[4,192,2,4,768]{4,3,2,1,0:T(4,128)(2,1)} %bitcast.348) | data formatting | bytes 18874368 | tf_op jit(solution)/shard_map/reshape;reshape | solution.py:128
  299.5 12.6 %copy.70 = bf16[6144,768]{1,0:T(8,128)(2,1)} copy(bf16[6144,768]{0,1:T(8,128)(2,1)} %bitcast.346) | data formatting | bytes 18874368 | tf_op jit(solution)/shard_map/dot_general | solution.py:46
  312.1 9.8 fusion.68
  322.0 6.1 fusion.127
  333.9 16.6 %collective-permute-done.4 = bf16[512,768]{1,0:T(8,128)(2,1)} collective-permute-done((bf16[512,768]{1,0:T(8,128)(2,1)}, bf16[512,768]{1,0:T(8,128)(2,1)}, u32[]{:S(2)}, u32[]{:S(2)}) %collective-permute-start.4) | collective-permute-done | bytes 786464 | tf_op jit(solution)/shard_map/ppermute | solution.py:246
  357.8 11.6 %all-gather.20.cloned.1.call-done = bf16[2,1024,12,64]{1,3,2,0:T(8,128)(2,1)} async-done(((bf16[2,512,12,64]{1,3,2,0:T(8,128)(2,1)}), bf16[2,1024,12,64]{1,3,2,0:T(8,128)(2,1)}) %all-gather.20.cloned.1.call-update) | async-done | bytes 3145744 | tf_op jit(solution)/shard_map/all_gather | solution.py:123
  369.4 11.7 %fusion.64 = f32[12,512,1024]{2,1,0:T(8,128)} fusion(bf16[2,1024,12,64]{1,3,2,0:T(8,128)(2,1)} %all-gather.20.cloned.1.call-done, bf16[512,12,32]{0,2,1:T(8,128)(2,1)S(1)} %get-tuple-element.71, bf16[512,12,32]{0,2,1:T(8,128)(2,1)S(1)} %get-tuple-element.70), kind=kOutput, calls=%fused_computation.145 | convolution fusion | flops 806879232 | bytes 27525120 | tf_op jit(solution)/shard_map/qhd,khd->hqk/dot_general | solution.py:94
  381.0 33.9 %fusion.128 = (f32[12,512]{1,0:T(8,128)}, f32[12,512,1024]{2,1,0:T(8,128)}) fusion(f32[12,512,1024]{2,1,0:T(8,128)} %fusion.64, pred[512,1024]{1,0:T(8,128)(4,1)S(1)} %copy-done.40), kind=kOutput, calls=%fused_computation.287 | output fusion | flops 37749760 | bytes 50880512 | tf_op jit(solution)/shard_map/sub | solution.py:96
  415.0 14.1 %divide_convert_fusion = bf16[12,512,1024]{2,1,0:T(8,128)(2,1)} fusion(f32[12,512,1024]{2,1,0:T(8,128)} %get-tuple-element.109, f32[12,512]{1,0:T(8,128)} %get-tuple-element.108), kind=kLoop, calls=%fused_computation.15 | loop fusion | flops 12582912 | bytes 37773312 | tf_op jit(solution)/shard_map/convert_element_type | solution.py:98
  429.1 9.6 convolution_convert_fusion.5
  442.0 8.2 fusion.79
  450.2 8.3 fusion.129
  459.9 10.9 multiply_bitcast_fusion.1
  470.9 8.2 add_convert_fusion.1
  479.1 8.7 copy.72
  487.8 11.4 %multiply_reduce_fusion.4 = (f32[512]{0:T(512)S(1)}, f32[512,768]{1,0:T(8,128)S(1)}) fusion(f32[512,768]{1,0:T(8,128)} %copy-done.8, f32[768]{0:T(1024)} %get-tuple-element.38, bf16[512,6144]{0,1:T(8,128)(2,1)} %bitcast.367, bf16[768,6144]{1,0:T(8,128)(2,1)} %reshape_reshape.5, f32[512,768]{1,0:T(8,128)} %copy-done.29, f32[512]{0:T(512)} %copy-done.63), kind=kOutput, calls=%fused_computation.111 | convolution fusion | flops 4833803776 | bytes 20454400 | tf_op jit(solution)/shard_map/dot_general | solution.py:46
  504.9 8.3 fusion.46
  513.2 10.1 fusion.63
  523.3 29.5 %fusion.49 = bf16[1,1024,12,64]{1,3,2,0:T(8,128)(2,1)} fusion(bf16[12,512,1024]{2,1,0:T(8,128)(2,1)} %divide_convert_fusion, f32[12,512,1024]{2,1,0:T(8,128)} %fusion.63, bf16[512,12,32]{0,2,1:T(8,128)(2,1)} %copy-done.26, bf16[512,12,32]{0,2,1:T(8,128)(2,1)S(1)} %get-tuple-element.70), kind=kOutput, calls=%fused_computation.125 | convolution fusion | flops 851713024 | bytes 40108032 | tf_op jit(solution)/shard_map/hqk,qhd->khd/dot_general | solution.py:111
  556.7 29.2 %fusion.52 = f32[512,12,64]{0,2,1:T(8,128)} fusion(bf16[12,512,1024]{2,1,0:T(8,128)(2,1)} %divide_convert_fusion, f32[12,512,1024]{2,1,0:T(8,128)} %fusion.63, bf16[2,1024,12,64]{1,3,2,0:T(8,128)(2,1)S(1)} %copy-done), kind=kOutput, calls=%fused_computation.128 | convolution fusion | flops 849353728 | bytes 78643200 | tf_op jit(solution)/shard_map/hqk,khd->qhd/dot_general | solution.py:110
  594.7 37.1 %collective-permute-done.5 = f32[512,768]{1,0:T(8,128)S(1)} collective-permute-done((f32[512,768]{1,0:T(8,128)S(1)}, f32[512,768]{1,0:T(8,128)S(1)}, u32[]{:S(2)}, u32[]{:S(2)}) %collective-permute-start.5) | collective-permute-done | bytes 1572896 | tf_op jit(solution)/shard_map/ppermute | solution.py:250
  634.0 11.7 %multiply_bitcast_fusion = (f32[512,1,3072]{2,0,1:T(8,128)}, f32[512,1,3072]{2,0,1:T(8,128)}, bf16[3072,512]{0,1:T(8,128)(2,1)}) fusion(f32[512,2,3072]{2,0,1:T(8,128)} %fusion.79, bf16[3072,768]{0,1:T(8,128)(2,1)S(1)} %bitcast.377, f32[512,768]{1,0:T(8,128)S(1)} %get-tuple-element.46, f32[512]{0:T(512)S(1)} %negate_multiply_fusion.1), kind=kOutput, calls=%fused_computation.60 | convolution fusion | flops 2438725632 | bytes 34605056 | tf_op jit(solution)/shard_map/dot_general | solution.py:46
  645.7 8.2 add_convert_fusion
  653.9 8.7 copy.74
  662.6 12.9 %multiply_reduce_fusion.1 = (f32[768]{0:T(1024)}, f32[512]{0:T(512)S(1)}, f32[768]{0:T(1024)}, f32[512,768]{1,0:T(8,128)S(1)}) fusion(f32[512,768]{1,0:T(8,128)} %copy-done.8, f32[512]{0:T(512)S(1)} %copy-done.43, f32[768]{0:T(1024)S(1)} %copy-done.49, bf16[512,6144]{0,1:T(8,128)(2,1)} %bitcast.365, bf16[768,6144]{1,0:T(8,128)(2,1)} %reshape_reshape.5, ...), kind=kOutput, calls=%fused_computation.107 | convolution fusion | flops 4835375104 | bytes 20462592 | tf_op jit(solution)/shard_map/dot_general | solution.py:46
  682.2 8.3 fusion.47
  690.6 10.1 fusion.62
  700.7 29.8 %fusion.50 = bf16[1,1024,12,64]{1,3,2,0:T(8,128)(2,1)} fusion(bf16[12,512,1024]{2,1,0:T(8,128)(2,1)} %divide_convert_fusion, f32[12,512,1024]{2,1,0:T(8,128)} %fusion.62, bf16[512,12,32]{0,2,1:T(8,128)(2,1)} %copy-done.26, bf16[512,12,32]{0,2,1:T(8,128)(2,1)} %copy-done.25), kind=kOutput, calls=%fused_computation.126 | convolution fusion | flops 851713024 | bytes 40108032 | tf_op jit(solution)/shard_map/hqk,qhd->khd/dot_general | solution.py:111
  762.0 29.5 %fusion.51 = f32[512,12,64]{0,2,1:T(8,128)} fusion(bf16[12,512,1024]{2,1,0:T(8,128)(2,1)} %divide_convert_fusion, f32[12,512,1024]{2,1,0:T(8,128)} %fusion.62, bf16[2,1024,12,64]{1,3,2,0:T(8,128)(2,1)S(1)} %copy-done), kind=kOutput, calls=%fused_computation.127 | convolution fusion | flops 849353728 | bytes 78643200 | tf_op jit(solution)/shard_map/hqk,khd->qhd/dot_general | solution.py:110
  804.0 10.4 convert_bitcast_fusion
  814.4 8.4 copy.81
  826.0 5.2 select_convert_fusion
  834.0 91.8 %all-reduce.6 = (f32[1536]{0:T(1024)S(1)}, f32[1536]{0:T(1024)S(1)}) all-reduce(f32[1536]{0:T(1024)S(1)} %pad_maximum_fusion.12, f32[1536]{0:T(1024)S(1)} %pad_maximum_fusion.13), channel_id=10, replica_groups=mesh['section'=2,'y'=2,'core'=2,'tensor'=4] {'y','core','tensor'}, use_global_device_ids=true, to_apply=%region_32.34.clone | all-reduce | flops 3072 | bytes 24576
  932.2 40.7 %reduce-scatter.11.cloned.1.call-done = bf16[1,192,3,192]{3,1,2,0:T(8,128)(2,1)} async-done(((bf16[16,192,3,192]{3,1,2,0:T(8,128)(2,1)}), bf16[1,192,3,192]{3,1,2,0:T(8,128)(2,1)}) %reduce-scatter.11.cloned.1.call-update) | async-done | bytes 221200 | tf_op jit(solution)/shard_map/reduce_scatter | solution.py:77
  974.7 113.1 %reduce-scatter.15.cloned.1.call-done = bf16[1,192,2,768]{3,1,2,0:T(8,128)(2,1)} async-done(((bf16[16,192,2,768]{3,1,2,0:T(8,128)(2,1)}), bf16[1,192,2,768]{3,1,2,0:T(8,128)(2,1)}) %reduce-scatter.15.cloned.1.call-update) | async-done | bytes 589840 | tf_op jit(solution)/shard_map/reduce_scatter | solution.py:77
  (308 shorter events, 156.2 us)
Async XLA Ops:
  7.2 70.5 %all-gather.10.cloned.1.call-start = ((), (), s32[]{:S(2)}) async-start(), calls=%async_computation.6 | async-start | bytes 5013504 | tf_op jit(solution)/shard_map/all_gather | solution.py:51
  7.9 114.5 %all-gather.14.cloned.1.call-start = ((), (), s32[]{:S(2)}) async-start(), calls=%async_computation.8 | async-start | bytes 1671168 | tf_op jit(solution)/shard_map/all_gather | solution.py:51
  8.7 165.8 %all-gather.18.cloned.1.call-start = ((), (), s32[]{:S(2)}) async-start(), calls=%async_computation.10 | async-start | bytes 5013504 | tf_op jit(solution)/shard_map/all_gather | solution.py:51
  9.4 177.1 %all-gather.12.cloned.1.call-start = ((), (), s32[]{:S(2)}) async-start(), calls=%async_computation.7 | async-start | bytes 4718592 | tf_op jit(solution)/shard_map/all_gather | solution.py:123
  10.6 5.7 collective-permute-start
  11.3 11.9 %collective-permute-start.1 = (bf16[256,768]{1,0:T(8,128)(2,1)S(1)}, bf16[256,768]{1,0:T(8,128)(2,1)S(1)}, u32[]{:S(2)}, u32[]{:S(2)}) collective-permute-start(bf16[256,768]{1,0:T(8,128)(2,1)S(1)} %get-tuple-element.84), channel_id=1, source_target_pairs={{0,1},{1,0},{2,5},{3,4},{4,3},{5,2},{6,7},{7,6},{8,9},{9,8},{10,13... | collective-permute-start | bytes 1179656 | tf_op jit(solution)/shard_map/ppermute | solution.py:203
  14.5 9.4 collective-permute-start.2
  15.2 24.8 %collective-permute-start.3 = (bf16[256,768]{1,0:T(8,128)(2,1)S(1)}, bf16[256,768]{1,0:T(8,128)(2,1)}, u32[]{:S(2)}, u32[]{:S(2)}) collective-permute-start(bf16[256,768]{1,0:T(8,128)(2,1)S(1)} %get-tuple-element.86), channel_id=1, source_target_pairs={{0,1},{1,0},{2,5},{3,4},{4,3},{5,2},{6,7},{7,6},{8,9},{9,8},{10,13... | collective-permute-start | bytes 1179656 | tf_op jit(solution)/shard_map/ppermute | solution.py:203
  95.0 256.7 %copy-start.1 = (bf16[768,2304]{0,1:T(8,128)(2,1)}, bf16[768,2304]{0,1:T(8,128)(2,1)S(1)}, u32[]{:S(2)}) copy-start(bf16[768,2304]{0,1:T(8,128)(2,1)S(1)} %reshape_reshape.4) | copy-start | bytes 10616836
  102.7 11.1 %copy-start.65 = (bf16[1,384]{1,0:T(2,128)(2,1)S(1)}, bf16[1,384]{1,0:T(2,128)(2,1)}, u32[]{:S(2)}) copy-start(bf16[1,384]{1,0:T(2,128)(2,1)} %param.19) | copy-start | bytes 2308
  102.7 169.2 %all-gather.16.cloned.1.call-start = ((), (), s32[]{:S(2)}) async-start(), calls=%async_computation.9 | async-start | bytes 10027008 | tf_op jit(solution)/shard_map/all_gather | solution.py:51
  104.7 264.7 %all-gather.20.cloned.1.call-start = ((), (), s32[]{:S(2)}) async-start(), calls=%async_computation.11 | async-start | bytes 4718592 | tf_op jit(solution)/shard_map/all_gather | solution.py:123
  121.2 207.2 %copy-start.46 = (f32[768]{0:T(1024)}, f32[768]{0:T(1024)S(1)}, u32[]{:S(2)}) copy-start(f32[768]{0:T(1024)S(1)} %get-tuple-element.39) | copy-start | bytes 9220
  235.7 11.1 %copy-start.19 = (bf16[2,256,768]{2,1,0:T(8,128)(2,1)S(1)}, bf16[2,256,768]{2,1,0:T(8,128)(2,1)}, u32[]{:S(2)}) copy-start(bf16[2,256,768]{2,1,0:T(8,128)(2,1)} %get-tuple-element.101) | copy-start | bytes 2359300
  235.7 11.1 %copy-start.32 = (bf16[768,768]{1,0:T(8,128)(2,1)S(1)}, bf16[768,768]{1,0:T(8,128)(2,1)}, u32[]{:S(2)}) copy-start(bf16[768,768]{1,0:T(8,128)(2,1)} %reshape.454) | copy-start | bytes 3538948
  247.7 36.6 %copy-start.55 = (f32[512]{0:T(512)}, f32[512]{0:T(512)S(1)}, u32[]{:S(2)}) copy-start(f32[512]{0:T(512)S(1)} %broadcast_multiply_fusion.4) | copy-start | bytes 6148
  299.5 12.6 %copy-start.48 = (f32[768]{0:T(1024)S(1)}, f32[768]{0:T(1024)}, u32[]{:S(2)}) copy-start(f32[768]{0:T(1024)} %get-tuple-element.38) | copy-start | bytes 9220
  299.5 12.6 %copy-start.50 = (f32[768]{0:T(1024)S(1)}, f32[768]{0:T(1024)}, u32[]{:S(2)}) copy-start(f32[768]{0:T(1024)} %get-tuple-element.40) | copy-start | bytes 9220
  329.6 20.9 %collective-permute-start.4 = (bf16[512,768]{1,0:T(8,128)(2,1)}, bf16[512,768]{1,0:T(8,128)(2,1)}, u32[]{:S(2)}, u32[]{:S(2)}) collective-permute-start(bf16[512,768]{1,0:T(8,128)(2,1)} %add_convert_fusion.2), channel_id=1, source_target_pairs={{0,16},{1,17},{2,18},{3,19},{4,20},{5,21},{6,22},{7,23},{8,24},{9,... | collective-permute-start | bytes 2359304 | tf_op jit(solution)/shard_map/ppermute | solution.py:246
  356.3 13.1 %copy-start.26 = (bf16[512,12,32]{0,2,1:T(8,128)(2,1)}, bf16[512,12,32]{0,2,1:T(8,128)(2,1)S(1)}, u32[]{:S(2)}) copy-start(bf16[512,12,32]{0,2,1:T(8,128)(2,1)S(1)} %get-tuple-element.71) | copy-start | bytes 1179652
  356.3 167.1 %copy-start.25 = (bf16[512,12,32]{0,2,1:T(8,128)(2,1)}, bf16[512,12,32]{0,2,1:T(8,128)(2,1)S(1)}, u32[]{:S(2)}) copy-start(bf16[512,12,32]{0,2,1:T(8,128)(2,1)S(1)} %get-tuple-element.70) | copy-start | bytes 1179652
  357.7 228.2 %reduce-scatter.7.cloned.1.call-start = ((), (), s32[]{:S(2)}) async-start(), calls=%async_computation.12 | async-start | bytes 4718592 | tf_op jit(solution)/shard_map/reduce_scatter | solution.py:168
  369.4 11.7 %copy-start.40 = (pred[512,1024]{1,0:T(8,128)(4,1)S(1)}, pred[512,1024]{1,0:T(8,128)(4,1)}, u32[]{:S(2)}) copy-start(pred[512,1024]{1,0:T(8,128)(4,1)} %broadcast_compare_fusion) | copy-start | bytes 1572868
  415.0 14.1 %copy-start = (bf16[2,1024,12,64]{1,3,2,0:T(8,128)(2,1)S(1)}, bf16[2,1024,12,64]{1,3,2,0:T(8,128)(2,1)}, u32[]{:S(2)}) copy-start(bf16[2,1024,12,64]{1,3,2,0:T(8,128)(2,1)} %all-gather.20.cloned.1.call-done) | copy-start | bytes 9437188
  429.1 12.6 %slice-start = ((s8[9437184]{0:T(1024)(128)(4,1)}), s8[1048576]{0:T(1024)(128)(4,1)S(1)}, s32[]{:S(2)}) async-start(s8[9437184]{0:T(1024)(128)(4,1)} %bitcast.360), calls=%async_computation.18 | async-start | bytes 2097152
  429.1 12.6 %slice-start.1 = ((s8[9437184]{0:T(1024)(128)(4,1)}), s8[4194304]{0:T(1024)(128)(4,1)S(1)}, s32[]{:S(2)}) async-start(s8[9437184]{0:T(1024)(128)(4,1)} %bitcast.360), calls=%async_computation.19 | async-start | bytes 8388608
  442.0 17.9 %slice-start.3 = ((s8[4718592]{0:T(1024)(128)(4,1)}), s8[524288]{0:T(1024)(128)(4,1)S(1)}, s32[]{:S(2)}) async-start(s8[4718592]{0:T(1024)(128)(4,1)} %bitcast.372), calls=%async_computation.21 | async-start | bytes 1048576
  459.1 11.7 %copy-start.44 = (f32[512]{0:T(512)}, f32[512]{0:T(512)S(1)}, u32[]{:S(2)}) copy-start(f32[512]{0:T(512)S(1)} %get-tuple-element.34) | copy-start | bytes 6148
  487.8 11.4 %copy-start.9 = (f32[512,768]{1,0:T(8,128)S(1)}, f32[512,768]{1,0:T(8,128)}, u32[]{:S(2)}) copy-start(f32[512,768]{1,0:T(8,128)} %copy-done.8) | copy-start | bytes 4718596
  487.8 11.4 %copy-start.42 = (f32[512]{0:T(512)S(1)}, f32[512]{0:T(512)}, u32[]{:S(2)}) copy-start(f32[512]{0:T(512)} %copy-done.41) | copy-start | bytes 6148
  556.6 234.9 %reduce-scatter.9.cloned.1.call-start = ((), (), s32[]{:S(2)}) async-start(), calls=%async_computation.13 | async-start | bytes 4718592 | tf_op jit(solution)/shard_map/reduce_scatter | solution.py:168
  587.9 46.1 %slice-start.5 = ((s8[4718592]{0:T(1024)(128)(4,1)}), s8[4194304]{0:T(1024)(128)(4,1)S(1)}, s32[]{:S(2)}) async-start(s8[4718592]{0:T(1024)(128)(4,1)} %bitcast.375), calls=%async_computation.23 | async-start | bytes 8388608
  591.2 40.6 %copy-start.5 = (f32[512,768]{1,0:T(8,128)S(1)}, f32[512,768]{1,0:T(8,128)}, u32[]{:S(2)}) copy-start(f32[512,768]{1,0:T(8,128)} %copy-done.4) | copy-start | bytes 4718596
  591.2 40.6 %copy-start.7 = (bf16[2,256,768]{2,1,0:T(8,128)(2,1)S(1)}, bf16[2,256,768]{2,1,0:T(8,128)(2,1)}, u32[]{:S(2)}) copy-start(bf16[2,256,768]{2,1,0:T(8,128)(2,1)} %get-tuple-element.100) | copy-start | bytes 2359300
  591.2 42.8 %slice-start.6 = ((s8[4718592]{0:T(1024)(128)(4,1)}), s8[524288]{0:T(1024)(128)(4,1)S(1)}, s32[]{:S(2)}) async-start(s8[4718592]{0:T(1024)(128)(4,1)} %bitcast.375), calls=%async_computation.24 | async-start | bytes 1048576
  593.3 39.8 %copy-start.45 = (f32[512]{0:T(512)S(1)}, f32[512]{0:T(512)}, u32[]{:S(2)}) copy-start(f32[512]{0:T(512)} %copy-done.44) | copy-start | bytes 6148
  593.4 38.4 %collective-permute-start.5 = (f32[512,768]{1,0:T(8,128)S(1)}, f32[512,768]{1,0:T(8,128)S(1)}, u32[]{:S(2)}, u32[]{:S(2)}) collective-permute-start(f32[512,768]{1,0:T(8,128)S(1)} %add_add_fusion.5), channel_id=1, source_target_pairs={{16,0},{17,1},{18,2},{19,3},{20,4},{21,5},{22,6},{23,7},{24,8},{25... | collective-permute-start | bytes 4718600 | tf_op jit(solution)/shard_map/ppermute | solution.py:250
  634.0 11.7 %copy-start.16 = (f32[512,768]{1,0:T(8,128)}, f32[512,768]{1,0:T(8,128)S(1)}, u32[]{:S(2)}) copy-start(f32[512,768]{1,0:T(8,128)S(1)} %get-tuple-element.46) | copy-start | bytes 4718596
  662.6 12.9 %copy-start.10 = (f32[512,768]{1,0:T(8,128)S(1)}, f32[512,768]{1,0:T(8,128)}, u32[]{:S(2)}) copy-start(f32[512,768]{1,0:T(8,128)} %copy-done.8) | copy-start | bytes 4718596
  662.6 12.9 %copy-start.52 = (f32[768]{0:T(1024)S(1)}, f32[768]{0:T(1024)}, u32[]{:S(2)}) copy-start(f32[768]{0:T(1024)} %get-tuple-element.40) | copy-start | bytes 9220
  677.1 57.3 %copy-start.57 = (f32[512]{0:T(512)}, f32[512]{0:T(512)S(1)}, u32[]{:S(2)}) copy-start(f32[512]{0:T(512)S(1)} %negate_multiply_fusion) | copy-start | bytes 6148
  734.3 192.6 %reduce-scatter.13.cloned.1.call-start = ((), (), s32[]{:S(2)}) async-start(), calls=%async_computation.15 | async-start | bytes 1671168 | tf_op jit(solution)/shard_map/reduce_scatter | solution.py:77
  742.8 187.6 %reduce-scatter.17.cloned.1.call-start = ((), (), s32[]{:S(2)}) async-start(), calls=%async_computation.17 | async-start | bytes 5013504 | tf_op jit(solution)/shard_map/reduce_scatter | solution.py:77
  759.7 213.2 %reduce-scatter.11.cloned.1.call-start = ((), (), s32[]{:S(2)}) async-start(), calls=%async_computation.14 | async-start | bytes 5013504 | tf_op jit(solution)/shard_map/reduce_scatter | solution.py:77
  802.6 285.2 %reduce-scatter.15.cloned.1.call-start = ((), (), s32[]{:S(2)}) async-start(), calls=%async_computation.16 | async-start | bytes 10027008 | tf_op jit(solution)/shard_map/reduce_scatter | solution.py:77
  831.2 98.1 %copy-start.67 = (pred[2]{0:T(512)(128)(4,1)S(1)}, pred[2]{0:T(512)(128)(4,1)}, u32[]{:S(2)}) copy-start(pred[2]{0:T(512)(128)(4,1)} %compare_and_fusion) | copy-start | bytes 10
  831.3 97.2 %collective-permute-start.6 = (bf16[256,768]{1,0:T(8,128)(2,1)S(1)}, bf16[256,768]{1,0:T(8,128)(2,1)S(1)}, u32[]{:S(2)}, u32[]{:S(2)}) collective-permute-start(bf16[256,768]{1,0:T(8,128)(2,1)S(1)} %get-tuple-element.81), channel_id=1, source_target_pairs={{0,0},{1,1},{4,2},{5,3},{2,4},{3,5},{6,6},{7,7},{8,8},{9,9},{12,10... | collective-permute-start | bytes 1179656 | tf_op jit(solution)/shard_map/ppermute | solution.py:217
  832.0 96.5 %collective-permute-start.7 = (bf16[256,768]{1,0:T(8,128)(2,1)S(1)}, bf16[256,768]{1,0:T(8,128)(2,1)S(1)}, u32[]{:S(2)}, u32[]{:S(2)}) collective-permute-start(bf16[256,768]{1,0:T(8,128)(2,1)S(1)} %get-tuple-element.82), channel_id=1, source_target_pairs={{1,0},{0,1},{5,2},{4,3},{3,4},{2,5},{7,6},{6,7},{9,8},{8,9},{13,10... | collective-permute-start | bytes 1179656 | tf_op jit(solution)/shard_map/ppermute | solution.py:217
  (47 other events, 219.6 us)
Sparse Core Ops, SparseCore 0:
  10.3 67.2 all-gather.9
  79.9 39.8 all-gather.13
  122.1 52.2 all-gather.17
  175.8 10.6 all-gather.11
  189.3 82.6 all-gather.15
  357.8 11.4 all-gather.19
  556.8 12.0 reduce-scatter.6
  734.5 11.2 reduce-scatter.8
  749.4 60.6 reduce-scatter.12
  814.3 80.0 reduce-scatter.16
  898.3 74.6 reduce-scatter.10
  977.4 110.3 reduce-scatter.14

commit v2 on v1

v2 whole, which is shorter than its diff:
```python
import functools

import jax
import jax.numpy as jnp
from jax import lax
from jax.experimental import pallas as pl
from jax.experimental.pallas import tpu as pltpu
from jax.sharding import Mesh, PartitionSpec as P

HD = 64
eps = 1e-05
neg_fill = -1e30
ALL = ("y", "core", "tensor")
BF = jnp.bfloat16
F32 = jnp.float32


def dg(a, b, dims):
    return lax.dot_general(a, b, (dims, ((), ())), preferred_element_type=F32)


NN = ((1,), (0,))
NT = ((1,), (1,))
TN = ((0,), (0,))


def low_lanes(shape):
    return lax.broadcasted_iota(jnp.int32, shape, 1) < HD


def swap64(v):
    return pltpu.roll(v, HD, axis=1)


def rope_fwd(t, cos, sin):
    lane = lax.broadcasted_iota(jnp.int32, t.shape, 1) % HD
    other = jnp.where(lane < HD // 2, pltpu.roll(t, 128 - HD // 2, axis=1), pltpu.roll(t, HD // 2, axis=1))
    return t * cos + other * sin


def qkv_kernel(x_ref, w_ref, cos_ref, sin_ref, q_ref, k_ref, v_ref):
    x = x_ref[...]
    width = x.shape[1]
    r = [dg(x, w_ref[:, e, :, :640].reshape(width, 640), NN) for e in range(2)]
    c = [[t[:, 128 * i : 128 * i + 128] for i in range(5)] for t in r]
    low = low_lanes(c[0][0].shape)
    qs = [c[0][0], jnp.where(low, c[0][3], swap64(c[1][3])), c[1][0]]
    ks = [c[0][1], jnp.where(low, swap64(c[0][3]), c[1][3]), c[1][1]]
    vs = [c[0][2], jnp.where(low, c[0][4], swap64(c[1][4])), c[1][2]]
    cos, sin = cos_ref[...], sin_ref[...]
    for i in range(3):
        q_ref[i] = (rope_fwd(qs[i], cos, sin) * HD**-0.5).astype(BF)
        k_ref[i] = rope_fwd(ks[i], cos, sin).astype(BF)
        v_ref[i] = vs[i].astype(BF)


def attn_kernel(q_ref, k_ref, v_ref, ko_ref, vo_ref, m_ref, o_ref, e_ref, l_ref):
    q = q_ref[0]
    k = jnp.concatenate([k_ref[0], ko_ref[0]], axis=0)
    v = jnp.concatenate([v_ref[0], vo_ref[0]], axis=0)
    vt = v.astype(F32).T.astype(BF)
    outs = []
    for h in range(2):
        low = low_lanes(q.shape)
        qm = jnp.where(low if h == 0 else jnp.logical_not(low), q, jnp.zeros_like(q))
        s = dg(k, qm, NT) + m_ref[...]
        e = jnp.exp(s - jnp.max(s, axis=0, keepdims=True))
        inv = 1.0 / jnp.sum(e, axis=0, keepdims=True)
        eb = e.astype(BF)
        e_ref[0, h] = eb
        l_ref[0, h] = jnp.broadcast_to(inv, l_ref.shape[2:])
        outs.append(dg(vt[HD * h : HD * h + HD], eb, NN) * inv)
    o_ref[0] = jnp.concatenate(outs, axis=0).T.astype(BF)


def norm_parts(r):
    center = r - jnp.mean(r, axis=-1, keepdims=True)
    inv = lax.rsqrt(jnp.mean(center * center, axis=-1, keepdims=True) + eps)
    return center * inv, inv


def norm_back(dn, n, inv):
    return inv * (dn - jnp.mean(dn, axis=-1, keepdims=True) - n * jnp.mean(dn * n, axis=-1, keepdims=True))


def out_weight(w_ref):
    c = [[w_ref[:, e, :, 128 * i : 128 * i + 128].reshape(-1, 128) for i in range(2)] for e in range(2)]
    low = low_lanes(c[0][0].shape)
    mid = jnp.where(low, swap64(c[0][0].astype(F32)), c[1][0].astype(F32)).astype(BF)
    return [c[0][1], mid, c[1][1]]


def ffn_kernel(x_ref, o_ref, wo_ref, wgu_ref, wd_ref, g_ref, b_ref, y_ref, gu_ref, n1_ref, i1_ref, n2_ref, i2_ref, h_ref, hb_ref, acc_ref):
    z = pl.program_id(0)
    width = x_ref.shape[1]

    @pl.when(z == 0)
    def _():
        r = x_ref[...].astype(F32)
        for p in range(2):
            w = jnp.concatenate(out_weight(wo_ref.at[:, 2 * p : 2 * p + 2]), axis=1)
            o = jnp.concatenate([o_ref[3 * p + i] for i in range(3)], axis=1)
            r = r + dg(o, w, NT)
        n, inv = norm_parts(r)
        n1_ref[...] = n
        i1_ref[...] = jnp.broadcast_to(inv, i1_ref.shape)
        h = n * g_ref[0:1] + b_ref[0:1]
        h_ref[...] = h
        hb_ref[...] = h.astype(BF)

    hb = hb_ref[...]
    w = wgu_ref[:, 0].reshape(width, -1)
    half = w.shape[1] // 2
    gate = dg(hb, w[:, :half], NN)
    up = dg(hb, w[:, half:], NN)
    gu_ref[0, 0] = gate.astype(BF)
    gu_ref[0, 1] = up.astype(BF)
    act = (gate / (1.0 + jnp.exp(-gate)) * up).astype(BF)
    part = dg(act, wd_ref[:, 0].reshape(width, -1), NT)

    @pl.when(z == 0)
    def _():
        acc_ref[...] = h_ref[...] + part

    @pl.when(z > 0)
    def _():
        acc_ref[...] += part

    @pl.when(z == pl.num_programs(0) - 1)
    def _():
        n, inv = norm_parts(acc_ref[...])
        n2_ref[...] = n
        i2_ref[...] = jnp.broadcast_to(inv, i2_ref.shape)
        y_ref[...] = (n * g_ref[1:2] + b_ref[1:2]).astype(BF)


def ffn_back_kernel(dy_ref, n1_ref, i1_ref, n2_ref, i2_ref, gu_ref, wgu_ref, wd_ref, g_ref, b_ref, ggu_ref, gd_ref, dr1_ref, da_ref, ng_ref, hb_ref, df_ref, acc_ref):
    z = pl.program_id(0)
    width = dy_ref.shape[1]

    @pl.when(z == 0)
    def _():
        dy = dy_ref[...].astype(F32)
        n = n2_ref[...]
        ng_ref[1:2] = jnp.sum(dy * n, axis=0, keepdims=True)
        ng_ref[3:4] = jnp.sum(dy, axis=0, keepdims=True)
        dr2 = norm_back(dy * g_ref[1:2], n, i2_ref[:, :1])
        acc_ref[...] = dr2
        df_ref[...] = dr2.astype(BF)
        hb_ref[...] = (n1_ref[...] * g_ref[0:1] + b_ref[0:1]).astype(BF)

    df = df_ref[...]
    gate = gu_ref[0, 0].astype(F32)
    up = gu_ref[0, 1].astype(F32)
    s = 1.0 / (1.0 + jnp.exp(-gate))
    silu = gate * s
    act = (silu * up).astype(BF)
    gd_ref[:, 0] = dg(df, act, TN).astype(BF).reshape(gd_ref.shape[0], -1, act.shape[1])
    d_act = dg(df, wd_ref[:, 0].reshape(width, -1), NN)
    d_gate = (d_act * up * (s * (1.0 + gate * (1.0 - s)))).astype(BF)
    d_up = (d_act * silu).astype(BF)
    half = d_up.shape[1]
    hb = hb_ref[...]
    ggu_ref[:, 0, :, :half] = dg(hb, d_gate, TN).astype(BF).reshape(ggu_ref.shape[0], -1, half)
    ggu_ref[:, 0, :, half:] = dg(hb, d_up, TN).astype(BF).reshape(ggu_ref.shape[0], -1, half)
    w = wgu_ref[:, 0].reshape(width, -1)
    acc_ref[...] += dg(d_gate, w[:, :half], NT) + dg(d_up, w[:, half:], NT)

    @pl.when(z == pl.num_programs(0) - 1)
    def _():
        dh = acc_ref[...]
        n = n1_ref[...]
        ng_ref[0:1] = jnp.sum(dh * n, axis=0, keepdims=True)
        ng_ref[2:3] = jnp.sum(dh, axis=0, keepdims=True)
        dr1 = norm_back(dh * g_ref[0:1], n, i1_ref[:, :1])
        dr1_ref[...] = dr1
        da_ref[...] = dr1.astype(BF)


def attn_back_kernel(da_ref, wo_ref, o_ref, q_ref, k_ref, v_ref, ko_ref, vo_ref, e_ref, l_ref, cos_ref, sin_ref, dq_ref, own_ref, oth_ref, dwo_ref):
    da = da_ref[...]
    rows = da.shape[0]
    w = jnp.concatenate(out_weight(wo_ref), axis=1)
    do3 = dg(da, w, NN).astype(BF)
    o3 = jnp.concatenate([o_ref[i] for i in range(3)], axis=1)
    dwo_ref[0] = dg(da, o3, TN).astype(BF)
    cos, sin = cos_ref[...], sin_ref[...]
    for i in range(3):
        dot = do3[:, 128 * i : 128 * i + 128].astype(F32).T
        ot = o_ref[i].astype(F32).T
        k = jnp.concatenate([k_ref[i], ko_ref[i]], axis=0)
        v = jnp.concatenate([v_ref[i], vo_ref[i]], axis=0)
        kt = k.astype(F32).T.astype(BF)
        qt = q_ref[i].astype(F32).T.astype(BF)
        dqs, dks, dvs = [], [], []
        for h in range(2):
            span = slice(HD * h, HD * h + HD)
            scaled = dot[span] * l_ref[i, h, 0:1]
            inner = jnp.sum(scaled * ot[span], axis=0, keepdims=True)
            sb = scaled.astype(BF)
            zero = jnp.zeros_like(sb)
            padded = jnp.concatenate([sb, zero] if h == 0 else [zero, sb], axis=0)
            dp = dg(v, padded, NN)
            et = e_ref[i, h]
            ds = (et.astype(F32) * (dp - inner)).astype(BF)
            dvs.append(dg(sb, et, NT))
            dks.append(dg(qt[span], ds, NT))
            dqt = dg(kt[span], ds, NN) * HD**-0.5
            d1, d2 = dqt[: HD // 2], dqt[HD // 2 :]
            dqs.append(d1 * cos + d2 * sin)
            dqs.append(d2 * cos - d1 * sin)
        dq_ref[i] = jnp.concatenate(dqs, axis=0).T.astype(BF)
        dk = jnp.concatenate(dks, axis=0)
        dv = jnp.concatenate(dvs, axis=0)
        own_ref[i, 0] = dk[:, :rows]
        own_ref[i, 1] = dv[:, :rows]
        oth_ref[i, 0] = dk[:, rows:].astype(BF)
        oth_ref[i, 1] = dv[:, rows:].astype(BF)


def joint_back_kernel(x_ref, w_ref, dr1_ref, dq_ref, own_ref, got_ref, dwo_ref, cos_ref, sin_ref, g_ref, dz_ref):
    p = pl.program_id(0)
    x = x_ref[...]
    width = x.shape[1]
    cos, sin = cos_ref[...], sin_ref[...]
    dq = [dq_ref[i].astype(F32) for i in range(3)]
    dk, dv = [], []
    for i in range(3):
        t = own_ref[i, 0] + got_ref[i, 0].astype(F32)
        parts = []
        for h in range(2):
            d1 = t[HD * h : HD * h + HD // 2]
            d2 = t[HD * h + HD // 2 : HD * h + HD]
            parts += [d1 * cos + d2 * sin, d2 * cos - d1 * sin]
        dk.append(jnp.concatenate(parts, axis=0).T)
        dv.append((own_ref[i, 1] + got_ref[i, 1].astype(F32)).T)
    low = low_lanes(dq[0].shape)
    zero = jnp.zeros_like(dv[1])
    d = [
        [dq[0], dk[0], dv[0], jnp.where(low, dq[1], swap64(dk[1])), jnp.where(low, dv[1], zero)],
        [dq[2], dk[2], dv[2], jnp.where(low, swap64(dq[1]), dk[1]), jnp.where(low, swap64(dv[1]), zero)],
    ]
    acc = None
    wlow = low_lanes((width, 128))
    mid = dwo_ref[0, :, 128:256].astype(F32)
    sides = [dwo_ref[0, :, 0:128], dwo_ref[0, :, 256:384]]
    mids = [swap64(mid), mid]
    for e in range(2):
        b = jnp.concatenate(d[e], axis=1).astype(BF)
        t = dg(b, w_ref[:, e, :, :640].reshape(width, 640), NT)
        acc = t if acc is None else acc + t
        g = dg(x, b, TN)
        blocks = g_ref.shape[0]
        g_ref[:, e, :, :512] = g[:, :512].astype(BF).reshape(blocks, -1, 512)
        g_ref[:, e, :, 512:640] = jnp.where(wlow, g[:, 512:], mids[e]).astype(BF).reshape(blocks, -1, 128)
        g_ref[:, e, :, 640:] = sides[e].reshape(blocks, -1, 128)

    @pl.when(p == 0)
    def _():
        dz_ref[...] = dr1_ref[...] + acc

    @pl.when(p > 0)
    def _():
        dz_ref[...] += acc


BIG = pltpu.CompilerParams(vmem_limit_bytes=58 << 20)
VM = pltpu.VMEM


def full(shape):
    return pl.BlockSpec(shape, lambda i: (0,) * len(shape))


def lead(shape, at=0):
    return pl.BlockSpec(shape, lambda i: tuple(i if j == at else 0 for j in range(len(shape))))


def sds(shape, kind):
    return jax.ShapeDtypeStruct(shape, kind)


def forward(x, weights, norms, mask, tabs):
    w1, w2, w3 = weights
    gains, biases = norms
    rows, width = x.shape
    heads = width // 128
    blocks, tp, depth = w1.shape[:3]
    steps = tp // 2
    cos, sin, cost, sint = tabs
    q, k, v = pl.pallas_call(
        qkv_kernel,
        grid=(steps,),
        in_specs=[full((rows, width)), lead((blocks, 2, depth, 768), 1), full((rows, 128)), full((rows, 128))],
        out_specs=[lead((3, rows, 128))] * 3,
        out_shape=[sds((heads, rows, 128), BF)] * 3,
        compiler_params=BIG,
        name="qkv",
    )(x, w1, cos, sin)
    ko, vo = lax.ppermute((k, v), "core", [(0, 1), (1, 0)])
    pair = lead((1, rows, 128))
    o, e, l = pl.pallas_call(
        attn_kernel,
        grid=(heads,),
        in_specs=[pair] * 5 + [full((2 * rows, rows))],
        out_specs=[pair, lead((1, 2, 2 * rows, rows)), lead((1, 2, 8, rows))],
        out_shape=[sds((heads, rows, 128), BF), sds((heads, 2, 2 * rows, rows), BF), sds((heads, 2, 8, rows), F32)],
        compiler_params=BIG,
        name="attn",
    )(q, k, v, ko, vo, mask)
    hidden = w2.shape[3] // 2
    y, gu, n1, i1, n2, i2 = pl.pallas_call(
        ffn_kernel,
        grid=(tp,),
        in_specs=[
            full((rows, width)),
            full((heads, rows, 128)),
            pl.BlockSpec((blocks, tp, depth, 256), lambda i: (0, 0, 0, 2)),
            lead((blocks, 1, depth, 2 * hidden), 1),
            lead((blocks, 1, depth, hidden), 1),
            full((2, width)),
            full((2, width)),
        ],
        out_specs=[full((rows, width)), lead((1, 2, rows, hidden))] + [full((rows, width)), full((rows, 128))] * 2,
        out_shape=[sds((rows, width), BF), sds((tp, 2, rows, hidden), BF)] + [sds((rows, width), F32), sds((rows, 128), F32)] * 2,
        scratch_shapes=[VM((rows, width), F32), VM((rows, width), BF), VM((rows, width), F32)],
        compiler_params=BIG,
        name="ffn",
    )(x, o, w1, w2, w3, gains, biases)
    return y, (q, k, v, ko, vo, o, e, l, gu, n1, i1, n2, i2)


def backward(x, dy, kept, weights, norms, tabs):
    w1, w2, w3 = weights
    gains, biases = norms
    q, k, v, ko, vo, o, e, l, gu, n1, i1, n2, i2 = kept
    rows, width = x.shape
    heads = width // 128
    blocks, tp, depth = w1.shape[:3]
    steps = tp // 2
    hidden = w2.shape[3] // 2
    cos, sin, cost, sint = tabs
    whole, stat = full((rows, width)), full((rows, 128))
    g2, g3, dr1, da, ng = pl.pallas_call(
        ffn_back_kernel,
        grid=(tp,),
        in_specs=[
            whole, whole, stat, whole, stat,
            lead((1, 2, rows, hidden)),
            lead((blocks, 1, depth, 2 * hidden), 1),
            lead((blocks, 1, depth, hidden), 1),
            full((2, width)), full((2, width)),
        ],
        out_specs=[
            lead((blocks, 1, depth, 2 * hidden), 1),
            lead((blocks, 1, depth, hidden), 1),
            whole, whole, full((8, width)),
        ],
        out_shape=[sds(w2.shape, BF), sds(w3.shape, BF), sds((rows, width), F32), sds((rows, width), BF), sds((8, width), F32)],
        scratch_shapes=[VM((rows, width), BF), VM((rows, width), BF), VM((rows, width), F32)],
        compiler_params=BIG,
        name="ffn_back",
    )(dy, n1, i1, n2, i2, gu, w2, w3, gains, biases)
    three = lead((3, rows, 128))
    dq, own, oth, dwo = pl.pallas_call(
        attn_back_kernel,
        grid=(steps,),
        in_specs=[
            whole,
            pl.BlockSpec((blocks, 2, depth, 256), lambda i: (0, i, 0, 2)),
            three, three, three, three, three, three,
            lead((3, 2, 2 * rows, rows)),
            lead((3, 2, 8, rows)),
            full((HD // 2, rows)), full((HD // 2, rows)),
        ],
        out_specs=[three, lead((3, 2, 128, rows)), lead((3, 2, 128, rows)), lead((1, width, 384))],
        out_shape=[
            sds((heads, rows, 128), BF),
            sds((heads, 2, 128, rows), F32),
            sds((heads, 2, 128, rows), BF),
            sds((steps, width, 384), BF),
        ],
        compiler_params=BIG,
        name="attn_back",
    )(da, w1, o, q, k, v, ko, vo, e, l, cost, sint)
    got = lax.ppermute(oth, "core", [(0, 1), (1, 0)])
    g1, dz = pl.pallas_call(
        joint_back_kernel,
        grid=(steps,),
        in_specs=[
            whole,
            lead((blocks, 2, depth, 768), 1),
            whole, three,
            lead((3, 2, 128, rows)), lead((3, 2, 128, rows)),
            lead((1, width, 384)),
            full((HD // 2, rows)), full((HD // 2, rows)),
        ],
        out_specs=[lead((blocks, 2, depth, 768), 1), whole],
        out_shape=[sds(w1.shape, BF), sds((rows, width), F32)],
        compiler_params=BIG,
        name="joint_back",
    )(x, w1, dr1, dq, own, got, dwo, cost, sint)
    return dz, (g1, g2, g3, ng)


def swap_pairs(tp, step, dp_axes):
    pairs = []
    half = tp // 2
    for core in range(2):
        for at in range(tp):
            source = core * tp + at
            target = (at // half) * tp + half * core + (at + step) % half
            pairs.append((source, target))
    return pairs


def to_sequences(rows, tp):
    half = tp // 2
    at = lax.axis_index("tensor")
    pieces = [None] * half
    got = []
    for step in range(half):
        piece = lax.dynamic_index_in_dim(rows, (at + step) % half, 0, keepdims=False)
        got.append(lax.ppermute(piece, ("core", "tensor"), swap_pairs(tp, step, None)))
    stacked = jnp.stack(got)
    order = (at - jnp.arange(half)) % half
    return jnp.take(stacked, order, axis=0).reshape(-1, rows.shape[-1])


def to_positions(rows, tp):
    half = tp // 2
    at = lax.axis_index("tensor")
    parts = rows.reshape(half, -1, rows.shape[-1])
    got = []
    for step in range(half):
        piece = lax.dynamic_index_in_dim(parts, (at - step) % half, 0, keepdims=False)
        back = [(target, source) for source, target in swap_pairs(tp, step, None)]
        got.append(lax.ppermute(piece, ("core", "tensor"), back))
    stacked = jnp.stack(got)
    order = (at + jnp.arange(half)) % half
    return jnp.take(stacked, (jnp.arange(half) - at) % half, axis=0)


def rope_tables(positions):
    halfway = HD // 2
    freqs = 1000.0 ** (-jnp.arange(halfway, dtype=F32) / halfway)
    angles = positions.astype(F32)[:, None] * freqs[None, :]
    cos, sin = jnp.cos(angles), jnp.sin(angles)
    wide = jnp.concatenate([cos] * 4, axis=1)
    signed = jnp.concatenate([-sin, sin] * 2, axis=1)
    return wide, signed, cos.T, sin.T


def pack_shard(w_qkv, w_out, w_gate_up, w_down):
    rows = w_qkv.shape[0]
    odd = lax.axis_index("tensor") % 2 == 1
    heads = w_qkv.reshape(rows, 3, 3, HD)
    mine = w_out.T.reshape(rows, 3, HD)
    heads = jnp.where(odd, jnp.roll(heads, -1, axis=2), heads)
    mine = jnp.where(odd, jnp.roll(mine, -1, axis=1), mine)
    first = jnp.concatenate(
        [heads[:, :, :2].reshape(rows, -1), heads[:, :, 2].reshape(rows, -1), mine[:, 2], mine[:, :2].reshape(rows, -1)], axis=1
    )
    return first, w_gate_up.reshape(rows, -1), w_down.T


def unpack_shard(first, pair, down):
    rows = first.shape[0]
    odd = lax.axis_index("tensor") % 2 == 1
    both = first[:, :384].reshape(rows, 3, 2, HD)
    single = first[:, 384:576].reshape(rows, 3, 1, HD)
    heads = jnp.concatenate([both, single], axis=2)
    mine = jnp.concatenate([first[:, 640:].reshape(rows, 2, HD), first[:, 576:640].reshape(rows, 1, HD)], axis=1)
    heads = jnp.where(odd, jnp.roll(heads, 1, axis=2), heads)
    mine = jnp.where(odd, jnp.roll(mine, 1, axis=1), mine)
    return (
        heads.reshape(rows, 3, -1),
        mine.reshape(rows, -1).T,
        pair.reshape(rows, 2, -1),
        down.T,
    )


BLOCKS = 4


def gather_shard(shard, dp, tp):
    rows, columns = shard.shape
    got = lax.all_gather(shard, ALL, axis=0, tiled=False)
    got = got.reshape(BLOCKS, dp // BLOCKS, tp, rows, columns)
    return got.transpose(0, 2, 1, 3, 4).reshape(BLOCKS, tp, -1, columns)


def scatter_sum(whole, dp, tp):
    columns = whole.shape[3]
    parts = whole.reshape(BLOCKS, tp, dp // BLOCKS, -1, columns).transpose(0, 2, 1, 3, 4)
    parts = parts.reshape(dp * tp, -1, columns)
    return lax.psum_scatter(parts, ALL, scatter_dimension=0, tiled=False).astype(F32)


def on_device(dp, tp, tokens, cotangent, lengths, w_qkv, w_out, w_gate_up, w_down, norm_gains, norm_biases):
    section = lax.axis_index("section")
    core = lax.axis_index("core")
    at = lax.axis_index("tensor")
    micro, own, width = tokens.shape
    assert micro * 2 == tp
    length = own * tp
    rows = length // 2
    shards = pack_shard(w_qkv[0], w_out[0], w_gate_up[0], w_down[0])
    weights = tuple(gather_shard(s, dp, tp) for s in shards)
    norms = jnp.concatenate([norm_gains, norm_biases])
    norms = lax.all_gather(norms, ("y", "core"), axis=1, tiled=True).astype(F32)
    norms = (norms[0].reshape(2, width), norms[1].reshape(2, width))
    tokens = to_sequences(tokens, tp)
    grad_top = to_sequences(cotangent, tp)
    chip_lengths = lax.all_gather(lengths, "core", axis=0, tiled=True)
    my_lengths = lax.dynamic_index_in_dim(chip_lengths, at, 0, keepdims=False)
    near = core * rows + jnp.arange(rows, dtype=jnp.int32)
    far = (1 - core) * rows + jnp.arange(rows, dtype=jnp.int32)
    ends_at = jnp.cumsum(my_lengths)

    def segment(positions):
        return jnp.sum((ends_at[None, :] <= positions[:, None]).astype(jnp.int32), axis=-1)

    seg_near = segment(near)
    seg_all = jnp.concatenate([seg_near, segment(far)])
    mask = jnp.where(seg_all[:, None] == seg_near[None, :], 0.0, neg_fill).astype(F32)
    tabs = rope_tables(near)

    y, kept = forward(tokens, weights, norms, mask, tabs)
    received = lax.ppermute(y, "section", [(0, 1)])
    inputs = jnp.where(section == 0, tokens, received)
    y, kept = forward(inputs, weights, norms, mask, tabs)
    dz, grads = backward(inputs, grad_top.astype(F32), kept, weights, norms, tabs)
    received = lax.ppermute(dz, "section", [(1, 0)])
    dy = jnp.where(section == 0, received, grad_top.astype(F32))
    dz, grads = backward(inputs, dy, kept, weights, norms, tabs)
    ends = to_positions(jnp.where(section == 0, dz.astype(BF), y), tp)
    sums = [scatter_sum(g, dp, tp) for g in grads[:3]]
    outs = unpack_shard(*sums)
    ng = grads[3]
    gains = lax.psum_scatter(ng[0:2].reshape(-1), ALL, scatter_dimension=0, tiled=True)
    biases = lax.psum_scatter(ng[2:4].reshape(-1), ALL, scatter_dimension=0, tiled=True)
    return (ends[None],) + tuple(t[None] for t in outs + (gains, biases))


def solution(mesh):
    sections, dp, tp = mesh.devices.shape
    fine = Mesh(mesh.devices.reshape(sections, dp // 2, 2, tp), ("section", "y", "core", "tensor"))
    both = ("y", "core")
    in_specs = (
        P(both, "tensor", None),
        P(both, "tensor", None),
        P(both, None),
        P("section", both, None, "tensor"),
        P("section", "tensor", both),
        P("section", both, None, "tensor"),
        P("section", "tensor", both),
        P("section", both),
        P("section", both),
    )
    out_specs = (
        P("section", both, "tensor", None),
        P("section", both, None, "tensor"),
        P("section", "tensor", both),
        P("section", both, None, "tensor"),
        P("section", "tensor", both),
        P("section", ALL),
        P("section", ALL),
    )
    return jax.shard_map(
        functools.partial(on_device, dp, tp), mesh=fine, in_specs=in_specs, out_specs=out_specs, check_vma=False
    )
```

time: 1110 us -> 735 us (0.66)
  matrix products: 321 us -> 0 us
  Pallas kernels: 0 us -> 198 us
  other arithmetic: 145 us -> 19.2 us
  local copies, waits for them, and re-layouts: 149 us -> 27.7 us
    dot_general x32 -> x0, matrix products: 321 us -> none  [the longest x20 120 us: dot(): return lax.dot_general(a, b, (dims, ((), ())), preferred_element_type=F32)]
    pallas_call x0 -> x12, Pallas kernels: none -> 198 us  [the longest x2 53.9 us: backward(): pl.pallas_call(ffn_back_kernel, grid=(tp,), in_specs=[whole, whole, stat,...]
    sub x3 -> x0, other arithmetic: 69.6 us -> none  [the longest x2 69.1 us: attend(): exps = jnp.exp(scores - jnp.max(scores, axis=-1, keepdims=True))]
    convert_element_type x12 -> x3, other arithmetic: 39.7 us -> 2.39 us  [the longest x1 1.34 us: on_device(): grad_top.astype(F32)]
    convert_element_type x10 -> x1, local copies, waits for them, and re-layouts: 36.9 us -> 2.85 us  [scatter_sum(): lax.psum_scatter(parts, ALL, scatter_dimension=0, tiled=False).astype(F32)]
    reshape x4 -> x3, local copies, waits for them, and re-layouts: 26.2 us -> 0.03 us  [the longest x1 0.01 us: on_device(): ng[0:2].reshape(-1)]
    dot_general x6 -> x0, local copies, waits for them, and re-layouts: 24.5 us -> none  [dot(): return lax.dot_general(a, b, (dims, ((), ())), preferred_element_type=F32)]
    all_gather x6 -> x3, waiting for transfers between devices: 116 us -> 136 us  [gather_shard(): got = lax.all_gather(shard, ALL, axis=0, tiled=False)]
  transfers between devices with their start and end apart: 20 -> 20, of which waited for: 11 -> 11; matrix products, arithmetic and copies ran while one was open for 22% -> 4% of each run, Pallas kernels for 0% -> 8%
where the time goes in v2:
time: 735 us; the launch traced here: 730 us
  waiting for transfers between devices  356 us (48%)
  Pallas kernels  198 us (27%)
  blocking collectives  96.2 us (13%)
  local copies, waits for them, and re-layouts  27.7 us (4%)
  other arithmetic  19.2 us (3%)
  starting transfers between devices  17.1 us (2%)
  between operations  15.7 us (2%)
    reduce_scatter x3, waiting for transfers between devices, scatter_sum(): lax.psum_scatter(parts, ALL, scatter_dimension=0, tiled=False).astype(F32)  147 us
    all_gather x3, waiting for transfers between devices, gather_shard(): got = lax.all_gather(shard, ALL, axis=0, tiled=False)  136 us
    unnamed x1, blocking collectives  83.5 us
    pallas_call x2, Pallas kernels, backward(): pl.pallas_call(ffn_back_kernel, grid=(tp,), in_specs=[whole, whole, stat,...  53.9 us
    pallas_call x2, Pallas kernels, backward(): pl.pallas_call(attn_back_kernel, grid=(steps,), in_specs=[whole, pl.Block...  40.5 us
    ppermute x1, waiting for transfers between devices, on_device(): received = lax.ppermute(dz, 'section', [(1, 0)])  37.3 us
    pallas_call x2, Pallas kernels, forward(): pl.pallas_call(ffn_kernel, grid=(tp,), in_specs=[full((rows, width)), ful...  34.5 us
    pallas_call x2, Pallas kernels, forward(): pl.pallas_call(attn_kernel, grid=(heads,), in_specs=[pair] * 5 + [full((2...  32.9 us
  transfers between devices with their start and end apart: 20, of which 11 were waited for; matrix products, arithmetic and copies ran while one was open for 4% of the time, Pallas kernels for 8%

profile of v2, /device:TPU:0, one launch (start us, length us, event | category | flops | bytes accessed | tf_op | source)
XLA Modules:
  0.0 730.0 jit_solution(2887303031381353746)
XLA Ops:
  9.8 1.1 copy.47
  12.9 1.2 all_gather_reshape_squeeze.3
  15.0 2.1 collective-permute-start.6
  17.1 1.4 collective-permute-start.5
  18.8 1.4 collective-permute-start
  21.8 7.3 all-gather.2
  31.1 1.1 pad_maximum_fusion.1
  32.8 10.5 %collective-permute-done.1 = bf16[256,768]{1,0:T(8,128)(2,1)S(1)} collective-permute-done((bf16[256,768]{1,0:T(8,128)(2,1)S(1)}, bf16[256,768]{1,0:T(8,128)(2,1)S(1)}, u32[]{:S(2)}, u32[]{:S(2)}) %collective-permute-start.1) | collective-permute-done | bytes 393248 | tf_op jit(solution)/shard_map/ppermute | solution.py:424
  43.2 1.1 pad_maximum_fusion
  44.9 1.1 broadcast_select_fusion
  46.0 35.2 %all-gather.9.cloned.1.call-done = bf16[3072,768]{1,0:T(8,128)(2,1)} async-done(((bf16[192,768]{1,0:T(8,128)(2,1)}), bf16[3072,768]{1,0:T(8,128)(2,1)}) %all-gather.9.cloned.1.call-update) | async-done | bytes 4718608 | tf_op jit(solution)/shard_map/all_gather | solution.py:489
  81.2 6.5 qkv.2
  87.7 4.4 collective-permute-start.2
  93.0 5.4 all_gather.27
  99.7 1.5 compare_select_fusion.m_ref
  102.4 16.4 %attn.2 = (bf16[6,512,128]{2,1,0:T(8,128)(2,1)}, bf16[6,2,1024,512]{3,2,1,0:T(8,128)(2,1)}, f32[6,2,8,512]{3,2,1,0:T(8,128)}) custom-call(bf16[6,512,128]{2,1,0:T(8,128)(2,1)} %get-tuple-element.43.q_ref, bf16[6,512,128]{2,1,0:T(8,128)(2,1)} %get-tuple-element.44.k_ref, bf16[6,512,128]{2,1,0:T(8,128)(2,1)} %get-tuple-element.45.v_ref, ...), custom_call_target="tpu_custom_call" | custom-call | tf_op jit(solution)/shard_map/attn/pallas_call | solution.py:302
  118.8 17.5 %all-gather.11.cloned.1.call-done = bf16[3072,768]{1,0:T(8,128)(2,1)} async-done(((bf16[192,768]{1,0:T(8,128)(2,1)}), bf16[3072,768]{1,0:T(8,128)(2,1)}) %all-gather.11.cloned.1.call-update) | async-done | bytes 4718608 | tf_op jit(solution)/shard_map/all_gather | solution.py:489
  136.3 82.9 %all-gather.7.cloned.1.call-done = bf16[16,192,1536]{2,1,0:T(8,128)(2,1)} async-done(((bf16[1,192,1536]{2,1,0:T(8,128)(2,1)}), bf16[16,192,1536]{2,1,0:T(8,128)(2,1)}) %all-gather.7.cloned.1.call-update) | async-done | bytes 9437200 | tf_op jit(solution)/shard_map/all_gather | solution.py:489
  219.2 17.2 %ffn.2 = (bf16[512,768]{1,0:T(8,128)(2,1)}, bf16[4,2,512,768]{3,2,1,0:T(8,128)(2,1)}, f32[512,768]{1,0:T(8,128)}, f32[512,128]{1,0:T(8,128)}, f32[512,768]{1,0:T(8,128)}, /*index=5*/f32[512,128]{1,0:T(8,128)}) custom-call(bf16[512,768]{1,0:T(8,128)(2,1)} %bitcast.98, bf16[6,512,128]{2,1,0:T(8,128)(2,1)} %get-tuple-element.46.o_ref, ...), custom_call_target="tpu_custom_call" | custom-call | tf_op jit(solution)/shard_map/ffn/pallas_call | solution.py:312
  236.5 3.9 collective-permute-start.4
  240.4 16.9 %collective-permute-done.4 = bf16[512,768]{1,0:T(8,128)(2,1)S(1)} collective-permute-done((bf16[512,768]{1,0:T(8,128)(2,1)}, bf16[512,768]{1,0:T(8,128)(2,1)S(1)}, u32[]{:S(2)}, u32[]{:S(2)}) %collective-permute-start.4) | collective-permute-done | bytes 786464 | tf_op jit(solution)/shard_map/ppermute | solution.py:531
  257.4 1.0 broadcast_select_fusion.3.x_ref
  258.4 6.5 qkv.3
  266.3 1.3 bitcast_convert_fusion.dy_ref
  269.4 16.4 %attn.3 = (bf16[6,512,128]{2,1,0:T(8,128)(2,1)}, bf16[6,2,1024,512]{3,2,1,0:T(8,128)(2,1)}, f32[6,2,8,512]{3,2,1,0:T(8,128)}) custom-call(bf16[6,512,128]{2,1,0:T(8,128)(2,1)} %get-tuple-element.48.q_ref, bf16[6,512,128]{2,1,0:T(8,128)(2,1)} %get-tuple-element.49.k_ref, bf16[6,512,128]{2,1,0:T(8,128)(2,1)} %get-tuple-element.50.v_ref, ...), custom_call_target="tpu_custom_call" | custom-call | tf_op jit(solution)/shard_map/attn/pallas_call | solution.py:302
  285.8 17.2 %ffn.3 = (bf16[512,768]{1,0:T(8,128)(2,1)}, bf16[4,2,512,768]{3,2,1,0:T(8,128)(2,1)}, f32[512,768]{1,0:T(8,128)}, f32[512,128]{1,0:T(8,128)}, f32[512,768]{1,0:T(8,128)}, /*index=5*/f32[512,128]{1,0:T(8,128)}) custom-call(bf16[512,768]{1,0:T(8,128)(2,1)} %broadcast_select_fusion.3.x_ref, bf16[6,512,128]{2,1,0:T(8,128)(2,1)} %get-tuple-element.51.o_ref, ...), custom_call_target="tpu_custom_call" | custom-call | tf_op jit(solution)/shard_map/ffn/pallas_call | solution.py:312
  303.0 27.0 %ffn_back.2 = (bf16[4,4,192,1536]{3,2,1,0:T(8,128)(2,1)}, bf16[4,4,192,768]{3,2,1,0:T(8,128)(2,1)}, f32[512,768]{1,0:T(8,128)}, bf16[512,768]{1,0:T(8,128)(2,1)}, f32[8,768]{1,0:T(8,128)}) custom-call(f32[512,768]{1,0:T(8,128)} %bitcast_convert_fusion.dy_ref, f32[512,768]{1,0:T(8,128)} %get-tuple-element.52.n1_ref, f32[512,128]{1,0:T(8,128)} %get-tuple-element.53.i1_ref, ...), custom_call_target="tpu_custom_call" | custom-call | tf_op jit(solution)/shard_map/ffn_back/pallas_call | solution.py:344
  330.1 20.0 %attn_back.2 = (bf16[6,512,128]{2,1,0:T(8,128)(2,1)}, f32[6,2,128,512]{3,2,1,0:T(8,128)}, bf16[6,2,128,512]{3,2,1,0:T(8,128)(2,1)}, bf16[2,768,384]{2,1,0:T(8,128)(2,1)}) custom-call(bf16[512,768]{1,0:T(8,128)(2,1)} %get-tuple-element.58.da_ref, bf16[4,4,192,768]{3,2,1,0:T(8,128)(2,1)} %bitcast.85, bf16[6,512,128]{2,1,0:T(8,128)(2,1)} %get-tuple-element.51.o_ref, ...), custom_call_target="tpu_custom_call" | custom-call | tf_op jit(solution)/shard_map/attn_back/pallas_call | solution.py:365
  350.3 3.5 collective-permute-done.9.got_ref
  353.8 1.2 copy-done.5
  354.9 11.8 %joint_back.2 = (bf16[4,4,192,768]{3,2,1,0:T(8,128)(2,1)}, f32[512,768]{1,0:T(8,128)}) custom-call(bf16[512,768]{1,0:T(8,128)(2,1)} %broadcast_select_fusion.3.x_ref, bf16[4,4,192,768]{3,2,1,0:T(8,128)(2,1)} %bitcast.86, f32[512,768]{1,0:T(8,128)} %get-tuple-element.57.dr1_ref, bf16[6,512,128]{2,1,0:T(8,128)(2,1)} %get-tuple-element.61.dq_ref, ...), custom_call_target="tpu_custom_call" | custom-call | tf_op jit(solution)/shard_map/joint_back/pallas_call | solution.py:387
  366.7 1.3 collective-permute-start.10
  368.0 37.3 %collective-permute-done.10 = f32[512,768]{1,0:T(8,128)S(1)} collective-permute-done((f32[512,768]{1,0:T(8,128)}, f32[512,768]{1,0:T(8,128)S(1)}, u32[]{:S(2)}, u32[]{:S(2)}) %collective-permute-start.10) | collective-permute-done | bytes 1572896 | tf_op jit(solution)/shard_map/ppermute | solution.py:535
  405.3 1.4 broadcast_select_fusion.2.dy_ref
  406.7 26.9 %ffn_back.3 = (bf16[4,4,192,1536]{3,2,1,0:T(8,128)(2,1)}, bf16[4,4,192,768]{3,2,1,0:T(8,128)(2,1)}, f32[512,768]{1,0:T(8,128)}, bf16[512,768]{1,0:T(8,128)(2,1)}, f32[8,768]{1,0:T(8,128)}) custom-call(f32[512,768]{1,0:T(8,128)} %broadcast_select_fusion.2.dy_ref, f32[512,768]{1,0:T(8,128)} %get-tuple-element.52.n1_ref, f32[512,128]{1,0:T(8,128)} %get-tuple-element.53.i1_ref, ...), custom_call_target="tpu_custom_call" | custom-call | tf_op jit(solution)/shard_map/ffn_back/pallas_call | solution.py:344
  433.7 20.5 %attn_back.3 = (bf16[6,512,128]{2,1,0:T(8,128)(2,1)}, f32[6,2,128,512]{3,2,1,0:T(8,128)}, bf16[6,2,128,512]{3,2,1,0:T(8,128)(2,1)}, bf16[2,768,384]{2,1,0:T(8,128)(2,1)}) custom-call(bf16[512,768]{1,0:T(8,128)(2,1)} %get-tuple-element.67.da_ref, bf16[4,4,192,768]{3,2,1,0:T(8,128)(2,1)} %bitcast.87, bf16[6,512,128]{2,1,0:T(8,128)(2,1)} %get-tuple-element.51.o_ref, ...), custom_call_target="tpu_custom_call" | custom-call | tf_op jit(solution)/shard_map/attn_back/pallas_call | solution.py:365
  454.3 3.6 collective-permute-done.11.got_ref
  457.9 1.2 copy-done.4
  459.1 11.6 %joint_back.3 = (bf16[4,4,192,768]{3,2,1,0:T(8,128)(2,1)}, f32[512,768]{1,0:T(8,128)}) custom-call(bf16[512,768]{1,0:T(8,128)(2,1)} %broadcast_select_fusion.3.x_ref, bf16[4,4,192,768]{3,2,1,0:T(8,128)(2,1)} %bitcast.88, f32[512,768]{1,0:T(8,128)} %get-tuple-element.66.dr1_ref, bf16[6,512,128]{2,1,0:T(8,128)(2,1)} %get-tuple-element.68.dq_ref, ...), custom_call_target="tpu_custom_call" | custom-call | tf_op jit(solution)/shard_map/joint_back/pallas_call | solution.py:387
  470.7 7.9 %copy.50 = bf16[16,192,768]{1,2,0:T(8,128)(2,1)} copy(bf16[16,192,768]{2,1,0:T(8,128)(2,1)} %bitcast.101) | data formatting | bytes 9437184 | tf_op jit(solution)/shard_map/reshape;transpose;reshape | solution.py:497
  482.2 83.5 %all-reduce.2 = (f32[1536]{0:T(1024)S(1)}, f32[1536]{0:T(1024)S(1)}) all-reduce(f32[1536]{0:T(1024)S(1)} %reshape.149, f32[1536]{0:T(1024)S(1)} %reshape.150), channel_id=7, replica_groups=mesh['section'=2,'y'=2,'core'=2,'tensor'=4] {'y','core','tensor'}, use_global_device_ids=true, to_apply=%region_6.8.clone | all-reduce | flops 3072 | bytes 24576
  567.5 1.0 select_bitcast_fusion
  568.5 1.8 convert_bitcast_fusion
  570.3 34.8 %reduce-scatter.4.cloned.1.call-done = bf16[1,192,768]{1,2,0:T(8,128)(2,1)} async-done(((bf16[16,192,768]{1,2,0:T(8,128)(2,1)}), bf16[1,192,768]{1,2,0:T(8,128)(2,1)}) %reduce-scatter.4.cloned.1.call-update) | async-done | bytes 294928 | tf_op jit(solution)/shard_map/reduce_scatter | solution.py:498
  605.2 1.0 bitcast_convert_fusion.1
  606.3 1.1 copy.53
  608.1 111.7 %reduce-scatter.6.cloned.1.call-done = bf16[1,192,1536]{2,1,0:T(8,128)(2,1)} async-done(((bf16[16,192,1536]{2,1,0:T(8,128)(2,1)}), bf16[1,192,1536]{2,1,0:T(8,128)(2,1)}) %reduce-scatter.6.cloned.1.call-update) | async-done | bytes 589840 | tf_op jit(solution)/shard_map/reduce_scatter | solution.py:498
  719.8 2.8 reshape.153
  (122 shorter events, 22.6 us)
Async XLA Ops:
  7.2 74.1 %all-gather.9.cloned.1.call-start = ((), (), s32[]{:S(2)}) async-start(), calls=%async_computation.7 | async-start | bytes 5013504 | tf_op jit(solution)/shard_map/all_gather | solution.py:489
  10.9 1.9 copy-start.11
  11.1 3.0 copy-start.6
  12.0 124.3 %all-gather.11.cloned.1.call-start = ((), (), s32[]{:S(2)}) async-start(), calls=%async_computation.8 | async-start | bytes 5013504 | tf_op jit(solution)/shard_map/all_gather | solution.py:489
  12.8 5.7 copy-start.7
  12.8 206.4 %all-gather.7.cloned.1.call-start = ((), (), s32[]{:S(2)}) async-start(), calls=%async_computation.3 | async-start | bytes 10027008 | tf_op jit(solution)/shard_map/all_gather | solution.py:489
  14.1 554.4 %reduce-scatter.8.cloned.1.call-start = ((), (), s32[]{:S(2)}) async-start(), calls=%async_computation.6 | async-start | bytes 5013504 | tf_op jit(solution)/shard_map/reduce_scatter | solution.py:498
  15.0 6.3 copy-start.15
  15.0 6.3 copy-start.16
  15.0 6.8 copy-start.17
  15.0 16.1 %collective-permute-start.6 = (bf16[256,768]{1,0:T(8,128)(2,1)}, bf16[256,768]{1,0:T(8,128)(2,1)S(1)}, u32[]{:S(2)}, u32[]{:S(2)}) collective-permute-start(bf16[256,768]{1,0:T(8,128)(2,1)} %get-tuple-element.115), channel_id=1, source_target_pairs={{0,1},{1,0},{2,5},{3,4},{4,3},{5,2},{6,7},{7,6},{8,9},{9,8},{10,13... | collective-permute-start | bytes 1179656 | tf_op jit(solution)/shard_map/ppermute | solution.py:424
  17.1 14.0 %collective-permute-start.5 = (bf16[256,768]{1,0:T(8,128)(2,1)S(1)}, bf16[256,768]{1,0:T(8,128)(2,1)}, u32[]{:S(2)}, u32[]{:S(2)}) collective-permute-start(bf16[256,768]{1,0:T(8,128)(2,1)S(1)} %get-tuple-element.114), channel_id=1, source_target_pairs={{0,0},{1,1},{2,4},{3,5},{4,2},{5,3},{6,6},{7,7},{8,8},{9,9},{10,12... | collective-permute-start | bytes 1179656 | tf_op jit(solution)/shard_map/ppermute | solution.py:424
  18.6 24.7 %collective-permute-start.1 = (bf16[256,768]{1,0:T(8,128)(2,1)S(1)}, bf16[256,768]{1,0:T(8,128)(2,1)S(1)}, u32[]{:S(2)}, u32[]{:S(2)}) collective-permute-start(bf16[256,768]{1,0:T(8,128)(2,1)S(1)} %get-tuple-element.117), channel_id=1, source_target_pairs={{0,1},{1,0},{2,5},{3,4},{4,3},{5,2},{6,7},{7,6},{8,9},{9,8},{10,13... | collective-permute-start | bytes 1179656 | tf_op jit(solution)/shard_map/ppermute | solution.py:424
  18.8 24.5 %collective-permute-start = (bf16[256,768]{1,0:T(8,128)(2,1)S(1)}, bf16[256,768]{1,0:T(8,128)(2,1)}, u32[]{:S(2)}, u32[]{:S(2)}) collective-permute-start(bf16[256,768]{1,0:T(8,128)(2,1)S(1)} %get-tuple-element.116), channel_id=1, source_target_pairs={{0,0},{1,1},{2,4},{3,5},{4,2},{5,3},{6,6},{7,7},{8,8},{9,9},{10,12... | collective-permute-start | bytes 1179656 | tf_op jit(solution)/shard_map/ppermute | solution.py:424
  20.2 10.9 %copy-start.13 = (f32[32]{0:T(128)}, f32[32]{0:T(128)S(1)}, u32[]{:S(2)}) copy-start(f32[32]{0:T(128)S(1)} %multiply_power_fusion) | copy-start | bytes 388
  43.2 1.7 copy-start.18
  87.7 13.6 %collective-permute-start.2 = (bf16[6,512,128]{2,1,0:T(8,128)(2,1)}, bf16[6,512,128]{2,1,0:T(8,128)(2,1)S(1)}, u32[]{:S(2)}, u32[]{:S(2)}) collective-permute-start(bf16[6,512,128]{2,1,0:T(8,128)(2,1)} %get-tuple-element.44.k_ref), channel_id=1, source_target_pairs={{0,4},{4,0},{1,5},{5,1},{2,6},{6,2},{3,7},{7,3},{8,12},{12,8},{9,1... | collective-permute-start | bytes 2359304 | tf_op jit(solution)/shard_map/ppermute | solution.py:300
  92.1 9.2 %collective-permute-start.3 = (bf16[6,512,128]{2,1,0:T(8,128)(2,1)}, bf16[6,512,128]{2,1,0:T(8,128)(2,1)S(1)}, u32[]{:S(2)}, u32[]{:S(2)}) collective-permute-start(bf16[6,512,128]{2,1,0:T(8,128)(2,1)} %get-tuple-element.45.v_ref), channel_id=1, source_target_pairs={{0,4},{4,0},{1,5},{5,1},{2,6},{6,2},{3,7},{7,3},{8,12},{12,8},{9,1... | collective-permute-start | bytes 2359304 | tf_op jit(solution)/shard_map/ppermute | solution.py:300
  101.3 0.9 copy-start.9
  101.3 1.1 copy-start.10
  219.2 38.1 %copy-start = (bf16[2,256,768]{2,1,0:T(8,128)(2,1)S(1)}, bf16[2,256,768]{2,1,0:T(8,128)(2,1)}, u32[]{:S(2)}) copy-start(bf16[2,256,768]{2,1,0:T(8,128)(2,1)} %get-tuple-element.126) | copy-start | bytes 2359300
  236.5 20.9 %collective-permute-start.4 = (bf16[512,768]{1,0:T(8,128)(2,1)}, bf16[512,768]{1,0:T(8,128)(2,1)S(1)}, u32[]{:S(2)}, u32[]{:S(2)}) collective-permute-start(bf16[512,768]{1,0:T(8,128)(2,1)} %get-tuple-element.47), channel_id=1, source_target_pairs={{0,16},{1,17},{2,18},{3,19},{4,20},{5,21},{6,22},{7,23},{8,24},{9,... | collective-permute-start | bytes 2359304 | tf_op jit(solution)/shard_map/ppermute | solution.py:531
  258.4 7.0 copy-start.14
  264.8 2.8 collective-permute-start.7
  264.8 3.6 collective-permute-start.8
  267.7 0.9 copy-start.1
  268.5 0.9 copy-start.2
  350.1 3.7 collective-permute-start.9
  353.8 1.2 copy-start.5
  366.7 38.6 %collective-permute-start.10 = (f32[512,768]{1,0:T(8,128)}, f32[512,768]{1,0:T(8,128)S(1)}, u32[]{:S(2)}, u32[]{:S(2)}) collective-permute-start(f32[512,768]{1,0:T(8,128)} %get-tuple-element.65), channel_id=1, source_target_pairs={{16,0},{17,1},{18,2},{19,3},{20,4},{21,5},{22,6},{23,7},{24,8},{25... | collective-permute-start | bytes 4718600 | tf_op jit(solution)/shard_map/ppermute | solution.py:535
  433.7 171.5 %reduce-scatter.4.cloned.1.call-start = ((), (), s32[]{:S(2)}) async-start(), calls=%async_computation.4 | async-start | bytes 6684672 | tf_op jit(solution)/shard_map/reduce_scatter | solution.py:498
  454.2 3.7 collective-permute-start.11
  457.9 1.2 copy-start.4
  478.6 241.2 %reduce-scatter.6.cloned.1.call-start = ((), (), s32[]{:S(2)}) async-start(), calls=%async_computation.5 | async-start | bytes 10027008 | tf_op jit(solution)/shard_map/reduce_scatter | solution.py:498
  478.7 0.7 copy-start.19
  478.7 1.9 copy-start.3
  478.7 1.9 copy-start.8
  480.7 1.4 copy-start.12
  480.8 86.0 %collective-permute-start.13 = (bf16[256,768]{1,0:T(8,128)(2,1)S(1)}, bf16[256,768]{1,0:T(8,128)(2,1)S(1)}, u32[]{:S(2)}, u32[]{:S(2)}) collective-permute-start(bf16[256,768]{1,0:T(8,128)(2,1)S(1)} %get-tuple-element.113), channel_id=1, source_target_pairs={{1,0},{0,1},{5,2},{4,3},{3,4},{2,5},{7,6},{6,7},{9,8},{8,9},{13,10... | collective-permute-start | bytes 1179656 | tf_op jit(solution)/shard_map/ppermute | solution.py:438
  481.4 85.4 %collective-permute-start.12 = (bf16[256,768]{1,0:T(8,128)(2,1)S(1)}, bf16[256,768]{1,0:T(8,128)(2,1)S(1)}, u32[]{:S(2)}, u32[]{:S(2)}) collective-permute-start(bf16[256,768]{1,0:T(8,128)(2,1)S(1)} %get-tuple-element.112), channel_id=1, source_target_pairs={{0,0},{1,1},{4,2},{5,3},{2,4},{3,5},{6,6},{7,7},{8,8},{9,9},{12,10... | collective-permute-start | bytes 1179656 | tf_op jit(solution)/shard_map/ppermute | solution.py:438
Sparse Core Ops, SparseCore 0:
  12.2 69.0 all-gather.8
  83.5 52.7 all-gather.10
  139.2 79.9 all-gather.6
  433.8 83.5 reduce-scatter.7
  521.7 83.4 reduce-scatter.3
  609.1 110.6 reduce-scatter.5

commit v3 on v2

--- a/solution.py
+++ b/solution.py
@@ -13,6 +13,7 @@
 ALL = ("y", "core", "tensor")
 BF = jnp.bfloat16
 F32 = jnp.float32
+MESH = pl.DeviceIdType.MESH
 
 
 def dg(a, b, dims):
@@ -134,7 +135,7 @@
         y_ref[...] = (n * g_ref[1:2] + b_ref[1:2]).astype(BF)
 
 
-def ffn_back_kernel(dy_ref, n1_ref, i1_ref, n2_ref, i2_ref, gu_ref, wgu_ref, wd_ref, g_ref, b_ref, ggu_ref, gd_ref, dr1_ref, da_ref, ng_ref, hb_ref, df_ref, acc_ref):
+def ffn_back_kernel(dy_ref, n1_ref, i1_ref, n2_ref, i2_ref, gu_ref, wgu_ref, wd_ref, g_ref, b_ref, g_out, dr1_ref, da_ref, ng_ref, hb_ref, df_ref, acc_ref):
     z = pl.program_id(0)
     width = dy_ref.shape[1]
 
@@ -155,14 +156,15 @@
     s = 1.0 / (1.0 + jnp.exp(-gate))
     silu = gate * s
     act = (silu * up).astype(BF)
-    gd_ref[:, 0] = dg(df, act, TN).astype(BF).reshape(gd_ref.shape[0], -1, act.shape[1])
+    half = act.shape[1]
+    blocks = g_out.shape[0]
+    g_out[:, 0, :, 3 * half :] = dg(df, act, TN).astype(BF).reshape(blocks, -1, half)
     d_act = dg(df, wd_ref[:, 0].reshape(width, -1), NN)
     d_gate = (d_act * up * (s * (1.0 + gate * (1.0 - s)))).astype(BF)
     d_up = (d_act * silu).astype(BF)
-    half = d_up.shape[1]
     hb = hb_ref[...]
-    ggu_ref[:, 0, :, :half] = dg(hb, d_gate, TN).astype(BF).reshape(ggu_ref.shape[0], -1, half)
-    ggu_ref[:, 0, :, half:] = dg(hb, d_up, TN).astype(BF).reshape(ggu_ref.shape[0], -1, half)
+    g_out[:, 0, :, :half] = dg(hb, d_gate, TN).astype(BF).reshape(blocks, -1, half)
+    g_out[:, 0, :, half : 2 * half] = dg(hb, d_up, TN).astype(BF).reshape(blocks, -1, half)
     w = wgu_ref[:, 0].reshape(width, -1)
     acc_ref[...] += dg(d_gate, w[:, :half], NT) + dg(d_up, w[:, half:], NT)
 
@@ -218,7 +220,7 @@
         oth_ref[i, 1] = dv[:, rows:].astype(BF)
 
 
-def joint_back_kernel(x_ref, w_ref, dr1_ref, dq_ref, own_ref, got_ref, dwo_ref, cos_ref, sin_ref, g_ref, dz_ref):
+def joint_back_kernel(old_ref, x_ref, w_ref, dr1_ref, dq_ref, own_ref, got_ref, dwo_ref, cos_ref, sin_ref, g_ref, dz_ref):
     p = pl.program_id(0)
     x = x_ref[...]
     width = x.shape[1]
@@ -276,27 +278,31 @@
     return pl.BlockSpec(shape, lambda i: tuple(i if j == at else 0 for j in range(len(shape))))
 
 
+def joint_block(w):
+    return pl.BlockSpec((w.shape[0], 2, w.shape[2], 768), lambda i: (0, i, 0, 2))
+
+
 def sds(shape, kind):
     return jax.ShapeDtypeStruct(shape, kind)
 
 
 def forward(x, weights, norms, mask, tabs):
-    w1, w2, w3 = weights
+    w = weights
     gains, biases = norms
     rows, width = x.shape
     heads = width // 128
-    blocks, tp, depth = w1.shape[:3]
+    blocks, tp, depth, columns = w.shape
     steps = tp // 2
     cos, sin, cost, sint = tabs
     q, k, v = pl.pallas_call(
         qkv_kernel,
         grid=(steps,),
-        in_specs=[full((rows, width)), lead((blocks, 2, depth, 768), 1), full((rows, 128)), full((rows, 128))],
+        in_specs=[full((rows, width)), joint_block(w), full((rows, 128)), full((rows, 128))],
         out_specs=[lead((3, rows, 128))] * 3,
         out_shape=[sds((heads, rows, 128), BF)] * 3,
         compiler_params=BIG,
         name="qkv",
-    )(x, w1, cos, sin)
+    )(x, w, cos, sin)
     ko, vo = lax.ppermute((k, v), "core", [(0, 1), (1, 0)])
     pair = lead((1, rows, 128))
     o, e, l = pl.pallas_call(
@@ -308,16 +314,16 @@
         compiler_params=BIG,
         name="attn",
     )(q, k, v, ko, vo, mask)
-    hidden = w2.shape[3] // 2
+    hidden = columns // 4
     y, gu, n1, i1, n2, i2 = pl.pallas_call(
         ffn_kernel,
         grid=(tp,),
         in_specs=[
             full((rows, width)),
             full((heads, rows, 128)),
-            pl.BlockSpec((blocks, tp, depth, 256), lambda i: (0, 0, 0, 2)),
+            pl.BlockSpec((blocks, tp, depth, 256), lambda i: (0, 0, 0, 8)),
             lead((blocks, 1, depth, 2 * hidden), 1),
-            lead((blocks, 1, depth, hidden), 1),
+            pl.BlockSpec((blocks, 1, depth, hidden), lambda i: (0, i, 0, 3)),
             full((2, width)),
             full((2, width)),
         ],
@@ -326,48 +332,47 @@
         scratch_shapes=[VM((rows, width), F32), VM((rows, width), BF), VM((rows, width), F32)],
         compiler_params=BIG,
         name="ffn",
-    )(x, o, w1, w2, w3, gains, biases)
+    )(x, o, w, w, w, gains, biases)
     return y, (q, k, v, ko, vo, o, e, l, gu, n1, i1, n2, i2)
 
 
 def backward(x, dy, kept, weights, norms, tabs):
-    w1, w2, w3 = weights
+    w = weights
     gains, biases = norms
     q, k, v, ko, vo, o, e, l, gu, n1, i1, n2, i2 = kept
     rows, width = x.shape
     heads = width // 128
-    blocks, tp, depth = w1.shape[:3]
+    blocks, tp, depth, columns = w.shape
     steps = tp // 2
-    hidden = w2.shape[3] // 2
+    hidden = columns // 4
     cos, sin, cost, sint = tabs
     whole, stat = full((rows, width)), full((rows, 128))
-    g2, g3, dr1, da, ng = pl.pallas_call(
+    g, dr1, da, ng = pl.pallas_call(
         ffn_back_kernel,
         grid=(tp,),
         in_specs=[
             whole, whole, stat, whole, stat,
             lead((1, 2, rows, hidden)),
             lead((blocks, 1, depth, 2 * hidden), 1),
-            lead((blocks, 1, depth, hidden), 1),
+            pl.BlockSpec((blocks, 1, depth, hidden), lambda i: (0, i, 0, 3)),
             full((2, width)), full((2, width)),
         ],
         out_specs=[
-            lead((blocks, 1, depth, 2 * hidden), 1),
-            lead((blocks, 1, depth, hidden), 1),
+            lead((blocks, 1, depth, columns), 1),
             whole, whole, full((8, width)),
         ],
-        out_shape=[sds(w2.shape, BF), sds(w3.shape, BF), sds((rows, width), F32), sds((rows, width), BF), sds((8, width), F32)],
+        out_shape=[sds(w.shape, BF), sds((rows, width), F32), sds((rows, width), BF), sds((8, width), F32)],
         scratch_shapes=[VM((rows, width), BF), VM((rows, width), BF), VM((rows, width), F32)],
         compiler_params=BIG,
         name="ffn_back",
-    )(dy, n1, i1, n2, i2, gu, w2, w3, gains, biases)
+    )(dy, n1, i1, n2, i2, gu, w, w, gains, biases)
     three = lead((3, rows, 128))
     dq, own, oth, dwo = pl.pallas_call(
         attn_back_kernel,
         grid=(steps,),
         in_specs=[
             whole,
-            pl.BlockSpec((blocks, 2, depth, 256), lambda i: (0, i, 0, 2)),
+            pl.BlockSpec((blocks, 2, depth, 256), lambda i: (0, i, 0, 8)),
             three, three, three, three, three, three,
             lead((3, 2, 2 * rows, rows)),
             lead((3, 2, 8, rows)),
@@ -382,25 +387,239 @@
         ],
         compiler_params=BIG,
         name="attn_back",
-    )(da, w1, o, q, k, v, ko, vo, e, l, cost, sint)
+    )(da, w, o, q, k, v, ko, vo, e, l, cost, sint)
     got = lax.ppermute(oth, "core", [(0, 1), (1, 0)])
-    g1, dz = pl.pallas_call(
+    g, dz = pl.pallas_call(
         joint_back_kernel,
         grid=(steps,),
         in_specs=[
+            pl.BlockSpec(memory_space=pl.ANY),
             whole,
-            lead((blocks, 2, depth, 768), 1),
+            joint_block(w),
             whole, three,
             lead((3, 2, 128, rows)), lead((3, 2, 128, rows)),
             lead((1, width, 384)),
             full((HD // 2, rows)), full((HD // 2, rows)),
         ],
-        out_specs=[lead((blocks, 2, depth, 768), 1), whole],
-        out_shape=[sds(w1.shape, BF), sds((rows, width), F32)],
+        out_specs=[joint_block(w), whole],
+        out_shape=[sds(w.shape, BF), sds((rows, width), F32)],
+        input_output_aliases={0: 0},
         compiler_params=BIG,
         name="joint_back",
-    )(x, w1, dr1, dq, own, got, dwo, cost, sint)
-    return dz, (g1, g2, g3, ng)
+    )(g, x, w, dr1, dq, own, got, dwo, cost, sint)
+    return dz, (g, ng)
+
+
+WIDE = 128
+
+
+def sum_kernel(parts, g_ref, ng_ref, out_ref, nout_ref, own, land_c, land_y, land_r, land_l, land_n, own_sem, cs_sem, cr_sem, ys_sem, yr_sem, rs_sem, rr_sem, ls_sem, lr_sem, ns_sem, nr_sem):
+    y, c, z = lax.axis_index("y"), lax.axis_index("core"), lax.axis_index("tensor")
+    last = 3
+    near = {"core": 1 - c}
+    across = {"y": 1 - y}
+    right, left = {"tensor": jnp.minimum(z + 1, last)}, {"tensor": jnp.maximum(z - 1, 0)}
+    pair = {"tensor": z + 1 - 2 * lax.rem(z, 2)}
+    far = {"tensor": lax.rem(z + 2, 4)}
+    barrier = pltpu.get_barrier_semaphore()
+
+    def greet(device):
+        pl.semaphore_signal(barrier, inc=1, device_id=device, device_id_type=MESH)
+
+    greet(near)
+    greet(across)
+    greet(far)
+
+    @pl.when(z < last)
+    def _():
+        greet(right)
+
+    @pl.when(z > 0)
+    def _():
+        greet(left)
+
+    pl.semaphore_wait(barrier, 3 + jnp.where(z < last, 1, 0) + jnp.where(z > 0, 1, 0))
+
+    def columns(j):
+        return pl.ds(pl.multiple_of(j * WIDE, WIDE), WIDE)
+
+    def remote(src, dst, send, recv, device):
+        return pltpu.make_async_remote_copy(src, dst, send, recv, device_id=device, device_id_type=MESH)
+
+    def load(j):
+        return pltpu.make_async_copy(g_ref.at[:, c, :, :, columns(j)], own.at[j], own_sem.at[j])
+
+    def to_core(j):
+        return remote(g_ref.at[:, 1 - c, :, :, columns(j)], land_c.at[j], cs_sem.at[j], cr_sem.at[j], near)
+
+    def to_y(j):
+        return remote(land_c.at[j, 1 - y], land_y.at[j], ys_sem.at[j], yr_sem.at[j], across)
+
+    def norm_copy(k):
+        return remote(land_n.at[2 * k], land_n.at[2 * k + 1], ns_sem.at[k], nr_sem.at[k], (near, across, pair, far)[k])
+
+    def go_right(j, first, src):
+        return remote(src, land_r.at[j, pl.ds(first - 1, 4 - first)], rs_sem.at[j], rr_sem.at[j], right)
+
+    def go_left(j, count, src):
+        return remote(src, land_l.at[j, pl.ds(0, count)], ls_sem.at[j], lr_sem.at[j], left)
+
+    for j in range(2):
+        to_core(j).start()
+        load(j).start()
+    land_n[0] = ng_ref[...]
+    norm_copy(0).start()
+
+    def step(i, carry):
+        @pl.when(i + 2 < parts)
+        def _():
+            to_core(i + 2).start()
+            load(i + 2).start()
+
+        @pl.when(i < parts)
+        def _():
+            load(i).wait()
+            to_core(i).wait_recv()
+            land_c[i] = land_c[i] + own[i]
+            to_y(i).start()
+
+        @pl.when(jnp.logical_and(i >= 4, i - 4 < parts))
+        def _():
+            j = i - 4
+
+            @pl.when(z == 1)
+            def _():
+                go_left(j, 2, land_l.at[j, pl.ds(0, 2)]).wait_recv()
+                land_l[j, 0] = land_l[j, 0] + land_c[j, y, 0]
+                go_left(j, 1, land_l.at[j, pl.ds(0, 1)]).start()
+
+            @pl.when(z == 2)
+            def _():
+                go_right(j, 2, land_r.at[j, pl.ds(1, 2)]).wait_recv()
+                land_r[j, 2] = land_r[j, 2] + land_c[j, y, 3]
+                go_right(j, 3, land_r.at[j, pl.ds(2, 1)]).start()
+
+        @pl.when(jnp.logical_and(i >= 3, i - 3 < parts))
+        def _():
+            j = i - 3
+
+            @pl.when(z == 1)
+            def _():
+                go_right(j, 1, land_r.at[j]).wait_recv()
+                for k in (2, 3):
+                    land_r[j, k - 1] = land_r[j, k - 1] + land_c[j, y, k]
+                go_right(j, 2, land_r.at[j, pl.ds(1, 2)]).start()
+
+            @pl.when(z == 2)
+            def _():
+                go_left(j, 3, land_l.at[j]).wait_recv()
+                for k in (0, 1):
+                    land_l[j, k] = land_l[j, k] + land_c[j, y, k]
+                go_left(j, 2, land_l.at[j, pl.ds(0, 2)]).start()
+
+        @pl.when(jnp.logical_and(i >= 2, i - 2 < parts))
+        def _():
+            j = i - 2
+            to_y(j).wait_recv()
+            land_c[j, y] = land_c[j, y] + land_y[j]
+
+            @pl.when(z == 0)
+            def _():
+                go_right(j, 1, land_c.at[j, y, pl.ds(1, 3)]).start()
+
+            @pl.when(z == last)
+            def _():
+                go_left(j, 3, land_c.at[j, y, pl.ds(0, 3)]).start()
+
+        @pl.when(i >= 5)
+        def _():
+            j = i - 5
+            mine = land_c[j, y, z].astype(F32)
+
+            @pl.when(z == 0)
+            def _():
+                go_left(j, 1, land_l.at[j, pl.ds(0, 1)]).wait_recv()
+                out_ref[:, columns(j)] = mine + land_l[j, 0].astype(F32)
+
+            @pl.when(z == 1)
+            def _():
+                out_ref[:, columns(j)] = mine + land_r[j, 0].astype(F32) + land_l[j, 1].astype(F32)
+
+            @pl.when(z == 2)
+            def _():
+                out_ref[:, columns(j)] = mine + land_r[j, 1].astype(F32) + land_l[j, 2].astype(F32)
+
+            @pl.when(z == last)
+            def _():
+                go_right(j, 3, land_r.at[j, pl.ds(2, 1)]).wait_recv()
+                out_ref[:, columns(j)] = mine + land_r[j, 2].astype(F32)
+
+        for k in range(4):
+
+            @pl.when(i == 3 * (k + 1))
+            def _():
+                norm_copy(k).wait()
+                total = land_n[2 * k] + land_n[2 * k + 1]
+                if k < 3:
+                    land_n[2 * k + 2] = total
+                    norm_copy(k + 1).start()
+                else:
+                    nout_ref[...] = total
+
+        return carry
+
+    lax.fori_loop(0, parts + 5, step, 0)
+
+    def finish(j, carry):
+        to_core(j).wait_send()
+        to_y(j).wait_send()
+
+        @pl.when(z == 0)
+        def _():
+            go_right(j, 1, land_c.at[j, y, pl.ds(1, 3)]).wait_send()
+
+        @pl.when(z == 1)
+        def _():
+            go_right(j, 2, land_r.at[j, pl.ds(1, 2)]).wait_send()
+            go_left(j, 1, land_l.at[j, pl.ds(0, 1)]).wait_send()
+
+        @pl.when(z == 2)
+        def _():
+            go_right(j, 3, land_r.at[j, pl.ds(2, 1)]).wait_send()
+            go_left(j, 2, land_l.at[j, pl.ds(0, 2)]).wait_send()
+
+        @pl.when(z == last)
+        def _():
+            go_left(j, 3, land_c.at[j, y, pl.ds(0, 3)]).wait_send()
+
+        return carry
+
+    lax.fori_loop(0, parts, finish, 0)
+
+
+def sum_over_section(g, ng):
+    rows, columns = g.shape[2:]
+    parts = columns // WIDE
+    g = g.reshape(2, 2, 4, rows, columns)
+    dma = pltpu.SemaphoreType.DMA
+    return pl.pallas_call(
+        functools.partial(sum_kernel, parts),
+        in_specs=[pl.BlockSpec(memory_space=pl.ANY), pl.BlockSpec(memory_space=VM)],
+        out_specs=[pl.BlockSpec(memory_space=VM)] * 2,
+        out_shape=[sds((rows, columns), F32), sds(ng.shape, F32)],
+        scratch_shapes=[
+            VM((parts, 2, 4, rows, WIDE), BF),
+            VM((parts, 2, 4, rows, WIDE), BF),
+            VM((parts, 4, rows, WIDE), BF),
+            VM((parts, 3, rows, WIDE), BF),
+            VM((parts, 3, rows, WIDE), BF),
+            VM((8,) + ng.shape, F32),
+        ]
+        + [dma((parts,))] * 9
+        + [dma((4,))] * 2,
+        compiler_params=pltpu.CompilerParams(collective_id=0, has_side_effects=True, vmem_limit_bytes=58 << 20),
+        name="grad_sum",
+    )(g, ng)
 
 
 def swap_pairs(tp, step, dp_axes):
@@ -461,11 +680,13 @@
     first = jnp.concatenate(
         [heads[:, :, :2].reshape(rows, -1), heads[:, :, 2].reshape(rows, -1), mine[:, 2], mine[:, :2].reshape(rows, -1)], axis=1
     )
-    return first, w_gate_up.reshape(rows, -1), w_down.T
-
-
-def unpack_shard(first, pair, down):
-    rows = first.shape[0]
+    return jnp.concatenate([w_gate_up.reshape(rows, -1), first, w_down.T], axis=1)
+
+
+def unpack_shard(packed):
+    rows, columns = packed.shape
+    half = columns // 2
+    pair, first, down = packed[:, :half], packed[:, half : half + 768], packed[:, half + 768 :]
     odd = lax.axis_index("tensor") % 2 == 1
     both = first[:, :384].reshape(rows, 3, 2, HD)
     single = first[:, 384:576].reshape(rows, 3, 1, HD)
@@ -506,8 +727,7 @@
     assert micro * 2 == tp
     length = own * tp
     rows = length // 2
-    shards = pack_shard(w_qkv[0], w_out[0], w_gate_up[0], w_down[0])
-    weights = tuple(gather_shard(s, dp, tp) for s in shards)
+    weights = gather_shard(pack_shard(w_qkv[0], w_out[0], w_gate_up[0], w_down[0]), dp, tp)
     norms = jnp.concatenate([norm_gains, norm_biases])
     norms = lax.all_gather(norms, ("y", "core"), axis=1, tiled=True).astype(F32)
     norms = (norms[0].reshape(2, width), norms[1].reshape(2, width))
@@ -531,16 +751,22 @@
     received = lax.ppermute(y, "section", [(0, 1)])
     inputs = jnp.where(section == 0, tokens, received)
     y, kept = forward(inputs, weights, norms, mask, tabs)
-    dz, grads = backward(inputs, grad_top.astype(F32), kept, weights, norms, tabs)
-    received = lax.ppermute(dz, "section", [(1, 0)])
-    dy = jnp.where(section == 0, received, grad_top.astype(F32))
+    dz, grads = backward(inputs, grad_top, kept, weights, norms, tabs)
+    received = lax.ppermute(dz.astype(BF), "section", [(1, 0)])
+    dy = jnp.where(section == 0, received, grad_top)
     dz, grads = backward(inputs, dy, kept, weights, norms, tabs)
     ends = to_positions(jnp.where(section == 0, dz.astype(BF), y), tp)
-    sums = [scatter_sum(g, dp, tp) for g in grads[:3]]
-    outs = unpack_shard(*sums)
-    ng = grads[3]
-    gains = lax.psum_scatter(ng[0:2].reshape(-1), ALL, scatter_dimension=0, tiled=True)
-    biases = lax.psum_scatter(ng[2:4].reshape(-1), ALL, scatter_dimension=0, tiled=True)
+    g, ng = grads
+    if dp == 4 and tp == 4:
+        mine, total = sum_over_section(g, ng)
+        index = lax.axis_index(ALL)
+        small = lax.dynamic_slice_in_dim(total[:4].reshape(2, dp * tp, -1), index, 1, 1)
+        gains, biases = small[0, 0], small[1, 0]
+    else:
+        mine = scatter_sum(g, dp, tp)
+        gains = lax.psum_scatter(ng[0:2].reshape(-1), ALL, scatter_dimension=0, tiled=True)
+        biases = lax.psum_scatter(ng[2:4].reshape(-1), ALL, scatter_dimension=0, tiled=True)
+    outs = unpack_shard(mine)
     return (ends[None],) + tuple(t[None] for t in outs + (gains, biases))
 
 

time: 735 us -> 582 us (0.79)
  waiting for transfers between devices: 356 us -> 150 us
  Pallas kernels: 198 us -> 330 us
  blocking collectives: 96.2 us -> 13.8 us
    reduce_scatter x3 -> x0, waiting for transfers between devices: 147 us -> none  [scatter_sum(): lax.psum_scatter(parts, ALL, scatter_dimension=0, tiled=False).astype(F32)]
    pallas_call x2 -> x3, Pallas kernels: 23.4 us -> 155 us  [the longest x1 131 us: sum_over_section(): pl.pallas_call(functools.partial(sum_kernel, parts), in_specs=[pl.BlockSp...]
    unnamed x1 -> x0, blocking collectives: 83.5 us -> none
    all_gather x3 -> x1, waiting for transfers between devices: 136 us -> 98.8 us  [gather_shard(): got = lax.all_gather(shard, ALL, axis=0, tiled=False)]
    ppermute x1, waiting for transfers between devices: 37.3 us -> 20.2 us  [on_device(): received = lax.ppermute(dz.astype(BF), 'section', [(1, 0)])]
  transfers between devices with their start and end apart: 20 -> 15, of which waited for: 11 -> 8; matrix products, arithmetic and copies ran while one was open for 4% -> 5% of each run, Pallas kernels for 8% -> 0%
where the time goes in v3:
time: 582 us; the launch traced here: 572 us
  Pallas kernels  330 us (57%)
  waiting for transfers between devices  150 us (26%)
  local copies, waits for them, and re-layouts  26.8 us (5%)
  other arithmetic  19.3 us (3%)
  starting transfers between devices  17 us (3%)
  between operations  15 us (3%)
  blocking collectives  13.8 us (2%)
    pallas_call x1, Pallas kernels, sum_over_section(): pl.pallas_call(functools.partial(sum_kernel, parts), in_specs=[pl.BlockSp...  131 us
    all_gather x1, waiting for transfers between devices, gather_shard(): got = lax.all_gather(shard, ALL, axis=0, tiled=False)  98.8 us
    pallas_call x2, Pallas kernels, backward(): pl.pallas_call(ffn_back_kernel, grid=(tp,), in_specs=[whole, whole, stat,...  54.4 us
    pallas_call x2, Pallas kernels, backward(): pl.pallas_call(attn_back_kernel, grid=(steps,), in_specs=[whole, pl.Block...  40.2 us
    pallas_call x2, Pallas kernels, forward(): pl.pallas_call(ffn_kernel, grid=(tp,), in_specs=[full((rows, width)), ful...  34.4 us
    pallas_call x2, Pallas kernels, forward(): pl.pallas_call(attn_kernel, grid=(heads,), in_specs=[pair] * 5 + [full((2...  32.7 us
    pallas_call x2, Pallas kernels, backward(): pl.pallas_call(joint_back_kernel, grid=(steps,), in_specs=[pl.BlockSpec(m...  23.6 us
    ppermute x1, waiting for transfers between devices, on_device(): received = lax.ppermute(dz.astype(BF), 'section', [(1, 0)])  20.2 us
  transfers between devices with their start and end apart: 15, of which 8 were waited for; matrix products, arithmetic and copies ran while one was open for 5% of the time, Pallas kernels for 0%

profile of v3, /device:TPU:0, one launch (start us, length us, event | category | flops | bytes accessed | tf_op | source)
XLA Modules:
  0.0 571.9 jit_solution(14953103289357338056)
XLA Ops:
  7.2 1.2 copy.69
  9.4 1.7 concatenate.39
  12.0 3.0 collective-permute-start.1
  15.1 1.4 collective-permute-start
  16.6 1.4 collective-permute-start.2
  20.4 8.6 %all-gather.1 = s32[2,2,8]{2,1,0:T(2,128)} all-gather(s32[1,2,8]{2,1,0:T(2,128)} %bitcast.111), channel_id=1, replica_groups=mesh['section'=2,'y'=2,'core'=2,'tensor'=4] {'core'}, dimensions={0}, use_global_device_ids=true | all-gather | bytes 192 | tf_op jit(solution)/shard_map/all_gather | solution.py:736
  31.0 1.1 pad_maximum_fusion
  32.7 5.0 collective-permute-done.3
  37.7 1.1 pad_maximum_fusion.1
  39.4 1.4 broadcast_select_fusion.1
  40.8 98.8 %all-gather.4.cloned.1.call-done = bf16[3072,3072]{1,0:T(8,128)(2,1)} async-done(((bf16[192,3072]{1,0:T(8,128)(2,1)}), bf16[3072,3072]{1,0:T(8,128)(2,1)}) %all-gather.4.cloned.1.call-update) | async-done | bytes 18874384 | tf_op jit(solution)/shard_map/all_gather | solution.py:710
  139.6 6.5 %qkv.2 = (bf16[6,512,128]{2,1,0:T(8,128)(2,1)}, bf16[6,512,128]{2,1,0:T(8,128)(2,1)}, bf16[6,512,128]{2,1,0:T(8,128)(2,1)}) custom-call(bf16[512,768]{1,0:T(8,128)(2,1)} %bitcast.87, bf16[4,4,192,3072]{3,2,1,0:T(8,128)(2,1)} %bitcast.70, f32[512,128]{1,0:T(8,128)} %pad_maximum_fusion.3.cos_ref, f32[512,128]{1,0:T(8,128)} %pad_maximum_fusion.4.sin_ref), custom_call_target="tpu_custom_call" | custom-call | tf_op jit(solution)/shard_map/qkv/pallas_call | solution.py:297
  147.4 5.1 all_gather.15
  153.9 1.5 compare_select_fusion.m_ref
  156.6 16.4 %attn.2 = (bf16[6,512,128]{2,1,0:T(8,128)(2,1)}, bf16[6,2,1024,512]{3,2,1,0:T(8,128)(2,1)}, f32[6,2,8,512]{3,2,1,0:T(8,128)}) custom-call(bf16[6,512,128]{2,1,0:T(8,128)(2,1)} %get-tuple-element.45.q_ref, bf16[6,512,128]{2,1,0:T(8,128)(2,1)} %get-tuple-element.46.k_ref, bf16[6,512,128]{2,1,0:T(8,128)(2,1)} %get-tuple-element.47.v_ref, ...), custom_call_target="tpu_custom_call" | custom-call | tf_op jit(solution)/shard_map/attn/pallas_call | solution.py:308
  173.0 17.3 %ffn.2 = (bf16[512,768]{1,0:T(8,128)(2,1)}, bf16[4,2,512,768]{3,2,1,0:T(8,128)(2,1)}, f32[512,768]{1,0:T(8,128)}, f32[512,128]{1,0:T(8,128)}, f32[512,768]{1,0:T(8,128)}, /*index=5*/f32[512,128]{1,0:T(8,128)}) custom-call(bf16[512,768]{1,0:T(8,128)(2,1)} %bitcast.88, bf16[6,512,128]{2,1,0:T(8,128)(2,1)} %get-tuple-element.48.o_ref, ...), custom_call_target="tpu_custom_call" | custom-call | tf_op jit(solution)/shard_map/ffn/pallas_call | solution.py:318
  190.2 3.9 collective-permute-start.6
  194.1 17.1 %collective-permute-done.6 = bf16[512,768]{1,0:T(8,128)(2,1)S(1)} collective-permute-done((bf16[512,768]{1,0:T(8,128)(2,1)}, bf16[512,768]{1,0:T(8,128)(2,1)S(1)}, u32[]{:S(2)}, u32[]{:S(2)}) %collective-permute-start.6) | collective-permute-done | bytes 786464 | tf_op jit(solution)/shard_map/ppermute | solution.py:751
  211.2 1.1 broadcast_select_fusion.3.x_ref
  212.3 6.5 %qkv.3 = (bf16[6,512,128]{2,1,0:T(8,128)(2,1)}, bf16[6,512,128]{2,1,0:T(8,128)(2,1)}, bf16[6,512,128]{2,1,0:T(8,128)(2,1)}) custom-call(bf16[512,768]{1,0:T(8,128)(2,1)} %broadcast_select_fusion.3.x_ref, bf16[4,4,192,3072]{3,2,1,0:T(8,128)(2,1)} %bitcast.74, f32[512,128]{1,0:T(8,128)} %pad_maximum_fusion.3.cos_ref, f32[512,128]{1,0:T(8,128)} %pad_maximum_fusion.4.sin_ref), custom_call_target="tpu_custom_call" | custom-call | tf_op jit(solution)/shard_map/qkv/pallas_call | solution.py:297
  220.3 1.0 collective-permute-done.7.ko_ref
  221.3 1.1 collective-permute-done.8.vo_ref
  223.3 16.4 %attn.3 = (bf16[6,512,128]{2,1,0:T(8,128)(2,1)}, bf16[6,2,1024,512]{3,2,1,0:T(8,128)(2,1)}, f32[6,2,8,512]{3,2,1,0:T(8,128)}) custom-call(bf16[6,512,128]{2,1,0:T(8,128)(2,1)} %get-tuple-element.50.q_ref, bf16[6,512,128]{2,1,0:T(8,128)(2,1)} %get-tuple-element.51.k_ref, bf16[6,512,128]{2,1,0:T(8,128)(2,1)} %get-tuple-element.52.v_ref, ...), custom_call_target="tpu_custom_call" | custom-call | tf_op jit(solution)/shard_map/attn/pallas_call | solution.py:308
  239.7 17.2 %ffn.3 = (bf16[512,768]{1,0:T(8,128)(2,1)}, bf16[4,2,512,768]{3,2,1,0:T(8,128)(2,1)}, f32[512,768]{1,0:T(8,128)}, f32[512,128]{1,0:T(8,128)}, f32[512,768]{1,0:T(8,128)}, /*index=5*/f32[512,128]{1,0:T(8,128)}) custom-call(bf16[512,768]{1,0:T(8,128)(2,1)} %broadcast_select_fusion.3.x_ref, bf16[6,512,128]{2,1,0:T(8,128)(2,1)} %get-tuple-element.53.o_ref, ...), custom_call_target="tpu_custom_call" | custom-call | tf_op jit(solution)/shard_map/ffn/pallas_call | solution.py:318
  256.9 27.2 %ffn_back.2 = (bf16[4,4,192,3072]{3,2,1,0:T(8,128)(2,1)}, f32[512,768]{1,0:T(8,128)}, bf16[512,768]{1,0:T(8,128)(2,1)}, f32[8,768]{1,0:T(8,128)}) custom-call(bf16[512,768]{1,0:T(8,128)(2,1)} %bitcast.89, f32[512,768]{1,0:T(8,128)} %get-tuple-element.54.n1_ref, f32[512,128]{1,0:T(8,128)} %get-tuple-element.55.i1_ref, f32[512,768]{1,0:T(8,128)} %get-tuple-element.56.n2_ref, ...), custom_call_target="tpu_custom_call" | custom-call | tf_op jit(solution)/shard_map/ffn_back/pallas_call | solution.py:350
  284.1 20.1 %attn_back.2 = (bf16[6,512,128]{2,1,0:T(8,128)(2,1)}, f32[6,2,128,512]{3,2,1,0:T(8,128)}, bf16[6,2,128,512]{3,2,1,0:T(8,128)(2,1)}, bf16[2,768,384]{2,1,0:T(8,128)(2,1)}) custom-call(bf16[512,768]{1,0:T(8,128)(2,1)} %get-tuple-element.61.da_ref, bf16[4,4,192,3072]{3,2,1,0:T(8,128)(2,1)} %bitcast.80, bf16[6,512,128]{2,1,0:T(8,128)(2,1)} %get-tuple-element.53.o_ref, ...), custom_call_target="tpu_custom_call" | custom-call | tf_op jit(solution)/shard_map/attn_back/pallas_call | solution.py:370
  304.4 3.5 collective-permute-done.9.got_ref
  307.9 1.2 copy-done.6
  309.0 11.7 %joint_back.2 = (bf16[4,4,192,3072]{3,2,1,0:T(8,128)(2,1)}, f32[512,768]{1,0:T(8,128)}) custom-call(bf16[4,4,192,3072]{3,2,1,0:T(8,128)(2,1)} %get-tuple-element.59.old_ref, bf16[512,768]{1,0:T(8,128)(2,1)} %broadcast_select_fusion.3.x_ref, bf16[4,4,192,3072]{3,2,1,0:T(8,128)(2,1)} %bitcast.81, ...), custom_call_target="tpu_custom_call", output_to_operand_aliasing={{0}: (0, {})} | custom-call | tf_op jit(solution)/shard_map/joint_back/pallas_call | solution.py:392
  320.7 1.6 convert_element_type.26
  322.3 1.3 collective-permute-start.10
  323.6 20.2 %collective-permute-done.10 = bf16[512,768]{1,0:T(8,128)(2,1)S(1)} collective-permute-done((bf16[512,768]{1,0:T(8,128)(2,1)S(1)}, bf16[512,768]{1,0:T(8,128)(2,1)S(1)}, u32[]{:S(2)}, u32[]{:S(2)}) %collective-permute-start.10) | collective-permute-done | bytes 786464 | tf_op jit(solution)/shard_map/ppermute | solution.py:755
  343.8 1.0 broadcast_select_fusion.2.dy_ref
  344.8 27.2 %ffn_back.3 = (bf16[4,4,192,3072]{3,2,1,0:T(8,128)(2,1)}, f32[512,768]{1,0:T(8,128)}, bf16[512,768]{1,0:T(8,128)(2,1)}, f32[8,768]{1,0:T(8,128)}) custom-call(bf16[512,768]{1,0:T(8,128)(2,1)} %broadcast_select_fusion.2.dy_ref, f32[512,768]{1,0:T(8,128)} %get-tuple-element.54.n1_ref, f32[512,128]{1,0:T(8,128)} %get-tuple-element.55.i1_ref, ...), custom_call_target="tpu_custom_call" | custom-call | tf_op jit(solution)/shard_map/ffn_back/pallas_call | solution.py:350
  372.0 20.1 %attn_back.3 = (bf16[6,512,128]{2,1,0:T(8,128)(2,1)}, f32[6,2,128,512]{3,2,1,0:T(8,128)}, bf16[6,2,128,512]{3,2,1,0:T(8,128)(2,1)}, bf16[2,768,384]{2,1,0:T(8,128)(2,1)}) custom-call(bf16[512,768]{1,0:T(8,128)(2,1)} %get-tuple-element.71.da_ref, bf16[4,4,192,3072]{3,2,1,0:T(8,128)(2,1)} %bitcast.84, bf16[6,512,128]{2,1,0:T(8,128)(2,1)} %get-tuple-element.53.o_ref, ...), custom_call_target="tpu_custom_call" | custom-call | tf_op jit(solution)/shard_map/attn_back/pallas_call | solution.py:370
  392.3 3.5 collective-permute-done.11.got_ref
  395.8 1.2 copy-done.5
  397.0 11.9 %joint_back.3 = (bf16[4,4,192,3072]{3,2,1,0:T(8,128)(2,1)}, f32[512,768]{1,0:T(8,128)}) custom-call(bf16[4,4,192,3072]{3,2,1,0:T(8,128)(2,1)} %get-tuple-element.69.old_ref, bf16[512,768]{1,0:T(8,128)(2,1)} %broadcast_select_fusion.3.x_ref, bf16[4,4,192,3072]{3,2,1,0:T(8,128)(2,1)} %bitcast.85, ...), custom_call_target="tpu_custom_call", output_to_operand_aliasing={{0}: (0, {})} | custom-call | tf_op jit(solution)/shard_map/joint_back/pallas_call | solution.py:392
  408.9 131.3 %grad_sum.1 = (f32[192,3072]{1,0:T(8,128)}, f32[8,768]{1,0:T(8,128)}) custom-call(bf16[2,2,4,192,3072]{4,3,2,1,0:T(8,128)(2,1)} %bitcast.86, f32[8,768]{1,0:T(8,128)} %get-tuple-element.79.ng_ref), custom_call_target="tpu_custom_call" | custom-call | tf_op jit(solution)/shard_map/grad_sum/pallas_call | solution.py:605
  542.2 1.6 slice_bitcast_fusion.1
  544.9 4.6 collective-permute-start.12
  552.1 2.1 copy.82
  554.2 1.6 copy.79
  555.8 1.6 copy.80
  557.4 1.8 broadcast_in_dim_reshape.4
  559.2 1.7 maximum_select_fusion.2
  561.8 1.2 pad_maximum_fusion.2
  563.6 1.0 select_bitcast_fusion
  (111 shorter events, 20.8 us)
Async XLA Ops:
  7.2 1.4 copy-start.14
  7.2 1.5 copy-start.13
  7.2 132.4 %all-gather.4.cloned.1.call-start = ((), (), s32[]{:S(2)}) async-start(), calls=%async_computation | async-start | bytes 20054016 | tf_op jit(solution)/shard_map/all_gather | solution.py:710
  8.5 1.0 copy-start.15
  8.9 2.3 copy-start.8
  9.4 7.0 %copy-start.9 = (bf16[2,256,768]{2,1,0:T(8,128)(2,1)S(1)}, bf16[2,256,768]{2,1,0:T(8,128)(2,1)}, u32[]{:S(2)}) copy-start(bf16[2,256,768]{2,1,0:T(8,128)(2,1)} %param.11) | copy-start | bytes 2359300
  12.0 18.9 %collective-permute-start.1 = (bf16[256,768]{1,0:T(8,128)(2,1)}, bf16[256,768]{1,0:T(8,128)(2,1)S(1)}, u32[]{:S(2)}, u32[]{:S(2)}) collective-permute-start(bf16[256,768]{1,0:T(8,128)(2,1)} %get-tuple-element.117), channel_id=1, source_target_pairs={{0,1},{1,0},{2,5},{3,4},{4,3},{5,2},{6,7},{7,6},{8,9},{9,8},{10,13... | collective-permute-start | bytes 1179656 | tf_op jit(solution)/shard_map/ppermute | solution.py:643
  15.1 15.9 %collective-permute-start = (bf16[256,768]{1,0:T(8,128)(2,1)S(1)}, bf16[256,768]{1,0:T(8,128)(2,1)}, u32[]{:S(2)}, u32[]{:S(2)}) collective-permute-start(bf16[256,768]{1,0:T(8,128)(2,1)S(1)} %get-tuple-element.116), channel_id=1, source_target_pairs={{0,0},{1,1},{2,4},{3,5},{4,2},{5,3},{6,6},{7,7},{8,8},{9,9},{10,12... | collective-permute-start | bytes 1179656 | tf_op jit(solution)/shard_map/ppermute | solution.py:643
  16.5 21.2 %collective-permute-start.3 = (bf16[256,768]{1,0:T(8,128)(2,1)S(1)}, bf16[256,768]{1,0:T(8,128)(2,1)S(1)}, u32[]{:S(2)}, u32[]{:S(2)}) collective-permute-start(bf16[256,768]{1,0:T(8,128)(2,1)S(1)} %get-tuple-element.119), channel_id=1, source_target_pairs={{0,1},{1,0},{2,5},{3,4},{4,3},{5,2},{6,7},{7,6},{8,9},{9,8},{10,13... | collective-permute-start | bytes 1179656 | tf_op jit(solution)/shard_map/ppermute | solution.py:643
  16.6 21.1 %collective-permute-start.2 = (bf16[256,768]{1,0:T(8,128)(2,1)S(1)}, bf16[256,768]{1,0:T(8,128)(2,1)}, u32[]{:S(2)}, u32[]{:S(2)}) collective-permute-start(bf16[256,768]{1,0:T(8,128)(2,1)S(1)} %get-tuple-element.118), channel_id=1, source_target_pairs={{0,0},{1,1},{2,4},{3,5},{4,2},{5,3},{6,6},{7,7},{8,8},{9,9},{10,12... | collective-permute-start | bytes 1179656 | tf_op jit(solution)/shard_map/ppermute | solution.py:643
  18.0 13.0 %copy-start.17 = (f32[32]{0:T(128)}, f32[32]{0:T(128)S(1)}, u32[]{:S(2)}) copy-start(f32[32]{0:T(128)S(1)} %multiply_power_fusion) | copy-start | bytes 388
  32.1 7.3 %copy-start.20 = (pred[2]{0:T(512)(128)(4,1)S(1)}, pred[2]{0:T(512)(128)(4,1)}, u32[]{:S(2)}) copy-start(pred[2]{0:T(512)(128)(4,1)} %get-tuple-element.130) | copy-start | bytes 10
  146.0 9.4 %collective-permute-start.4 = (bf16[6,512,128]{2,1,0:T(8,128)(2,1)}, bf16[6,512,128]{2,1,0:T(8,128)(2,1)S(1)}, u32[]{:S(2)}, u32[]{:S(2)}) collective-permute-start(bf16[6,512,128]{2,1,0:T(8,128)(2,1)} %get-tuple-element.46.k_ref), channel_id=1, source_target_pairs={{0,4},{4,0},{1,5},{5,1},{2,6},{6,2},{3,7},{7,3},{8,12},{12,8},{9,1... | collective-permute-start | bytes 2359304 | tf_op jit(solution)/shard_map/ppermute | solution.py:306
  146.0 9.4 %collective-permute-start.5 = (bf16[6,512,128]{2,1,0:T(8,128)(2,1)}, bf16[6,512,128]{2,1,0:T(8,128)(2,1)S(1)}, u32[]{:S(2)}, u32[]{:S(2)}) collective-permute-start(bf16[6,512,128]{2,1,0:T(8,128)(2,1)} %get-tuple-element.47.v_ref), channel_id=1, source_target_pairs={{0,4},{4,0},{1,5},{5,1},{2,6},{6,2},{3,7},{7,3},{8,12},{12,8},{9,1... | collective-permute-start | bytes 2359304 | tf_op jit(solution)/shard_map/ppermute | solution.py:306
  155.4 0.9 copy-start.11
  155.5 1.1 copy-start.12
  173.0 38.2 %copy-start = (bf16[2,256,768]{2,1,0:T(8,128)(2,1)S(1)}, bf16[2,256,768]{2,1,0:T(8,128)(2,1)}, u32[]{:S(2)}) copy-start(bf16[2,256,768]{2,1,0:T(8,128)(2,1)} %get-tuple-element.128) | copy-start | bytes 2359300
  190.2 21.0 %collective-permute-start.6 = (bf16[512,768]{1,0:T(8,128)(2,1)}, bf16[512,768]{1,0:T(8,128)(2,1)S(1)}, u32[]{:S(2)}, u32[]{:S(2)}) collective-permute-start(bf16[512,768]{1,0:T(8,128)(2,1)} %get-tuple-element.49), channel_id=1, source_target_pairs={{0,16},{1,17},{2,18},{3,19},{4,20},{5,21},{6,22},{7,23},{8,24},{9,... | collective-permute-start | bytes 2359304 | tf_op jit(solution)/shard_map/ppermute | solution.py:751
  212.3 7.0 %copy-start.18 = (f32[32]{0:T(128)S(1)}, f32[32]{0:T(128)}, u32[]{:S(2)}) copy-start(f32[32]{0:T(128)} %copy-done.17) | copy-start | bytes 388
  218.8 2.5 collective-permute-start.7
  218.8 3.6 collective-permute-start.8
  221.3 1.1 copy-start.2
  222.4 0.9 copy-start.3
  304.2 3.7 collective-permute-start.9
  307.9 1.2 copy-start.6
  320.7 23.1 %copy-start.1 = (bf16[2,256,768]{2,1,0:T(8,128)(2,1)S(1)}, bf16[2,256,768]{2,1,0:T(8,128)(2,1)}, u32[]{:S(2)}) copy-start(bf16[2,256,768]{2,1,0:T(8,128)(2,1)} %get-tuple-element.127) | copy-start | bytes 2359300
  322.3 21.5 %collective-permute-start.10 = (bf16[512,768]{1,0:T(8,128)(2,1)S(1)}, bf16[512,768]{1,0:T(8,128)(2,1)S(1)}, u32[]{:S(2)}, u32[]{:S(2)}) collective-permute-start(bf16[512,768]{1,0:T(8,128)(2,1)S(1)} %convert_element_type.26), channel_id=1, source_target_pairs={{16,0},{17,1},{18,2},{19,3},{20,4},{21,5},{22,6},{23,7},{24,8},{25... | collective-permute-start | bytes 2359304 | tf_op jit(solution)/shard_map/ppermute | solution.py:755
  392.1 3.7 collective-permute-start.11
  395.8 1.2 copy-start.5
  408.9 134.9 %copy-start.7 = (f32[512,768]{1,0:T(8,128)S(1)}, f32[512,768]{1,0:T(8,128)}, u32[]{:S(2)}) copy-start(f32[512,768]{1,0:T(8,128)} %get-tuple-element.76) | copy-start | bytes 4718596
  408.9 134.9 %copy-start.10 = (bf16[512,768]{1,0:T(8,128)(2,1)S(1)}, bf16[512,768]{1,0:T(8,128)(2,1)}, u32[]{:S(2)}) copy-start(bf16[512,768]{1,0:T(8,128)(2,1)} %get-tuple-element.77) | copy-start | bytes 2359300
  544.0 5.8 %copy-start.16 = (f32[8,768]{1,0:T(8,128)S(1)}, f32[8,768]{1,0:T(8,128)}, u32[]{:S(2)}) copy-start(f32[8,768]{1,0:T(8,128)} %get-tuple-element.81) | copy-start | bytes 73732
  544.0 7.3 %copy-start.4 = (f32[192,3072]{1,0:T(8,128)S(1)}, f32[192,3072]{1,0:T(8,128)}, u32[]{:S(2)}) copy-start(f32[192,3072]{1,0:T(8,128)} %get-tuple-element.80) | copy-start | bytes 7077892
  544.9 16.9 %collective-permute-start.13 = (bf16[256,768]{1,0:T(8,128)(2,1)}, bf16[256,768]{1,0:T(8,128)(2,1)}, u32[]{:S(2)}, u32[]{:S(2)}) collective-permute-start(bf16[256,768]{1,0:T(8,128)(2,1)} %get-tuple-element.115), channel_id=1, source_target_pairs={{1,0},{0,1},{5,2},{4,3},{3,4},{2,5},{7,6},{6,7},{9,8},{8,9},{13,10... | collective-permute-start | bytes 1179656 | tf_op jit(solution)/shard_map/ppermute | solution.py:657
  544.9 16.9 %collective-permute-start.12 = (bf16[256,768]{1,0:T(8,128)(2,1)}, bf16[256,768]{1,0:T(8,128)(2,1)}, u32[]{:S(2)}, u32[]{:S(2)}) collective-permute-start(bf16[256,768]{1,0:T(8,128)(2,1)} %get-tuple-element.114), channel_id=1, source_target_pairs={{0,0},{1,1},{4,2},{5,3},{2,4},{3,5},{6,6},{7,7},{8,8},{9,9},{12,10... | collective-permute-start | bytes 1179656 | tf_op jit(solution)/shard_map/ppermute | solution.py:657
  560.9 2.7 copy-start.19
Sparse Core Ops, SparseCore 0:
  11.3 128.2 all-gather.3

commit v4 on v3

--- a/solution.py
+++ b/solution.py
@@ -2,6 +2,7 @@
 
 import jax
 import jax.numpy as jnp
+import numpy as np
 from jax import lax
 from jax.experimental import pallas as pl
 from jax.experimental.pallas import tpu as pltpu
@@ -91,7 +92,15 @@
     return [c[0][1], mid, c[1][1]]
 
 
-def ffn_kernel(x_ref, o_ref, wo_ref, wgu_ref, wd_ref, g_ref, b_ref, y_ref, gu_ref, n1_ref, i1_ref, n2_ref, i2_ref, h_ref, hb_ref, acc_ref):
+GROUP = 384
+WIDE = 128
+
+
+def unit_weights(load):
+    return [jnp.concatenate([load(t, m) for t in range(4)], axis=1) for m in range(3)]
+
+
+def ffn_kernel(x_ref, o_ref, wo_ref, w_ref, g_ref, b_ref, y_ref, gu_ref, n1_ref, i1_ref, n2_ref, i2_ref, h_ref, hb_ref, acc_ref):
     z = pl.program_id(0)
     width = x_ref.shape[1]
 
@@ -110,14 +119,13 @@
         hb_ref[...] = h.astype(BF)
 
     hb = hb_ref[...]
-    w = wgu_ref[:, 0].reshape(width, -1)
-    half = w.shape[1] // 2
-    gate = dg(hb, w[:, :half], NN)
-    up = dg(hb, w[:, half:], NN)
+    wg, wu, wd = unit_weights(lambda t, m: w_ref[:, t, :, 128 * m : 128 * m + 128].reshape(width, 128))
+    gate = dg(hb, wg, NN)
+    up = dg(hb, wu, NN)
     gu_ref[0, 0] = gate.astype(BF)
     gu_ref[0, 1] = up.astype(BF)
     act = (gate / (1.0 + jnp.exp(-gate)) * up).astype(BF)
-    part = dg(act, wd_ref[:, 0].reshape(width, -1), NT)
+    part = dg(act, wd, NT)
 
     @pl.when(z == 0)
     def _():
@@ -135,7 +143,7 @@
         y_ref[...] = (n * g_ref[1:2] + b_ref[1:2]).astype(BF)
 
 
-def ffn_back_kernel(dy_ref, n1_ref, i1_ref, n2_ref, i2_ref, gu_ref, wgu_ref, wd_ref, g_ref, b_ref, g_out, dr1_ref, da_ref, ng_ref, hb_ref, df_ref, acc_ref):
+def ffn_back_kernel(dy_ref, n1_ref, i1_ref, n2_ref, i2_ref, gu_ref, w_ref, g_ref, b_ref, g_out, dr1_ref, da_ref, ng_ref, hb_ref, df_ref, acc_ref):
     z = pl.program_id(0)
     width = dy_ref.shape[1]
 
@@ -156,17 +164,20 @@
     s = 1.0 / (1.0 + jnp.exp(-gate))
     silu = gate * s
     act = (silu * up).astype(BF)
-    half = act.shape[1]
-    blocks = g_out.shape[0]
-    g_out[:, 0, :, 3 * half :] = dg(df, act, TN).astype(BF).reshape(blocks, -1, half)
-    d_act = dg(df, wd_ref[:, 0].reshape(width, -1), NN)
+    wg, wu, wd = unit_weights(lambda t, m: w_ref[:, t, :, 128 * m : 128 * m + 128].reshape(width, 128))
+
+    def keep(m, grad):
+        for t in range(g_out.shape[1]):
+            g_out[:, t, :, 128 * m : 128 * m + 128] = grad[:, 128 * t : 128 * t + 128].astype(BF).reshape(g_out.shape[0], -1, 128)
+
+    keep(2, dg(df, act, TN))
+    d_act = dg(df, wd, NN)
     d_gate = (d_act * up * (s * (1.0 + gate * (1.0 - s)))).astype(BF)
     d_up = (d_act * silu).astype(BF)
     hb = hb_ref[...]
-    g_out[:, 0, :, :half] = dg(hb, d_gate, TN).astype(BF).reshape(blocks, -1, half)
-    g_out[:, 0, :, half : 2 * half] = dg(hb, d_up, TN).astype(BF).reshape(blocks, -1, half)
-    w = wgu_ref[:, 0].reshape(width, -1)
-    acc_ref[...] += dg(d_gate, w[:, :half], NT) + dg(d_up, w[:, half:], NT)
+    keep(0, dg(hb, d_gate, TN))
+    keep(1, dg(hb, d_up, TN))
+    acc_ref[...] += dg(d_gate, wg, NT) + dg(d_up, wu, NT)
 
     @pl.when(z == pl.num_programs(0) - 1)
     def _():
@@ -279,7 +290,11 @@
 
 
 def joint_block(w):
-    return pl.BlockSpec((w.shape[0], 2, w.shape[2], 768), lambda i: (0, i, 0, 2))
+    return pl.BlockSpec((w.shape[0], 2, w.shape[2], 768), lambda i: (0, i, 0, 0))
+
+
+def group_block(w):
+    return pl.BlockSpec((w.shape[0], w.shape[1], w.shape[2], GROUP), lambda i: (0, 0, 0, 2 + i))
 
 
 def sds(shape, kind):
@@ -314,25 +329,25 @@
         compiler_params=BIG,
         name="attn",
     )(q, k, v, ko, vo, mask)
-    hidden = columns // 4
+    groups = (columns - width) // GROUP
+    units = tp * 128
     y, gu, n1, i1, n2, i2 = pl.pallas_call(
         ffn_kernel,
-        grid=(tp,),
+        grid=(groups,),
         in_specs=[
             full((rows, width)),
             full((heads, rows, 128)),
-            pl.BlockSpec((blocks, tp, depth, 256), lambda i: (0, 0, 0, 8)),
-            lead((blocks, 1, depth, 2 * hidden), 1),
-            pl.BlockSpec((blocks, 1, depth, hidden), lambda i: (0, i, 0, 3)),
+            pl.BlockSpec((blocks, tp, depth, 256), lambda i: (0, 0, 0, 2)),
+            group_block(w),
             full((2, width)),
             full((2, width)),
         ],
-        out_specs=[full((rows, width)), lead((1, 2, rows, hidden))] + [full((rows, width)), full((rows, 128))] * 2,
-        out_shape=[sds((rows, width), BF), sds((tp, 2, rows, hidden), BF)] + [sds((rows, width), F32), sds((rows, 128), F32)] * 2,
+        out_specs=[full((rows, width)), lead((1, 2, rows, units))] + [full((rows, width)), full((rows, 128))] * 2,
+        out_shape=[sds((rows, width), BF), sds((groups, 2, rows, units), BF)] + [sds((rows, width), F32), sds((rows, 128), F32)] * 2,
         scratch_shapes=[VM((rows, width), F32), VM((rows, width), BF), VM((rows, width), F32)],
         compiler_params=BIG,
         name="ffn",
-    )(x, o, w, w, w, gains, biases)
+    )(x, o, w, w, gains, biases)
     return y, (q, k, v, ko, vo, o, e, l, gu, n1, i1, n2, i2)
 
 
@@ -344,35 +359,35 @@
     heads = width // 128
     blocks, tp, depth, columns = w.shape
     steps = tp // 2
-    hidden = columns // 4
+    groups = (columns - width) // GROUP
+    units = tp * 128
     cos, sin, cost, sint = tabs
     whole, stat = full((rows, width)), full((rows, 128))
     g, dr1, da, ng = pl.pallas_call(
         ffn_back_kernel,
-        grid=(tp,),
+        grid=(groups,),
         in_specs=[
             whole, whole, stat, whole, stat,
-            lead((1, 2, rows, hidden)),
-            lead((blocks, 1, depth, 2 * hidden), 1),
-            pl.BlockSpec((blocks, 1, depth, hidden), lambda i: (0, i, 0, 3)),
+            lead((1, 2, rows, units)),
+            group_block(w),
             full((2, width)), full((2, width)),
         ],
         out_specs=[
-            lead((blocks, 1, depth, columns), 1),
+            group_block(w),
             whole, whole, full((8, width)),
         ],
         out_shape=[sds(w.shape, BF), sds((rows, width), F32), sds((rows, width), BF), sds((8, width), F32)],
         scratch_shapes=[VM((rows, width), BF), VM((rows, width), BF), VM((rows, width), F32)],
         compiler_params=BIG,
         name="ffn_back",
-    )(dy, n1, i1, n2, i2, gu, w, w, gains, biases)
+    )(dy, n1, i1, n2, i2, gu, w, gains, biases)
     three = lead((3, rows, 128))
     dq, own, oth, dwo = pl.pallas_call(
         attn_back_kernel,
         grid=(steps,),
         in_specs=[
             whole,
-            pl.BlockSpec((blocks, 2, depth, 256), lambda i: (0, i, 0, 8)),
+            pl.BlockSpec((blocks, 2, depth, 256), lambda i: (0, i, 0, 2)),
             three, three, three, three, three, three,
             lead((3, 2, 2 * rows, rows)),
             lead((3, 2, 8, rows)),
@@ -410,9 +425,6 @@
     return dz, (g, ng)
 
 
-WIDE = 128
-
-
 def sum_kernel(parts, g_ref, ng_ref, out_ref, nout_ref, own, land_c, land_y, land_r, land_l, land_n, own_sem, cs_sem, cr_sem, ys_sem, yr_sem, rs_sem, rr_sem, ls_sem, lr_sem, ns_sem, nr_sem):
     y, c, z = lax.axis_index("y"), lax.axis_index("core"), lax.axis_index("tensor")
     last = 3
@@ -622,6 +634,335 @@
     )(g, ng)
 
 
+LAG = 6
+
+
+def first_kernel(
+    parts, tok_ref, shard_ref, extra_ref, len_ref, cos_ref, sin_ref,
+    w_out, y_out, x_out, mask_out, norm_out,
+    w, xin, q, kv, land_kv, o, h1, hb, acc, ext, lens,
+    tok_sem, tok_send, tok_recv, shard_sem, back_sem, kv_send, kv_recv,
+    small_send, small_recv, rs_sem, rr_sem, ls_sem, lr_sem, ys_sem, yr_sem, cs_sem, cr_sem,
+):
+    y, c, z = lax.axis_index("y"), lax.axis_index("core"), lax.axis_index("tensor")
+    last = 3
+    rows, width = xin.shape[0] * xin.shape[1], xin.shape[2]
+    near, across = {"core": 1 - c}, {"y": 1 - y}
+    right, left = {"tensor": jnp.minimum(z + 1, last)}, {"tensor": jnp.maximum(z - 1, 0)}
+    side = z // 2
+    barrier = pltpu.get_barrier_semaphore()
+
+    def greet(device):
+        pl.semaphore_signal(barrier, inc=1, device_id=device, device_id_type=MESH)
+
+    def remote(src, dst, send, recv, device):
+        return pltpu.make_async_remote_copy(src, dst, send, recv, device_id=device, device_id_type=MESH)
+
+    def target(i):
+        return {"core": side, "tensor": 2 * c + i}
+
+    def at_home(i):
+        return jnp.logical_and(side == c, 2 * c + i == z)
+
+    def token_copy(i):
+        return remote(tok_ref.at[i], xin.at[z % 2], tok_send.at[i], tok_recv.at[z % 2], target(i))
+
+    def token_home(i):
+        return pltpu.make_async_copy(tok_ref.at[i], xin.at[z % 2], tok_sem)
+
+    load = pltpu.make_async_copy(shard_ref, w.at[y, c, z], shard_sem)
+    load.start()
+    greet(near)
+    greet(across)
+
+    @pl.when(z < last)
+    def _():
+        greet(right)
+
+    @pl.when(z > 0)
+    def _():
+        greet(left)
+
+    for i in range(2):
+
+        @pl.when(jnp.logical_not(at_home(i)))
+        def _():
+            greet(target(i))
+
+    count = 4 + jnp.where(z < last, 1, 0) + jnp.where(z > 0, 1, 0) - jnp.where(side == c, 1, 0)
+    pl.semaphore_wait(barrier, count)
+
+    for i in range(2):
+
+        @pl.when(at_home(i))
+        def _():
+            token_home(i).start()
+
+        @pl.when(jnp.logical_not(at_home(i)))
+        def _():
+            token_copy(i).start()
+
+    ext[y, c] = extra_ref[...]
+    lens[c] = len_ref[...]
+
+    def small(k):
+        if k == 0:
+            return remote(lens.at[c], lens.at[c], small_send.at[0], small_recv.at[0], near)
+        if k == 1:
+            return remote(ext.at[y, c], ext.at[y, c], small_send.at[1], small_recv.at[1], across)
+        return remote(ext.at[:, c], ext.at[:, c], small_send.at[2], small_recv.at[2], near)
+
+    small(0).start()
+    small(1).start()
+    load.wait()
+
+    def columns(j):
+        return pl.ds(pl.multiple_of(j * WIDE, WIDE), WIDE)
+
+    def go_right(j, h):
+        b = jnp.maximum(z - h, 0)
+        return remote(w.at[y, c, b, :, columns(j)], w.at[y, c, b, :, columns(j)], rs_sem.at[j, h], rr_sem.at[j, h], right)
+
+    def go_left(j, h):
+        b = jnp.minimum(z + h, last)
+        return remote(w.at[y, c, b, :, columns(j)], w.at[y, c, b, :, columns(j)], ls_sem.at[j, h], lr_sem.at[j, h], left)
+
+    def to_y(j):
+        return remote(w.at[y, c, :, :, columns(j)], w.at[y, c, :, :, columns(j)], ys_sem.at[j], yr_sem.at[j], across)
+
+    def to_core(j):
+        return remote(w.at[:, c, :, :, columns(j)], w.at[:, c, :, :, columns(j)], cs_sem.at[j], cr_sem.at[j], near)
+
+    def write_back(j):
+        return pltpu.make_async_copy(w.at[:, :, :, :, columns(j)], w_out.at[:, :, :, :, columns(j)], back_sem.at[j])
+
+    def stage(r, lag, body):
+        @pl.when(jnp.logical_and(r >= lag, r - lag < parts))
+        def _():
+            body(r - lag)
+
+    def send_own(j):
+        @pl.when(z < last)
+        def _():
+            go_right(j, 0).start()
+
+        @pl.when(z > 0)
+        def _():
+            go_left(j, 0).start()
+
+    def hop(h, j):
+        @pl.when(z >= h)
+        def _():
+            go_right(j, h - 1).wait_recv()
+
+        @pl.when(z + h <= last)
+        def _():
+            go_left(j, h - 1).wait_recv()
+
+        if h < last:
+
+            @pl.when(jnp.logical_and(z >= h, z < last))
+            def _():
+                go_right(j, h).start()
+
+            @pl.when(jnp.logical_and(z + h <= last, z > 0))
+            def _():
+                go_left(j, h).start()
+
+        else:
+            to_y(j).start()
+
+    def over_core(j):
+        to_y(j).wait_recv()
+        to_core(j).start()
+
+    def complete(j):
+        to_core(j).wait_recv()
+        write_back(j).start()
+
+    def round_(r):
+        stage(r, 0, send_own)
+        stage(r, 1, functools.partial(hop, 1))
+        stage(r, 2, functools.partial(hop, 2))
+        stage(r, 3, functools.partial(hop, 3))
+        stage(r, 5, over_core)
+        stage(r, LAG, complete)
+
+    def rounds(first, end):
+        lax.fori_loop(first, end, lambda r, t: (round_(r), t)[1], 0)
+
+    lead_parts = width // WIDE
+    rounds(0, 3)
+    small(0).wait()
+    small(1).wait()
+    small(2).start()
+
+    mine = jnp.where(side == 0, lens[0], lens[1])
+    mine = jnp.where(z % 2 == 0, mine[0:1], mine[1:2])
+    at_q = c * rows + lax.broadcasted_iota(jnp.int32, (1, rows), 1)
+    at_k = lax.broadcasted_iota(jnp.int32, (2 * rows, 1), 0)
+    at_k = jnp.where(at_k < rows, c * rows + at_k, (1 - c) * rows + at_k - rows)
+    seg_q, seg_k = jnp.zeros((1, rows), jnp.int32), jnp.zeros((2 * rows, 1), jnp.int32)
+    end = jnp.zeros((1, 1), jnp.int32)
+    for n in range(8):
+        end = end + mine[:, n : n + 1]
+        seg_q = seg_q + jnp.where(end <= at_q, 1, 0)
+        seg_k = seg_k + jnp.where(end <= at_k, 1, 0)
+    mask_out[...] = jnp.where(seg_k == seg_q, 0.0, neg_fill).astype(F32)
+    rounds(3, lead_parts + LAG)
+
+    small(2).wait()
+    halves = [ext[i // 2, i % 2].astype(F32) for i in range(4)]
+    for k in range(2):
+        for half in range(2):
+            pieces = [halves[2 * half + i][3 * k + m : 3 * k + m + 1] for i in range(2) for m in range(3)]
+            norm_out[2 * k + half : 2 * k + half + 1] = jnp.concatenate(pieces, axis=1)
+
+    for i in range(2):
+
+        @pl.when(at_home(i))
+        def _():
+            token_home(i).wait()
+
+        @pl.when(jnp.logical_not(at_home(i)))
+        def _():
+            token_copy(i).wait_send()
+            remote(tok_ref.at[i], xin.at[i], tok_send.at[i], tok_recv.at[i], target(i)).wait_recv()
+
+    x = xin[...].reshape(rows, width)
+    x_out[...] = x
+    cos, sin = cos_ref[pl.ds(c * rows, rows)], sin_ref[pl.ds(c * rows, rows)]
+    low = low_lanes((rows, 128))
+    for p in range(2):
+        r = [dg(x, w[:, :, 2 * p + e, :, :640].reshape(width, 640), NN) for e in range(2)]
+        t = [[v[:, 128 * i : 128 * i + 128] for i in range(5)] for v in r]
+        qs = [t[0][0], jnp.where(low, t[0][3], swap64(t[1][3])), t[1][0]]
+        ks = [t[0][1], jnp.where(low, swap64(t[0][3]), t[1][3]), t[1][1]]
+        vs = [t[0][2], jnp.where(low, t[0][4], swap64(t[1][4])), t[1][2]]
+        for i in range(3):
+            q[3 * p + i] = (rope_fwd(qs[i], cos, sin) * HD**-0.5).astype(BF)
+            kv[0, 3 * p + i] = rope_fwd(ks[i], cos, sin).astype(BF)
+            kv[1, 3 * p + i] = vs[i].astype(BF)
+    share = remote(kv, land_kv, kv_send, kv_recv, near)
+    share.start()
+    start = lead_parts + LAG
+    rounds(start, start + 1)
+    share.wait()
+
+    def pair(p, carry):
+        k = jnp.concatenate([kv[0, p], land_kv[0, p]], axis=0)
+        v = jnp.concatenate([kv[1, p], land_kv[1, p]], axis=0)
+        vt = v.astype(F32).T.astype(BF)
+        outs = []
+        for h in range(2):
+            qm = jnp.where(low if h == 0 else jnp.logical_not(low), q[p], jnp.zeros((rows, 128), BF))
+            s = dg(k, qm, NT) + mask_out[...]
+            e = jnp.exp(s - jnp.max(s, axis=0, keepdims=True))
+            inv = 1.0 / jnp.sum(e, axis=0, keepdims=True)
+            outs.append(dg(vt[HD * h : HD * h + HD], e.astype(BF), NN) * inv)
+        o[p] = jnp.concatenate(outs, axis=0).T.astype(BF)
+        round_(start + 1 + p)
+        return carry
+
+    lax.fori_loop(0, 6, pair, 0)
+    r = x.astype(F32)
+    for p in range(2):
+        wo = []
+        for e in range(2):
+            wo.append([w[:, :, 2 * p + e, :, 512 + 128 * i : 640 + 128 * i].reshape(width, 128) for i in range(2)])
+        mid = jnp.where(low_lanes((width, 128)), swap64(wo[0][0].astype(F32)), wo[1][0].astype(F32)).astype(BF)
+        r = r + dg(
+            jnp.concatenate([o[3 * p + i] for i in range(3)], axis=1),
+            jnp.concatenate([wo[0][1], mid, wo[1][1]], axis=1),
+            NT,
+        )
+    n, inv = norm_parts(r)
+    h = n * norm_out[0:1] + norm_out[2:3]
+    hb[...] = h.astype(BF)
+    acc[...] = h
+    rounds(start + 7, start + 8)
+
+    def units(k, carry):
+        lax.fori_loop(
+            jnp.maximum(start + 8, lead_parts + 3 * k + LAG),
+            lead_parts + 3 * k + LAG + 3,
+            lambda i, t: (round_(i), t)[1],
+            0,
+        )
+        wg, wu, wd = unit_weights(
+            lambda t, m: w[:, :, t, :, pl.ds(pl.multiple_of(width + GROUP * k + 128 * m, 128), 128)].reshape(width, 128)
+        )
+        gate = dg(hb[...], wg, NN)
+        up = dg(hb[...], wu, NN)
+        act = (gate / (1.0 + jnp.exp(-gate)) * up).astype(BF)
+        acc[...] += dg(act, wd, NT)
+        return carry
+
+    lax.fori_loop(0, 6, units, 0)
+    n, inv = norm_parts(acc[...])
+    y_out[...] = (n * norm_out[1:2] + norm_out[3:4]).astype(BF)
+
+    def finish(j, carry):
+        write_back(j).wait()
+        to_y(j).wait_send()
+        to_core(j).wait_send()
+        for h in range(last):
+
+            @pl.when(jnp.logical_and(z >= h, z < last))
+            def _():
+                go_right(j, h).wait_send()
+
+            @pl.when(jnp.logical_and(z + h <= last, z > 0))
+            def _():
+                go_left(j, h).wait_send()
+
+        return carry
+
+    lax.fori_loop(0, parts, finish, 0)
+
+
+def first_layer(tokens, shard, extra, lengths, cos, sin):
+    micro, own, width = tokens.shape
+    depth, columns = shard.shape
+    rows = 2 * own
+    parts = columns // WIDE
+    heads = width // 128
+    dma = pltpu.SemaphoreType.DMA
+    hbm = pl.BlockSpec(memory_space=pl.ANY)
+    vm = pl.BlockSpec(memory_space=VM)
+    return pl.pallas_call(
+        functools.partial(first_kernel, parts),
+        in_specs=[hbm, hbm, vm, vm, vm, vm],
+        out_specs=[hbm, vm, vm, vm, vm],
+        out_shape=[
+            sds((2, 2, 4, depth, columns), BF),
+            sds((rows, width), BF),
+            sds((rows, width), BF),
+            sds((2 * rows, rows), F32),
+            sds((4, width), F32),
+        ],
+        scratch_shapes=[
+            VM((2, 2, 4, depth, columns), BF),
+            VM((2, own, width), BF),
+            VM((heads, rows, 128), BF),
+            VM((2, heads, rows, 128), BF),
+            VM((2, heads, rows, 128), BF),
+            VM((heads, rows, 128), BF),
+            VM((8, 128), F32),
+            VM((rows, width), BF),
+            VM((rows, width), F32),
+            VM((2, 2) + extra.shape, BF),
+            VM((2,) + lengths.shape, jnp.int32),
+            dma, dma((2,)), dma((2,)), dma, dma((parts,)), dma, dma,
+            dma((3,)), dma((3,)),
+            dma((parts, 3)), dma((parts, 3)), dma((parts, 3)), dma((parts, 3)),
+            dma((parts,)), dma((parts,)), dma((parts,)), dma((parts,)),
+        ],
+        compiler_params=pltpu.CompilerParams(collective_id=1, has_side_effects=True, vmem_limit_bytes=60 << 20),
+        name="first",
+    )(tokens, shard, extra, lengths, cos, sin)
+
+
 def swap_pairs(tp, step, dp_axes):
     pairs = []
     half = tp // 2
@@ -680,13 +1021,16 @@
     first = jnp.concatenate(
         [heads[:, :, :2].reshape(rows, -1), heads[:, :, 2].reshape(rows, -1), mine[:, 2], mine[:, :2].reshape(rows, -1)], axis=1
     )
-    return jnp.concatenate([w_gate_up.reshape(rows, -1), first, w_down.T], axis=1)
+    units = jnp.concatenate([w_gate_up, w_down.T[:, None]], axis=1)
+    units = units.reshape(rows, 3, -1, 128).transpose(0, 2, 1, 3)
+    return jnp.concatenate([first, units.reshape(rows, -1)], axis=1)
 
 
 def unpack_shard(packed):
     rows, columns = packed.shape
-    half = columns // 2
-    pair, first, down = packed[:, :half], packed[:, half : half + 768], packed[:, half + 768 :]
+    first = packed[:, :768]
+    units = packed[:, 768:].reshape(rows, -1, 3, 128).transpose(0, 2, 1, 3).reshape(rows, 3, -1)
+    pair, down = units[:, :2], units[:, 2]
     odd = lax.axis_index("tensor") % 2 == 1
     both = first[:, :384].reshape(rows, 3, 2, HD)
     single = first[:, 384:576].reshape(rows, 3, 1, HD)
@@ -697,9 +1041,17 @@
     return (
         heads.reshape(rows, 3, -1),
         mine.reshape(rows, -1).T,
-        pair.reshape(rows, 2, -1),
+        pair,
         down.T,
     )
+
+
+def host_tables(length):
+    halfway = HD // 2
+    freqs = np.float32(1000.0) ** (-np.arange(halfway, dtype=np.float32) / np.float32(halfway))
+    angles = np.arange(length, dtype=np.float32)[:, None] * freqs[None, :]
+    cos, sin = np.cos(angles), np.sin(angles)
+    return np.concatenate([cos] * 4, axis=1), np.concatenate([-sin, sin] * 2, axis=1)
 
 
 BLOCKS = 4
@@ -727,27 +1079,36 @@
     assert micro * 2 == tp
     length = own * tp
     rows = length // 2
-    weights = gather_shard(pack_shard(w_qkv[0], w_out[0], w_gate_up[0], w_down[0]), dp, tp)
-    norms = jnp.concatenate([norm_gains, norm_biases])
-    norms = lax.all_gather(norms, ("y", "core"), axis=1, tiled=True).astype(F32)
-    norms = (norms[0].reshape(2, width), norms[1].reshape(2, width))
-    tokens = to_sequences(tokens, tp)
-    grad_top = to_sequences(cotangent, tp)
-    chip_lengths = lax.all_gather(lengths, "core", axis=0, tiled=True)
-    my_lengths = lax.dynamic_index_in_dim(chip_lengths, at, 0, keepdims=False)
+    shard = pack_shard(w_qkv[0], w_out[0], w_gate_up[0], w_down[0])
     near = core * rows + jnp.arange(rows, dtype=jnp.int32)
     far = (1 - core) * rows + jnp.arange(rows, dtype=jnp.int32)
-    ends_at = jnp.cumsum(my_lengths)
-
-    def segment(positions):
-        return jnp.sum((ends_at[None, :] <= positions[:, None]).astype(jnp.int32), axis=-1)
-
-    seg_near = segment(near)
-    seg_all = jnp.concatenate([seg_near, segment(far)])
-    mask = jnp.where(seg_all[:, None] == seg_near[None, :], 0.0, neg_fill).astype(F32)
     tabs = rope_tables(near)
-
-    y, kept = forward(tokens, weights, norms, mask, tabs)
+    grad_top = to_sequences(cotangent, tp)
+    if dp == 4 and tp == 4:
+        extra = jnp.concatenate([norm_gains.reshape(-1, 128), norm_biases.reshape(-1, 128)])
+        extra = jnp.pad(extra, ((0, 16 - extra.shape[0]), (0, 0)))
+        padded = jnp.pad(lengths, ((0, 8 - lengths.shape[0]), (0, 128 - lengths.shape[1])))
+        wide, signed = host_tables(length)
+        weights, y, tokens, mask, small = first_layer(tokens, shard, extra, padded, wide, signed)
+        weights = weights.reshape((BLOCKS,) + weights.shape[2:])
+        norms = (small[:2], small[2:])
+    else:
+        weights = gather_shard(shard, dp, tp)
+        norms = jnp.concatenate([norm_gains, norm_biases])
+        norms = lax.all_gather(norms, ("y", "core"), axis=1, tiled=True).astype(F32)
+        norms = (norms[0].reshape(2, width), norms[1].reshape(2, width))
+        tokens = to_sequences(tokens, tp)
+        chip_lengths = lax.all_gather(lengths, "core", axis=0, tiled=True)
+        my_lengths = lax.dynamic_index_in_dim(chip_lengths, at, 0, keepdims=False)
+        ends_at = jnp.cumsum(my_lengths)
+
+        def segment(positions):
+            return jnp.sum((ends_at[None, :] <= positions[:, None]).astype(jnp.int32), axis=-1)
+
+        seg_near = segment(near)
+        seg_all = jnp.concatenate([seg_near, segment(far)])
+        mask = jnp.where(seg_all[:, None] == seg_near[None, :], 0.0, neg_fill).astype(F32)
+        y, unused = forward(tokens, weights, norms, mask, tabs)
     received = lax.ppermute(y, "section", [(0, 1)])
     inputs = jnp.where(section == 0, tokens, received)
     y, kept = forward(inputs, weights, norms, mask, tabs)

time: 582 us -> 529 us (0.909)
  waiting for transfers between devices: 150 us -> 40.9 us
  Pallas kernels: 330 us -> 421 us
  blocking collectives: 13.8 us -> 0 us
  between operations: 15 us -> 1.67 us
  local copies, waits for them, and re-layouts: 26.8 us -> 37.1 us
  other arithmetic: 19.3 us -> 12 us
    pallas_call x4, Pallas kernels: 88.9 us -> 212 us  [the longest x1 144 us: first_layer(): pl.pallas_call(functools.partial(first_kernel, parts), in_specs=[hbm, hbm...]
    all_gather x1 -> x0, waiting for transfers between devices: 98.8 us -> none  [gather_shard(): got = lax.all_gather(shard, ALL, axis=0, tiled=False)]
    pallas_call x2 -> x1, Pallas kernels: 32.7 us -> 16.4 us  [forward(): pl.pallas_call(attn_kernel, grid=(heads,), in_specs=[pair] * 5 + [full((2...]
    all_gather x2 -> x0, blocking collectives: 13.8 us -> none  [the longest x1 8.64 us: on_device(): chip_lengths = lax.all_gather(lengths, 'core', axis=0, tiled=True)]
    pallas_call x1, Pallas kernels: 131 us -> 122 us  [sum_over_section(): pl.pallas_call(functools.partial(sum_kernel, parts), in_specs=[pl.BlockSp...]
    pallas_call x2 -> x1, Pallas kernels: 13 us -> 6.5 us  [forward(): pl.pallas_call(qkv_kernel, grid=(steps,), in_specs=[full((rows, width)),...]
    reshape x0 -> x5, local copies, waits for them, and re-layouts: none -> 6.34 us  [the longest x2 4.59 us: unpack_shard(): packed[:, 768:].reshape(rows, -1, 3, 128).transpose(0, 2, 1, 3)]
  transfers between devices with their start and end apart: 15 -> 10, of which waited for: 8 -> 5; matrix products, arithmetic and copies ran while one was open for 5% -> 4% of each run, Pallas kernels for 0% -> 1%
where the time goes in v4:
time: 529 us; the launch traced here: 525 us
  Pallas kernels  421 us (80%)
  waiting for transfers between devices  40.9 us (8%)
  local copies, waits for them, and re-layouts  37.1 us (7%)
  other arithmetic  12 us (2%)
  starting transfers between devices  11.3 us (2%)
    pallas_call x1, Pallas kernels, first_layer(): pl.pallas_call(functools.partial(first_kernel, parts), in_specs=[hbm, hbm...  144 us
    pallas_call x1, Pallas kernels, sum_over_section(): pl.pallas_call(functools.partial(sum_kernel, parts), in_specs=[pl.BlockSp...  122 us
    pallas_call x2, Pallas kernels, backward(): pl.pallas_call(ffn_back_kernel, grid=(groups,), in_specs=[whole, whole, s...  50.2 us
    pallas_call x2, Pallas kernels, backward(): pl.pallas_call(attn_back_kernel, grid=(steps,), in_specs=[whole, pl.Block...  40.1 us
    pallas_call x2, Pallas kernels, backward(): pl.pallas_call(joint_back_kernel, grid=(steps,), in_specs=[pl.BlockSpec(m...  23.7 us
    ppermute x1, waiting for transfers between devices, on_device(): received = lax.ppermute(dz.astype(BF), 'section', [(1, 0)])  20.2 us
    pallas_call x1, Pallas kernels, forward(): pl.pallas_call(ffn_kernel, grid=(groups,), in_specs=[full((rows, width)),...  18.1 us
    pallas_call x1, Pallas kernels, forward(): pl.pallas_call(attn_kernel, grid=(heads,), in_specs=[pair] * 5 + [full((2...  16.4 us
  transfers between devices with their start and end apart: 10, of which 5 were waited for; matrix products, arithmetic and copies ran while one was open for 4% of the time, Pallas kernels for 1%

profile of v4, /device:TPU:0, one launch (start us, length us, event | category | flops | bytes accessed | tf_op | source)
XLA Modules:
  0.0 524.5 jit_solution(12348781066405335896)
XLA Ops:
  0.6 1.2 copy.53
  4.2 1.2 copy.59
  7.5 1.7 concatenate.47.shard_ref
  9.3 144.0 %first.1 = (bf16[2,2,4,192,3072]{4,3,2,1,0:T(8,128)(2,1)}, bf16[512,768]{1,0:T(8,128)(2,1)}, bf16[512,768]{1,0:T(8,128)(2,1)}, f32[1024,512]{1,0:T(8,128)}, f32[4,768]{1,0:T(4,128)}) custom-call(bf16[2,256,768]{2,1,0:T(8,128)(2,1)} %tok_ref.1, bf16[192,3072]{1,0:T(8,128)(2,1)} %concatenate.47.shard_ref, bf16[16,128]{1,0:T(8,128)(2,1)} %fusion.3.extra_ref, ...), custom_call_target="tpu_custom_call" | custom-call | tf_op jit(solution)/shard_map/first/pallas_call | solution.py:933
  153.3 3.4 collective-permute-start.2
  157.0 1.2 collective-permute-start
  158.2 1.0 fusion
  159.2 1.3 pad_maximum_fusion.2
  161.1 13.3 %collective-permute-done.2 = bf16[512,768]{1,0:T(8,128)(2,1)S(1)} collective-permute-done((bf16[512,768]{1,0:T(8,128)(2,1)}, bf16[512,768]{1,0:T(8,128)(2,1)S(1)}, u32[]{:S(2)}, u32[]{:S(2)}) %collective-permute-start.2) | collective-permute-done | bytes 786464 | tf_op jit(solution)/shard_map/ppermute | solution.py:1112
  174.4 1.0 broadcast_select_fusion.2.x_ref
  175.4 6.5 %qkv.1 = (bf16[6,512,128]{2,1,0:T(8,128)(2,1)}, bf16[6,512,128]{2,1,0:T(8,128)(2,1)}, bf16[6,512,128]{2,1,0:T(8,128)(2,1)}) custom-call(bf16[512,768]{1,0:T(8,128)(2,1)} %broadcast_select_fusion.2.x_ref, bf16[4,4,192,3072]{3,2,1,0:T(8,128)(2,1)} %bitcast.69, f32[512,128]{1,0:T(8,128)} %get-tuple-element.111.cos_ref, f32[512,128]{1,0:T(8,128)} %get-tuple-element.112.sin_ref), custom_call_target="tpu_custom_call" | custom-call | tf_op jit(solution)/shard_map/qkv/pallas_call | solution.py:312
  182.4 1.0 multiply_sine_fusion.1
  184.1 1.0 broadcast_select_fusion
  186.4 16.4 %attn.1 = (bf16[6,512,128]{2,1,0:T(8,128)(2,1)}, bf16[6,2,1024,512]{3,2,1,0:T(8,128)(2,1)}, f32[6,2,8,512]{3,2,1,0:T(8,128)}) custom-call(bf16[6,512,128]{2,1,0:T(8,128)(2,1)} %get-tuple-element.48.q_ref, bf16[6,512,128]{2,1,0:T(8,128)(2,1)} %get-tuple-element.49.k_ref, bf16[6,512,128]{2,1,0:T(8,128)(2,1)} %get-tuple-element.50.v_ref, ...), custom_call_target="tpu_custom_call" | custom-call | tf_op jit(solution)/shard_map/attn/pallas_call | solution.py:323
  202.8 18.1 %ffn.1 = (bf16[512,768]{1,0:T(8,128)(2,1)}, bf16[6,2,512,512]{3,2,1,0:T(8,128)(2,1)}, f32[512,768]{1,0:T(8,128)}, f32[512,128]{1,0:T(8,128)}, f32[512,768]{1,0:T(8,128)}, /*index=5*/f32[512,128]{1,0:T(8,128)}) custom-call(bf16[512,768]{1,0:T(8,128)(2,1)} %broadcast_select_fusion.2.x_ref, bf16[6,512,128]{2,1,0:T(8,128)(2,1)} %get-tuple-element.52.o_ref, ...), custom_call_target="tpu_custom_call" | custom-call | tf_op jit(solution)/shard_map/ffn/pallas_call | solution.py:334
  220.9 25.1 %ffn_back.2 = (bf16[4,4,192,3072]{3,2,1,0:T(8,128)(2,1)}, f32[512,768]{1,0:T(8,128)}, bf16[512,768]{1,0:T(8,128)(2,1)}, f32[8,768]{1,0:T(8,128)}) custom-call(bf16[512,768]{1,0:T(8,128)(2,1)} %bitcast.80, f32[512,768]{1,0:T(8,128)} %get-tuple-element.54.n1_ref, f32[512,128]{1,0:T(8,128)} %get-tuple-element.55.i1_ref, f32[512,768]{1,0:T(8,128)} %get-tuple-element.56.n2_ref, ...), custom_call_target="tpu_custom_call" | custom-call | tf_op jit(solution)/shard_map/ffn_back/pallas_call | solution.py:366
  246.0 20.0 %attn_back.2 = (bf16[6,512,128]{2,1,0:T(8,128)(2,1)}, f32[6,2,128,512]{3,2,1,0:T(8,128)}, bf16[6,2,128,512]{3,2,1,0:T(8,128)(2,1)}, bf16[2,768,384]{2,1,0:T(8,128)(2,1)}) custom-call(bf16[512,768]{1,0:T(8,128)(2,1)} %get-tuple-element.61.da_ref, bf16[4,4,192,3072]{3,2,1,0:T(8,128)(2,1)} %bitcast.73, bf16[6,512,128]{2,1,0:T(8,128)(2,1)} %get-tuple-element.52.o_ref, ...), custom_call_target="tpu_custom_call" | custom-call | tf_op jit(solution)/shard_map/attn_back/pallas_call | solution.py:385
  266.3 3.5 collective-permute-done.5.got_ref
  269.8 1.2 copy-done.4
  270.9 11.7 %joint_back.2 = (bf16[4,4,192,3072]{3,2,1,0:T(8,128)(2,1)}, f32[512,768]{1,0:T(8,128)}) custom-call(bf16[4,4,192,3072]{3,2,1,0:T(8,128)(2,1)} %get-tuple-element.59.old_ref, bf16[512,768]{1,0:T(8,128)(2,1)} %broadcast_select_fusion.2.x_ref, bf16[4,4,192,3072]{3,2,1,0:T(8,128)(2,1)} %bitcast.74, ...), custom_call_target="tpu_custom_call", output_to_operand_aliasing={{0}: (0, {})} | custom-call | tf_op jit(solution)/shard_map/joint_back/pallas_call | solution.py:407
  282.7 1.6 convert_element_type.16
  284.2 1.3 collective-permute-start.6
  285.5 20.2 %collective-permute-done.6 = bf16[512,768]{1,0:T(8,128)(2,1)S(1)} collective-permute-done((bf16[512,768]{1,0:T(8,128)(2,1)S(1)}, bf16[512,768]{1,0:T(8,128)(2,1)S(1)}, u32[]{:S(2)}, u32[]{:S(2)}) %collective-permute-start.6) | collective-permute-done | bytes 786464 | tf_op jit(solution)/shard_map/ppermute | solution.py:1116
  305.7 1.0 broadcast_select_fusion.1.dy_ref
  306.7 25.1 %ffn_back.3 = (bf16[4,4,192,3072]{3,2,1,0:T(8,128)(2,1)}, f32[512,768]{1,0:T(8,128)}, bf16[512,768]{1,0:T(8,128)(2,1)}, f32[8,768]{1,0:T(8,128)}) custom-call(bf16[512,768]{1,0:T(8,128)(2,1)} %broadcast_select_fusion.1.dy_ref, f32[512,768]{1,0:T(8,128)} %get-tuple-element.54.n1_ref, f32[512,128]{1,0:T(8,128)} %get-tuple-element.55.i1_ref, ...), custom_call_target="tpu_custom_call" | custom-call | tf_op jit(solution)/shard_map/ffn_back/pallas_call | solution.py:366
  331.8 20.1 %attn_back.3 = (bf16[6,512,128]{2,1,0:T(8,128)(2,1)}, f32[6,2,128,512]{3,2,1,0:T(8,128)}, bf16[6,2,128,512]{3,2,1,0:T(8,128)(2,1)}, bf16[2,768,384]{2,1,0:T(8,128)(2,1)}) custom-call(bf16[512,768]{1,0:T(8,128)(2,1)} %get-tuple-element.71.da_ref, bf16[4,4,192,3072]{3,2,1,0:T(8,128)(2,1)} %bitcast.76, bf16[6,512,128]{2,1,0:T(8,128)(2,1)} %get-tuple-element.52.o_ref, ...), custom_call_target="tpu_custom_call" | custom-call | tf_op jit(solution)/shard_map/attn_back/pallas_call | solution.py:385
  352.1 3.5 collective-permute-done.7.got_ref
  355.6 1.2 copy-done.3
  356.8 11.9 %joint_back.3 = (bf16[4,4,192,3072]{3,2,1,0:T(8,128)(2,1)}, f32[512,768]{1,0:T(8,128)}) custom-call(bf16[4,4,192,3072]{3,2,1,0:T(8,128)(2,1)} %get-tuple-element.69.old_ref, bf16[512,768]{1,0:T(8,128)(2,1)} %broadcast_select_fusion.2.x_ref, bf16[4,4,192,3072]{3,2,1,0:T(8,128)(2,1)} %bitcast.77, ...), custom_call_target="tpu_custom_call", output_to_operand_aliasing={{0}: (0, {})} | custom-call | tf_op jit(solution)/shard_map/joint_back/pallas_call | solution.py:407
  368.7 122.5 %grad_sum.1 = (f32[192,3072]{1,0:T(8,128)}, f32[8,768]{1,0:T(8,128)}) custom-call(bf16[2,2,4,192,3072]{4,3,2,1,0:T(8,128)(2,1)} %bitcast.78, f32[8,768]{1,0:T(8,128)} %get-tuple-element.79.ng_ref), custom_call_target="tpu_custom_call" | custom-call | tf_op jit(solution)/shard_map/grad_sum/pallas_call | solution.py:617
  491.2 1.0 slice.88
  492.2 0.9 slice.87
  493.1 0.9 slice.90
  494.0 1.6 slice_bitcast_fusion.2
  495.6 3.0 slice.91
  498.7 1.0 dynamic-slice_bitcast_fusion.1
  499.7 4.5 collective-permute-start.8
  504.2 0.9 copy.65
  506.8 2.7 reshape.124
  509.5 1.7 copy.72
  511.3 1.8 reshape.125
  513.3 0.9 copy-done.6
  515.0 1.1 copy.73
  516.1 1.8 copy.71
  517.9 1.9 copy.74
  520.4 0.9 slice_bitcast_fusion.1
  521.3 1.2 pad_maximum_fusion.1
  523.1 1.0 select_bitcast_fusion
  (97 shorter events, 11.9 us)
Async XLA Ops:
  0.6 1.4 copy-start.15
  1.9 1.0 copy-start.14
  2.0 1.2 copy-start.12
  5.4 0.9 copy-start.18
  5.4 0.9 copy-start.19
  5.4 0.9 copy-start.20
  9.3 147.5 %copy-start.9 = (bf16[2,256,768]{2,1,0:T(8,128)(2,1)S(1)}, bf16[2,256,768]{2,1,0:T(8,128)(2,1)}, u32[]{:S(2)}) copy-start(bf16[2,256,768]{2,1,0:T(8,128)(2,1)} %param.14) | copy-start | bytes 2359300
  153.3 21.1 %collective-permute-start.2 = (bf16[512,768]{1,0:T(8,128)(2,1)}, bf16[512,768]{1,0:T(8,128)(2,1)S(1)}, u32[]{:S(2)}, u32[]{:S(2)}) collective-permute-start(bf16[512,768]{1,0:T(8,128)(2,1)} %get-tuple-element.46), channel_id=1, source_target_pairs={{0,16},{1,17},{2,18},{3,19},{4,20},{5,21},{6,22},{7,23},{8,24},{9,... | collective-permute-start | bytes 2359304 | tf_op jit(solution)/shard_map/ppermute | solution.py:1112
  156.8 3.7 copy-start.16
  156.8 17.6 %copy-start.7 = (bf16[512,768]{1,0:T(8,128)(2,1)S(1)}, bf16[512,768]{1,0:T(8,128)(2,1)}, u32[]{:S(2)}) copy-start(bf16[512,768]{1,0:T(8,128)(2,1)} %get-tuple-element.45) | copy-start | bytes 2359300
  156.9 26.5 %collective-permute-start.1 = (bf16[256,768]{1,0:T(8,128)(2,1)S(1)}, bf16[256,768]{1,0:T(8,128)(2,1)S(1)}, u32[]{:S(2)}, u32[]{:S(2)}) collective-permute-start(bf16[256,768]{1,0:T(8,128)(2,1)S(1)} %get-tuple-element.99), channel_id=1, source_target_pairs={{0,1},{1,0},{2,5},{3,4},{4,3},{5,2},{6,7},{7,6},{8,9},{9,8},{10,13... | collective-permute-start | bytes 1179656 | tf_op jit(solution)/shard_map/ppermute | solution.py:984
  157.0 26.5 %collective-permute-start = (bf16[256,768]{1,0:T(8,128)(2,1)S(1)}, bf16[256,768]{1,0:T(8,128)(2,1)S(1)}, u32[]{:S(2)}, u32[]{:S(2)}) collective-permute-start(bf16[256,768]{1,0:T(8,128)(2,1)S(1)} %get-tuple-element.98), channel_id=1, source_target_pairs={{0,0},{1,1},{2,4},{3,5},{4,2},{5,3},{6,6},{7,7},{8,8},{9,9},{10,12... | collective-permute-start | bytes 1179656 | tf_op jit(solution)/shard_map/ppermute | solution.py:984
  181.9 3.2 collective-permute-start.3
  181.9 3.6 collective-permute-start.4
  185.1 0.9 copy-start.1
  185.5 0.9 copy-start.2
  266.1 3.7 collective-permute-start.5
  269.8 1.2 copy-start.4
  282.7 23.1 %copy-start = (bf16[2,256,768]{2,1,0:T(8,128)(2,1)S(1)}, bf16[2,256,768]{2,1,0:T(8,128)(2,1)}, u32[]{:S(2)}) copy-start(bf16[2,256,768]{2,1,0:T(8,128)(2,1)} %broadcast_select_fusion) | copy-start | bytes 2359300
  284.2 21.5 %collective-permute-start.6 = (bf16[512,768]{1,0:T(8,128)(2,1)S(1)}, bf16[512,768]{1,0:T(8,128)(2,1)S(1)}, u32[]{:S(2)}, u32[]{:S(2)}) collective-permute-start(bf16[512,768]{1,0:T(8,128)(2,1)S(1)} %convert_element_type.16), channel_id=1, source_target_pairs={{16,0},{17,1},{18,2},{19,3},{20,4},{21,5},{22,6},{23,7},{24,8},{25... | collective-permute-start | bytes 2359304 | tf_op jit(solution)/shard_map/ppermute | solution.py:1116
  351.9 3.7 collective-permute-start.7
  355.6 1.2 copy-start.3
  495.6 3.0 copy-start.5
  495.6 3.0 copy-start.11
  499.7 21.6 %collective-permute-start.9 = (bf16[256,768]{1,0:T(8,128)(2,1)}, bf16[256,768]{1,0:T(8,128)(2,1)}, u32[]{:S(2)}, u32[]{:S(2)}) collective-permute-start(bf16[256,768]{1,0:T(8,128)(2,1)} %get-tuple-element.97), channel_id=1, source_target_pairs={{1,0},{0,1},{5,2},{4,3},{3,4},{2,5},{7,6},{6,7},{9,8},{8,9},{13,10... | collective-permute-start | bytes 1179656 | tf_op jit(solution)/shard_map/ppermute | solution.py:998
  499.7 21.6 %collective-permute-start.8 = (bf16[256,768]{1,0:T(8,128)(2,1)}, bf16[256,768]{1,0:T(8,128)(2,1)}, u32[]{:S(2)}, u32[]{:S(2)}) collective-permute-start(bf16[256,768]{1,0:T(8,128)(2,1)} %get-tuple-element.96), channel_id=1, source_target_pairs={{0,0},{1,1},{4,2},{5,3},{2,4},{3,5},{6,6},{7,7},{8,8},{9,9},{12,10... | collective-permute-start | bytes 1179656 | tf_op jit(solution)/shard_map/ppermute | solution.py:998
  513.1 1.0 copy-start.6
  513.1 1.0 copy-start.10
  513.1 1.1 copy-start.8
  513.2 1.1 copy-start.13
  516.1 3.7 copy-start.17

commit v5 on v4

--- a/solution.py
+++ b/solution.py
@@ -143,7 +143,11 @@
         y_ref[...] = (n * g_ref[1:2] + b_ref[1:2]).astype(BF)
 
 
-def ffn_back_kernel(dy_ref, n1_ref, i1_ref, n2_ref, i2_ref, gu_ref, w_ref, g_ref, b_ref, g_out, dr1_ref, da_ref, ng_ref, hb_ref, df_ref, acc_ref):
+def ffn_back_kernel(grads, dy_ref, n1_ref, i1_ref, n2_ref, i2_ref, gu_ref, w_ref, g_ref, b_ref, *refs):
+    if grads:
+        g_out, dr1_ref, da_ref, ng_ref, hb_ref, df_ref, acc_ref = refs
+    else:
+        dr1_ref, da_ref, df_ref, acc_ref = refs
     z = pl.program_id(0)
     width = dy_ref.shape[1]
 
@@ -151,122 +155,145 @@
     def _():
         dy = dy_ref[...].astype(F32)
         n = n2_ref[...]
-        ng_ref[1:2] = jnp.sum(dy * n, axis=0, keepdims=True)
-        ng_ref[3:4] = jnp.sum(dy, axis=0, keepdims=True)
+        if grads:
+            ng_ref[1:2] = jnp.sum(dy * n, axis=0, keepdims=True)
+            ng_ref[3:4] = jnp.sum(dy, axis=0, keepdims=True)
+            hb_ref[...] = (n1_ref[...] * g_ref[0:1] + b_ref[0:1]).astype(BF)
         dr2 = norm_back(dy * g_ref[1:2], n, i2_ref[:, :1])
         acc_ref[...] = dr2
         df_ref[...] = dr2.astype(BF)
-        hb_ref[...] = (n1_ref[...] * g_ref[0:1] + b_ref[0:1]).astype(BF)
 
     df = df_ref[...]
     gate = gu_ref[0, 0].astype(F32)
     up = gu_ref[0, 1].astype(F32)
     s = 1.0 / (1.0 + jnp.exp(-gate))
     silu = gate * s
-    act = (silu * up).astype(BF)
     wg, wu, wd = unit_weights(lambda t, m: w_ref[:, t, :, 128 * m : 128 * m + 128].reshape(width, 128))
 
     def keep(m, grad):
         for t in range(g_out.shape[1]):
             g_out[:, t, :, 128 * m : 128 * m + 128] = grad[:, 128 * t : 128 * t + 128].astype(BF).reshape(g_out.shape[0], -1, 128)
 
-    keep(2, dg(df, act, TN))
+    if grads:
+        keep(2, dg(df, (silu * up).astype(BF), TN))
     d_act = dg(df, wd, NN)
     d_gate = (d_act * up * (s * (1.0 + gate * (1.0 - s)))).astype(BF)
     d_up = (d_act * silu).astype(BF)
-    hb = hb_ref[...]
-    keep(0, dg(hb, d_gate, TN))
-    keep(1, dg(hb, d_up, TN))
+    if grads:
+        hb = hb_ref[...]
+        keep(0, dg(hb, d_gate, TN))
+        keep(1, dg(hb, d_up, TN))
     acc_ref[...] += dg(d_gate, wg, NT) + dg(d_up, wu, NT)
 
     @pl.when(z == pl.num_programs(0) - 1)
     def _():
         dh = acc_ref[...]
         n = n1_ref[...]
-        ng_ref[0:1] = jnp.sum(dh * n, axis=0, keepdims=True)
-        ng_ref[2:3] = jnp.sum(dh, axis=0, keepdims=True)
+        if grads:
+            ng_ref[0:1] = jnp.sum(dh * n, axis=0, keepdims=True)
+            ng_ref[2:3] = jnp.sum(dh, axis=0, keepdims=True)
         dr1 = norm_back(dh * g_ref[0:1], n, i1_ref[:, :1])
         dr1_ref[...] = dr1
         da_ref[...] = dr1.astype(BF)
 
 
-def attn_back_kernel(da_ref, wo_ref, o_ref, q_ref, k_ref, v_ref, ko_ref, vo_ref, e_ref, l_ref, cos_ref, sin_ref, dq_ref, own_ref, oth_ref, dwo_ref):
-    da = da_ref[...]
-    rows = da.shape[0]
-    w = jnp.concatenate(out_weight(wo_ref), axis=1)
-    do3 = dg(da, w, NN).astype(BF)
-    o3 = jnp.concatenate([o_ref[i] for i in range(3)], axis=1)
-    dwo_ref[0] = dg(da, o3, TN).astype(BF)
-    cos, sin = cos_ref[...], sin_ref[...]
-    for i in range(3):
-        dot = do3[:, 128 * i : 128 * i + 128].astype(F32).T
-        ot = o_ref[i].astype(F32).T
-        k = jnp.concatenate([k_ref[i], ko_ref[i]], axis=0)
-        v = jnp.concatenate([v_ref[i], vo_ref[i]], axis=0)
-        kt = k.astype(F32).T.astype(BF)
-        qt = q_ref[i].astype(F32).T.astype(BF)
-        dqs, dks, dvs = [], [], []
-        for h in range(2):
-            span = slice(HD * h, HD * h + HD)
-            scaled = dot[span] * l_ref[i, h, 0:1]
-            inner = jnp.sum(scaled * ot[span], axis=0, keepdims=True)
-            sb = scaled.astype(BF)
-            zero = jnp.zeros_like(sb)
-            padded = jnp.concatenate([sb, zero] if h == 0 else [zero, sb], axis=0)
-            dp = dg(v, padded, NN)
-            et = e_ref[i, h]
-            ds = (et.astype(F32) * (dp - inner)).astype(BF)
-            dvs.append(dg(sb, et, NT))
-            dks.append(dg(qt[span], ds, NT))
-            dqt = dg(kt[span], ds, NN) * HD**-0.5
-            d1, d2 = dqt[: HD // 2], dqt[HD // 2 :]
-            dqs.append(d1 * cos + d2 * sin)
-            dqs.append(d2 * cos - d1 * sin)
-        dq_ref[i] = jnp.concatenate(dqs, axis=0).T.astype(BF)
-        dk = jnp.concatenate(dks, axis=0)
-        dv = jnp.concatenate(dvs, axis=0)
-        own_ref[i, 0] = dk[:, :rows]
-        own_ref[i, 1] = dv[:, :rows]
-        oth_ref[i, 0] = dk[:, rows:].astype(BF)
-        oth_ref[i, 1] = dv[:, rows:].astype(BF)
-
-
-def joint_back_kernel(old_ref, x_ref, w_ref, dr1_ref, dq_ref, own_ref, got_ref, dwo_ref, cos_ref, sin_ref, g_ref, dz_ref):
-    p = pl.program_id(0)
-    x = x_ref[...]
-    width = x.shape[1]
-    cos, sin = cos_ref[...], sin_ref[...]
-    dq = [dq_ref[i].astype(F32) for i in range(3)]
-    dk, dv = [], []
-    for i in range(3):
-        t = own_ref[i, 0] + got_ref[i, 0].astype(F32)
+def pair_back(do, o, q, k, v, ko, vo, e, l, cos, sin):
+    dot = do.astype(F32).T
+    ot = o.astype(F32).T
+    k = jnp.concatenate([k, ko], axis=0)
+    v = jnp.concatenate([v, vo], axis=0)
+    kt = k.astype(F32).T.astype(BF)
+    qt = q.astype(F32).T.astype(BF)
+    dqs, dks, dvs = [], [], []
+    for h in range(2):
+        span = slice(HD * h, HD * h + HD)
+        scaled = dot[span] * l[h]
+        inner = jnp.sum(scaled * ot[span], axis=0, keepdims=True)
+        sb = scaled.astype(BF)
+        zero = jnp.zeros_like(sb)
+        padded = jnp.concatenate([sb, zero] if h == 0 else [zero, sb], axis=0)
+        dp = dg(v, padded, NN)
+        et = e[h]
+        ds = (et.astype(F32) * (dp - inner)).astype(BF)
+        dvs.append(dg(sb, et, NT))
+        dks.append(dg(qt[span], ds, NT))
+        dqt = dg(kt[span], ds, NN) * HD**-0.5
+        d1, d2 = dqt[: HD // 2], dqt[HD // 2 :]
+        dqs.append(d1 * cos + d2 * sin)
+        dqs.append(d2 * cos - d1 * sin)
+    return [jnp.concatenate(t, axis=0) for t in (dqs, dks, dvs)]
+
+
+def joint_parts(dq, dkt, dvt, cos, sin):
+    dk = []
+    for t in dkt:
         parts = []
         for h in range(2):
             d1 = t[HD * h : HD * h + HD // 2]
             d2 = t[HD * h + HD // 2 : HD * h + HD]
             parts += [d1 * cos + d2 * sin, d2 * cos - d1 * sin]
         dk.append(jnp.concatenate(parts, axis=0).T)
-        dv.append((own_ref[i, 1] + got_ref[i, 1].astype(F32)).T)
+    dv = [t.T for t in dvt]
     low = low_lanes(dq[0].shape)
     zero = jnp.zeros_like(dv[1])
     d = [
         [dq[0], dk[0], dv[0], jnp.where(low, dq[1], swap64(dk[1])), jnp.where(low, dv[1], zero)],
         [dq[2], dk[2], dv[2], jnp.where(low, swap64(dq[1]), dk[1]), jnp.where(low, swap64(dv[1]), zero)],
     ]
+    return [jnp.concatenate(t, axis=1).astype(BF) for t in d]
+
+
+def attn_back_kernel(grads, da_ref, wo_ref, o_ref, q_ref, k_ref, v_ref, ko_ref, vo_ref, e_ref, l_ref, cos_ref, sin_ref, dq_ref, own_ref, oth_ref, *dwo_ref):
+    da = da_ref[...]
+    rows = da.shape[0]
+    w = jnp.concatenate(out_weight(wo_ref), axis=1)
+    do3 = dg(da, w, NN).astype(BF)
+    if grads:
+        o3 = jnp.concatenate([o_ref[i] for i in range(3)], axis=1)
+        dwo_ref[0][0] = dg(da, o3, TN).astype(BF)
+    cos, sin = cos_ref[...], sin_ref[...]
+    for i in range(3):
+        dqt, dk, dv = pair_back(
+            do3[:, 128 * i : 128 * i + 128], o_ref[i], q_ref[i], k_ref[i], v_ref[i], ko_ref[i], vo_ref[i],
+            [e_ref[i, h] for h in range(2)], [l_ref[i, h, 0:1] for h in range(2)], cos, sin,
+        )
+        dq_ref[i] = dqt.T.astype(BF)
+        own_ref[i, 0] = dk[:, :rows]
+        own_ref[i, 1] = dv[:, :rows]
+        oth_ref[i, 0] = dk[:, rows:].astype(BF)
+        oth_ref[i, 1] = dv[:, rows:].astype(BF)
+
+
+def joint_back_kernel(grads, *refs):
+    if grads:
+        old_ref, x_ref, w_ref, dr1_ref, dq_ref, own_ref, got_ref, dwo_ref, cos_ref, sin_ref, g_ref, dz_ref = refs
+    else:
+        w_ref, dr1_ref, dq_ref, own_ref, got_ref, cos_ref, sin_ref, dz_ref, dzb_ref = refs
+    p = pl.program_id(0)
+    width = dr1_ref.shape[1]
+    d = joint_parts(
+        [dq_ref[i].astype(F32) for i in range(3)],
+        [own_ref[i, 0] + got_ref[i, 0].astype(F32) for i in range(3)],
+        [own_ref[i, 1] + got_ref[i, 1].astype(F32) for i in range(3)],
+        cos_ref[...],
+        sin_ref[...],
+    )
     acc = None
-    wlow = low_lanes((width, 128))
-    mid = dwo_ref[0, :, 128:256].astype(F32)
-    sides = [dwo_ref[0, :, 0:128], dwo_ref[0, :, 256:384]]
-    mids = [swap64(mid), mid]
     for e in range(2):
-        b = jnp.concatenate(d[e], axis=1).astype(BF)
-        t = dg(b, w_ref[:, e, :, :640].reshape(width, 640), NT)
+        t = dg(d[e], w_ref[:, e, :, :640].reshape(width, 640), NT)
         acc = t if acc is None else acc + t
-        g = dg(x, b, TN)
-        blocks = g_ref.shape[0]
-        g_ref[:, e, :, :512] = g[:, :512].astype(BF).reshape(blocks, -1, 512)
-        g_ref[:, e, :, 512:640] = jnp.where(wlow, g[:, 512:], mids[e]).astype(BF).reshape(blocks, -1, 128)
-        g_ref[:, e, :, 640:] = sides[e].reshape(blocks, -1, 128)
+    if grads:
+        x = x_ref[...]
+        wlow = low_lanes((width, 128))
+        mid = dwo_ref[0, :, 128:256].astype(F32)
+        sides = [dwo_ref[0, :, 0:128], dwo_ref[0, :, 256:384]]
+        mids = [swap64(mid), mid]
+        for e in range(2):
+            g = dg(x, d[e], TN)
+            blocks = g_ref.shape[0]
+            g_ref[:, e, :, :512] = g[:, :512].astype(BF).reshape(blocks, -1, 512)
+            g_ref[:, e, :, 512:640] = jnp.where(wlow, g[:, 512:], mids[e]).astype(BF).reshape(blocks, -1, 128)
+            g_ref[:, e, :, 640:] = sides[e].reshape(blocks, -1, 128)
 
     @pl.when(p == 0)
     def _():
@@ -274,7 +301,10 @@
 
     @pl.when(p > 0)
     def _():
-        dz_ref[...] += acc
+        total = dz_ref[...] + acc
+        dz_ref[...] = total
+        if not grads:
+            dzb_ref[...] = total.astype(BF)
 
 
 BIG = pltpu.CompilerParams(vmem_limit_bytes=58 << 20)
@@ -351,39 +381,52 @@
     return y, (q, k, v, ko, vo, o, e, l, gu, n1, i1, n2, i2)
 
 
-def backward(x, dy, kept, weights, norms, tabs):
-    w = weights
+def ffn_backward(dy, kept, w, norms, grads):
     gains, biases = norms
-    q, k, v, ko, vo, o, e, l, gu, n1, i1, n2, i2 = kept
-    rows, width = x.shape
+    gu, n1, i1, n2, i2 = kept[8:]
+    rows, width = dy.shape
+    blocks, tp, depth, columns = w.shape
+    groups = (columns - width) // GROUP
+    whole, stat = full((rows, width)), full((rows, 128))
+    outs = [whole, whole]
+    shapes = [sds((rows, width), F32), sds((rows, width), BF)]
+    scratch = [VM((rows, width), BF), VM((rows, width), F32)]
+    if grads:
+        outs = [group_block(w)] + outs + [full((8, width))]
+        shapes = [sds(w.shape, BF)] + shapes + [sds((8, width), F32)]
+        scratch = [VM((rows, width), BF)] + scratch
+    return pl.pallas_call(
+        functools.partial(ffn_back_kernel, grads),
+        grid=(groups,),
+        in_specs=[
+            whole, whole, stat, whole, stat,
+            lead((1, 2, rows, tp * 128)),
+            group_block(w),
+            full((2, width)), full((2, width)),
+        ],
+        out_specs=outs,
+        out_shape=shapes,
+        scratch_shapes=scratch,
+        compiler_params=BIG,
+        name="ffn_back" if grads else "ffn_back_light",
+    )(dy, n1, i1, n2, i2, gu, w, gains, biases)
+
+
+def attn_backward(x, da, dr1, g, kept, w, tabs):
+    grads = g is not None
+    q, k, v, ko, vo, o, e, l = kept[:8]
+    rows, width = da.shape
     heads = width // 128
     blocks, tp, depth, columns = w.shape
     steps = tp // 2
-    groups = (columns - width) // GROUP
-    units = tp * 128
     cos, sin, cost, sint = tabs
-    whole, stat = full((rows, width)), full((rows, 128))
-    g, dr1, da, ng = pl.pallas_call(
-        ffn_back_kernel,
-        grid=(groups,),
-        in_specs=[
-            whole, whole, stat, whole, stat,
-            lead((1, 2, rows, units)),
-            group_block(w),
-            full((2, width)), full((2, width)),
-        ],
-        out_specs=[
-            group_block(w),
-            whole, whole, full((8, width)),
-        ],
-        out_shape=[sds(w.shape, BF), sds((rows, width), F32), sds((rows, width), BF), sds((8, width), F32)],
-        scratch_shapes=[VM((rows, width), BF), VM((rows, width), BF), VM((rows, width), F32)],
-        compiler_params=BIG,
-        name="ffn_back",
-    )(dy, n1, i1, n2, i2, gu, w, gains, biases)
+    whole = full((rows, width))
     three = lead((3, rows, 128))
-    dq, own, oth, dwo = pl.pallas_call(
-        attn_back_kernel,
+    side = lead((3, 2, 128, rows))
+    table = full((HD // 2, rows))
+    extra = [lead((1, width, 384))] if grads else []
+    dq, own, oth, *dwo = pl.pallas_call(
+        functools.partial(attn_back_kernel, grads),
         grid=(steps,),
         in_specs=[
             whole,
@@ -391,78 +434,96 @@
             three, three, three, three, three, three,
             lead((3, 2, 2 * rows, rows)),
             lead((3, 2, 8, rows)),
-            full((HD // 2, rows)), full((HD // 2, rows)),
+            table, table,
         ],
-        out_specs=[three, lead((3, 2, 128, rows)), lead((3, 2, 128, rows)), lead((1, width, 384))],
+        out_specs=[three, side, side] + extra,
         out_shape=[
             sds((heads, rows, 128), BF),
             sds((heads, 2, 128, rows), F32),
             sds((heads, 2, 128, rows), BF),
-            sds((steps, width, 384), BF),
-        ],
+        ]
+        + ([sds((steps, width, 384), BF)] if grads else []),
         compiler_params=BIG,
         name="attn_back",
     )(da, w, o, q, k, v, ko, vo, e, l, cost, sint)
     got = lax.ppermute(oth, "core", [(0, 1), (1, 0)])
-    g, dz = pl.pallas_call(
-        joint_back_kernel,
+    if grads:
+        specs = [pl.BlockSpec(memory_space=pl.ANY), whole, joint_block(w), whole, three, side, side] + extra
+        args = (g, x, w, dr1, dq, own, got, *dwo)
+        outs, shapes = [joint_block(w), whole], [sds(w.shape, BF), sds((rows, width), F32)]
+    else:
+        specs = [joint_block(w), whole, three, side, side]
+        args = (w, dr1, dq, own, got)
+        outs, shapes = [whole, whole], [sds((rows, width), F32), sds((rows, width), BF)]
+    return pl.pallas_call(
+        functools.partial(joint_back_kernel, grads),
         grid=(steps,),
-        in_specs=[
-            pl.BlockSpec(memory_space=pl.ANY),
-            whole,
-            joint_block(w),
-            whole, three,
-            lead((3, 2, 128, rows)), lead((3, 2, 128, rows)),
-            lead((1, width, 384)),
-            full((HD // 2, rows)), full((HD // 2, rows)),
-        ],
-        out_specs=[joint_block(w), whole],
-        out_shape=[sds(w.shape, BF), sds((rows, width), F32)],
-        input_output_aliases={0: 0},
+        in_specs=specs + [table, table],
+        out_specs=outs,
+        out_shape=shapes,
+        input_output_aliases={0: 0} if grads else {},
         compiler_params=BIG,
         name="joint_back",
-    )(g, x, w, dr1, dq, own, got, dwo, cost, sint)
-    return dz, (g, ng)
-
-
-def sum_kernel(parts, g_ref, ng_ref, out_ref, nout_ref, own, land_c, land_y, land_r, land_l, land_n, own_sem, cs_sem, cr_sem, ys_sem, yr_sem, rs_sem, rr_sem, ls_sem, lr_sem, ns_sem, nr_sem):
+    )(*args, cost, sint)
+
+
+def last_kernel(
+    parts, da_ref, wo_ref, o_ref, q_ref, k_ref, v_ref, ko_ref, vo_ref, e_ref, l_ref, cos_ref, sin_ref,
+    x_ref, w_ref, dr1_ref, y_ref, g_ref, ng_ref,
+    first_out, pair_out, down_out, ends_out, norm_out,
+    do3, dwo, dq, keep, oth, got, dz, g1, e_send, e_land, tmp, own, land_c, land_y, land_r, land_l, land_n,
+    oth_send, oth_recv, end_sem, end_send, end_recv,
+    own_sem, cs_sem, cr_sem, ys_sem, yr_sem, rs_sem, rr_sem, ls_sem, lr_sem, ns_sem, nr_sem,
+):
+    step = pl.program_id(0)
+    section = lax.axis_index("section")
     y, c, z = lax.axis_index("y"), lax.axis_index("core"), lax.axis_index("tensor")
     last = 3
-    near = {"core": 1 - c}
-    across = {"y": 1 - y}
+    rows, width = da_ref.shape
+    early = parts - width // WIDE
+    near, across = {"core": 1 - c}, {"y": 1 - y}
     right, left = {"tensor": jnp.minimum(z + 1, last)}, {"tensor": jnp.maximum(z - 1, 0)}
     pair = {"tensor": z + 1 - 2 * lax.rem(z, 2)}
     far = {"tensor": lax.rem(z + 2, 4)}
+    side = z // 2
     barrier = pltpu.get_barrier_semaphore()
 
     def greet(device):
         pl.semaphore_signal(barrier, inc=1, device_id=device, device_id_type=MESH)
 
-    greet(near)
-    greet(across)
-    greet(far)
-
-    @pl.when(z < last)
-    def _():
-        greet(right)
-
-    @pl.when(z > 0)
-    def _():
-        greet(left)
-
-    pl.semaphore_wait(barrier, 3 + jnp.where(z < last, 1, 0) + jnp.where(z > 0, 1, 0))
+    def remote(src, dst, send, recv, device):
+        return pltpu.make_async_remote_copy(src, dst, send, recv, device_id=device, device_id_type=MESH)
+
+    def target(i):
+        return {"core": side, "tensor": 2 * c + i}
+
+    def at_home(i):
+        return jnp.logical_and(side == c, 2 * c + i == z)
+
+    def end_copy(i):
+        return remote(e_send.at[i], e_land.at[z % 2], end_send.at[i], end_recv.at[z % 2], target(i))
+
+    def end_home(i):
+        return pltpu.make_async_copy(e_send.at[i], e_land.at[z % 2], end_sem)
+
+    def oth_copy(p):
+        return remote(oth.at[p], got.at[p], oth_send.at[p], oth_recv.at[p], near)
 
     def columns(j):
         return pl.ds(pl.multiple_of(j * WIDE, WIDE), WIDE)
 
-    def remote(src, dst, send, recv, device):
-        return pltpu.make_async_remote_copy(src, dst, send, recv, device_id=device, device_id_type=MESH)
+    def late(j):
+        return columns(j - early)
 
     def load(j):
-        return pltpu.make_async_copy(g_ref.at[:, c, :, :, columns(j)], own.at[j], own_sem.at[j])
-
-    def to_core(j):
-        return remote(g_ref.at[:, 1 - c, :, :, columns(j)], land_c.at[j], cs_sem.at[j], cr_sem.at[j], near)
+        return pltpu.make_async_copy(g_ref.at[:, c, :, :, columns(j + parts - early)], own.at[j % 4], own_sem.at[j])
+
+    def to_core(j, kept=False):
+        src = g1.at[:, 1 - c, :, :, late(j)] if kept else g_ref.at[:, 1 - c, :, :, columns(j + parts - early)]
+        return remote(src, land_c.at[j], cs_sem.at[j], cr_sem.at[j], near)
+
+    def from_core(j):
+        return remote(land_c.at[j], land_c.at[j], cs_sem.at[j], cr_sem.at[j], near)
 
     def to_y(j):
         return remote(land_c.at[j, 1 - y], land_y.at[j], ys_sem.at[j], yr_sem.at[j], across)
@@ -476,96 +537,119 @@
     def go_left(j, count, src):
         return remote(src, land_l.at[j, pl.ds(0, count)], ls_sem.at[j], lr_sem.at[j], left)
 
-    for j in range(2):
-        to_core(j).start()
-        load(j).start()
-    land_n[0] = ng_ref[...]
-    norm_copy(0).start()
-
-    def step(i, carry):
-        @pl.when(i + 2 < parts)
-        def _():
-            to_core(i + 2).start()
-            load(i + 2).start()
-
-        @pl.when(i < parts)
-        def _():
-            load(i).wait()
-            to_core(i).wait_recv()
-            land_c[i] = land_c[i] + own[i]
-            to_y(i).start()
-
-        @pl.when(jnp.logical_and(i >= 4, i - 4 < parts))
-        def _():
-            j = i - 4
-
-            @pl.when(z == 1)
+    def prepare(j):
+        @pl.when(j < early)
+        def _():
+            to_core(j).start()
+            load(j).start()
+
+        @pl.when(jnp.logical_and(j >= early, j < parts))
+        def _():
+            to_core(j, True).start()
+
+    def stage(i, lag, body):
+        @pl.when(jnp.logical_and(i >= lag, i - lag < parts))
+        def _():
+            body(i - lag)
+
+    def first_sum(j):
+        from_core(j).wait_recv()
+
+        @pl.when(j < early)
+        def _():
+            load(j).wait()
+            land_c[j] = land_c[j] + own[j % 4]
+
+        @pl.when(j >= early)
+        def _():
+            land_c[j] = land_c[j] + g1[:, c, :, :, late(j)]
+
+        to_y(j).start()
+
+    def last_hop(j):
+        @pl.when(z == 1)
+        def _():
+            go_left(j, 2, land_l.at[j, pl.ds(0, 2)]).wait_recv()
+            land_l[j, 0] = land_l[j, 0] + land_c[j, y, 0]
+            go_left(j, 1, land_l.at[j, pl.ds(0, 1)]).start()
+
+        @pl.when(z == 2)
+        def _():
+            go_right(j, 2, land_r.at[j, pl.ds(1, 2)]).wait_recv()
+            land_r[j, 2] = land_r[j, 2] + land_c[j, y, 3]
+            go_right(j, 3, land_r.at[j, pl.ds(2, 1)]).start()
+
+    def next_hop(j):
+        @pl.when(z == 1)
+        def _():
+            go_right(j, 1, land_r.at[j]).wait_recv()
+            for k in (2, 3):
+                land_r[j, k - 1] = land_r[j, k - 1] + land_c[j, y, k]
+            go_right(j, 2, land_r.at[j, pl.ds(1, 2)]).start()
+
+        @pl.when(z == 2)
+        def _():
+            go_left(j, 3, land_l.at[j]).wait_recv()
+            for k in (0, 1):
+                land_l[j, k] = land_l[j, k] + land_c[j, y, k]
+            go_left(j, 2, land_l.at[j, pl.ds(0, 2)]).start()
+
+    def first_hop(j):
+        to_y(j).wait_recv()
+        land_c[j, y] = land_c[j, y] + land_y[j]
+
+        @pl.when(z == 0)
+        def _():
+            go_right(j, 1, land_c.at[j, y, pl.ds(1, 3)]).start()
+
+        @pl.when(z == last)
+        def _():
+            go_left(j, 3, land_c.at[j, y, pl.ds(0, 3)]).start()
+
+    def result(j):
+        mine = land_c[j, y, z].astype(F32)
+
+        @pl.when(z == 0)
+        def _():
+            go_left(j, 1, land_l.at[j, pl.ds(0, 1)]).wait_recv()
+            tmp[...] = mine + land_l[j, 0].astype(F32)
+
+        @pl.when(z == 1)
+        def _():
+            tmp[...] = mine + land_r[j, 0].astype(F32) + land_l[j, 1].astype(F32)
+
+        @pl.when(z == 2)
+        def _():
+            tmp[...] = mine + land_r[j, 1].astype(F32) + land_l[j, 2].astype(F32)
+
+        @pl.when(z == last)
+        def _():
+            go_right(j, 3, land_r.at[j, pl.ds(2, 1)]).wait_recv()
+            tmp[...] = mine + land_r[j, 2].astype(F32)
+
+        group = j // 3
+
+        @pl.when(j >= early)
+        def _():
+            first_out[:, late(j)] = tmp[...]
+
+        for m in range(2):
+
+            @pl.when(jnp.logical_and(j < early, j % 3 == m))
             def _():
-                go_left(j, 2, land_l.at[j, pl.ds(0, 2)]).wait_recv()
-                land_l[j, 0] = land_l[j, 0] + land_c[j, y, 0]
-                go_left(j, 1, land_l.at[j, pl.ds(0, 1)]).start()
-
-            @pl.when(z == 2)
-            def _():
-                go_right(j, 2, land_r.at[j, pl.ds(1, 2)]).wait_recv()
-                land_r[j, 2] = land_r[j, 2] + land_c[j, y, 3]
-                go_right(j, 3, land_r.at[j, pl.ds(2, 1)]).start()
-
-        @pl.when(jnp.logical_and(i >= 3, i - 3 < parts))
-        def _():
-            j = i - 3
-
-            @pl.when(z == 1)
-            def _():
-                go_right(j, 1, land_r.at[j]).wait_recv()
-                for k in (2, 3):
-                    land_r[j, k - 1] = land_r[j, k - 1] + land_c[j, y, k]
-                go_right(j, 2, land_r.at[j, pl.ds(1, 2)]).start()
-
-            @pl.when(z == 2)
-            def _():
-                go_left(j, 3, land_l.at[j]).wait_recv()
-                for k in (0, 1):
-                    land_l[j, k] = land_l[j, k] + land_c[j, y, k]
-                go_left(j, 2, land_l.at[j, pl.ds(0, 2)]).start()
-
-        @pl.when(jnp.logical_and(i >= 2, i - 2 < parts))
-        def _():
-            j = i - 2
-            to_y(j).wait_recv()
-            land_c[j, y] = land_c[j, y] + land_y[j]
-
-            @pl.when(z == 0)
-            def _():
-                go_right(j, 1, land_c.at[j, y, pl.ds(1, 3)]).start()
-
-            @pl.when(z == last)
-            def _():
-                go_left(j, 3, land_c.at[j, y, pl.ds(0, 3)]).start()
-
-        @pl.when(i >= 5)
-        def _():
-            j = i - 5
-            mine = land_c[j, y, z].astype(F32)
-
-            @pl.when(z == 0)
-            def _():
-                go_left(j, 1, land_l.at[j, pl.ds(0, 1)]).wait_recv()
-                out_ref[:, columns(j)] = mine + land_l[j, 0].astype(F32)
-
-            @pl.when(z == 1)
-            def _():
-                out_ref[:, columns(j)] = mine + land_r[j, 0].astype(F32) + land_l[j, 1].astype(F32)
-
-            @pl.when(z == 2)
-            def _():
-                out_ref[:, columns(j)] = mine + land_r[j, 1].astype(F32) + land_l[j, 2].astype(F32)
-
-            @pl.when(z == last)
-            def _():
-                go_right(j, 3, land_r.at[j, pl.ds(2, 1)]).wait_recv()
-                out_ref[:, columns(j)] = mine + land_r[j, 2].astype(F32)
-
+                pair_out[:, columns(group + m * (early // 3))] = tmp[...]
+
+        @pl.when(jnp.logical_and(j < early, j % 3 == 2))
+        def _():
+            down_out[columns(group), :] = tmp[...].T
+
+    def round_(i):
+        prepare(i + 2)
+        stage(i, 0, first_sum)
+        stage(i, 4, last_hop)
+        stage(i, 3, next_hop)
+        stage(i, 2, first_hop)
+        stage(i, 5, result)
         for k in range(4):
 
             @pl.when(i == 3 * (k + 1))
@@ -576,62 +660,213 @@
                     land_n[2 * k + 2] = total
                     norm_copy(k + 1).start()
                 else:
-                    nout_ref[...] = total
-
-        return carry
-
-    lax.fori_loop(0, parts + 5, step, 0)
-
-    def finish(j, carry):
-        to_core(j).wait_send()
-        to_y(j).wait_send()
-
-        @pl.when(z == 0)
-        def _():
-            go_right(j, 1, land_c.at[j, y, pl.ds(1, 3)]).wait_send()
-
-        @pl.when(z == 1)
-        def _():
-            go_right(j, 2, land_r.at[j, pl.ds(1, 2)]).wait_send()
-            go_left(j, 1, land_l.at[j, pl.ds(0, 1)]).wait_send()
-
-        @pl.when(z == 2)
-        def _():
-            go_right(j, 3, land_r.at[j, pl.ds(2, 1)]).wait_send()
-            go_left(j, 2, land_l.at[j, pl.ds(0, 2)]).wait_send()
-
-        @pl.when(z == last)
-        def _():
-            go_left(j, 3, land_c.at[j, y, pl.ds(0, 3)]).wait_send()
-
-        return carry
-
-    lax.fori_loop(0, parts, finish, 0)
-
-
-def sum_over_section(g, ng):
-    rows, columns = g.shape[2:]
+                    norm_out[...] = total
+
+    @pl.when(step == 0)
+    def _():
+        greet(near)
+        greet(across)
+        greet(far)
+
+        @pl.when(z < last)
+        def _():
+            greet(right)
+
+        @pl.when(z > 0)
+        def _():
+            greet(left)
+
+        for i in range(2):
+
+            @pl.when(jnp.logical_not(at_home(i)))
+            def _():
+                greet(target(i))
+
+        count = 5 + jnp.where(z < last, 1, 0) + jnp.where(z > 0, 1, 0) - jnp.where(side == c, 1, 0)
+        pl.semaphore_wait(barrier, count)
+        prepare(0)
+        prepare(1)
+        land_n[0] = ng_ref[...]
+        norm_copy(0).start()
+
+    cos, sin = cos_ref[...], sin_ref[...]
+
+    @pl.when(jnp.logical_and(step < 6, step % 3 == 0))
+    def _():
+        w = jnp.concatenate(out_weight(wo_ref), axis=1)
+        t = dg(da_ref[...], w, NN).astype(BF)
+        for i in range(3):
+            do3[i] = t[:, 128 * i : 128 * i + 128]
+        o3 = jnp.concatenate([o_ref[step + i] for i in range(3)], axis=1)
+        dwo[step // 3] = dg(da_ref[...], o3, TN).astype(BF)
+
+    @pl.when(step < 6)
+    def _():
+        dqt, dk, dv = pair_back(
+            do3[step % 3], o_ref[step], q_ref[0], k_ref[0], v_ref[0], ko_ref[0], vo_ref[0],
+            [e_ref[0, h] for h in range(2)], [l_ref[0, h, 0:1] for h in range(2)], cos, sin,
+        )
+        dq[step] = dqt.T.astype(BF)
+        keep[step, 0] = dk[:, :rows]
+        keep[step, 1] = dv[:, :rows]
+        oth[step, 0] = dk[:, rows:].astype(BF)
+        oth[step, 1] = dv[:, rows:].astype(BF)
+        oth_copy(step).start()
+
+    @pl.when(step >= 6)
+    def _():
+        p = step - 6
+        for i in range(3):
+            oth_copy(3 * p + i).wait()
+        d = joint_parts(
+            [dq[3 * p + i].astype(F32) for i in range(3)],
+            [keep[3 * p + i, 0] + got[3 * p + i, 0].astype(F32) for i in range(3)],
+            [keep[3 * p + i, 1] + got[3 * p + i, 1].astype(F32) for i in range(3)],
+            cos, sin,
+        )
+        acc = None
+        wlow = low_lanes((width, 128))
+        mid = dwo[p, :, 128:256].astype(F32)
+        sides = [dwo[p, :, 0:128], dwo[p, :, 256:384]]
+        mids = [swap64(mid), mid]
+        for e in range(2):
+            t = dg(d[e], w_ref[:, e, :, :640].reshape(width, 640), NT)
+            acc = t if acc is None else acc + t
+            g = dg(x_ref[...], d[e], TN)
+            shape = (2, 2, width // 4)
+            g1[:, :, 2 * p + e, :, :512] = g[:, :512].astype(BF).reshape(shape + (512,))
+            g1[:, :, 2 * p + e, :, 512:640] = jnp.where(wlow, g[:, 512:], mids[e]).astype(BF).reshape(shape + (128,))
+            g1[:, :, 2 * p + e, :, 640:] = sides[e].reshape(shape + (128,))
+
+        @pl.when(p == 0)
+        def _():
+            dz[...] = dr1_ref[...] + acc
+
+        @pl.when(p > 0)
+        def _():
+            value = jnp.where(section == 0, (dz[...] + acc).astype(BF), y_ref[...])
+            e_send[...] = value.reshape(e_send.shape)
+            for i in range(2):
+
+                @pl.when(at_home(i))
+                def _():
+                    end_home(i).start()
+
+                @pl.when(jnp.logical_not(at_home(i)))
+                def _():
+                    end_copy(i).start()
+
+    round_(step)
+
+    @pl.when(step == 7)
+    def _():
+        lax.fori_loop(8, parts + 5, lambda i, t: (round_(i), t)[1], 0)
+        for i in range(2):
+
+            @pl.when(at_home(i))
+            def _():
+                end_home(i).wait()
+
+            @pl.when(jnp.logical_not(at_home(i)))
+            def _():
+                end_copy(i).wait_send()
+                remote(e_send.at[i], e_land.at[i], end_send.at[i], end_recv.at[i], target(i)).wait_recv()
+
+        ends_out[...] = e_land[...]
+
+        def finish(j, carry):
+            from_core(j).wait_send()
+            to_y(j).wait_send()
+
+            @pl.when(z == 0)
+            def _():
+                go_right(j, 1, land_c.at[j, y, pl.ds(1, 3)]).wait_send()
+
+            @pl.when(z == 1)
+            def _():
+                go_right(j, 2, land_r.at[j, pl.ds(1, 2)]).wait_send()
+                go_left(j, 1, land_l.at[j, pl.ds(0, 1)]).wait_send()
+
+            @pl.when(z == 2)
+            def _():
+                go_right(j, 3, land_r.at[j, pl.ds(2, 1)]).wait_send()
+                go_left(j, 2, land_l.at[j, pl.ds(0, 2)]).wait_send()
+
+            @pl.when(z == last)
+            def _():
+                go_left(j, 3, land_c.at[j, y, pl.ds(0, 3)]).wait_send()
+
+            return carry
+
+        lax.fori_loop(0, parts, finish, 0)
+
+
+def last_back(x, y, da, dr1, g, ng, kept, w, tabs):
+    q, k, v, ko, vo, o, e, l = kept[:8]
+    rows, width = x.shape
+    heads = width // 128
+    depth, columns = w.shape[2:]
     parts = columns // WIDE
-    g = g.reshape(2, 2, 4, rows, columns)
+    units = (columns - width) // 3
+    cos, sin, cost, sint = tabs
     dma = pltpu.SemaphoreType.DMA
+
+    def once(shape):
+        return pl.BlockSpec(shape, lambda i: (0,) * len(shape), pipeline_mode=pl.Buffered(1))
+
+    def by_pair(shape):
+        return pl.BlockSpec(shape, lambda i: (jnp.minimum(i, 5),) + (0,) * (len(shape) - 1))
+
+    pair = by_pair((1, rows, 128))
     return pl.pallas_call(
-        functools.partial(sum_kernel, parts),
-        in_specs=[pl.BlockSpec(memory_space=pl.ANY), pl.BlockSpec(memory_space=VM)],
-        out_specs=[pl.BlockSpec(memory_space=VM)] * 2,
-        out_shape=[sds((rows, columns), F32), sds(ng.shape, F32)],
+        functools.partial(last_kernel, parts),
+        grid=(8,),
+        in_specs=[
+            once((rows, width)),
+            pl.BlockSpec((4, 2, depth, 256), lambda i: (0, jnp.minimum(i // 3, 1), 0, 2), pipeline_mode=pl.Buffered(1)),
+            once((heads, rows, 128)),
+            pair, pair, pair, pair, pair,
+            by_pair((1, 2, 2 * rows, rows)),
+            by_pair((1, 2, 8, rows)),
+            once((HD // 2, rows)), once((HD // 2, rows)),
+            once((rows, width)),
+            pl.BlockSpec((4, 2, depth, 768), lambda i: (0, jnp.maximum(i - 6, 0), 0, 0), pipeline_mode=pl.Buffered(1)),
+            once((rows, width)), once((rows, width)),
+            pl.BlockSpec(memory_space=pl.ANY),
+            once(ng.shape),
+        ],
+        out_specs=[
+            once((depth, width)), once((depth, 2 * units)), once((units, depth)), once((2, rows // 2, width)), once(ng.shape),
+        ],
+        out_shape=[
+            sds((depth, width), F32), sds((depth, 2 * units), F32), sds((units, depth), F32),
+            sds((2, rows // 2, width), BF), sds(ng.shape, F32),
+        ],
         scratch_shapes=[
-            VM((parts, 2, 4, rows, WIDE), BF),
-            VM((parts, 2, 4, rows, WIDE), BF),
-            VM((parts, 4, rows, WIDE), BF),
-            VM((parts, 3, rows, WIDE), BF),
-            VM((parts, 3, rows, WIDE), BF),
+            VM((3, rows, 128), BF),
+            VM((2, width, 384), BF),
+            VM((heads, rows, 128), BF),
+            VM((heads, 2, 128, rows), F32),
+            VM((heads, 2, 128, rows), BF),
+            VM((heads, 2, 128, rows), BF),
+            VM((rows, width), F32),
+            VM((2, 2, 4, depth, width), BF),
+            VM((2, rows // 2, width), BF),
+            VM((2, rows // 2, width), BF),
+            VM((depth, WIDE), F32),
+            VM((4, 2, 4, depth, WIDE), BF),
+            VM((parts, 2, 4, depth, WIDE), BF),
+            VM((parts, 4, depth, WIDE), BF),
+            VM((parts, 3, depth, WIDE), BF),
+            VM((parts, 3, depth, WIDE), BF),
             VM((8,) + ng.shape, F32),
+            dma((6,)), dma((6,)), dma, dma((2,)), dma((2,)),
         ]
         + [dma((parts,))] * 9
         + [dma((4,))] * 2,
-        compiler_params=pltpu.CompilerParams(collective_id=0, has_side_effects=True, vmem_limit_bytes=58 << 20),
-        name="grad_sum",
-    )(g, ng)
+        compiler_params=pltpu.CompilerParams(collective_id=0, has_side_effects=True, vmem_limit_bytes=62 << 20),
+        name="last",
+    )(da, w, o, q, k, v, ko, vo, e, l, cost, sint, x, w, dr1, y, g.reshape(2, 2, 4, depth, columns), ng)
 
 
 LAG = 6
@@ -664,8 +899,8 @@
     def at_home(i):
         return jnp.logical_and(side == c, 2 * c + i == z)
 
-    def token_copy(i):
-        return remote(tok_ref.at[i], xin.at[z % 2], tok_send.at[i], tok_recv.at[z % 2], target(i))
+    def token_copy(i, part):
+        return remote(tok_ref.at[i, part], xin.at[z % 2, part], tok_send.at[i], tok_recv.at[z % 2], target(i))
 
     def token_home(i):
         return pltpu.make_async_copy(tok_ref.at[i], xin.at[z % 2], tok_sem)
@@ -691,16 +926,6 @@
 
     count = 4 + jnp.where(z < last, 1, 0) + jnp.where(z > 0, 1, 0) - jnp.where(side == c, 1, 0)
     pl.semaphore_wait(barrier, count)
-
-    for i in range(2):
-
-        @pl.when(at_home(i))
-        def _():
-            token_home(i).start()
-
-        @pl.when(jnp.logical_not(at_home(i)))
-        def _():
-            token_copy(i).start()
 
     ext[y, c] = extra_ref[...]
     lens[c] = len_ref[...]
@@ -730,6 +955,9 @@
     def to_y(j):
         return remote(w.at[y, c, :, :, columns(j)], w.at[y, c, :, :, columns(j)], ys_sem.at[j], yr_sem.at[j], across)
 
+    def block_to_y(j, b):
+        return remote(w.at[y, c, b, :, columns(j)], w.at[y, c, b, :, columns(j)], ys_sem.at[j], yr_sem.at[j], across)
+
     def to_core(j):
         return remote(w.at[:, c, :, :, columns(j)], w.at[:, c, :, :, columns(j)], cs_sem.at[j], cr_sem.at[j], near)
 
@@ -750,14 +978,18 @@
         def _():
             go_left(j, 0).start()
 
+        block_to_y(j, z).start()
+
     def hop(h, j):
         @pl.when(z >= h)
         def _():
             go_right(j, h - 1).wait_recv()
+            block_to_y(j, z - h).start()
 
         @pl.when(z + h <= last)
         def _():
             go_left(j, h - 1).wait_recv()
+            block_to_y(j, z + h).start()
 
         if h < last:
 
@@ -768,9 +1000,6 @@
             @pl.when(jnp.logical_and(z + h <= last, z > 0))
             def _():
                 go_left(j, h).start()
-
-        else:
-            to_y(j).start()
 
     def over_core(j):
         to_y(j).wait_recv()
@@ -792,7 +1021,26 @@
         lax.fori_loop(first, end, lambda r, t: (round_(r), t)[1], 0)
 
     lead_parts = width // WIDE
-    rounds(0, 3)
+    start = 17
+    token_rows = xin.shape[1] // 16
+    for i in range(2):
+
+        @pl.when(at_home(i))
+        def _():
+            token_home(i).start()
+
+    def early(r, carry):
+        round_(r)
+        part = pl.ds(pl.multiple_of(r * token_rows, token_rows), token_rows)
+        for i in range(2):
+
+            @pl.when(jnp.logical_not(at_home(i)))
+            def _():
+                token_copy(i, part).start()
+
+        return carry
+
+    lax.fori_loop(0, 3, early, 0)
     small(0).wait()
     small(1).wait()
     small(2).start()
@@ -809,7 +1057,8 @@
         seg_q = seg_q + jnp.where(end <= at_q, 1, 0)
         seg_k = seg_k + jnp.where(end <= at_k, 1, 0)
     mask_out[...] = jnp.where(seg_k == seg_q, 0.0, neg_fill).astype(F32)
-    rounds(3, lead_parts + LAG)
+    lax.fori_loop(3, 16, early, 0)
+    rounds(16, start)
 
     small(2).wait()
     halves = [ext[i // 2, i % 2].astype(F32) for i in range(4)]
@@ -826,7 +1075,7 @@
 
         @pl.when(jnp.logical_not(at_home(i)))
         def _():
-            token_copy(i).wait_send()
+            token_copy(i, pl.ds(0, xin.shape[1])).wait_send()
             remote(tok_ref.at[i], xin.at[i], tok_send.at[i], tok_recv.at[i], target(i)).wait_recv()
 
     x = xin[...].reshape(rows, width)
@@ -845,7 +1094,6 @@
             kv[1, 3 * p + i] = vs[i].astype(BF)
     share = remote(kv, land_kv, kv_send, kv_recv, near)
     share.start()
-    start = lead_parts + LAG
     rounds(start, start + 1)
     share.wait()
 
@@ -883,12 +1131,10 @@
     rounds(start + 7, start + 8)
 
     def units(k, carry):
-        lax.fori_loop(
-            jnp.maximum(start + 8, lead_parts + 3 * k + LAG),
-            lead_parts + 3 * k + LAG + 3,
-            lambda i, t: (round_(i), t)[1],
-            0,
-        )
+        @pl.when(k != 4)
+        def _():
+            round_(start + 8 + k - k // 5)
+
         wg, wu, wd = unit_weights(
             lambda t, m: w[:, :, t, :, pl.ds(pl.multiple_of(width + GROUP * k + 128 * m, 128), 128)].reshape(width, 128)
         )
@@ -1026,11 +1272,8 @@
     return jnp.concatenate([first, units.reshape(rows, -1)], axis=1)
 
 
-def unpack_shard(packed):
-    rows, columns = packed.shape
-    first = packed[:, :768]
-    units = packed[:, 768:].reshape(rows, -1, 3, 128).transpose(0, 2, 1, 3).reshape(rows, 3, -1)
-    pair, down = units[:, :2], units[:, 2]
+def unpack_first(first):
+    rows = first.shape[0]
     odd = lax.axis_index("tensor") % 2 == 1
     both = first[:, :384].reshape(rows, 3, 2, HD)
     single = first[:, 384:576].reshape(rows, 3, 1, HD)
@@ -1038,12 +1281,7 @@
     mine = jnp.concatenate([first[:, 640:].reshape(rows, 2, HD), first[:, 576:640].reshape(rows, 1, HD)], axis=1)
     heads = jnp.where(odd, jnp.roll(heads, 1, axis=2), heads)
     mine = jnp.where(odd, jnp.roll(mine, 1, axis=1), mine)
-    return (
-        heads.reshape(rows, 3, -1),
-        mine.reshape(rows, -1).T,
-        pair,
-        down.T,
-    )
+    return heads.reshape(rows, 3, -1), mine.reshape(rows, -1).T
 
 
 def host_tables(length):
@@ -1083,13 +1321,14 @@
     near = core * rows + jnp.arange(rows, dtype=jnp.int32)
     far = (1 - core) * rows + jnp.arange(rows, dtype=jnp.int32)
     tabs = rope_tables(near)
-    grad_top = to_sequences(cotangent, tp)
     if dp == 4 and tp == 4:
         extra = jnp.concatenate([norm_gains.reshape(-1, 128), norm_biases.reshape(-1, 128)])
         extra = jnp.pad(extra, ((0, 16 - extra.shape[0]), (0, 0)))
         padded = jnp.pad(lengths, ((0, 8 - lengths.shape[0]), (0, 128 - lengths.shape[1])))
         wide, signed = host_tables(length)
-        weights, y, tokens, mask, small = first_layer(tokens, shard, extra, padded, wide, signed)
+        rows_in = jnp.where(section == 0, tokens, cotangent)
+        weights, y, tokens, mask, small = first_layer(rows_in, shard, extra, padded, wide, signed)
+        grad_top = tokens
         weights = weights.reshape((BLOCKS,) + weights.shape[2:])
         norms = (small[:2], small[2:])
     else:
@@ -1097,6 +1336,7 @@
         norms = jnp.concatenate([norm_gains, norm_biases])
         norms = lax.all_gather(norms, ("y", "core"), axis=1, tiled=True).astype(F32)
         norms = (norms[0].reshape(2, width), norms[1].reshape(2, width))
+        grad_top = to_sequences(cotangent, tp)
         tokens = to_sequences(tokens, tp)
         chip_lengths = lax.all_gather(lengths, "core", axis=0, tiled=True)
         my_lengths = lax.dynamic_index_in_dim(chip_lengths, at, 0, keepdims=False)
@@ -1112,23 +1352,27 @@
     received = lax.ppermute(y, "section", [(0, 1)])
     inputs = jnp.where(section == 0, tokens, received)
     y, kept = forward(inputs, weights, norms, mask, tabs)
-    dz, grads = backward(inputs, grad_top, kept, weights, norms, tabs)
-    received = lax.ppermute(dz.astype(BF), "section", [(1, 0)])
+    dr1, da = ffn_backward(grad_top, kept, weights, norms, False)
+    unused, dz = attn_backward(inputs, da, dr1, None, kept, weights, tabs)
+    received = lax.ppermute(dz, "section", [(1, 0)])
     dy = jnp.where(section == 0, received, grad_top)
-    dz, grads = backward(inputs, dy, kept, weights, norms, tabs)
-    ends = to_positions(jnp.where(section == 0, dz.astype(BF), y), tp)
-    g, ng = grads
+    g, dr1, da, ng = ffn_backward(dy, kept, weights, norms, True)
     if dp == 4 and tp == 4:
-        mine, total = sum_over_section(g, ng)
-        index = lax.axis_index(ALL)
-        small = lax.dynamic_slice_in_dim(total[:4].reshape(2, dp * tp, -1), index, 1, 1)
+        first, pair, down, ends, total = last_back(inputs, y, da, dr1, g, ng, kept, weights, tabs)
+        small = lax.dynamic_slice_in_dim(total[:4].reshape(2, dp * tp, -1), lax.axis_index(ALL), 1, 1)
         gains, biases = small[0, 0], small[1, 0]
     else:
+        g, dz = attn_backward(inputs, da, dr1, g, kept, weights, tabs)
+        ends = to_positions(jnp.where(section == 0, dz.astype(BF), y), tp)
         mine = scatter_sum(g, dp, tp)
+        first = mine[:, :width]
+        units = mine[:, width:].reshape(first.shape[0], -1, 3, 128).transpose(0, 2, 1, 3).reshape(first.shape[0], 3, -1)
+        pair, down = units[:, :2], units[:, 2].T
         gains = lax.psum_scatter(ng[0:2].reshape(-1), ALL, scatter_dimension=0, tiled=True)
         biases = lax.psum_scatter(ng[2:4].reshape(-1), ALL, scatter_dimension=0, tiled=True)
-    outs = unpack_shard(mine)
-    return (ends[None],) + tuple(t[None] for t in outs + (gains, biases))
+    joint, mix = unpack_first(first)
+    outs = (joint, mix, pair.reshape(pair.shape[0], 2, -1), down, gains, biases)
+    return (ends[None],) + tuple(t[None] for t in outs)
 
 
 def solution(mesh):

time: 529 us -> 460 us (0.87)
  Pallas kernels: 421 us -> 378 us
  local copies, waits for them, and re-layouts: 37.1 us -> 22.2 us
    pallas_call x7 -> x5, Pallas kernels: 236 us -> 213 us  [the longest x1 141 us: last_back(): pl.pallas_call(functools.partial(last_kernel, parts), grid=(8,), in_specs...]
    pallas_call x1, Pallas kernels: 144 us -> 124 us  [first_layer(): pl.pallas_call(functools.partial(first_kernel, parts), in_specs=[hbm, hbm...]
    reshape x4 -> x2, local copies, waits for them, and re-layouts: 7.01 us -> 1.09 us  [the longest x1 0.97 us: unpack_first(): first[:, 576:640].reshape(rows, 1, HD)]
    ppermute x7 -> x2, starting transfers between devices: 7.34 us -> 1.48 us  [the longest x1 1.28 us: on_device(): received = lax.ppermute(dz, 'section', [(1, 0)])]
    ppermute x7 -> x2, waiting for transfers between devices: 27.2 us -> 23.9 us  [the longest x1 20.4 us: on_device(): received = lax.ppermute(dz, 'section', [(1, 0)])]
  transfers between devices with their start and end apart: 10 -> 5, of which waited for: 5 -> 5; matrix products, arithmetic and copies ran while one was open for 4% -> 1% of each run, Pallas kernels for 1% -> 0%
where the time goes in v5:
time: 460 us; the launch traced here: 456 us
  Pallas kernels  378 us (82%)
  waiting for transfers between devices  40.1 us (9%)
  local copies, waits for them, and re-layouts  22.2 us (5%)
  other arithmetic  7.26 us (2%)
  starting transfers between devices  6.95 us (2%)
    pallas_call x1, Pallas kernels, last_back(): pl.pallas_call(functools.partial(last_kernel, parts), grid=(8,), in_specs...  141 us
    pallas_call x1, Pallas kernels, first_layer(): pl.pallas_call(functools.partial(first_kernel, parts), in_specs=[hbm, hbm...  124 us
    pallas_call x2, Pallas kernels, ffn_backward(): pl.pallas_call(functools.partial(ffn_back_kernel, grads), grid=(groups,),...  42.9 us
    ppermute x1, waiting for transfers between devices, on_device(): received = lax.ppermute(dz, 'section', [(1, 0)])  20.4 us
    pallas_call x1, Pallas kernels, attn_backward(): pl.pallas_call(functools.partial(attn_back_kernel, grads), grid=(steps,),...  20.3 us
    pallas_call x1, Pallas kernels, forward(): pl.pallas_call(ffn_kernel, grid=(groups,), in_specs=[full((rows, width)),...  18.1 us
    pallas_call x1, Pallas kernels, forward(): pl.pallas_call(attn_kernel, grid=(heads,), in_specs=[pair] * 5 + [full((2...  16.4 us
    ppermute x1, waiting for transfers between devices, on_device(): received = lax.ppermute(y, 'section', [(0, 1)])  14.7 us
  transfers between devices with their start and end apart: 5, of which 5 were waited for; matrix products, arithmetic and copies ran while one was open for 1% of the time, Pallas kernels for 0%

profile of v5, /device:TPU:0, one launch (start us, length us, event | category | flops | bytes accessed | tf_op | source)
XLA Modules:
  0.0 456.0 jit_solution(6954934377807737)
XLA Ops:
  0.6 1.1 copy.51
  1.8 1.1 copy.50
  3.2 0.6 pad.9.len_ref
  4.3 0.3 concatenate.45
  4.7 0.7 concatenate.44
  5.4 0.3 maximum_bitcast_fusion
  5.7 1.2 copy.56
  6.9 0.8 reshape.96
  7.7 0.6 fusion.3.extra_ref
  8.3 1.0 broadcast_select_fusion.tok_ref
  9.3 1.7 concatenate.47.shard_ref
  11.0 124.3 %first.1 = (bf16[2,2,4,192,3072]{4,3,2,1,0:T(8,128)(2,1)}, bf16[512,768]{1,0:T(8,128)(2,1)}, bf16[512,768]{1,0:T(8,128)(2,1)}, f32[1024,512]{1,0:T(8,128)}, f32[4,768]{1,0:T(4,128)}) custom-call(bf16[2,256,768]{2,1,0:T(8,128)(2,1)} %broadcast_select_fusion.tok_ref, bf16[192,3072]{1,0:T(8,128)(2,1)} %concatenate.47.shard_ref, ...), custom_call_target="tpu_custom_call" | custom-call | tf_op jit(solution)/shard_map/first/pallas_call | solution.py:1179
  135.3 5.0 %collective-permute-start = (bf16[512,768]{1,0:T(8,128)(2,1)}, bf16[512,768]{1,0:T(8,128)(2,1)S(1)}, u32[]{:S(2)}, u32[]{:S(2)}) collective-permute-start(bf16[512,768]{1,0:T(8,128)(2,1)} %get-tuple-element.41), channel_id=1, source_target_pairs={{0,16},{1,17},{2,18},{3,19},{4,20},{5,21},{6,22},{7,23},{8,24},{9,... | collective-permute-start | bytes 2359304 | tf_op jit(solution)/shard_map/ppermute | solution.py:1352
  140.3 1.0 fusion
  141.3 1.3 pad_maximum_fusion
  142.6 14.7 %collective-permute-done = bf16[512,768]{1,0:T(8,128)(2,1)S(1)} collective-permute-done((bf16[512,768]{1,0:T(8,128)(2,1)}, bf16[512,768]{1,0:T(8,128)(2,1)S(1)}, u32[]{:S(2)}, u32[]{:S(2)}) %collective-permute-start) | collective-permute-done | bytes 786464 | tf_op jit(solution)/shard_map/ppermute | solution.py:1352
  157.3 1.0 broadcast_select_fusion.2.x_ref
  158.2 6.5 %qkv.1 = (bf16[6,512,128]{2,1,0:T(8,128)(2,1)}, bf16[6,512,128]{2,1,0:T(8,128)(2,1)}, bf16[6,512,128]{2,1,0:T(8,128)(2,1)}) custom-call(bf16[512,768]{1,0:T(8,128)(2,1)} %broadcast_select_fusion.2.x_ref, bf16[4,4,192,3072]{3,2,1,0:T(8,128)(2,1)} %bitcast.43, f32[512,128]{1,0:T(8,128)} %get-tuple-element.101.cos_ref, f32[512,128]{1,0:T(8,128)} %get-tuple-element.102.sin_ref), custom_call_target="tpu_custom_call" | custom-call | tf_op jit(solution)/shard_map/qkv/pallas_call | solution.py:342
  164.7 0.5 collective-permute-start.2
  165.2 0.6 fusion.4
  165.8 1.0 multiply_sine_fusion.1
  166.8 0.4 collective-permute-done.1.ko_ref
  167.2 1.1 collective-permute-done.2.vo_ref
  168.3 0.9 copy-done.1
  169.3 16.4 %attn.1 = (bf16[6,512,128]{2,1,0:T(8,128)(2,1)}, bf16[6,2,1024,512]{3,2,1,0:T(8,128)(2,1)}, f32[6,2,8,512]{3,2,1,0:T(8,128)}) custom-call(bf16[6,512,128]{2,1,0:T(8,128)(2,1)} %get-tuple-element.42.q_ref, bf16[6,512,128]{2,1,0:T(8,128)(2,1)} %get-tuple-element.43.k_ref, bf16[6,512,128]{2,1,0:T(8,128)(2,1)} %get-tuple-element.44.v_ref, ...), custom_call_target="tpu_custom_call" | custom-call | tf_op jit(solution)/shard_map/attn/pallas_call | solution.py:353
  185.6 18.1 %ffn.1 = (bf16[512,768]{1,0:T(8,128)(2,1)}, bf16[6,2,512,512]{3,2,1,0:T(8,128)(2,1)}, f32[512,768]{1,0:T(8,128)}, f32[512,128]{1,0:T(8,128)}, f32[512,768]{1,0:T(8,128)}, /*index=5*/f32[512,128]{1,0:T(8,128)}) custom-call(bf16[512,768]{1,0:T(8,128)(2,1)} %broadcast_select_fusion.2.x_ref, bf16[6,512,128]{2,1,0:T(8,128)(2,1)} %get-tuple-element.46.o_ref, ...), custom_call_target="tpu_custom_call" | custom-call | tf_op jit(solution)/shard_map/ffn/pallas_call | solution.py:364
  203.7 17.8 %ffn_back_light.1 = (f32[512,768]{1,0:T(8,128)}, bf16[512,768]{1,0:T(8,128)(2,1)}) custom-call(bf16[512,768]{1,0:T(8,128)(2,1)} %get-tuple-element.40.dy_ref, f32[512,768]{1,0:T(8,128)} %get-tuple-element.48.n1_ref, f32[512,128]{1,0:T(8,128)} %get-tuple-element.49.i1_ref, f32[512,768]{1,0:T(8,128)} %get-tuple-element.50.n2_ref, ...), custom_call_target="tpu_custom_call" | custom-call | tf_op jit(solution)/shard_map/ffn_back_light/pallas_call | solution.py:398
  221.5 20.3 %attn_back.1 = (bf16[6,512,128]{2,1,0:T(8,128)(2,1)}, f32[6,2,128,512]{3,2,1,0:T(8,128)}, bf16[6,2,128,512]{3,2,1,0:T(8,128)(2,1)}) custom-call(bf16[512,768]{1,0:T(8,128)(2,1)} %get-tuple-element.54.da_ref, bf16[4,4,192,3072]{3,2,1,0:T(8,128)(2,1)} %bitcast.47, bf16[6,512,128]{2,1,0:T(8,128)(2,1)} %get-tuple-element.46.o_ref, ...), custom_call_target="tpu_custom_call" | custom-call | tf_op jit(solution)/shard_map/attn_back/pallas_call | solution.py:428
  241.8 0.2 collective-permute-start.3
  242.0 3.5 collective-permute-done.3.refs_4_
  245.5 1.2 copy-done.4
  246.8 8.4 %joint_back.1 = (f32[512,768]{1,0:T(8,128)}, bf16[512,768]{1,0:T(8,128)(2,1)}) custom-call(bf16[4,4,192,3072]{3,2,1,0:T(8,128)(2,1)} %bitcast.48, f32[512,768]{1,0:T(8,128)} %get-tuple-element.53.refs_1_, bf16[6,512,128]{2,1,0:T(8,128)(2,1)} %get-tuple-element.57.refs_2_, f32[6,2,128,512]{3,2,1,0:T(8,128)} %get-tuple-element.58.refs_3_, ...), custom_call_target="tpu_custom_call" | custom-call | tf_op jit(solution)/shard_map/joint_back/pallas_call | solution.py:458
  255.1 1.3 collective-permute-start.4
  256.4 20.4 %collective-permute-done.4 = bf16[512,768]{1,0:T(8,128)(2,1)S(1)} collective-permute-done((bf16[512,768]{1,0:T(8,128)(2,1)}, bf16[512,768]{1,0:T(8,128)(2,1)S(1)}, u32[]{:S(2)}, u32[]{:S(2)}) %collective-permute-start.4) | collective-permute-done | bytes 786464 | tf_op jit(solution)/shard_map/ppermute | solution.py:1357
  276.8 1.0 broadcast_select_fusion.1.dy_ref
  277.8 25.1 %ffn_back.1 = (bf16[4,4,192,3072]{3,2,1,0:T(8,128)(2,1)}, f32[512,768]{1,0:T(8,128)}, bf16[512,768]{1,0:T(8,128)(2,1)}, f32[8,768]{1,0:T(8,128)}) custom-call(bf16[512,768]{1,0:T(8,128)(2,1)} %broadcast_select_fusion.1.dy_ref, f32[512,768]{1,0:T(8,128)} %get-tuple-element.48.n1_ref, f32[512,128]{1,0:T(8,128)} %get-tuple-element.49.i1_ref, ...), custom_call_target="tpu_custom_call" | custom-call | tf_op jit(solution)/shard_map/ffn_back/pallas_call | solution.py:398
  302.9 141.5 %last.1 = (f32[192,768]{1,0:T(8,128)}, f32[192,1536]{1,0:T(8,128)}, f32[768,192]{1,0:T(8,128)}, bf16[2,256,768]{2,1,0:T(8,128)(2,1)}, f32[8,768]{1,0:T(8,128)}) custom-call(bf16[512,768]{1,0:T(8,128)(2,1)} %get-tuple-element.61.da_ref, bf16[4,4,192,3072]{3,2,1,0:T(8,128)(2,1)} %bitcast.50, bf16[6,512,128]{2,1,0:T(8,128)(2,1)} %get-tuple-element.46.o_ref, ...), custom_call_target="tpu_custom_call" | custom-call | tf_op jit(solution)/shard_map/last/pallas_call | solution.py:821
  444.4 0.9 slice.76
  445.3 1.0 slice_bitcast_fusion
  446.3 0.9 slice.73
  447.2 1.0 slice.74
  448.2 0.7 slice.77
  449.3 0.8 copy.68
  450.5 1.1 copy.69
  451.6 1.1 copy.70
  452.6 1.8 broadcast_in_dim_reshape.4
  454.4 0.5 dynamic-slice_bitcast_fusion
  455.0 0.9 copy.72
  (55 shorter events, 1.5 us)
Async XLA Ops:
  1.8 1.4 copy-start.12
  1.8 1.4 copy-start.13
  1.8 1.4 copy-start.14
  3.0 1.3 copy-start.10
  3.0 1.6 copy-start.9
  6.9 1.4 copy-start.6
  135.3 22.0 %copy-start.2 = (bf16[512,768]{1,0:T(8,128)(2,1)S(1)}, bf16[512,768]{1,0:T(8,128)(2,1)}, u32[]{:S(2)}) copy-start(bf16[512,768]{1,0:T(8,128)(2,1)} %get-tuple-element.40.dy_ref) | copy-start | bytes 2359300
  135.3 21.9 %collective-permute-start = (bf16[512,768]{1,0:T(8,128)(2,1)}, bf16[512,768]{1,0:T(8,128)(2,1)S(1)}, u32[]{:S(2)}, u32[]{:S(2)}) collective-permute-start(bf16[512,768]{1,0:T(8,128)(2,1)} %get-tuple-element.41), channel_id=1, source_target_pairs={{0,16},{1,17},{2,18},{3,19},{4,20},{5,21},{6,22},{7,23},{8,24},{9,... | collective-permute-start | bytes 2359304 | tf_op jit(solution)/shard_map/ppermute | solution.py:1352
  158.2 7.0 %copy-start.11 = (f32[4,768]{1,0:T(4,128)S(1)}, f32[4,768]{1,0:T(4,128)}, u32[]{:S(2)}) copy-start(f32[4,768]{1,0:T(4,128)} %get-tuple-element.47) | copy-start | bytes 36868
  164.7 2.5 collective-permute-start.1
  164.7 3.6 collective-permute-start.2
  167.2 1.1 copy-start
  168.3 0.9 copy-start.1
  241.8 3.7 collective-permute-start.3
  245.5 1.2 copy-start.4
  246.8 30.1 %copy-start.3 = (bf16[512,768]{1,0:T(8,128)(2,1)S(1)}, bf16[512,768]{1,0:T(8,128)(2,1)}, u32[]{:S(2)}) copy-start(bf16[512,768]{1,0:T(8,128)(2,1)} %get-tuple-element.40.dy_ref) | copy-start | bytes 2359300
  255.1 21.7 %collective-permute-start.4 = (bf16[512,768]{1,0:T(8,128)(2,1)}, bf16[512,768]{1,0:T(8,128)(2,1)S(1)}, u32[]{:S(2)}, u32[]{:S(2)}) collective-permute-start(bf16[512,768]{1,0:T(8,128)(2,1)} %get-tuple-element.60), channel_id=1, source_target_pairs={{16,0},{17,1},{18,2},{19,3},{20,4},{21,5},{22,6},{23,7},{24,8},{25... | collective-permute-start | bytes 2359304 | tf_op jit(solution)/shard_map/ppermute | solution.py:1357
  450.3 1.3 copy-start.8
  450.5 2.2 copy-start.5
  451.6 3.4 copy-start.7

commit v6 on v5

--- a/solution.py
+++ b/solution.py
@@ -112,7 +112,7 @@
             o = jnp.concatenate([o_ref[3 * p + i] for i in range(3)], axis=1)
             r = r + dg(o, w, NT)
         n, inv = norm_parts(r)
-        n1_ref[...] = n
+        n1_ref[...] = n.astype(BF)
         i1_ref[...] = jnp.broadcast_to(inv, i1_ref.shape)
         h = n * g_ref[0:1] + b_ref[0:1]
         h_ref[...] = h
@@ -138,7 +138,7 @@
     @pl.when(z == pl.num_programs(0) - 1)
     def _():
         n, inv = norm_parts(acc_ref[...])
-        n2_ref[...] = n
+        n2_ref[...] = n.astype(BF)
         i2_ref[...] = jnp.broadcast_to(inv, i2_ref.shape)
         y_ref[...] = (n * g_ref[1:2] + b_ref[1:2]).astype(BF)
 
@@ -154,11 +154,11 @@
     @pl.when(z == 0)
     def _():
         dy = dy_ref[...].astype(F32)
-        n = n2_ref[...]
+        n = n2_ref[...].astype(F32)
         if grads:
             ng_ref[1:2] = jnp.sum(dy * n, axis=0, keepdims=True)
             ng_ref[3:4] = jnp.sum(dy, axis=0, keepdims=True)
-            hb_ref[...] = (n1_ref[...] * g_ref[0:1] + b_ref[0:1]).astype(BF)
+            hb_ref[...] = (n1_ref[...].astype(F32) * g_ref[0:1] + b_ref[0:1]).astype(BF)
         dr2 = norm_back(dy * g_ref[1:2], n, i2_ref[:, :1])
         acc_ref[...] = dr2
         df_ref[...] = dr2.astype(BF)
@@ -188,7 +188,7 @@
     @pl.when(z == pl.num_programs(0) - 1)
     def _():
         dh = acc_ref[...]
-        n = n1_ref[...]
+        n = n1_ref[...].astype(F32)
         if grads:
             ng_ref[0:1] = jnp.sum(dh * n, axis=0, keepdims=True)
             ng_ref[2:3] = jnp.sum(dh, axis=0, keepdims=True)
@@ -213,7 +213,7 @@
         zero = jnp.zeros_like(sb)
         padded = jnp.concatenate([sb, zero] if h == 0 else [zero, sb], axis=0)
         dp = dg(v, padded, NN)
-        et = e[h]
+        et = e[h][...]
         ds = (et.astype(F32) * (dp - inner)).astype(BF)
         dvs.append(dg(sb, et, NT))
         dks.append(dg(qt[span], ds, NT))
@@ -333,7 +333,6 @@
 
 def forward(x, weights, norms, mask, tabs):
     w = weights
-    gains, biases = norms
     rows, width = x.shape
     heads = width // 128
     blocks, tp, depth, columns = w.shape
@@ -349,6 +348,15 @@
         name="qkv",
     )(x, w, cos, sin)
     ko, vo = lax.ppermute((k, v), "core", [(0, 1), (1, 0)])
+    return attend(x, (q, k, v, ko, vo), w, norms, mask)
+
+
+def attend(x, joint, w, norms, mask):
+    gains, biases = norms
+    q, k, v, ko, vo = joint
+    rows, width = x.shape
+    heads = width // 128
+    blocks, tp, depth, columns = w.shape
     pair = lead((1, rows, 128))
     o, e, l = pl.pallas_call(
         attn_kernel,
@@ -373,7 +381,7 @@
             full((2, width)),
         ],
         out_specs=[full((rows, width)), lead((1, 2, rows, units))] + [full((rows, width)), full((rows, 128))] * 2,
-        out_shape=[sds((rows, width), BF), sds((groups, 2, rows, units), BF)] + [sds((rows, width), F32), sds((rows, 128), F32)] * 2,
+        out_shape=[sds((rows, width), BF), sds((groups, 2, rows, units), BF)] + [sds((rows, width), BF), sds((rows, 128), F32)] * 2,
         scratch_shapes=[VM((rows, width), F32), VM((rows, width), BF), VM((rows, width), F32)],
         compiler_params=BIG,
         name="ffn",
@@ -467,19 +475,25 @@
     )(*args, cost, sint)
 
 
+PAIRS = 6
+FIRST_PAIR = 6
+FIRST_JOINT = 12
+LAST_STEP = 13
+
+
 def last_kernel(
-    parts, da_ref, wo_ref, o_ref, q_ref, k_ref, v_ref, ko_ref, vo_ref, e_ref, l_ref, cos_ref, sin_ref,
-    x_ref, w_ref, dr1_ref, y_ref, g_ref, ng_ref,
+    parts, n1_ref, i1_ref, n2_ref, i2_ref, gu_ref, wa_ref, wb_ref, gain_ref, bias_ref,
+    o_ref, q_ref, k_ref, v_ref, ko_ref, vo_ref, l_ref, cos_ref, sin_ref, dy_hbm, x_hbm, y_hbm, e_hbm,
     first_out, pair_out, down_out, ends_out, norm_out,
-    do3, dwo, dq, keep, oth, got, dz, g1, e_send, e_land, tmp, own, land_c, land_y, land_r, land_l, land_n,
-    oth_send, oth_recv, end_sem, end_send, end_recv,
-    own_sem, cs_sem, cr_sem, ys_sem, yr_sem, rs_sem, rr_sem, ls_sem, lr_sem, ns_sem, nr_sem,
+    acc, df, hb, ring, do3, dwo, dq, keep, oth, got, eb, e_send, e_land, tmp, land_c, land_y, land_r, land_l, land_n,
+    dy_sem, x_sem, y_sem, e_sem, oth_send, oth_recv, end_sem, end_send, end_recv,
+    cs_sem, cr_sem, ys_sem, yr_sem, rs_sem, rr_sem, ls_sem, lr_sem, ns_sem, nr_sem,
 ):
     step = pl.program_id(0)
     section = lax.axis_index("section")
     y, c, z = lax.axis_index("y"), lax.axis_index("core"), lax.axis_index("tensor")
     last = 3
-    rows, width = da_ref.shape
+    rows, width = acc.shape
     early = parts - width // WIDE
     near, across = {"core": 1 - c}, {"y": 1 - y}
     right, left = {"tensor": jnp.minimum(z + 1, last)}, {"tensor": jnp.maximum(z - 1, 0)}
@@ -500,8 +514,8 @@
     def at_home(i):
         return jnp.logical_and(side == c, 2 * c + i == z)
 
-    def end_copy(i):
-        return remote(e_send.at[i], e_land.at[z % 2], end_send.at[i], end_recv.at[z % 2], target(i))
+    def end_copy(i, part):
+        return remote(e_send.at[i, part], e_land.at[z % 2, part], end_send.at[i], end_recv.at[z % 2], target(i))
 
     def end_home(i):
         return pltpu.make_async_copy(e_send.at[i], e_land.at[z % 2], end_sem)
@@ -509,21 +523,22 @@
     def oth_copy(p):
         return remote(oth.at[p], got.at[p], oth_send.at[p], oth_recv.at[p], near)
 
+    dy_copy = pltpu.make_async_copy(dy_hbm, e_send, dy_sem)
+    x_copy = pltpu.make_async_copy(x_hbm, hb, x_sem)
+    y_copy = pltpu.make_async_copy(y_hbm, e_send, y_sem)
+
+    def probs_copy(p):
+        return pltpu.make_async_copy(e_hbm.at[p], eb, e_sem)
+
     def columns(j):
         return pl.ds(pl.multiple_of(j * WIDE, WIDE), WIDE)
 
-    def late(j):
-        return columns(j - early)
-
-    def load(j):
-        return pltpu.make_async_copy(g_ref.at[:, c, :, :, columns(j + parts - early)], own.at[j % 4], own_sem.at[j])
-
-    def to_core(j, kept=False):
-        src = g1.at[:, 1 - c, :, :, late(j)] if kept else g_ref.at[:, 1 - c, :, :, columns(j + parts - early)]
-        return remote(src, land_c.at[j], cs_sem.at[j], cr_sem.at[j], near)
-
-    def from_core(j):
-        return remote(land_c.at[j], land_c.at[j], cs_sem.at[j], cr_sem.at[j], near)
+    def slot(j):
+        return (j // 3) % 2, columns(j % 3)
+
+    def to_core(j):
+        r, cols = slot(j)
+        return remote(ring.at[r, :, 1 - c, :, :, cols], land_c.at[j], cs_sem.at[j], cr_sem.at[j], near)
 
     def to_y(j):
         return remote(land_c.at[j, 1 - y], land_y.at[j], ys_sem.at[j], yr_sem.at[j], across)
@@ -537,34 +552,23 @@
     def go_left(j, count, src):
         return remote(src, land_l.at[j, pl.ds(0, count)], ls_sem.at[j], lr_sem.at[j], left)
 
-    def prepare(j):
-        @pl.when(j < early)
-        def _():
-            to_core(j).start()
-            load(j).start()
-
-        @pl.when(jnp.logical_and(j >= early, j < parts))
-        def _():
-            to_core(j, True).start()
-
     def stage(i, lag, body):
         @pl.when(jnp.logical_and(i >= lag, i - lag < parts))
         def _():
             body(i - lag)
 
-    def first_sum(j):
-        from_core(j).wait_recv()
-
-        @pl.when(j < early)
-        def _():
-            load(j).wait()
-            land_c[j] = land_c[j] + own[j % 4]
-
-        @pl.when(j >= early)
-        def _():
-            land_c[j] = land_c[j] + g1[:, c, :, :, late(j)]
-
-        to_y(j).start()
+    def add_cores(group):
+        def one(m, carry):
+            j = 3 * group + m
+            r, cols = slot(j)
+            to_core(j).wait()
+            land_c[j] = land_c[j] + ring[r, :, c, :, :, cols]
+            return carry
+
+        lax.fori_loop(0, 3, one, 0)
+
+    def send_cores(group):
+        lax.fori_loop(0, 3, lambda m, t: (to_core(3 * group + m).start(), t)[1], 0)
 
     def last_hop(j):
         @pl.when(z == 1)
@@ -631,7 +635,7 @@
 
         @pl.when(j >= early)
         def _():
-            first_out[:, late(j)] = tmp[...]
+            first_out[:, columns(j - early)] = tmp[...]
 
         for m in range(2):
 
@@ -644,15 +648,14 @@
             down_out[columns(group), :] = tmp[...].T
 
     def round_(i):
-        prepare(i + 2)
-        stage(i, 0, first_sum)
-        stage(i, 4, last_hop)
-        stage(i, 3, next_hop)
+        stage(i, 0, lambda j: to_y(j).start())
+        stage(i, 6, last_hop)
+        stage(i, 4, next_hop)
         stage(i, 2, first_hop)
-        stage(i, 5, result)
+        stage(i, 8, result)
         for k in range(4):
 
-            @pl.when(i == 3 * (k + 1))
+            @pl.when(i == 3 * k + 8)
             def _():
                 norm_copy(k).wait()
                 total = land_n[2 * k] + land_n[2 * k + 1]
@@ -664,6 +667,7 @@
 
     @pl.when(step == 0)
     def _():
+        dy_copy.start()
         greet(near)
         greet(across)
         greet(far)
@@ -684,27 +688,319 @@
 
         count = 5 + jnp.where(z < last, 1, 0) + jnp.where(z > 0, 1, 0) - jnp.where(side == c, 1, 0)
         pl.semaphore_wait(barrier, count)
-        prepare(0)
-        prepare(1)
-        land_n[0] = ng_ref[...]
+        dy_copy.wait()
+        dy = e_send[...].reshape(rows, width).astype(F32)
+        n = n2_ref[...].astype(F32)
+        land_n[0] = jnp.zeros(land_n.shape[1:], F32)
+        land_n[0, 1:2] = jnp.sum(dy * n, axis=0, keepdims=True)
+        land_n[0, 3:4] = jnp.sum(dy, axis=0, keepdims=True)
+        dr2 = norm_back(dy * gain_ref[1:2], n, i2_ref[:, :1])
+        acc[...] = dr2
+        df[...] = dr2.astype(BF)
+        hb[...] = (n1_ref[...].astype(F32) * gain_ref[0:1] + bias_ref[0:1]).astype(BF)
+
+    @pl.when(step < FIRST_PAIR)
+    def _():
+        gate = gu_ref[0, 0].astype(F32)
+        up = gu_ref[0, 1].astype(F32)
+        s = 1.0 / (1.0 + jnp.exp(-gate))
+        silu = gate * s
+        wg, wu, wd = unit_weights(lambda t, m: wa_ref[:, t, :, 128 * m : 128 * m + 128].reshape(width, 128))
+        place = step % 2
+
+        def put(m, grad):
+            for t in range(4):
+                ring[place, :, :, t, :, 128 * m : 128 * m + 128] = (
+                    grad[:, 128 * t : 128 * t + 128].astype(BF).reshape(2, 2, -1, 128)
+                )
+
+        put(2, dg(df[...], (silu * up).astype(BF), TN))
+        d_act = dg(df[...], wd, NN)
+        d_gate = (d_act * up * (s * (1.0 + gate * (1.0 - s)))).astype(BF)
+        d_up = (d_act * silu).astype(BF)
+        put(0, dg(hb[...], d_gate, TN))
+        put(1, dg(hb[...], d_up, TN))
+        send_cores(step)
+        acc[...] += dg(d_gate, wg, NT) + dg(d_up, wu, NT)
+
+    @pl.when(step == FIRST_PAIR - 1)
+    def _():
+        dh = acc[...]
+        n = n1_ref[...].astype(F32)
+        land_n[0, 0:1] = jnp.sum(dh * n, axis=0, keepdims=True)
+        land_n[0, 2:3] = jnp.sum(dh, axis=0, keepdims=True)
+        dr1 = norm_back(dh * gain_ref[0:1], n, i1_ref[:, :1])
+        acc[...] = dr1
+        df[...] = dr1.astype(BF)
+        x_copy.start()
+        probs_copy(0).start()
         norm_copy(0).start()
 
-    cos, sin = cos_ref[...], sin_ref[...]
-
-    @pl.when(jnp.logical_and(step < 6, step % 3 == 0))
-    def _():
-        w = jnp.concatenate(out_weight(wo_ref), axis=1)
+    cos, sin = cos_ref[:, pl.ds(c * rows, rows)], sin_ref[:, pl.ds(c * rows, rows)]
+    in_pairs = jnp.logical_and(step >= FIRST_PAIR, step < FIRST_JOINT)
+    p = step - FIRST_PAIR
+
+    @pl.when(jnp.logical_and(in_pairs, p % 3 == 0))
+    def _():
+        w = jnp.concatenate(out_weight(wb_ref.at[:, pl.ds(2 * (p // 3), 2), :, 128:384]), axis=1)
+        t = dg(df[...], w, NN).astype(BF)
+        for i in range(3):
+            do3[i] = t[:, 128 * i : 128 * i + 128]
+        o3 = jnp.concatenate([o_ref[p + i] for i in range(3)], axis=1)
+        dwo[p // 3] = dg(df[...], o3, TN).astype(BF)
+
+    @pl.when(in_pairs)
+    def _():
+        probs_copy(p).wait()
+        dqt, dk, dv = pair_back(
+            do3[p % 3], o_ref[p], q_ref[0], k_ref[0], v_ref[0], ko_ref[0], vo_ref[0],
+            [eb.at[h] for h in range(2)], [l_ref[0, h, 0:1] for h in range(2)], cos, sin,
+        )
+        dq[p] = dqt.T.astype(BF)
+        keep[p, 0] = dk[:, :rows].astype(BF)
+        keep[p, 1] = dv[:, :rows].astype(BF)
+        oth[p, 0] = dk[:, rows:].astype(BF)
+        oth[p, 1] = dv[:, rows:].astype(BF)
+        oth_copy(p).start()
+
+        @pl.when(p + 1 < PAIRS)
+        def _():
+            probs_copy(p + 1).start()
+
+    @pl.when(step >= FIRST_JOINT)
+    def _():
+        half = step - FIRST_JOINT
+
+        @pl.when(half == 0)
+        def _():
+            x_copy.wait()
+
+        for i in range(3):
+            oth_copy(3 * half + i).wait()
+        d = joint_parts(
+            [dq[3 * half + i].astype(F32) for i in range(3)],
+            [keep[3 * half + i, 0].astype(F32) + got[3 * half + i, 0].astype(F32) for i in range(3)],
+            [keep[3 * half + i, 1].astype(F32) + got[3 * half + i, 1].astype(F32) for i in range(3)],
+            cos, sin,
+        )
+        total = None
+        wlow = low_lanes((width, 128))
+        mid = dwo[half, :, 128:256].astype(F32)
+        sides = [dwo[half, :, 0:128], dwo[half, :, 256:384]]
+        mids = [swap64(mid), mid]
+        shape = (2, 2, width // 4)
+        for e in range(2):
+            t = 2 * half + e
+            w = jnp.concatenate([wa_ref[:, t].reshape(width, GROUP), wb_ref[:, t, :, :256].reshape(width, 256)], axis=1)
+            part = dg(d[e], w, NT)
+            total = part if total is None else total + part
+            g = dg(hb[...], d[e], TN)
+            ring[0, :, :, t] = g[:, :GROUP].astype(BF).reshape(shape + (GROUP,))
+            ring[1, :, :, t, :, :128] = g[:, GROUP:512].astype(BF).reshape(shape + (128,))
+            ring[1, :, :, t, :, 128:256] = jnp.where(wlow, g[:, 512:], mids[e]).astype(BF).reshape(shape + (128,))
+            ring[1, :, :, t, :, 256:] = sides[e].reshape(shape + (128,))
+        acc[...] += total
+
+    @pl.when(step == LAST_STEP)
+    def _():
+        for k in range(2):
+            send_cores(early // 3 + k)
+
+        @pl.when(section == 0)
+        def _():
+            e_send[...] = acc[...].astype(BF).reshape(e_send.shape)
+
+        @pl.when(section == 1)
+        def _():
+            y_copy.start()
+            y_copy.wait()
+
+        for i in range(2):
+
+            @pl.when(at_home(i))
+            def _():
+                end_home(i).start()
+
+    @pl.when(step < FIRST_PAIR)
+    def _():
+        add_cores(step)
+
+    @pl.when(step == 0)
+    def _():
+        round_(0)
+
+    round_(step + 1)
+
+    @pl.when(step == LAST_STEP)
+    def _():
+        for k in range(2):
+            add_cores(early // 3 + k)
+        end_rows = e_send.shape[1] // 8
+
+        def late(i, carry):
+            part = pl.ds(pl.multiple_of((i - LAST_STEP - 2) * end_rows, end_rows), end_rows)
+            for k in range(2):
+
+                @pl.when(jnp.logical_not(at_home(k)))
+                def _():
+                    end_copy(k, part).start()
+
+            round_(i)
+            return carry
+
+        lax.fori_loop(LAST_STEP + 2, LAST_STEP + 10, late, 0)
+        lax.fori_loop(LAST_STEP + 10, parts + 8, lambda i, t: (round_(i), t)[1], 0)
+        for i in range(2):
+
+            @pl.when(at_home(i))
+            def _():
+                end_home(i).wait()
+
+            @pl.when(jnp.logical_not(at_home(i)))
+            def _():
+                end_copy(i, pl.ds(0, e_send.shape[1])).wait_send()
+                remote(e_send.at[i], e_land.at[i], end_send.at[i], end_recv.at[i], target(i)).wait_recv()
+
+        ends_out[...] = e_land[...]
+
+        def finish(j, carry):
+            to_y(j).wait_send()
+
+            @pl.when(z == 0)
+            def _():
+                go_right(j, 1, land_c.at[j, y, pl.ds(1, 3)]).wait_send()
+
+            @pl.when(z == 1)
+            def _():
+                go_right(j, 2, land_r.at[j, pl.ds(1, 2)]).wait_send()
+                go_left(j, 1, land_l.at[j, pl.ds(0, 1)]).wait_send()
+
+            @pl.when(z == 2)
+            def _():
+                go_right(j, 3, land_r.at[j, pl.ds(2, 1)]).wait_send()
+                go_left(j, 2, land_l.at[j, pl.ds(0, 2)]).wait_send()
+
+            @pl.when(z == last)
+            def _():
+                go_left(j, 3, land_c.at[j, y, pl.ds(0, 3)]).wait_send()
+
+            return carry
+
+        lax.fori_loop(0, parts, finish, 0)
+
+
+def last_back(x, y, dy, kept, w, norms, cost, sint):
+    q, k, v, ko, vo, o, e, l, gu, n1, i1, n2, i2 = kept
+    gains, biases = norms
+    rows, width = x.shape
+    heads = width // 128
+    depth, columns = w.shape[2:]
+    parts = columns // WIDE
+    units = (columns - width) // 3
+    dma = pltpu.SemaphoreType.DMA
+    hbm = pl.BlockSpec(memory_space=pl.ANY)
+    halves = (2, rows // 2, width)
+
+    def once(shape, at=None):
+        return pl.BlockSpec(shape, lambda i: at or (0,) * len(shape), pipeline_mode=pl.Buffered(1))
+
+    def by_pair(shape):
+        return pl.BlockSpec(shape, lambda i: (jnp.clip(i - FIRST_PAIR, 0, PAIRS - 1),) + (0,) * (len(shape) - 1))
+
+    pair = by_pair((1, rows, 128))
+    group = (4, 4, depth, GROUP)
+    return pl.pallas_call(
+        functools.partial(last_kernel, parts),
+        grid=(LAST_STEP + 1,),
+        in_specs=[
+            once((rows, width)), once((rows, 128)), once((rows, width)), once((rows, 128)),
+            pl.BlockSpec((1, 2, rows, 512), lambda i: (jnp.minimum(i, FIRST_PAIR - 1), 0, 0, 0)),
+            pl.BlockSpec(group, lambda i: (0, 0, 0, jnp.where(i < FIRST_PAIR, 2 + i, 0))),
+            once(group, (0, 0, 0, 1)),
+            once((2, width)), once((2, width)),
+            once((heads, rows, 128)),
+            pair, pair, pair, pair, pair,
+            by_pair((1, 2, 8, rows)),
+            once(cost.shape), once(sint.shape),
+            hbm, hbm, hbm, hbm,
+        ],
+        out_specs=[once((depth, width)), once((depth, 2 * units)), once((units, depth)), once(halves), once((8, width))],
+        out_shape=[
+            sds((depth, width), F32), sds((depth, 2 * units), F32), sds((units, depth), F32),
+            sds(halves, BF), sds((8, width), F32),
+        ],
+        scratch_shapes=[
+            VM((rows, width), F32),
+            VM((rows, width), BF),
+            VM((rows, width), BF),
+            VM((2, 2, 2, 4, depth, GROUP), BF),
+            VM((3, rows, 128), BF),
+            VM((2, width, 384), BF),
+            VM((heads, rows, 128), BF),
+            VM((heads, 2, 128, rows), BF),
+            VM((heads, 2, 128, rows), BF),
+            VM((heads, 2, 128, rows), BF),
+            VM((2, 2 * rows, rows), BF),
+            VM(halves, BF),
+            VM(halves, BF),
+            VM((depth, WIDE), F32),
+            VM((parts, 2, 4, depth, WIDE), BF),
+            VM((parts, 4, depth, WIDE), BF),
+            VM((parts, 3, depth, WIDE), BF),
+            VM((parts, 3, depth, WIDE), BF),
+            VM((8, 8, width), F32),
+            dma, dma, dma, dma,
+            dma((6,)), dma((6,)), dma, dma((2,)), dma((2,)),
+        ]
+        + [dma((parts,))] * 8
+        + [dma((4,))] * 2,
+        compiler_params=pltpu.CompilerParams(collective_id=0, has_side_effects=True, vmem_limit_bytes=63 << 20),
+        name="last",
+    )(n1, i1, n2, i2, gu, w, w, gains, biases, o, q, k, v, ko, vo, l, cost, sint, dy.reshape(halves), x, y.reshape(halves), e)
+
+
+def mid_kernel(
+    da_ref, dr1_ref, w_ref, o_ref, q_ref, k_ref, v_ref, ko_ref, vo_ref, e_ref, l_ref, cos_ref, sin_ref, top_ref,
+    dy_out,
+    do3, dq, keep, oth, got, d, send, land,
+    oth_send, oth_recv, row_send, row_recv,
+):
+    step = pl.program_id(0)
+    section, c = lax.axis_index("section"), lax.axis_index("core")
+    rows, width = da_ref.shape
+    pieces = send.shape[0]
+    near, other = {"core": 1 - c}, {"section": 1 - section}
+
+    def remote(src, dst, send, recv, device):
+        return pltpu.make_async_remote_copy(src, dst, send, recv, device_id=device, device_id_type=MESH)
+
+    def oth_copy(p):
+        return remote(oth.at[p], got.at[p], oth_send.at[p], oth_recv.at[p], near)
+
+    def row_copy(b):
+        return remote(send.at[b], land.at[b], row_send.at[b], row_recv.at[b], other)
+
+    @pl.when(step == 0)
+    def _():
+        barrier = pltpu.get_barrier_semaphore()
+        for device in (near, other):
+            pl.semaphore_signal(barrier, inc=1, device_id=device, device_id_type=MESH)
+        pl.semaphore_wait(barrier, 2)
+
+    cos, sin = cos_ref[:, pl.ds(c * rows, rows)], sin_ref[:, pl.ds(c * rows, rows)]
+
+    @pl.when(jnp.logical_and(step < PAIRS, step % 3 == 0))
+    def _():
+        w = jnp.concatenate(out_weight(w_ref.at[:, pl.ds(2 * (step // 3), 2), :, 512:768]), axis=1)
         t = dg(da_ref[...], w, NN).astype(BF)
         for i in range(3):
             do3[i] = t[:, 128 * i : 128 * i + 128]
-        o3 = jnp.concatenate([o_ref[step + i] for i in range(3)], axis=1)
-        dwo[step // 3] = dg(da_ref[...], o3, TN).astype(BF)
-
-    @pl.when(step < 6)
+
+    @pl.when(step < PAIRS)
     def _():
         dqt, dk, dv = pair_back(
             do3[step % 3], o_ref[step], q_ref[0], k_ref[0], v_ref[0], ko_ref[0], vo_ref[0],
-            [e_ref[0, h] for h in range(2)], [l_ref[0, h, 0:1] for h in range(2)], cos, sin,
+            [e_ref.at[0, h] for h in range(2)], [l_ref[0, h, 0:1] for h in range(2)], cos, sin,
         )
         dq[step] = dqt.T.astype(BF)
         keep[step, 0] = dk[:, :rows]
@@ -713,160 +1009,93 @@
         oth[step, 1] = dv[:, rows:].astype(BF)
         oth_copy(step).start()
 
-    @pl.when(step >= 6)
-    def _():
-        p = step - 6
+    def joint(half):
         for i in range(3):
-            oth_copy(3 * p + i).wait()
-        d = joint_parts(
-            [dq[3 * p + i].astype(F32) for i in range(3)],
-            [keep[3 * p + i, 0] + got[3 * p + i, 0].astype(F32) for i in range(3)],
-            [keep[3 * p + i, 1] + got[3 * p + i, 1].astype(F32) for i in range(3)],
+            oth_copy(3 * half + i).wait()
+        parts = joint_parts(
+            [dq[3 * half + i].astype(F32) for i in range(3)],
+            [keep[3 * half + i, 0] + got[3 * half + i, 0].astype(F32) for i in range(3)],
+            [keep[3 * half + i, 1] + got[3 * half + i, 1].astype(F32) for i in range(3)],
             cos, sin,
         )
-        acc = None
-        wlow = low_lanes((width, 128))
-        mid = dwo[p, :, 128:256].astype(F32)
-        sides = [dwo[p, :, 0:128], dwo[p, :, 256:384]]
-        mids = [swap64(mid), mid]
         for e in range(2):
-            t = dg(d[e], w_ref[:, e, :, :640].reshape(width, 640), NT)
-            acc = t if acc is None else acc + t
-            g = dg(x_ref[...], d[e], TN)
-            shape = (2, 2, width // 4)
-            g1[:, :, 2 * p + e, :, :512] = g[:, :512].astype(BF).reshape(shape + (512,))
-            g1[:, :, 2 * p + e, :, 512:640] = jnp.where(wlow, g[:, 512:], mids[e]).astype(BF).reshape(shape + (128,))
-            g1[:, :, 2 * p + e, :, 640:] = sides[e].reshape(shape + (128,))
-
-        @pl.when(p == 0)
-        def _():
-            dz[...] = dr1_ref[...] + acc
-
-        @pl.when(p > 0)
-        def _():
-            value = jnp.where(section == 0, (dz[...] + acc).astype(BF), y_ref[...])
-            e_send[...] = value.reshape(e_send.shape)
-            for i in range(2):
-
-                @pl.when(at_home(i))
-                def _():
-                    end_home(i).start()
-
-                @pl.when(jnp.logical_not(at_home(i)))
-                def _():
-                    end_copy(i).start()
-
-    round_(step)
-
-    @pl.when(step == 7)
-    def _():
-        lax.fori_loop(8, parts + 5, lambda i, t: (round_(i), t)[1], 0)
-        for i in range(2):
-
-            @pl.when(at_home(i))
+            d[2 * half + e] = parts[e]
+
+    @pl.when(step == PAIRS - 1)
+    def _():
+        joint(0)
+
+    @pl.when(step == PAIRS)
+    def _():
+        joint(1)
+
+        def rows_of(b, carry):
+            part = pl.ds(pl.multiple_of(b * (rows // pieces), rows // pieces), rows // pieces)
+            total = dr1_ref[part]
+            for t in range(4):
+                total += dg(d[t, part], w_ref[:, t, :, :640].reshape(width, 640), NT)
+            send[b] = total.astype(BF)
+
+            @pl.when(section == 1)
             def _():
-                end_home(i).wait()
-
-            @pl.when(jnp.logical_not(at_home(i)))
-            def _():
-                end_copy(i).wait_send()
-                remote(e_send.at[i], e_land.at[i], end_send.at[i], end_recv.at[i], target(i)).wait_recv()
-
-        ends_out[...] = e_land[...]
-
-        def finish(j, carry):
-            from_core(j).wait_send()
-            to_y(j).wait_send()
-
-            @pl.when(z == 0)
-            def _():
-                go_right(j, 1, land_c.at[j, y, pl.ds(1, 3)]).wait_send()
-
-            @pl.when(z == 1)
-            def _():
-                go_right(j, 2, land_r.at[j, pl.ds(1, 2)]).wait_send()
-                go_left(j, 1, land_l.at[j, pl.ds(0, 1)]).wait_send()
-
-            @pl.when(z == 2)
-            def _():
-                go_right(j, 3, land_r.at[j, pl.ds(2, 1)]).wait_send()
-                go_left(j, 2, land_l.at[j, pl.ds(0, 2)]).wait_send()
-
-            @pl.when(z == last)
-            def _():
-                go_left(j, 3, land_c.at[j, y, pl.ds(0, 3)]).wait_send()
+                row_copy(b).start()
 
             return carry
 
-        lax.fori_loop(0, parts, finish, 0)
-
-
-def last_back(x, y, da, dr1, g, ng, kept, w, tabs):
+        lax.fori_loop(0, pieces, rows_of, 0)
+
+        @pl.when(section == 1)
+        def _():
+            lax.fori_loop(0, pieces, lambda b, t: (row_copy(b).wait_send(), t)[1], 0)
+            dy_out[...] = top_ref[...]
+
+        @pl.when(section == 0)
+        def _():
+            lax.fori_loop(0, pieces, lambda b, t: (row_copy(b).wait_recv(), t)[1], 0)
+            dy_out[...] = land[...].reshape(rows, width)
+
+
+def mid_back(top, da, dr1, kept, w, cost, sint):
     q, k, v, ko, vo, o, e, l = kept[:8]
-    rows, width = x.shape
+    rows, width = da.shape
     heads = width // 128
-    depth, columns = w.shape[2:]
-    parts = columns // WIDE
-    units = (columns - width) // 3
-    cos, sin, cost, sint = tabs
+    depth = w.shape[2]
+    pieces = 4
     dma = pltpu.SemaphoreType.DMA
 
     def once(shape):
         return pl.BlockSpec(shape, lambda i: (0,) * len(shape), pipeline_mode=pl.Buffered(1))
 
     def by_pair(shape):
-        return pl.BlockSpec(shape, lambda i: (jnp.minimum(i, 5),) + (0,) * (len(shape) - 1))
+        return pl.BlockSpec(shape, lambda i: (jnp.minimum(i, PAIRS - 1),) + (0,) * (len(shape) - 1))
 
     pair = by_pair((1, rows, 128))
     return pl.pallas_call(
-        functools.partial(last_kernel, parts),
-        grid=(8,),
+        mid_kernel,
+        grid=(PAIRS + 1,),
         in_specs=[
-            once((rows, width)),
-            pl.BlockSpec((4, 2, depth, 256), lambda i: (0, jnp.minimum(i // 3, 1), 0, 2), pipeline_mode=pl.Buffered(1)),
-            once((heads, rows, 128)),
+            once((rows, width)), once((rows, width)), once((4, 4, depth, width)), once((heads, rows, 128)),
             pair, pair, pair, pair, pair,
             by_pair((1, 2, 2 * rows, rows)),
             by_pair((1, 2, 8, rows)),
-            once((HD // 2, rows)), once((HD // 2, rows)),
-            once((rows, width)),
-            pl.BlockSpec((4, 2, depth, 768), lambda i: (0, jnp.maximum(i - 6, 0), 0, 0), pipeline_mode=pl.Buffered(1)),
-            once((rows, width)), once((rows, width)),
-            pl.BlockSpec(memory_space=pl.ANY),
-            once(ng.shape),
+            once(cost.shape), once(sint.shape), once((rows, width)),
         ],
-        out_specs=[
-            once((depth, width)), once((depth, 2 * units)), once((units, depth)), once((2, rows // 2, width)), once(ng.shape),
-        ],
-        out_shape=[
-            sds((depth, width), F32), sds((depth, 2 * units), F32), sds((units, depth), F32),
-            sds((2, rows // 2, width), BF), sds(ng.shape, F32),
-        ],
+        out_specs=once((rows, width)),
+        out_shape=sds((rows, width), BF),
         scratch_shapes=[
             VM((3, rows, 128), BF),
-            VM((2, width, 384), BF),
             VM((heads, rows, 128), BF),
             VM((heads, 2, 128, rows), F32),
             VM((heads, 2, 128, rows), BF),
             VM((heads, 2, 128, rows), BF),
-            VM((rows, width), F32),
-            VM((2, 2, 4, depth, width), BF),
-            VM((2, rows // 2, width), BF),
-            VM((2, rows // 2, width), BF),
-            VM((depth, WIDE), F32),
-            VM((4, 2, 4, depth, WIDE), BF),
-            VM((parts, 2, 4, depth, WIDE), BF),
-            VM((parts, 4, depth, WIDE), BF),
-            VM((parts, 3, depth, WIDE), BF),
-            VM((parts, 3, depth, WIDE), BF),
-            VM((8,) + ng.shape, F32),
-            dma((6,)), dma((6,)), dma, dma((2,)), dma((2,)),
-        ]
-        + [dma((parts,))] * 9
-        + [dma((4,))] * 2,
-        compiler_params=pltpu.CompilerParams(collective_id=0, has_side_effects=True, vmem_limit_bytes=62 << 20),
-        name="last",
-    )(da, w, o, q, k, v, ko, vo, e, l, cost, sint, x, w, dr1, y, g.reshape(2, 2, 4, depth, columns), ng)
+            VM((4, rows, 640), BF),
+            VM((pieces, rows // pieces, width), BF),
+            VM((pieces, rows // pieces, width), BF),
+            dma((PAIRS,)), dma((PAIRS,)), dma((pieces,)), dma((pieces,)),
+        ],
+        compiler_params=pltpu.CompilerParams(collective_id=2, has_side_effects=True, vmem_limit_bytes=58 << 20),
+        name="mid",
+    )(da, dr1, w, o, q, k, v, ko, vo, e, l, cost, sint, top)
 
 
 LAG = 6
@@ -874,15 +1103,16 @@
 
 def first_kernel(
     parts, tok_ref, shard_ref, extra_ref, len_ref, cos_ref, sin_ref,
-    w_out, y_out, x_out, mask_out, norm_out,
-    w, xin, q, kv, land_kv, o, h1, hb, acc, ext, lens,
-    tok_sem, tok_send, tok_recv, shard_sem, back_sem, kv_send, kv_recv,
+    w_out, q_out, k_out, v_out, ko_out, vo_out, x_out, top_out, mask_out, norm_out,
+    w, xin, q, kv, land_kv, late_kv, o, hb, acc, relay, land_rows, ext, lens,
+    tok_sem, tok_send, tok_recv, shard_sem, back_sem, kv_send, kv_recv, out_sem, row_send, row_recv,
     small_send, small_recv, rs_sem, rr_sem, ls_sem, lr_sem, ys_sem, yr_sem, cs_sem, cr_sem,
 ):
+    section = lax.axis_index("section")
     y, c, z = lax.axis_index("y"), lax.axis_index("core"), lax.axis_index("tensor")
     last = 3
     rows, width = xin.shape[0] * xin.shape[1], xin.shape[2]
-    near, across = {"core": 1 - c}, {"y": 1 - y}
+    near, across, other = {"core": 1 - c}, {"y": 1 - y}, {"section": 1 - section}
     right, left = {"tensor": jnp.minimum(z + 1, last)}, {"tensor": jnp.maximum(z - 1, 0)}
     side = z // 2
     barrier = pltpu.get_barrier_semaphore()
@@ -909,6 +1139,7 @@
     load.start()
     greet(near)
     greet(across)
+    greet(other)
 
     @pl.when(z < last)
     def _():
@@ -924,7 +1155,7 @@
         def _():
             greet(target(i))
 
-    count = 4 + jnp.where(z < last, 1, 0) + jnp.where(z > 0, 1, 0) - jnp.where(side == c, 1, 0)
+    count = 5 + jnp.where(z < last, 1, 0) + jnp.where(z > 0, 1, 0) - jnp.where(side == c, 1, 0)
     pl.semaphore_wait(barrier, count)
 
     ext[y, c] = extra_ref[...]
@@ -1078,21 +1309,27 @@
             token_copy(i, pl.ds(0, xin.shape[1])).wait_send()
             remote(tok_ref.at[i], xin.at[i], tok_send.at[i], tok_recv.at[i], target(i)).wait_recv()
 
+    def project(at, count, x):
+        here = pl.ds(at, count)
+        cos, sin = cos_ref[pl.ds(c * rows + at, count)], sin_ref[pl.ds(c * rows + at, count)]
+        low = low_lanes((count, 128))
+        for p in range(2):
+            r = [dg(x, w[:, :, 2 * p + e, :, :640].reshape(width, 640), NN) for e in range(2)]
+            t = [[v[:, 128 * i : 128 * i + 128] for i in range(5)] for v in r]
+            qs = [t[0][0], jnp.where(low, t[0][3], swap64(t[1][3])), t[1][0]]
+            ks = [t[0][1], jnp.where(low, swap64(t[0][3]), t[1][3]), t[1][1]]
+            vs = [t[0][2], jnp.where(low, t[0][4], swap64(t[1][4])), t[1][2]]
+            for i in range(3):
+                q[3 * p + i, here] = (rope_fwd(qs[i], cos, sin) * HD**-0.5).astype(BF)
+                kv[0, 3 * p + i, here] = rope_fwd(ks[i], cos, sin).astype(BF)
+                kv[1, 3 * p + i, here] = vs[i].astype(BF)
+
     x = xin[...].reshape(rows, width)
     x_out[...] = x
-    cos, sin = cos_ref[pl.ds(c * rows, rows)], sin_ref[pl.ds(c * rows, rows)]
+    top_out[...] = x
+    project(0, rows, x)
     low = low_lanes((rows, 128))
-    for p in range(2):
-        r = [dg(x, w[:, :, 2 * p + e, :, :640].reshape(width, 640), NN) for e in range(2)]
-        t = [[v[:, 128 * i : 128 * i + 128] for i in range(5)] for v in r]
-        qs = [t[0][0], jnp.where(low, t[0][3], swap64(t[1][3])), t[1][0]]
-        ks = [t[0][1], jnp.where(low, swap64(t[0][3]), t[1][3]), t[1][1]]
-        vs = [t[0][2], jnp.where(low, t[0][4], swap64(t[1][4])), t[1][2]]
-        for i in range(3):
-            q[3 * p + i] = (rope_fwd(qs[i], cos, sin) * HD**-0.5).astype(BF)
-            kv[0, 3 * p + i] = rope_fwd(ks[i], cos, sin).astype(BF)
-            kv[1, 3 * p + i] = vs[i].astype(BF)
-    share = remote(kv, land_kv, kv_send, kv_recv, near)
+    share = remote(kv, land_kv, kv_send.at[0], kv_recv.at[0], near)
     share.start()
     rounds(start, start + 1)
     share.wait()
@@ -1145,8 +1382,47 @@
         return carry
 
     lax.fori_loop(0, 6, units, 0)
-    n, inv = norm_parts(acc[...])
-    y_out[...] = (n * norm_out[1:2] + norm_out[3:4]).astype(BF)
+    pieces = relay.shape[0]
+    piece_rows = rows // pieces
+
+    def row_copy(b):
+        return remote(relay.at[b], land_rows.at[b], row_send.at[b], row_recv.at[b], other)
+
+    def keep(arrays):
+        outs = (q_out, k_out, v_out, ko_out, vo_out)
+        copies = [pltpu.make_async_copy(t, out, out_sem.at[i]) for i, (t, out) in enumerate(zip(arrays, outs))]
+        for t in copies:
+            t.start()
+        for t in copies:
+            t.wait()
+
+    @pl.when(section == 0)
+    def _():
+        def send_rows(b, carry):
+            part = pl.ds(pl.multiple_of(b * piece_rows, piece_rows), piece_rows)
+            n, inv = norm_parts(acc[part])
+            relay[b] = (n * norm_out[1:2] + norm_out[3:4]).astype(BF)
+            row_copy(b).start()
+            return carry
+
+        lax.fori_loop(0, pieces, send_rows, 0)
+        keep((q, kv.at[0], kv.at[1], land_kv.at[0], land_kv.at[1]))
+        lax.fori_loop(0, pieces, lambda b, t: (row_copy(b).wait_send(), t)[1], 0)
+
+    @pl.when(section == 1)
+    def _():
+        def project_rows(b, carry):
+            at = pl.multiple_of(b * piece_rows, piece_rows)
+            row_copy(b).wait_recv()
+            x_out[pl.ds(at, piece_rows)] = land_rows[b]
+            project(at, piece_rows, land_rows[b])
+            return carry
+
+        lax.fori_loop(0, pieces, project_rows, 0)
+        again = remote(kv, late_kv, kv_send.at[1], kv_recv.at[1], near)
+        again.start()
+        again.wait()
+        keep((q, kv.at[0], kv.at[1], late_kv.at[0], late_kv.at[1]))
 
     def finish(j, carry):
         write_back(j).wait()
@@ -1179,9 +1455,10 @@
     return pl.pallas_call(
         functools.partial(first_kernel, parts),
         in_specs=[hbm, hbm, vm, vm, vm, vm],
-        out_specs=[hbm, vm, vm, vm, vm],
-        out_shape=[
-            sds((2, 2, 4, depth, columns), BF),
+        out_specs=[hbm] * 6 + [vm] * 4,
+        out_shape=[sds((2, 2, 4, depth, columns), BF)]
+        + [sds((heads, rows, 128), BF)] * 5
+        + [
             sds((rows, width), BF),
             sds((rows, width), BF),
             sds((2 * rows, rows), F32),
@@ -1193,13 +1470,15 @@
             VM((heads, rows, 128), BF),
             VM((2, heads, rows, 128), BF),
             VM((2, heads, rows, 128), BF),
+            VM((2, heads, rows, 128), BF),
             VM((heads, rows, 128), BF),
-            VM((8, 128), F32),
             VM((rows, width), BF),
             VM((rows, width), F32),
+            VM((4, rows // 4, width), BF),
+            VM((4, rows // 4, width), BF),
             VM((2, 2) + extra.shape, BF),
             VM((2,) + lengths.shape, jnp.int32),
-            dma, dma((2,)), dma((2,)), dma, dma((parts,)), dma, dma,
+            dma, dma((2,)), dma((2,)), dma, dma((parts,)), dma((2,)), dma((2,)), dma((5,)), dma((4,)), dma((4,)),
             dma((3,)), dma((3,)),
             dma((parts, 3)), dma((parts, 3)), dma((parts, 3)), dma((parts, 3)),
             dma((parts,)), dma((parts,)), dma((parts,)), dma((parts,)),
@@ -1289,7 +1568,7 @@
     freqs = np.float32(1000.0) ** (-np.arange(halfway, dtype=np.float32) / np.float32(halfway))
     angles = np.arange(length, dtype=np.float32)[:, None] * freqs[None, :]
     cos, sin = np.cos(angles), np.sin(angles)
-    return np.concatenate([cos] * 4, axis=1), np.concatenate([-sin, sin] * 2, axis=1)
+    return np.concatenate([cos] * 4, axis=1), np.concatenate([-sin, sin] * 2, axis=1), cos.T.copy(), sin.T.copy()
 
 
 BLOCKS = 4
@@ -1318,20 +1597,25 @@
     length = own * tp
     rows = length // 2
     shard = pack_shard(w_qkv[0], w_out[0], w_gate_up[0], w_down[0])
-    near = core * rows + jnp.arange(rows, dtype=jnp.int32)
-    far = (1 - core) * rows + jnp.arange(rows, dtype=jnp.int32)
-    tabs = rope_tables(near)
     if dp == 4 and tp == 4:
         extra = jnp.concatenate([norm_gains.reshape(-1, 128), norm_biases.reshape(-1, 128)])
         extra = jnp.pad(extra, ((0, 16 - extra.shape[0]), (0, 0)))
         padded = jnp.pad(lengths, ((0, 8 - lengths.shape[0]), (0, 128 - lengths.shape[1])))
-        wide, signed = host_tables(length)
+        wide, signed, cost, sint = host_tables(length)
         rows_in = jnp.where(section == 0, tokens, cotangent)
-        weights, y, tokens, mask, small = first_layer(rows_in, shard, extra, padded, wide, signed)
-        grad_top = tokens
+        weights, *joint, inputs, grad_top, mask, small = first_layer(rows_in, shard, extra, padded, wide, signed)
         weights = weights.reshape((BLOCKS,) + weights.shape[2:])
         norms = (small[:2], small[2:])
+        y, kept = attend(inputs, tuple(joint), weights, norms, mask)
+        dr1, da = ffn_backward(grad_top, kept, weights, norms, False)
+        dy = mid_back(grad_top, da, dr1, kept, weights, cost, sint)
+        first, pair, down, ends, total = last_back(inputs, y, dy, kept, weights, norms, cost, sint)
+        small = lax.dynamic_slice_in_dim(total[:4].reshape(2, dp * tp, -1), lax.axis_index(ALL), 1, 1)
+        gains, biases = small[0, 0], small[1, 0]
     else:
+        near = core * rows + jnp.arange(rows, dtype=jnp.int32)
+        far = (1 - core) * rows + jnp.arange(rows, dtype=jnp.int32)
+        tabs = rope_tables(near)
         weights = gather_shard(shard, dp, tp)
         norms = jnp.concatenate([norm_gains, norm_biases])
         norms = lax.all_gather(norms, ("y", "core"), axis=1, tiled=True).astype(F32)
@@ -1349,19 +1633,14 @@
         seg_all = jnp.concatenate([seg_near, segment(far)])
         mask = jnp.where(seg_all[:, None] == seg_near[None, :], 0.0, neg_fill).astype(F32)
         y, unused = forward(tokens, weights, norms, mask, tabs)
-    received = lax.ppermute(y, "section", [(0, 1)])
-    inputs = jnp.where(section == 0, tokens, received)
-    y, kept = forward(inputs, weights, norms, mask, tabs)
-    dr1, da = ffn_backward(grad_top, kept, weights, norms, False)
-    unused, dz = attn_backward(inputs, da, dr1, None, kept, weights, tabs)
-    received = lax.ppermute(dz, "section", [(1, 0)])
-    dy = jnp.where(section == 0, received, grad_top)
-    g, dr1, da, ng = ffn_backward(dy, kept, weights, norms, True)
-    if dp == 4 and tp == 4:
-        first, pair, down, ends, total = last_back(inputs, y, da, dr1, g, ng, kept, weights, tabs)
-        small = lax.dynamic_slice_in_dim(total[:4].reshape(2, dp * tp, -1), lax.axis_index(ALL), 1, 1)
-        gains, biases = small[0, 0], small[1, 0]
-    else:
+        received = lax.ppermute(y, "section", [(0, 1)])
+        inputs = jnp.where(section == 0, tokens, received)
+        y, kept = forward(inputs, weights, norms, mask, tabs)
+        dr1, da = ffn_backward(grad_top, kept, weights, norms, False)
+        unused, dz = attn_backward(inputs, da, dr1, None, kept, weights, tabs)
+        received = lax.ppermute(dz, "section", [(1, 0)])
+        dy = jnp.where(section == 0, received, grad_top)
+        g, dr1, da, ng = ffn_backward(dy, kept, weights, norms, True)
         g, dz = attn_backward(inputs, da, dr1, g, kept, weights, tabs)
         ends = to_positions(jnp.where(section == 0, dz.astype(BF), y), tp)
         mine = scatter_sum(g, dp, tp)

time: 460 us -> 410 us (0.89)
  waiting for transfers between devices: 40.1 us -> 0 us
  starting transfers between devices: 6.95 us -> 0 us
    ppermute x5 -> x0, waiting for transfers between devices: 40.1 us -> none  [the longest x1 20.4 us: on_device(): received = lax.ppermute(dz, 'section', [(1, 0)])]
    pallas_call x2 -> x1, Pallas kernels: 42.9 us -> 17.4 us  [ffn_backward(): pl.pallas_call(functools.partial(ffn_back_kernel, grads), grid=(groups,),...]
    pallas_call x1, Pallas kernels: 124 us -> 142 us  [first_layer(): pl.pallas_call(functools.partial(first_kernel, parts), in_specs=[hbm, hbm...]
    pallas_call x6 -> x4, Pallas kernels: 211 us -> 223 us  [the longest x1 137 us: last_back(): pl.pallas_call(functools.partial(last_kernel, parts), grid=(LAST_STEP + 1...]
    ppermute x5 -> x0, starting transfers between devices: 6.95 us -> none  [the longest x1 4.96 us: on_device(): received = lax.ppermute(y, 'section', [(0, 1)])]
  transfers between devices with their start and end apart: 5 -> 0, of which waited for: 5 -> 0; matrix products, arithmetic and copies ran while one was open for 1% -> 0% of each run, Pallas kernels for 0% -> 0%
where the time goes in v6:
time: 410 us; the launch traced here: 406 us
  Pallas kernels  382 us (93%)
  local copies, waits for them, and re-layouts  19.3 us (5%)
    pallas_call x1, Pallas kernels, first_layer(): pl.pallas_call(functools.partial(first_kernel, parts), in_specs=[hbm, hbm...  142 us
    pallas_call x1, Pallas kernels, last_back(): pl.pallas_call(functools.partial(last_kernel, parts), grid=(LAST_STEP + 1...  137 us
    pallas_call x1, Pallas kernels, mid_back(): pl.pallas_call(mid_kernel, grid=(PAIRS + 1,), in_specs=[once((rows, width...  52.3 us
    pallas_call x1, Pallas kernels, attend(): pl.pallas_call(ffn_kernel, grid=(groups,), in_specs=[full((rows, width)),...  17.6 us
    pallas_call x1, Pallas kernels, ffn_backward(): pl.pallas_call(functools.partial(ffn_back_kernel, grads), grid=(groups,),...  17.4 us
    pallas_call x1, Pallas kernels, attend(): pl.pallas_call(attn_kernel, grid=(heads,), in_specs=[pair] * 5 + [full((2...  16.4 us

profile of v6, /device:TPU:0, one launch (start us, length us, event | category | flops | bytes accessed | tf_op | source)
XLA Modules:
  0.0 406.2 jit_solution(11770950842782169364)
XLA Ops:
  0.6 0.0 copy-start.7
  0.7 0.7 reduce
  1.4 0.7 reduce.1
  2.1 0.6 fusion.2.extra_ref
  2.7 1.3 pad.9.len_ref
  4.0 1.0 copy.33
  5.1 0.1 copy.36
  5.2 0.1 copy.41
  5.3 0.0 copy-done.7
  5.4 0.2 copy.32
  5.6 0.0 copy-start.8
  5.6 0.0 copy-start.6
  5.6 0.1 maximum_select_fusion.1
  5.7 0.1 copy.39
  5.9 0.1 copy.40
  6.0 0.6 copy-done.8
  6.5 0.3 concatenate.39
  6.9 0.1 copy.37
  6.9 0.7 concatenate.38
  7.6 0.3 maximum_bitcast_fusion
  7.9 1.2 copy.38
  9.1 0.8 reshape.88
  9.9 0.0 copy-start.2
  9.9 0.0 copy-start.3
  9.9 1.7 concatenate.41.shard_ref
  11.7 1.0 broadcast_select_fusion.tok_ref
  12.7 141.8 %first.1 = (bf16[2,2,4,192,3072]{4,3,2,1,0:T(8,128)(2,1)}, bf16[6,512,128]{2,1,0:T(8,128)(2,1)}, bf16[6,512,128]{2,1,0:T(8,128)(2,1)}, bf16[6,512,128]{2,1,0:T(8...) custom-call(bf16[2,256,768]{2,1,0:T(8,128)(2,1)} %broadcast_select_f, ...), custom_call_target="tpu_custom_call" | custom-call | tf_op jit(solution)/shard_map/first/pallas_call | solution.py:1455
  154.5 1.4 fusion.3
  155.9 16.4 %attn.1 = (bf16[6,512,128]{2,1,0:T(8,128)(2,1)}, bf16[6,2,1024,512]{3,2,1,0:T(8,128)(2,1)}, f32[6,2,8,512]{3,2,1,0:T(8,128)}) custom-call(bf16[6,512,128]{2,1,0:T(8,128)(2,1)} %get-tuple-element.34.q_ref, bf16[6,512,128]{2,1,0:T(8,128)(2,1)} %get-tuple-element.35.k_ref, bf16[6,512,128]{2,1,0:T(8,128)(2,1)} %get-tuple-element.36.v_ref, ...), custom_call_target="tpu_custom_call" | custom-call | tf_op jit(solution)/shard_map/attn/pallas_call | solution.py:361
  172.2 17.6 %ffn.1 = (bf16[512,768]{1,0:T(8,128)(2,1)}, bf16[6,2,512,512]{3,2,1,0:T(8,128)(2,1)}, bf16[512,768]{1,0:T(8,128)(2,1)}, f32[512,128]{1,0:T(8,128)}, bf16[512,768]{1,0:T(8,128)(2,1)}, /*index=5*/f32[512,128]{1,0:T(8,128)}) custom-call(bf16[512,768]{1,0:T(8,128)(2,1)} %get-tuple-element.33.x_ref.x_hbm, bf16[6,512,128]{2,1,0:T(8,128)(2,1)} %get-tuple-element.40.o_ref, ...), custom_call_target="tpu_custom_call" | custom-call | tf_op jit(solution)/shard_map/ffn/pallas_call | solution.py:372
  189.8 17.4 %ffn_back_light.1 = (f32[512,768]{1,0:T(8,128)}, bf16[512,768]{1,0:T(8,128)(2,1)}) custom-call(bf16[512,768]{1,0:T(8,128)(2,1)} %get-tuple-element.49.dy_ref.top_ref, bf16[512,768]{1,0:T(8,128)(2,1)} %get-tuple-element.43.n1_ref, f32[512,128]{1,0:T(8,128)} %get-tuple-element.44.i1_ref, bf16[512,768]{1,0:T(8,128)(2,1)} %get-tuple-element.45.n2_ref, ...), custom_call_target="tpu_custom_call" | custom-call | tf_op jit(solution)/shard_map/ffn_back_light/pallas_call | solution.py:406
  207.3 52.3 %mid.1 = bf16[512,768]{1,0:T(8,128)(2,1)} custom-call(bf16[512,768]{1,0:T(8,128)(2,1)} %get-tuple-element.50.da_ref, f32[512,768]{1,0:T(8,128)} %get-tuple-element.51.dr1_ref, bf16[4,4,192,3072]{3,2,1,0:T(8,128)(2,1)} %bitcast.47, bf16[6,512,128]{2,1,0:T(8,128)(2,1)} %get-tuple-element.40.o_ref, bf16[6,512,128]{2,1,0:T(8,128)(2,1)} %get-tuple-element.34.q_ref, ...), custom_call_target="tpu_custom_call" | custom-call | tf_op jit(solution)/shard_map/mid/pallas_call | solution.py:1073
  259.6 136.8 %last.1 = (f32[192,768]{1,0:T(8,128)}, f32[192,1536]{1,0:T(8,128)}, f32[768,192]{1,0:T(8,128)}, bf16[2,256,768]{2,1,0:T(8,128)(2,1)}, f32[8,768]{1,0:T(8,128)}) custom-call(bf16[512,768]{1,0:T(8,128)(2,1)} %get-tuple-element.43.n1_ref, f32[512,128]{1,0:T(8,128)} %get-tuple-element.44.i1_ref, bf16[512,768]{1,0:T(8,128)(2,1)} %get-tuple-element.45.n2_ref, ...), custom_call_target="tpu_custom_call" | custom-call | tf_op jit(solution)/shard_map/last/pallas_call | solution.py:912
  396.4 0.8 slice.77
  397.2 0.1 reshape.98
  397.3 0.5 dynamic-slice_bitcast_fusion
  397.8 0.9 slice.76
  398.7 0.1 copy.46
  398.8 0.1 copy.47
  399.0 1.0 slice_bitcast_fusion
  400.0 0.8 copy.49
  400.8 0.1 copy.42
  401.0 0.2 copy.43
  401.1 0.1 maximum_select_fusion
  401.2 1.1 copy.50
  402.3 1.1 copy.51
  403.4 1.8 broadcast_in_dim_reshape.4
  405.2 0.9 copy.53
  (23 shorter events, 0.2 us)
Async XLA Ops:
  0.6 4.7 %copy-start.7 = (bf16[1,192,3,192]{3,1,2,0:T(8,128)(2,1)S(1)}, bf16[1,192,3,192]{3,1,2,0:T(8,128)(2,1)}, u32[]{:S(2)}) copy-start(bf16[1,192,3,192]{3,1,2,0:T(8,128)(2,1)} %param.16) | copy-start | bytes 663556
  5.6 1.0 copy-start.8
  5.6 1.3 copy-start.6
  9.9 1.8 copy-start.2
  9.9 1.8 copy-start.3
  396.4 4.4 %copy-start.1 = (f32[192,768]{1,0:T(8,128)S(1)}, f32[192,768]{1,0:T(8,128)}, u32[]{:S(2)}) copy-start(f32[192,768]{1,0:T(8,128)} %get-tuple-element.55) | copy-start | bytes 1769476
  401.1 1.1 copy-start.5
  401.2 2.1 copy-start
  403.4 1.8 copy-start.4

commit v7 on v6

--- a/solution.py
+++ b/solution.py
@@ -959,153 +959,17 @@
     )(n1, i1, n2, i2, gu, w, w, gains, biases, o, q, k, v, ko, vo, l, cost, sint, dy.reshape(halves), x, y.reshape(halves), e)
 
 
-def mid_kernel(
-    da_ref, dr1_ref, w_ref, o_ref, q_ref, k_ref, v_ref, ko_ref, vo_ref, e_ref, l_ref, cos_ref, sin_ref, top_ref,
-    dy_out,
-    do3, dq, keep, oth, got, d, send, land,
-    oth_send, oth_recv, row_send, row_recv,
-):
-    step = pl.program_id(0)
-    section, c = lax.axis_index("section"), lax.axis_index("core")
-    rows, width = da_ref.shape
-    pieces = send.shape[0]
-    near, other = {"core": 1 - c}, {"section": 1 - section}
-
-    def remote(src, dst, send, recv, device):
-        return pltpu.make_async_remote_copy(src, dst, send, recv, device_id=device, device_id_type=MESH)
-
-    def oth_copy(p):
-        return remote(oth.at[p], got.at[p], oth_send.at[p], oth_recv.at[p], near)
-
-    def row_copy(b):
-        return remote(send.at[b], land.at[b], row_send.at[b], row_recv.at[b], other)
-
-    @pl.when(step == 0)
-    def _():
-        barrier = pltpu.get_barrier_semaphore()
-        for device in (near, other):
-            pl.semaphore_signal(barrier, inc=1, device_id=device, device_id_type=MESH)
-        pl.semaphore_wait(barrier, 2)
-
-    cos, sin = cos_ref[:, pl.ds(c * rows, rows)], sin_ref[:, pl.ds(c * rows, rows)]
-
-    @pl.when(jnp.logical_and(step < PAIRS, step % 3 == 0))
-    def _():
-        w = jnp.concatenate(out_weight(w_ref.at[:, pl.ds(2 * (step // 3), 2), :, 512:768]), axis=1)
-        t = dg(da_ref[...], w, NN).astype(BF)
-        for i in range(3):
-            do3[i] = t[:, 128 * i : 128 * i + 128]
-
-    @pl.when(step < PAIRS)
-    def _():
-        dqt, dk, dv = pair_back(
-            do3[step % 3], o_ref[step], q_ref[0], k_ref[0], v_ref[0], ko_ref[0], vo_ref[0],
-            [e_ref.at[0, h] for h in range(2)], [l_ref[0, h, 0:1] for h in range(2)], cos, sin,
-        )
-        dq[step] = dqt.T.astype(BF)
-        keep[step, 0] = dk[:, :rows]
-        keep[step, 1] = dv[:, :rows]
-        oth[step, 0] = dk[:, rows:].astype(BF)
-        oth[step, 1] = dv[:, rows:].astype(BF)
-        oth_copy(step).start()
-
-    def joint(half):
-        for i in range(3):
-            oth_copy(3 * half + i).wait()
-        parts = joint_parts(
-            [dq[3 * half + i].astype(F32) for i in range(3)],
-            [keep[3 * half + i, 0] + got[3 * half + i, 0].astype(F32) for i in range(3)],
-            [keep[3 * half + i, 1] + got[3 * half + i, 1].astype(F32) for i in range(3)],
-            cos, sin,
-        )
-        for e in range(2):
-            d[2 * half + e] = parts[e]
-
-    @pl.when(step == PAIRS - 1)
-    def _():
-        joint(0)
-
-    @pl.when(step == PAIRS)
-    def _():
-        joint(1)
-
-        def rows_of(b, carry):
-            part = pl.ds(pl.multiple_of(b * (rows // pieces), rows // pieces), rows // pieces)
-            total = dr1_ref[part]
-            for t in range(4):
-                total += dg(d[t, part], w_ref[:, t, :, :640].reshape(width, 640), NT)
-            send[b] = total.astype(BF)
-
-            @pl.when(section == 1)
-            def _():
-                row_copy(b).start()
-
-            return carry
-
-        lax.fori_loop(0, pieces, rows_of, 0)
-
-        @pl.when(section == 1)
-        def _():
-            lax.fori_loop(0, pieces, lambda b, t: (row_copy(b).wait_send(), t)[1], 0)
-            dy_out[...] = top_ref[...]
-
-        @pl.when(section == 0)
-        def _():
-            lax.fori_loop(0, pieces, lambda b, t: (row_copy(b).wait_recv(), t)[1], 0)
-            dy_out[...] = land[...].reshape(rows, width)
-
-
-def mid_back(top, da, dr1, kept, w, cost, sint):
-    q, k, v, ko, vo, o, e, l = kept[:8]
-    rows, width = da.shape
-    heads = width // 128
-    depth = w.shape[2]
-    pieces = 4
-    dma = pltpu.SemaphoreType.DMA
-
-    def once(shape):
-        return pl.BlockSpec(shape, lambda i: (0,) * len(shape), pipeline_mode=pl.Buffered(1))
-
-    def by_pair(shape):
-        return pl.BlockSpec(shape, lambda i: (jnp.minimum(i, PAIRS - 1),) + (0,) * (len(shape) - 1))
-
-    pair = by_pair((1, rows, 128))
-    return pl.pallas_call(
-        mid_kernel,
-        grid=(PAIRS + 1,),
-        in_specs=[
-            once((rows, width)), once((rows, width)), once((4, 4, depth, width)), once((heads, rows, 128)),
-            pair, pair, pair, pair, pair,
-            by_pair((1, 2, 2 * rows, rows)),
-            by_pair((1, 2, 8, rows)),
-            once(cost.shape), once(sint.shape), once((rows, width)),
-        ],
-        out_specs=once((rows, width)),
-        out_shape=sds((rows, width), BF),
-        scratch_shapes=[
-            VM((3, rows, 128), BF),
-            VM((heads, rows, 128), BF),
-            VM((heads, 2, 128, rows), F32),
-            VM((heads, 2, 128, rows), BF),
-            VM((heads, 2, 128, rows), BF),
-            VM((4, rows, 640), BF),
-            VM((pieces, rows // pieces, width), BF),
-            VM((pieces, rows // pieces, width), BF),
-            dma((PAIRS,)), dma((PAIRS,)), dma((pieces,)), dma((pieces,)),
-        ],
-        compiler_params=pltpu.CompilerParams(collective_id=2, has_side_effects=True, vmem_limit_bytes=58 << 20),
-        name="mid",
-    )(da, dr1, w, o, q, k, v, ko, vo, e, l, cost, sint, top)
-
-
 LAG = 6
 
 
 def first_kernel(
-    parts, tok_ref, shard_ref, extra_ref, len_ref, cos_ref, sin_ref,
-    w_out, q_out, k_out, v_out, ko_out, vo_out, x_out, top_out, mask_out, norm_out,
+    parts, tok_ref, shard_ref, extra_ref, len_ref, cos_ref, sin_ref, cost_ref, sint_ref,
+    w_out, q_out, k_out, v_out, ko_out, vo_out, y_out, e_out, o_out, gu_out, n1_out, n2_out,
+    x_out, dy_out, l_out, i1_out, i2_out, norm_out,
     w, xin, q, kv, land_kv, late_kv, o, hb, acc, relay, land_rows, ext, lens,
+    mask, eb, gu, n1, n2, df, do3, dq, keep, oth, got, d,
     tok_sem, tok_send, tok_recv, shard_sem, back_sem, kv_send, kv_recv, out_sem, row_send, row_recv,
+    e_sem, gu_sem, oth_send, oth_recv, dz_send, dz_recv,
     small_send, small_recv, rs_sem, rr_sem, ls_sem, lr_sem, ys_sem, yr_sem, cs_sem, cr_sem,
 ):
     section = lax.axis_index("section")
@@ -1287,7 +1151,7 @@
         end = end + mine[:, n : n + 1]
         seg_q = seg_q + jnp.where(end <= at_q, 1, 0)
         seg_k = seg_k + jnp.where(end <= at_k, 1, 0)
-    mask_out[...] = jnp.where(seg_k == seg_q, 0.0, neg_fill).astype(F32)
+    mask[...] = jnp.where(seg_k == seg_q, 0.0, neg_fill).astype(F32)
     lax.fori_loop(3, 16, early, 0)
     rounds(16, start)
 
@@ -1326,7 +1190,6 @@
 
     x = xin[...].reshape(rows, width)
     x_out[...] = x
-    top_out[...] = x
     project(0, rows, x)
     low = low_lanes((rows, 128))
     share = remote(kv, land_kv, kv_send.at[0], kv_recv.at[0], near)
@@ -1334,34 +1197,55 @@
     rounds(start, start + 1)
     share.wait()
 
-    def pair(p, carry):
-        k = jnp.concatenate([kv[0, p], land_kv[0, p]], axis=0)
-        v = jnp.concatenate([kv[1, p], land_kv[1, p]], axis=0)
+    def heads_of(p, others, save):
+        k = jnp.concatenate([kv[0, p], others[0, p]], axis=0)
+        v = jnp.concatenate([kv[1, p], others[1, p]], axis=0)
         vt = v.astype(F32).T.astype(BF)
+        ones = jnp.ones((16, 2 * rows), BF)
         outs = []
         for h in range(2):
             qm = jnp.where(low if h == 0 else jnp.logical_not(low), q[p], jnp.zeros((rows, 128), BF))
-            s = dg(k, qm, NT) + mask_out[...]
-            e = jnp.exp(s - jnp.max(s, axis=0, keepdims=True))
-            inv = 1.0 / jnp.sum(e, axis=0, keepdims=True)
-            outs.append(dg(vt[HD * h : HD * h + HD], e.astype(BF), NN) * inv)
+            s = dg(k, qm, NT) + mask[...]
+            e = jnp.exp(s - jnp.max(s, axis=0, keepdims=True)).astype(BF)
+            t = dg(jnp.concatenate([vt[HD * h : HD * h + HD], ones], axis=0), e, NN)
+            inv = 1.0 / t[HD : HD + 1]
+            save(h, e, inv)
+            outs.append(t[:HD] * inv)
         o[p] = jnp.concatenate(outs, axis=0).T.astype(BF)
+
+    def pair(p, carry):
+        heads_of(p, land_kv, lambda h, e, inv: None)
         round_(start + 1 + p)
         return carry
 
-    lax.fori_loop(0, 6, pair, 0)
-    r = x.astype(F32)
-    for p in range(2):
+    def out_part(p):
         wo = []
         for e in range(2):
             wo.append([w[:, :, 2 * p + e, :, 512 + 128 * i : 640 + 128 * i].reshape(width, 128) for i in range(2)])
         mid = jnp.where(low_lanes((width, 128)), swap64(wo[0][0].astype(F32)), wo[1][0].astype(F32)).astype(BF)
-        r = r + dg(
-            jnp.concatenate([o[3 * p + i] for i in range(3)], axis=1),
-            jnp.concatenate([wo[0][1], mid, wo[1][1]], axis=1),
-            NT,
+        return jnp.concatenate([wo[0][1], mid, wo[1][1]], axis=1)
+
+    def mix(x):
+        r = x.astype(F32)
+        for p in range(2):
+            r = r + dg(jnp.concatenate([o[3 * p + i] for i in range(3)], axis=1), out_part(p), NT)
+        return norm_parts(r)
+
+    def group_of(k):
+        return unit_weights(
+            lambda t, m: w[:, :, t, :, pl.ds(pl.multiple_of(width + GROUP * k + 128 * m, 128), 128)].reshape(width, 128)
         )
-    n, inv = norm_parts(r)
+
+    def unit(k, save):
+        wg, wu, wd = group_of(k)
+        gate = dg(hb[...], wg, NN)
+        up = dg(hb[...], wu, NN)
+        save(gate, up)
+        act = (gate / (1.0 + jnp.exp(-gate)) * up).astype(BF)
+        acc[...] += dg(act, wd, NT)
+
+    lax.fori_loop(0, 6, pair, 0)
+    n, inv = mix(x)
     h = n * norm_out[0:1] + norm_out[2:3]
     hb[...] = h.astype(BF)
     acc[...] = h
@@ -1372,13 +1256,7 @@
         def _():
             round_(start + 8 + k - k // 5)
 
-        wg, wu, wd = unit_weights(
-            lambda t, m: w[:, :, t, :, pl.ds(pl.multiple_of(width + GROUP * k + 128 * m, 128), 128)].reshape(width, 128)
-        )
-        gate = dg(hb[...], wg, NN)
-        up = dg(hb[...], wu, NN)
-        act = (gate / (1.0 + jnp.exp(-gate)) * up).astype(BF)
-        acc[...] += dg(act, wd, NT)
+        unit(k, lambda gate, up: None)
         return carry
 
     lax.fori_loop(0, 6, units, 0)
@@ -1388,13 +1266,12 @@
     def row_copy(b):
         return remote(relay.at[b], land_rows.at[b], row_send.at[b], row_recv.at[b], other)
 
-    def keep(arrays):
-        outs = (q_out, k_out, v_out, ko_out, vo_out)
-        copies = [pltpu.make_async_copy(t, out, out_sem.at[i]) for i, (t, out) in enumerate(zip(arrays, outs))]
-        for t in copies:
-            t.start()
-        for t in copies:
-            t.wait()
+    kept_out = []
+
+    def keep_out(src, dst):
+        copy = pltpu.make_async_copy(src, dst, out_sem.at[len(kept_out)])
+        kept_out.append(copy)
+        copy.start()
 
     @pl.when(section == 0)
     def _():
@@ -1406,8 +1283,9 @@
             return carry
 
         lax.fori_loop(0, pieces, send_rows, 0)
-        keep((q, kv.at[0], kv.at[1], land_kv.at[0], land_kv.at[1]))
-        lax.fori_loop(0, pieces, lambda b, t: (row_copy(b).wait_send(), t)[1], 0)
+        same = pltpu.make_async_copy(land_kv, late_kv, kv_send.at[1])
+        same.start()
+        same.wait()
 
     @pl.when(section == 1)
     def _():
@@ -1422,7 +1300,168 @@
         again = remote(kv, late_kv, kv_send.at[1], kv_recv.at[1], near)
         again.start()
         again.wait()
-        keep((q, kv.at[0], kv.at[1], late_kv.at[0], late_kv.at[1]))
+
+    for src, dst in ((q, q_out), (kv.at[0], k_out), (kv.at[1], v_out), (late_kv.at[0], ko_out), (late_kv.at[1], vo_out)):
+        keep_out(src, dst)
+
+    def probs_out(p):
+        return pltpu.make_async_copy(eb.at[p % 2], e_out.at[p], e_sem.at[p % 2])
+
+    def probs_in(p):
+        return pltpu.make_async_copy(e_out.at[p], eb.at[p % 2], e_sem.at[p % 2])
+
+    def pair_kept(p, carry):
+        @pl.when(p >= 2)
+        def _():
+            probs_out(p - 2).wait()
+
+        def save(h, e, inv):
+            eb[p % 2, h] = e
+            l_out[p, h] = jnp.broadcast_to(inv, l_out.shape[2:])
+
+        heads_of(p, late_kv, save)
+        probs_out(p).start()
+        return carry
+
+    lax.fori_loop(0, PAIRS, pair_kept, 0)
+    keep_out(o, o_out)
+    n, inv = mix(x_out[...])
+    n1[...] = n.astype(BF)
+    i1_out[...] = jnp.broadcast_to(inv, i1_out.shape)
+    keep_out(n1, n1_out)
+    h = n * norm_out[0:1] + norm_out[2:3]
+    hb[...] = h.astype(BF)
+    acc[...] = h
+
+    def units_out(k):
+        return pltpu.make_async_copy(gu.at[k % 2], gu_out.at[k], gu_sem.at[k % 2])
+
+    def units_in(k):
+        return pltpu.make_async_copy(gu_out.at[k], gu.at[k % 2], gu_sem.at[k % 2])
+
+    def unit_kept(k, carry):
+        @pl.when(k >= 2)
+        def _():
+            units_out(k - 2).wait()
+
+        def save(gate, up):
+            gu[k % 2, 0] = gate.astype(BF)
+            gu[k % 2, 1] = up.astype(BF)
+
+        unit(k, save)
+        units_out(k).start()
+        return carry
+
+    lax.fori_loop(0, 6, unit_kept, 0)
+    n, inv = norm_parts(acc[...])
+    n2[...] = n.astype(BF)
+    i2_out[...] = jnp.broadcast_to(inv, i2_out.shape)
+    keep_out(n2, n2_out)
+    hb[...] = (n * norm_out[1:2] + norm_out[3:4]).astype(BF)
+    keep_out(hb, y_out)
+    for p in (PAIRS - 2, PAIRS - 1):
+        probs_out(p).wait()
+        units_out(p).wait()
+
+    def dz_copy(b):
+        return remote(relay.at[b], land_rows.at[b], dz_send.at[b], dz_recv.at[b], other)
+
+    def oth_copy(p):
+        return remote(oth.at[p], got.at[p], oth_send.at[p], oth_recv.at[p], near)
+
+    @pl.when(section == 1)
+    def _():
+        dr2 = norm_back(xin[...].reshape(rows, width).astype(F32) * norm_out[1:2], n, inv)
+        acc[...] = dr2
+        df[...] = dr2.astype(BF)
+        for p in range(2):
+            probs_in(p).start()
+            units_in(p).start()
+
+        def unit_back(k, carry):
+            wg, wu, wd = group_of(k)
+            units_in(k).wait()
+            gate = gu[k % 2, 0].astype(F32)
+            up = gu[k % 2, 1].astype(F32)
+            s = 1.0 / (1.0 + jnp.exp(-gate))
+            d_act = dg(df[...], wd, NN)
+            d_gate = (d_act * up * (s * (1.0 + gate * (1.0 - s)))).astype(BF)
+            d_up = (d_act * (gate * s)).astype(BF)
+            acc[...] += dg(d_gate, wg, NT) + dg(d_up, wu, NT)
+
+            @pl.when(k + 2 < 6)
+            def _():
+                units_in(k + 2).start()
+
+            return carry
+
+        lax.fori_loop(0, 6, unit_back, 0)
+        dr1 = norm_back(acc[...] * norm_out[0:1], n1[...].astype(F32), i1_out[:, :1])
+        acc[...] = dr1
+        df[...] = dr1.astype(BF)
+        cost, sint = cost_ref[:, pl.ds(c * rows, rows)], sint_ref[:, pl.ds(c * rows, rows)]
+
+        def pair_of(p, carry):
+            probs_in(p).wait()
+            dqt, dk, dv = pair_back(
+                do3[p % 3], o[p], q[p], kv[0, p], kv[1, p], late_kv[0, p], late_kv[1, p],
+                [eb.at[p % 2, h] for h in range(2)], [l_out[p, h, 0:1] for h in range(2)], cost, sint,
+            )
+
+            @pl.when(p + 2 < PAIRS)
+            def _():
+                probs_in(p + 2).start()
+
+            dq[p] = dqt.T.astype(BF)
+            keep[p, 0] = dk[:, :rows].astype(BF)
+            keep[p, 1] = dv[:, :rows].astype(BF)
+            oth[p, 0] = dk[:, rows:].astype(BF)
+            oth[p, 1] = dv[:, rows:].astype(BF)
+            oth_copy(p).start()
+            return carry
+
+        def joint(half):
+            def total(i, m):
+                return keep[i, m].astype(F32) + got[i, m].astype(F32)
+
+            three = range(3 * half, 3 * half + 3)
+            for i in three:
+                oth_copy(i).wait()
+            parts = joint_parts(
+                [dq[i].astype(F32) for i in three], [total(i, 0) for i in three], [total(i, 1) for i in three], cost, sint
+            )
+            for e in range(2):
+                d[2 * half + e] = parts[e]
+
+        for half in range(2):
+            t = dg(df[...], out_part(half), NN).astype(BF)
+            for i in range(3):
+                do3[i] = t[:, 128 * i : 128 * i + 128]
+            lax.fori_loop(3 * half, 3 * half + 3, pair_of, 0)
+        for half in range(2):
+            joint(half)
+
+        def send_back(b, carry):
+            part = pl.ds(pl.multiple_of(b * piece_rows, piece_rows), piece_rows)
+            total = acc[part]
+            for t in range(4):
+                total += dg(d[t, part], w[:, :, t, :, :640].reshape(width, 640), NT)
+            relay[b] = total.astype(BF)
+            dz_copy(b).start()
+            return carry
+
+        lax.fori_loop(0, pieces, send_back, 0)
+        dy_out[...] = xin[...].reshape(rows, width)
+        lax.fori_loop(0, pieces, lambda b, t: (dz_copy(b).wait_send(), t)[1], 0)
+
+    @pl.when(section == 0)
+    def _():
+        lax.fori_loop(0, pieces, lambda b, t: (row_copy(b).wait_send(), t)[1], 0)
+        lax.fori_loop(0, pieces, lambda b, t: (dz_copy(b).wait_recv(), t)[1], 0)
+        dy_out[...] = land_rows[...].reshape(rows, width)
+
+    for copy in kept_out:
+        copy.wait()
 
     def finish(j, carry):
         write_back(j).wait()
@@ -1443,7 +1482,7 @@
     lax.fori_loop(0, parts, finish, 0)
 
 
-def first_layer(tokens, shard, extra, lengths, cos, sin):
+def first_layer(tokens, shard, extra, lengths, cos, sin, cost, sint):
     micro, own, width = tokens.shape
     depth, columns = shard.shape
     rows = 2 * own
@@ -1454,14 +1493,22 @@
     vm = pl.BlockSpec(memory_space=VM)
     return pl.pallas_call(
         functools.partial(first_kernel, parts),
-        in_specs=[hbm, hbm, vm, vm, vm, vm],
-        out_specs=[hbm] * 6 + [vm] * 4,
+        in_specs=[hbm, hbm] + [vm] * 6,
+        out_specs=[hbm] * 12 + [vm] * 6,
         out_shape=[sds((2, 2, 4, depth, columns), BF)]
         + [sds((heads, rows, 128), BF)] * 5
         + [
             sds((rows, width), BF),
+            sds((heads, 2, 2 * rows, rows), BF),
+            sds((heads, rows, 128), BF),
+            sds((6, 2, rows, 512), BF),
             sds((rows, width), BF),
-            sds((2 * rows, rows), F32),
+            sds((rows, width), BF),
+            sds((rows, width), BF),
+            sds((rows, width), BF),
+            sds((heads, 2, 8, rows), F32),
+            sds((rows, 128), F32),
+            sds((rows, 128), F32),
             sds((4, width), F32),
         ],
         scratch_shapes=[
@@ -1478,14 +1525,27 @@
             VM((4, rows // 4, width), BF),
             VM((2, 2) + extra.shape, BF),
             VM((2,) + lengths.shape, jnp.int32),
-            dma, dma((2,)), dma((2,)), dma, dma((parts,)), dma((2,)), dma((2,)), dma((5,)), dma((4,)), dma((4,)),
+            VM((2 * rows, rows), F32),
+            VM((2, 2, 2 * rows, rows), BF),
+            VM((2, 2, rows, 512), BF),
+            VM((rows, width), BF),
+            VM((rows, width), BF),
+            VM((rows, width), BF),
+            VM((3, rows, 128), BF),
+            VM((heads, rows, 128), BF),
+            VM((heads, 2, 128, rows), BF),
+            VM((heads, 2, 128, rows), BF),
+            VM((heads, 2, 128, rows), BF),
+            VM((4, rows, 640), BF),
+            dma, dma((2,)), dma((2,)), dma, dma((parts,)), dma((2,)), dma((2,)), dma((9,)), dma((4,)), dma((4,)),
+            dma((2,)), dma((2,)), dma((6,)), dma((6,)), dma((4,)), dma((4,)),
             dma((3,)), dma((3,)),
             dma((parts, 3)), dma((parts, 3)), dma((parts, 3)), dma((parts, 3)),
             dma((parts,)), dma((parts,)), dma((parts,)), dma((parts,)),
         ],
-        compiler_params=pltpu.CompilerParams(collective_id=1, has_side_effects=True, vmem_limit_bytes=60 << 20),
+        compiler_params=pltpu.CompilerParams(collective_id=1, has_side_effects=True, vmem_limit_bytes=63 << 20),
         name="first",
-    )(tokens, shard, extra, lengths, cos, sin)
+    )(tokens, shard, extra, lengths, cos, sin, cost, sint)
 
 
 def swap_pairs(tp, step, dp_axes):
@@ -1603,12 +1663,12 @@
         padded = jnp.pad(lengths, ((0, 8 - lengths.shape[0]), (0, 128 - lengths.shape[1])))
         wide, signed, cost, sint = host_tables(length)
         rows_in = jnp.where(section == 0, tokens, cotangent)
-        weights, *joint, inputs, grad_top, mask, small = first_layer(rows_in, shard, extra, padded, wide, signed)
+        (
+            weights, q, k, v, ko, vo, y, e, o, gu, n1, n2, inputs, dy, l, i1, i2, small,
+        ) = first_layer(rows_in, shard, extra, padded, wide, signed, cost, sint)
         weights = weights.reshape((BLOCKS,) + weights.shape[2:])
         norms = (small[:2], small[2:])
-        y, kept = attend(inputs, tuple(joint), weights, norms, mask)
-        dr1, da = ffn_backward(grad_top, kept, weights, norms, False)
-        dy = mid_back(grad_top, da, dr1, kept, weights, cost, sint)
+        kept = (q, k, v, ko, vo, o, e, l, gu, n1, i1, n2, i2)
         first, pair, down, ends, total = last_back(inputs, y, dy, kept, weights, norms, cost, sint)
         small = lax.dynamic_slice_in_dim(total[:4].reshape(2, dp * tp, -1), lax.axis_index(ALL), 1, 1)
         gains, biases = small[0, 0], small[1, 0]

time: 410 us -> 392 us (0.956)
  Pallas kernels: 382 us -> 364 us
    pallas_call x4 -> x0, Pallas kernels: 104 us -> none  [the longest x1 52.3 us: mid_back(): pl.pallas_call(mid_kernel, grid=(PAIRS + 1,), in_specs=[once((rows, width...]
    pallas_call x1, Pallas kernels: 142 us -> 228 us  [first_layer(): pl.pallas_call(functools.partial(first_kernel, parts), in_specs=[hbm, hbm...]
where the time goes in v7:
time: 392 us; the launch traced here: 388 us
  Pallas kernels  364 us (93%)
  local copies, waits for them, and re-layouts  19.3 us (5%)
    pallas_call x1, Pallas kernels, first_layer(): pl.pallas_call(functools.partial(first_kernel, parts), in_specs=[hbm, hbm...  228 us
    pallas_call x1, Pallas kernels, last_back(): pl.pallas_call(functools.partial(last_kernel, parts), grid=(LAST_STEP + 1...  137 us

profile of v7, /device:TPU:0, one launch (start us, length us, event | category | flops | bytes accessed | tf_op | source)
XLA Modules:
  0.0 388.2 jit_solution(3407722231395077685)
XLA Ops:
  0.6 0.0 copy-start.7
  0.7 0.7 reduce
  1.4 0.7 reduce.1
  2.1 0.6 fusion.2.extra_ref
  2.7 1.3 pad.9.len_ref
  4.0 1.0 copy.33
  5.1 0.1 copy.36
  5.2 0.1 copy.41
  5.3 0.0 copy-done.7
  5.4 0.2 copy.32
  5.6 0.0 copy-start.8
  5.6 0.0 copy-start.6
  5.6 0.1 maximum_select_fusion.1
  5.7 0.1 copy.39
  5.9 0.1 copy.40
  6.0 0.6 copy-done.8
  6.5 0.3 concatenate.39
  6.9 0.0 copy-done.6
  6.9 0.1 copy.37
  6.9 0.7 concatenate.38
  7.6 0.3 maximum_bitcast_fusion
  7.9 1.2 copy.38
  9.1 0.8 reshape.88
  9.9 0.0 copy-start.2
  9.9 0.0 copy-start.3
  9.9 1.7 concatenate.41.shard_ref
  11.7 0.0 copy-done.2
  11.7 1.0 broadcast_select_fusion.tok_ref
  12.7 227.7 %first.1 = (bf16[2,2,4,192,3072]{4,3,2,1,0:T(8,128)(2,1)}, bf16[6,512,128]{2,1,0:T(8,128)(2,1)}, bf16[6,512,128]{2,1,0:T(8,128)(2,1)}, bf16[6,512,128]{2,1,0:T(8...) custom-call(bf16[2,256,768]{2,1,0:T(8,128)(2,1)} %broadcast_select_f, ...), custom_call_target="tpu_custom_call" | custom-call | tf_op jit(solution)/shard_map/first/pallas_call | solution.py:1494
  240.4 1.4 fusion.3
  241.8 136.6 %last.1 = (f32[192,768]{1,0:T(8,128)}, f32[192,1536]{1,0:T(8,128)}, f32[768,192]{1,0:T(8,128)}, bf16[2,256,768]{2,1,0:T(8,128)(2,1)}, f32[8,768]{1,0:T(8,128)}) custom-call(bf16[512,768]{1,0:T(8,128)(2,1)} %get-tuple-element.30.n1_ref, f32[512,128]{1,0:T(8,128)} %get-tuple-element.31.i1_ref, bf16[512,768]{1,0:T(8,128)(2,1)} %get-tuple-element.32.n2_ref, ...), custom_call_target="tpu_custom_call" | custom-call | tf_op jit(solution)/shard_map/last/pallas_call | solution.py:912
  378.3 0.0 copy-start.1
  378.4 0.8 slice.77
  379.2 0.1 reshape.98
  379.2 0.5 dynamic-slice_bitcast_fusion
  379.8 0.9 slice.76
  380.7 0.1 copy.46
  380.8 0.1 copy.47
  380.9 1.0 slice_bitcast_fusion
  381.9 0.8 copy.49
  382.8 0.1 copy.42
  382.9 0.2 copy.43
  383.1 0.1 maximum_select_fusion
  383.1 1.1 copy.50
  384.2 1.1 copy.51
  385.3 0.0 copy-done
  385.3 1.8 broadcast_in_dim_reshape.4
  387.1 0.9 copy.53
  (19 shorter events, 0.2 us)
Async XLA Ops:
  0.6 4.7 %copy-start.7 = (bf16[1,192,3,192]{3,1,2,0:T(8,128)(2,1)S(1)}, bf16[1,192,3,192]{3,1,2,0:T(8,128)(2,1)}, u32[]{:S(2)}) copy-start(bf16[1,192,3,192]{3,1,2,0:T(8,128)(2,1)} %param.16) | copy-start | bytes 663556
  5.6 1.0 copy-start.8
  5.6 1.3 copy-start.6
  9.9 1.8 copy-start.2
  9.9 1.8 copy-start.3
  378.3 4.4 %copy-start.1 = (f32[192,768]{1,0:T(8,128)S(1)}, f32[192,768]{1,0:T(8,128)}, u32[]{:S(2)}) copy-start(f32[192,768]{1,0:T(8,128)} %get-tuple-element.49) | copy-start | bytes 1769476
  383.1 1.1 copy-start.5
  383.1 2.1 copy-start
  385.3 1.8 copy-start.4

commit v8 on v7

--- a/solution.py
+++ b/solution.py
@@ -119,7 +119,7 @@
         hb_ref[...] = h.astype(BF)
 
     hb = hb_ref[...]
-    wg, wu, wd = unit_weights(lambda t, m: w_ref[:, t, :, 128 * m : 128 * m + 128].reshape(width, 128))
+    wd, wg, wu = unit_weights(lambda t, m: w_ref[:, t, :, 128 * m : 128 * m + 128].reshape(width, 128))
     gate = dg(hb, wg, NN)
     up = dg(hb, wu, NN)
     gu_ref[0, 0] = gate.astype(BF)
@@ -168,21 +168,21 @@
     up = gu_ref[0, 1].astype(F32)
     s = 1.0 / (1.0 + jnp.exp(-gate))
     silu = gate * s
-    wg, wu, wd = unit_weights(lambda t, m: w_ref[:, t, :, 128 * m : 128 * m + 128].reshape(width, 128))
+    wd, wg, wu = unit_weights(lambda t, m: w_ref[:, t, :, 128 * m : 128 * m + 128].reshape(width, 128))
 
     def keep(m, grad):
         for t in range(g_out.shape[1]):
             g_out[:, t, :, 128 * m : 128 * m + 128] = grad[:, 128 * t : 128 * t + 128].astype(BF).reshape(g_out.shape[0], -1, 128)
 
     if grads:
-        keep(2, dg(df, (silu * up).astype(BF), TN))
+        keep(0, dg(df, (silu * up).astype(BF), TN))
     d_act = dg(df, wd, NN)
     d_gate = (d_act * up * (s * (1.0 + gate * (1.0 - s)))).astype(BF)
     d_up = (d_act * silu).astype(BF)
     if grads:
         hb = hb_ref[...]
-        keep(0, dg(hb, d_gate, TN))
-        keep(1, dg(hb, d_up, TN))
+        keep(1, dg(hb, d_gate, TN))
+        keep(2, dg(hb, d_up, TN))
     acc_ref[...] += dg(d_gate, wg, NT) + dg(d_up, wu, NT)
 
     @pl.when(z == pl.num_programs(0) - 1)
@@ -481,13 +481,17 @@
 LAST_STEP = 13
 
 
+FAR = 2
+FAR_AT = 4
 def last_kernel(
-    parts, n1_ref, i1_ref, n2_ref, i2_ref, gu_ref, wa_ref, wb_ref, gain_ref, bias_ref,
-    o_ref, q_ref, k_ref, v_ref, ko_ref, vo_ref, l_ref, cos_ref, sin_ref, dy_hbm, x_hbm, y_hbm, e_hbm,
-    first_out, pair_out, down_out, ends_out, norm_out,
-    acc, df, hb, ring, do3, dwo, dq, keep, oth, got, eb, e_send, e_land, tmp, land_c, land_y, land_r, land_l, land_n,
-    dy_sem, x_sem, y_sem, e_sem, oth_send, oth_recv, end_sem, end_send, end_recv,
+    parts, n1_ref, i1_ref, n2_ref, i2_ref, gu_ref, wa_ref, gain_ref, bias_ref,
+    q_ref, k_ref, v_ref, ko_ref, vo_ref, l_ref, cos_ref, sin_ref, dy_hbm, x_hbm, y_hbm, e_hbm, o_hbm, w_hbm,
+    joint_out, mix_out, pair_out, down_out, ends_out, norm_out,
+    acc, df, hb, o_ref, wb_ref, ring, do3, dwo, dq, keep, oth, got, eb, e_send, e_land, tmp, land_c, land_y, land_r, land_l, land_n,
+    z_sum, far_y, far_r, far_l,
+    o_sem, wb_sem, dy_sem, x_sem, y_sem, e_sem, oth_send, oth_recv, end_sem, end_send, end_recv,
     cs_sem, cr_sem, ys_sem, yr_sem, rs_sem, rr_sem, ls_sem, lr_sem, ns_sem, nr_sem,
+    fys_sem, fyr_sem, frs_sem, frr_sem, fls_sem, flr_sem,
 ):
     step = pl.program_id(0)
     section = lax.axis_index("section")
@@ -495,6 +499,7 @@
     last = 3
     rows, width = acc.shape
     early = parts - width // WIDE
+    usual = parts - FAR
     near, across = {"core": 1 - c}, {"y": 1 - y}
     right, left = {"tensor": jnp.minimum(z + 1, last)}, {"tensor": jnp.maximum(z - 1, 0)}
     pair = {"tensor": z + 1 - 2 * lax.rem(z, 2)}
@@ -525,6 +530,8 @@
 
     dy_copy = pltpu.make_async_copy(dy_hbm, e_send, dy_sem)
     x_copy = pltpu.make_async_copy(x_hbm, hb, x_sem)
+    o_copy = pltpu.make_async_copy(o_hbm, o_ref, o_sem)
+    wb_copy = pltpu.make_async_copy(w_hbm.at[:, :, :, pl.ds(GROUP, GROUP)], wb_ref, wb_sem)
     y_copy = pltpu.make_async_copy(y_hbm, e_send, y_sem)
 
     def probs_copy(p):
@@ -535,13 +542,16 @@
 
     def slot(j):
         return (j // 3) % 2, columns(j % 3)
+
+    def chunk(j):
+        return j + FAR * ((j + usual - FAR_AT) // usual)
 
     def to_core(j):
         r, cols = slot(j)
         return remote(ring.at[r, :, 1 - c, :, :, cols], land_c.at[j], cs_sem.at[j], cr_sem.at[j], near)
 
     def to_y(j):
-        return remote(land_c.at[j, 1 - y], land_y.at[j], ys_sem.at[j], yr_sem.at[j], across)
+        return remote(land_c.at[chunk(j), 1 - y], land_y.at[j], ys_sem.at[j], yr_sem.at[j], across)
 
     def norm_copy(k):
         return remote(land_n.at[2 * k], land_n.at[2 * k + 1], ns_sem.at[k], nr_sem.at[k], (near, across, pair, far)[k])
@@ -553,34 +563,104 @@
         return remote(src, land_l.at[j, pl.ds(0, count)], ls_sem.at[j], lr_sem.at[j], left)
 
     def stage(i, lag, body):
-        @pl.when(jnp.logical_and(i >= lag, i - lag < parts))
+        @pl.when(jnp.logical_and(i >= lag, i - lag < usual))
         def _():
             body(i - lag)
 
-    def add_cores(group):
-        def one(m, carry):
-            j = 3 * group + m
-            r, cols = slot(j)
-            to_core(j).wait()
-            land_c[j] = land_c[j] + ring[r, :, c, :, :, cols]
-            return carry
-
-        lax.fori_loop(0, 3, one, 0)
-
-    def send_cores(group):
-        lax.fori_loop(0, 3, lambda m, t: (to_core(3 * group + m).start(), t)[1], 0)
+    def add_core(j):
+        r, cols = slot(j)
+        to_core(j).wait()
+        land_c[j] = land_c[j] + ring[r, :, c, :, :, cols]
+
+    def far_right(b, first, src):
+        return remote(src, far_r.at[b, :, pl.ds(first - 1, 4 - first)], frs_sem.at[b], frr_sem.at[b], right)
+
+    def far_left(b, count, src):
+        return remote(src, far_l.at[b, :, pl.ds(0, count)], fls_sem.at[b], flr_sem.at[b], left)
+
+    def far_across(b):
+        return remote(z_sum.at[b, 1 - y], far_y.at[b], fys_sem.at[b], fyr_sem.at[b], across)
+
+    def far_first(b):
+        j = FAR_AT + b
+
+        @pl.when(z == 0)
+        def _():
+            far_right(b, 1, land_c.at[j, :, pl.ds(1, 3)]).start()
+
+        @pl.when(z == last)
+        def _():
+            far_left(b, 3, land_c.at[j, :, pl.ds(0, 3)]).start()
+
+    def far_next(b):
+        j = FAR_AT + b
+
+        @pl.when(z == 1)
+        def _():
+            far_right(b, 1, far_r.at[b]).wait_recv()
+            for k in (2, 3):
+                far_r[b, :, k - 1] = far_r[b, :, k - 1] + land_c[j, :, k]
+            far_right(b, 2, far_r.at[b, :, pl.ds(1, 2)]).start()
+
+        @pl.when(z == 2)
+        def _():
+            far_left(b, 3, far_l.at[b]).wait_recv()
+            for k in (0, 1):
+                far_l[b, :, k] = far_l[b, :, k] + land_c[j, :, k]
+            far_left(b, 2, far_l.at[b, :, pl.ds(0, 2)]).start()
+
+    def far_last(b):
+        j = FAR_AT + b
+
+        @pl.when(z == 1)
+        def _():
+            far_left(b, 2, far_l.at[b, :, pl.ds(0, 2)]).wait_recv()
+            far_l[b, :, 0] = far_l[b, :, 0] + land_c[j, :, 0]
+            far_left(b, 1, far_l.at[b, :, pl.ds(0, 1)]).start()
+
+        @pl.when(z == 2)
+        def _():
+            far_right(b, 2, far_r.at[b, :, pl.ds(1, 2)]).wait_recv()
+            far_r[b, :, 2] = far_r[b, :, 2] + land_c[j, :, 3]
+            far_right(b, 3, far_r.at[b, :, pl.ds(2, 1)]).start()
+
+    def far_sum(b):
+        mine = land_c[FAR_AT + b, :, z]
+
+        @pl.when(z == 0)
+        def _():
+            far_left(b, 1, far_l.at[b, :, pl.ds(0, 1)]).wait_recv()
+            z_sum[b] = mine + far_l[b, :, 0]
+
+        @pl.when(z == 1)
+        def _():
+            z_sum[b] = mine + far_r[b, :, 0] + far_l[b, :, 1]
+
+        @pl.when(z == 2)
+        def _():
+            z_sum[b] = mine + far_r[b, :, 1] + far_l[b, :, 2]
+
+        @pl.when(z == last)
+        def _():
+            far_right(b, 3, far_r.at[b, :, pl.ds(2, 1)]).wait_recv()
+            z_sum[b] = mine + far_r[b, :, 2]
+
+    def far_result(b):
+        far_across(b).wait_recv()
+        tmp[...] = z_sum[b, y].astype(F32) + far_y[b].astype(F32)
+        emit(FAR_AT + b)
 
     def last_hop(j):
         @pl.when(z == 1)
         def _():
             go_left(j, 2, land_l.at[j, pl.ds(0, 2)]).wait_recv()
-            land_l[j, 0] = land_l[j, 0] + land_c[j, y, 0]
+            land_l[j, 0] = land_l[j, 0] + land_c[chunk(j), y, 0]
             go_left(j, 1, land_l.at[j, pl.ds(0, 1)]).start()
 
         @pl.when(z == 2)
         def _():
             go_right(j, 2, land_r.at[j, pl.ds(1, 2)]).wait_recv()
-            land_r[j, 2] = land_r[j, 2] + land_c[j, y, 3]
+            land_r[j, 2] = land_r[j, 2] + land_c[chunk(j), y, 3]
             go_right(j, 3, land_r.at[j, pl.ds(2, 1)]).start()
 
     def next_hop(j):
@@ -588,30 +668,30 @@
         def _():
             go_right(j, 1, land_r.at[j]).wait_recv()
             for k in (2, 3):
-                land_r[j, k - 1] = land_r[j, k - 1] + land_c[j, y, k]
+                land_r[j, k - 1] = land_r[j, k - 1] + land_c[chunk(j), y, k]
             go_right(j, 2, land_r.at[j, pl.ds(1, 2)]).start()
 
         @pl.when(z == 2)
         def _():
             go_left(j, 3, land_l.at[j]).wait_recv()
             for k in (0, 1):
-                land_l[j, k] = land_l[j, k] + land_c[j, y, k]
+                land_l[j, k] = land_l[j, k] + land_c[chunk(j), y, k]
             go_left(j, 2, land_l.at[j, pl.ds(0, 2)]).start()
 
     def first_hop(j):
         to_y(j).wait_recv()
-        land_c[j, y] = land_c[j, y] + land_y[j]
+        land_c[chunk(j), y] = land_c[chunk(j), y] + land_y[j]
 
         @pl.when(z == 0)
         def _():
-            go_right(j, 1, land_c.at[j, y, pl.ds(1, 3)]).start()
+            go_right(j, 1, land_c.at[chunk(j), y, pl.ds(1, 3)]).start()
 
         @pl.when(z == last)
         def _():
-            go_left(j, 3, land_c.at[j, y, pl.ds(0, 3)]).start()
+            go_left(j, 3, land_c.at[chunk(j), y, pl.ds(0, 3)]).start()
 
     def result(j):
-        mine = land_c[j, y, z].astype(F32)
+        mine = land_c[chunk(j), y, z].astype(F32)
 
         @pl.when(z == 0)
         def _():
@@ -631,21 +711,42 @@
             go_right(j, 3, land_r.at[j, pl.ds(2, 1)]).wait_recv()
             tmp[...] = mine + land_r[j, 2].astype(F32)
 
+        emit(chunk(j))
+
+    def emit(j):
         group = j // 3
 
-        @pl.when(j >= early)
-        def _():
-            first_out[:, columns(j - early)] = tmp[...]
-
-        for m in range(2):
+        @pl.when(jnp.logical_and(j < early, j % 3 == 0))
+        def _():
+            down_out[columns(group), :] = tmp[...].T
+
+        for m in (1, 2):
 
             @pl.when(jnp.logical_and(j < early, j % 3 == m))
             def _():
-                pair_out[:, columns(group + m * (early // 3))] = tmp[...]
-
-        @pl.when(jnp.logical_and(j < early, j % 3 == 2))
-        def _():
-            down_out[columns(group), :] = tmp[...].T
+                pair_out[:, columns(group + (m - 1) * (early // 3))] = tmp[...]
+
+        for odd in range(2):
+            two = slice(HD, 3 * HD) if odd else slice(0, 2 * HD)
+            one = slice(0, HD) if odd else slice(2 * HD, 3 * HD)
+
+            def when(n, body, odd=odd):
+                pl.when(jnp.logical_and(j == early + n, z % 2 == odd))(body)
+
+            def store(out, place, part):
+                def body():
+                    out[:, place] = tmp[:, part]
+
+                return body
+
+            whole, low, high = slice(0, 128), slice(0, HD), slice(HD, 128)
+            for n in range(3):
+                when(n, store(joint_out.at[n], two, whole))
+            when(3, store(joint_out.at[0], one, low))
+            when(3, store(joint_out.at[1], one, high))
+            when(4, store(joint_out.at[2], one, low))
+            when(4, store(mix_out, one, high))
+            when(5, store(mix_out, two, whole))
 
     def round_(i):
         stage(i, 0, lambda j: to_y(j).start())
@@ -653,6 +754,12 @@
         stage(i, 4, next_hop)
         stage(i, 2, first_hop)
         stage(i, 8, result)
+        for b in range(FAR):
+            rounds = (4 + 3 * b, 7 + 3 * b, 10 + 3 * b, 13 + 3 * b, usual - 1 + b, usual + 3 + b)
+            bodies = (far_first, far_next, far_last, far_sum, lambda b: far_across(b).start(), far_result)
+            for at, body in zip(rounds, bodies):
+                pl.when(i == at)(functools.partial(body, b))
+
         for k in range(4):
 
             @pl.when(i == 3 * k + 8)
@@ -668,6 +775,8 @@
     @pl.when(step == 0)
     def _():
         dy_copy.start()
+        o_copy.start()
+        wb_copy.start()
         greet(near)
         greet(across)
         greet(far)
@@ -705,7 +814,7 @@
         up = gu_ref[0, 1].astype(F32)
         s = 1.0 / (1.0 + jnp.exp(-gate))
         silu = gate * s
-        wg, wu, wd = unit_weights(lambda t, m: wa_ref[:, t, :, 128 * m : 128 * m + 128].reshape(width, 128))
+        wd, wg, wu = unit_weights(lambda t, m: wa_ref[:, t, :, 128 * m : 128 * m + 128].reshape(width, 128))
         place = step % 2
 
         def put(m, grad):
@@ -714,13 +823,29 @@
                     grad[:, 128 * t : 128 * t + 128].astype(BF).reshape(2, 2, -1, 128)
                 )
 
-        put(2, dg(df[...], (silu * up).astype(BF), TN))
+        j = 3 * step
+
+        def earlier(m):
+            pl.when(step > (1 if m == 0 else 0))(lambda: add_core(j - 3 + m))
+
+        put(0, dg(df[...], (silu * up).astype(BF), TN))
+        to_core(j).start()
+        earlier(0)
         d_act = dg(df[...], wd, NN)
         d_gate = (d_act * up * (s * (1.0 + gate * (1.0 - s)))).astype(BF)
         d_up = (d_act * silu).astype(BF)
-        put(0, dg(hb[...], d_gate, TN))
-        put(1, dg(hb[...], d_up, TN))
-        send_cores(step)
+        put(1, dg(hb[...], d_gate, TN))
+        to_core(j + 1).start()
+        earlier(1)
+
+        @pl.when(step == 0)
+        def _():
+            add_core(0)
+            round_(0)
+
+        put(2, dg(hb[...], d_up, TN))
+        to_core(j + 2).start()
+        earlier(2)
         acc[...] += dg(d_gate, wg, NT) + dg(d_up, wu, NT)
 
     @pl.when(step == FIRST_PAIR - 1)
@@ -739,6 +864,13 @@
     cos, sin = cos_ref[:, pl.ds(c * rows, rows)], sin_ref[:, pl.ds(c * rows, rows)]
     in_pairs = jnp.logical_and(step >= FIRST_PAIR, step < FIRST_JOINT)
     p = step - FIRST_PAIR
+
+    @pl.when(step == FIRST_PAIR)
+    def _():
+        for m in range(3):
+            add_core(3 * FIRST_PAIR - 3 + m)
+        o_copy.wait()
+        wb_copy.wait()
 
     @pl.when(jnp.logical_and(in_pairs, p % 3 == 0))
     def _():
@@ -803,8 +935,7 @@
 
     @pl.when(step == LAST_STEP)
     def _():
-        for k in range(2):
-            send_cores(early // 3 + k)
+        lax.fori_loop(early, parts, lambda j, t: (to_core(j).start(), t)[1], 0)
 
         @pl.when(section == 0)
         def _():
@@ -821,20 +952,17 @@
             def _():
                 end_home(i).start()
 
-    @pl.when(step < FIRST_PAIR)
-    def _():
-        add_cores(step)
-
-    @pl.when(step == 0)
-    def _():
-        round_(0)
-
-    round_(step + 1)
+    @pl.when(step == 1)
+    def _():
+        round_(1)
+
+    @pl.when(step >= 1)
+    def _():
+        round_(step + 1)
 
     @pl.when(step == LAST_STEP)
     def _():
-        for k in range(2):
-            add_cores(early // 3 + k)
+        lax.fori_loop(early, parts, lambda j, t: (add_core(j), t)[1], 0)
         end_rows = e_send.shape[1] // 8
 
         def late(i, carry):
@@ -849,7 +977,7 @@
             return carry
 
         lax.fori_loop(LAST_STEP + 2, LAST_STEP + 10, late, 0)
-        lax.fori_loop(LAST_STEP + 10, parts + 8, lambda i, t: (round_(i), t)[1], 0)
+        lax.fori_loop(LAST_STEP + 10, usual + 8, lambda i, t: (round_(i), t)[1], 0)
         for i in range(2):
 
             @pl.when(at_home(i))
@@ -868,7 +996,7 @@
 
             @pl.when(z == 0)
             def _():
-                go_right(j, 1, land_c.at[j, y, pl.ds(1, 3)]).wait_send()
+                go_right(j, 1, land_c.at[chunk(j), y, pl.ds(1, 3)]).wait_send()
 
             @pl.when(z == 1)
             def _():
@@ -882,11 +1010,37 @@
 
             @pl.when(z == last)
             def _():
-                go_left(j, 3, land_c.at[j, y, pl.ds(0, 3)]).wait_send()
+                go_left(j, 3, land_c.at[chunk(j), y, pl.ds(0, 3)]).wait_send()
 
             return carry
 
-        lax.fori_loop(0, parts, finish, 0)
+        lax.fori_loop(0, usual, finish, 0)
+
+        def finish_far(b, carry):
+            j = FAR_AT + b
+            far_across(b).wait_send()
+
+            @pl.when(z == 0)
+            def _():
+                far_right(b, 1, land_c.at[j, :, pl.ds(1, 3)]).wait_send()
+
+            @pl.when(z == 1)
+            def _():
+                far_right(b, 2, far_r.at[b, :, pl.ds(1, 2)]).wait_send()
+                far_left(b, 1, far_l.at[b, :, pl.ds(0, 1)]).wait_send()
+
+            @pl.when(z == 2)
+            def _():
+                far_right(b, 3, far_r.at[b, :, pl.ds(2, 1)]).wait_send()
+                far_left(b, 2, far_l.at[b, :, pl.ds(0, 2)]).wait_send()
+
+            @pl.when(z == last)
+            def _():
+                far_left(b, 3, land_c.at[j, :, pl.ds(0, 3)]).wait_send()
+
+            return carry
+
+        lax.fori_loop(0, FAR, finish_far, 0)
 
 
 def last_back(x, y, dy, kept, w, norms, cost, sint):
@@ -916,23 +1070,25 @@
             once((rows, width)), once((rows, 128)), once((rows, width)), once((rows, 128)),
             pl.BlockSpec((1, 2, rows, 512), lambda i: (jnp.minimum(i, FIRST_PAIR - 1), 0, 0, 0)),
             pl.BlockSpec(group, lambda i: (0, 0, 0, jnp.where(i < FIRST_PAIR, 2 + i, 0))),
-            once(group, (0, 0, 0, 1)),
             once((2, width)), once((2, width)),
-            once((heads, rows, 128)),
             pair, pair, pair, pair, pair,
             by_pair((1, 2, 8, rows)),
             once(cost.shape), once(sint.shape),
-            hbm, hbm, hbm, hbm,
+            hbm, hbm, hbm, hbm, hbm, hbm,
         ],
-        out_specs=[once((depth, width)), once((depth, 2 * units)), once((units, depth)), once(halves), once((8, width))],
+        out_specs=[
+            once((3, depth, depth)), once((depth, depth)), once((depth, 2 * units)), once((units, depth)), once(halves), once((8, width)),
+        ],
         out_shape=[
-            sds((depth, width), F32), sds((depth, 2 * units), F32), sds((units, depth), F32),
+            sds((3, depth, depth), F32), sds((depth, depth), F32), sds((depth, 2 * units), F32), sds((units, depth), F32),
             sds(halves, BF), sds((8, width), F32),
         ],
         scratch_shapes=[
             VM((rows, width), F32),
             VM((rows, width), BF),
             VM((rows, width), BF),
+            VM((heads, rows, 128), BF),
+            VM(group, BF),
             VM((2, 2, 2, 4, depth, GROUP), BF),
             VM((3, rows, 128), BF),
             VM((2, width, 384), BF),
@@ -945,25 +1101,30 @@
             VM(halves, BF),
             VM((depth, WIDE), F32),
             VM((parts, 2, 4, depth, WIDE), BF),
-            VM((parts, 4, depth, WIDE), BF),
-            VM((parts, 3, depth, WIDE), BF),
-            VM((parts, 3, depth, WIDE), BF),
+            VM((parts - FAR, 4, depth, WIDE), BF),
+            VM((parts - FAR, 3, depth, WIDE), BF),
+            VM((parts - FAR, 3, depth, WIDE), BF),
             VM((8, 8, width), F32),
-            dma, dma, dma, dma,
+            VM((FAR, 2, depth, WIDE), BF),
+            VM((FAR, depth, WIDE), BF),
+            VM((FAR, 2, 3, depth, WIDE), BF),
+            VM((FAR, 2, 3, depth, WIDE), BF),
+            dma, dma, dma, dma, dma, dma,
             dma((6,)), dma((6,)), dma, dma((2,)), dma((2,)),
         ]
         + [dma((parts,))] * 8
-        + [dma((4,))] * 2,
+        + [dma((4,))] * 2
+        + [dma((FAR,))] * 6,
         compiler_params=pltpu.CompilerParams(collective_id=0, has_side_effects=True, vmem_limit_bytes=63 << 20),
         name="last",
-    )(n1, i1, n2, i2, gu, w, w, gains, biases, o, q, k, v, ko, vo, l, cost, sint, dy.reshape(halves), x, y.reshape(halves), e)
+    )(n1, i1, n2, i2, gu, w, gains, biases, q, k, v, ko, vo, l, cost, sint, dy.reshape(halves), x, y.reshape(halves), e, o, w)
 
 
 LAG = 6
 
 
 def first_kernel(
-    parts, tok_ref, shard_ref, extra_ref, len_ref, cos_ref, sin_ref, cost_ref, sint_ref,
+    parts, tok_ref, top_ref, shard_ref, gain_ref, bias_ref, len_ref, cos_ref, sin_ref, cost_ref, sint_ref,
     w_out, q_out, k_out, v_out, ko_out, vo_out, y_out, e_out, o_out, gu_out, n1_out, n2_out,
     x_out, dy_out, l_out, i1_out, i2_out, norm_out,
     w, xin, q, kv, land_kv, late_kv, o, hb, acc, relay, land_rows, ext, lens,
@@ -993,11 +1154,15 @@
     def at_home(i):
         return jnp.logical_and(side == c, 2 * c + i == z)
 
-    def token_copy(i, part):
-        return remote(tok_ref.at[i, part], xin.at[z % 2, part], tok_send.at[i], tok_recv.at[z % 2], target(i))
-
-    def token_home(i):
-        return pltpu.make_async_copy(tok_ref.at[i], xin.at[z % 2], tok_sem)
+    def token_copy(src, i, part):
+        return remote(src.at[i, part], xin.at[z % 2, part], tok_send.at[i], tok_recv.at[z % 2], target(i))
+
+    def token_home(src, i):
+        return pltpu.make_async_copy(src.at[i], xin.at[z % 2], tok_sem)
+
+    def by_section(body):
+        for n, src in enumerate((tok_ref, top_ref)):
+            pl.when(section == n)(functools.partial(body, src))
 
     load = pltpu.make_async_copy(shard_ref, w.at[y, c, z], shard_sem)
     load.start()
@@ -1022,7 +1187,8 @@
     count = 5 + jnp.where(z < last, 1, 0) + jnp.where(z > 0, 1, 0) - jnp.where(side == c, 1, 0)
     pl.semaphore_wait(barrier, count)
 
-    ext[y, c] = extra_ref[...]
+    ext[y, c, 0:1] = gain_ref[...].astype(F32)
+    ext[y, c, 1:2] = bias_ref[...].astype(F32)
     lens[c] = len_ref[...]
 
     def small(k):
@@ -1122,7 +1288,7 @@
 
         @pl.when(at_home(i))
         def _():
-            token_home(i).start()
+            by_section(lambda src: token_home(src, i).start())
 
     def early(r, carry):
         round_(r)
@@ -1131,7 +1297,7 @@
 
             @pl.when(jnp.logical_not(at_home(i)))
             def _():
-                token_copy(i, part).start()
+                by_section(lambda src: token_copy(src, i, part).start())
 
         return carry
 
@@ -1156,21 +1322,19 @@
     rounds(16, start)
 
     small(2).wait()
-    halves = [ext[i // 2, i % 2].astype(F32) for i in range(4)]
     for k in range(2):
         for half in range(2):
-            pieces = [halves[2 * half + i][3 * k + m : 3 * k + m + 1] for i in range(2) for m in range(3)]
-            norm_out[2 * k + half : 2 * k + half + 1] = jnp.concatenate(pieces, axis=1)
+            norm_out[2 * k + half : 2 * k + half + 1] = jnp.concatenate([ext[half, i, k : k + 1] for i in range(2)], axis=1)
 
     for i in range(2):
 
         @pl.when(at_home(i))
         def _():
-            token_home(i).wait()
+            token_home(tok_ref, i).wait()
 
         @pl.when(jnp.logical_not(at_home(i)))
         def _():
-            token_copy(i, pl.ds(0, xin.shape[1])).wait_send()
+            token_copy(tok_ref, i, pl.ds(0, xin.shape[1])).wait_send()
             remote(tok_ref.at[i], xin.at[i], tok_send.at[i], tok_recv.at[i], target(i)).wait_recv()
 
     def project(at, count, x):
@@ -1237,7 +1401,7 @@
         )
 
     def unit(k, save):
-        wg, wu, wd = group_of(k)
+        wd, wg, wu = group_of(k)
         gate = dg(hb[...], wg, NN)
         up = dg(hb[...], wu, NN)
         save(gate, up)
@@ -1379,7 +1543,7 @@
             units_in(p).start()
 
         def unit_back(k, carry):
-            wg, wu, wd = group_of(k)
+            wd, wg, wu = group_of(k)
             units_in(k).wait()
             gate = gu[k % 2, 0].astype(F32)
             up = gu[k % 2, 1].astype(F32)
@@ -1482,7 +1646,7 @@
     lax.fori_loop(0, parts, finish, 0)
 
 
-def first_layer(tokens, shard, extra, lengths, cos, sin, cost, sint):
+def first_layer(tokens, top, shard, gains, biases, lengths, cos, sin, cost, sint):
     micro, own, width = tokens.shape
     depth, columns = shard.shape
     rows = 2 * own
@@ -1493,7 +1657,7 @@
     vm = pl.BlockSpec(memory_space=VM)
     return pl.pallas_call(
         functools.partial(first_kernel, parts),
-        in_specs=[hbm, hbm] + [vm] * 6,
+        in_specs=[hbm] * 3 + [vm] * 7,
         out_specs=[hbm] * 12 + [vm] * 6,
         out_shape=[sds((2, 2, 4, depth, columns), BF)]
         + [sds((heads, rows, 128), BF)] * 5
@@ -1523,7 +1687,7 @@
             VM((rows, width), F32),
             VM((4, rows // 4, width), BF),
             VM((4, rows // 4, width), BF),
-            VM((2, 2) + extra.shape, BF),
+            VM((2, 2, 8, gains.shape[1]), F32),
             VM((2,) + lengths.shape, jnp.int32),
             VM((2 * rows, rows), F32),
             VM((2, 2, 2 * rows, rows), BF),
@@ -1545,7 +1709,7 @@
         ],
         compiler_params=pltpu.CompilerParams(collective_id=1, has_side_effects=True, vmem_limit_bytes=63 << 20),
         name="first",
-    )(tokens, shard, extra, lengths, cos, sin, cost, sint)
+    )(tokens, top, shard, gains, biases, lengths, cos, sin, cost, sint)
 
 
 def swap_pairs(tp, step, dp_axes):
@@ -1606,7 +1770,7 @@
     first = jnp.concatenate(
         [heads[:, :, :2].reshape(rows, -1), heads[:, :, 2].reshape(rows, -1), mine[:, 2], mine[:, :2].reshape(rows, -1)], axis=1
     )
-    units = jnp.concatenate([w_gate_up, w_down.T[:, None]], axis=1)
+    units = jnp.concatenate([w_down.T[:, None], w_gate_up], axis=1)
     units = units.reshape(rows, 3, -1, 128).transpose(0, 2, 1, 3)
     return jnp.concatenate([first, units.reshape(rows, -1)], axis=1)
 
@@ -1658,20 +1822,17 @@
     rows = length // 2
     shard = pack_shard(w_qkv[0], w_out[0], w_gate_up[0], w_down[0])
     if dp == 4 and tp == 4:
-        extra = jnp.concatenate([norm_gains.reshape(-1, 128), norm_biases.reshape(-1, 128)])
-        extra = jnp.pad(extra, ((0, 16 - extra.shape[0]), (0, 0)))
-        padded = jnp.pad(lengths, ((0, 8 - lengths.shape[0]), (0, 128 - lengths.shape[1])))
         wide, signed, cost, sint = host_tables(length)
-        rows_in = jnp.where(section == 0, tokens, cotangent)
         (
             weights, q, k, v, ko, vo, y, e, o, gu, n1, n2, inputs, dy, l, i1, i2, small,
-        ) = first_layer(rows_in, shard, extra, padded, wide, signed, cost, sint)
+        ) = first_layer(tokens, cotangent, shard, norm_gains, norm_biases, lengths, wide, signed, cost, sint)
         weights = weights.reshape((BLOCKS,) + weights.shape[2:])
         norms = (small[:2], small[2:])
         kept = (q, k, v, ko, vo, o, e, l, gu, n1, i1, n2, i2)
-        first, pair, down, ends, total = last_back(inputs, y, dy, kept, weights, norms, cost, sint)
+        joint, mix, pair, down, ends, total = last_back(inputs, y, dy, kept, weights, norms, cost, sint)
         small = lax.dynamic_slice_in_dim(total[:4].reshape(2, dp * tp, -1), lax.axis_index(ALL), 1, 1)
         gains, biases = small[0, 0], small[1, 0]
+        joint, mix = joint.transpose(1, 0, 2), mix.T
     else:
         near = core * rows + jnp.arange(rows, dtype=jnp.int32)
         far = (1 - core) * rows + jnp.arange(rows, dtype=jnp.int32)
@@ -1706,10 +1867,10 @@
         mine = scatter_sum(g, dp, tp)
         first = mine[:, :width]
         units = mine[:, width:].reshape(first.shape[0], -1, 3, 128).transpose(0, 2, 1, 3).reshape(first.shape[0], 3, -1)
-        pair, down = units[:, :2], units[:, 2].T
+        pair, down = units[:, 1:], units[:, 0].T
+        joint, mix = unpack_first(first)
         gains = lax.psum_scatter(ng[0:2].reshape(-1), ALL, scatter_dimension=0, tiled=True)
         biases = lax.psum_scatter(ng[2:4].reshape(-1), ALL, scatter_dimension=0, tiled=True)
-    joint, mix = unpack_first(first)
     outs = (joint, mix, pair.reshape(pair.shape[0], 2, -1), down, gains, biases)
     return (ends[None],) + tuple(t[None] for t in outs)
 

time: 392 us -> 379 us (0.967)
  Pallas kernels: 364 us -> 356 us
    pallas_call x1, Pallas kernels: 137 us -> 128 us  [last_back(): pl.pallas_call(functools.partial(last_kernel, parts), grid=(LAST_STEP + 1...]
where the time goes in v8:
time: 379 us; the launch traced here: 375 us
  Pallas kernels  356 us (94%)
  local copies, waits for them, and re-layouts  17.9 us (5%)
    pallas_call x1, Pallas kernels, first_layer(): pl.pallas_call(functools.partial(first_kernel, parts), in_specs=[hbm] * 3...  228 us
    pallas_call x1, Pallas kernels, last_back(): pl.pallas_call(functools.partial(last_kernel, parts), grid=(LAST_STEP + 1...  128 us

profile of v8, /device:TPU:0, one launch (start us, length us, event | category | flops | bytes accessed | tf_op | source)
XLA Modules:
  0.0 375.4 jit_solution(16019809730729379110)
XLA Ops:
  0.6 0.0 copy-start.4
  0.7 1.1 copy.30
  1.9 0.1 copy.33
  2.0 0.1 copy.38
  2.1 0.0 copy-done.4
  2.1 0.2 copy.29
  2.3 0.0 copy-start.5
  2.3 0.0 copy-start.2
  2.3 0.1 maximum_select_fusion
  2.4 0.1 copy.36
  2.6 0.1 copy.37
  2.7 0.6 copy-done.5
  3.2 0.3 concatenate.21
  3.6 0.0 copy-done.2
  3.6 0.1 copy.34
  3.7 0.7 concatenate.22
  4.3 0.2 maximum_bitcast_fusion
  4.6 1.2 copy.35
  5.8 0.8 reshape.46
  6.6 1.7 concatenate.24.shard_ref
  8.4 227.9 %first.1 = (bf16[2,2,4,192,3072]{4,3,2,1,0:T(8,128)(2,1)}, bf16[6,512,128]{2,1,0:T(8,128)(2,1)}, bf16[6,512,128]{2,1,0:T(8,128)(2,1)}, bf16[6,512,128]{2,1,0:T(8...) custom-call(bf16[2,256,768]{2,1,0:T(8,128)(2,1)} %tok_ref.1, ...), custom_call_target="tpu_custom_call" | custom-call | tf_op jit(solution)/shard_map/first/pallas_call | solution.py:1658
  236.3 1.4 fusion
  237.7 128.2 %last.1 = (f32[3,192,192]{2,1,0:T(8,128)}, f32[192,192]{1,0:T(8,128)}, f32[192,1536]{1,0:T(8,128)}, f32[768,192]{1,0:T(8,128)}, bf16[2,256,768]{2,1,0:T(8,128)(2,1)}, /*index=5*/f32[8,768]{1,0:T(8,128)}) custom-call(bf16[512,768]{1,0:T(8,128)(2,1)} %get-tuple-element.31.n1_ref, f32[512,128]{1,0:T(8,128)} %get-tuple-element.32.i1_ref, ...), custom_call_target="tpu_custom_call" | custom-call | tf_op jit(solution)/shard_map/last/pallas_call | solution.py:1066
  365.9 0.0 copy-start
  365.9 0.8 slice.53
  366.7 0.1 reshape.50
  366.8 0.5 dynamic-slice_bitcast_fusion
  367.3 1.7 copy.39
  369.1 2.2 copy.40
  371.3 0.0 copy-done
  371.3 0.0 copy-start.1
  371.3 1.8 broadcast_in_dim_reshape.3
  373.1 0.0 copy-done.1
  373.1 0.0 copy-start.3
  373.1 0.9 copy.43
  373.9 0.5 copy-done.3
  374.4 0.8 copy.44
  (9 shorter events, 0.1 us)
Async XLA Ops:
  0.6 1.4 copy-start.4
  2.3 1.0 copy-start.5
  2.3 1.3 copy-start.2
  365.9 5.4 %copy-start = (f32[192,1536]{1,0:T(8,128)S(1)}, f32[192,1536]{1,0:T(8,128)}, u32[]{:S(2)}) copy-start(f32[192,1536]{1,0:T(8,128)} %get-tuple-element.52) | copy-start | bytes 3538948
  371.3 1.8 copy-start.1
  373.1 1.3 copy-start.3

commit v9 on v8

--- a/solution.py
+++ b/solution.py
@@ -484,7 +484,7 @@
 FAR = 2
 FAR_AT = 4
 def last_kernel(
-    parts, n1_ref, i1_ref, n2_ref, i2_ref, gu_ref, wa_ref, gain_ref, bias_ref,
+    parts, n1_ref, i1_ref, n2_ref, i2_ref, gu_ref, wa_ref, norm_ref,
     q_ref, k_ref, v_ref, ko_ref, vo_ref, l_ref, cos_ref, sin_ref, dy_hbm, x_hbm, y_hbm, e_hbm, o_hbm, w_hbm,
     joint_out, mix_out, pair_out, down_out, ends_out, norm_out,
     acc, df, hb, o_ref, wb_ref, ring, do3, dwo, dq, keep, oth, got, eb, e_send, e_land, tmp, land_c, land_y, land_r, land_l, land_n,
@@ -718,7 +718,7 @@
 
         @pl.when(jnp.logical_and(j < early, j % 3 == 0))
         def _():
-            down_out[columns(group), :] = tmp[...].T
+            down_out[:, columns(group)] = tmp[...]
 
         for m in (1, 2):
 
@@ -736,6 +736,12 @@
             def store(out, place, part):
                 def body():
                     out[:, place] = tmp[:, part]
+
+                return body
+
+            def turn(place, part):
+                def body():
+                    mix_out[place, :] = tmp[...].T[part]
 
                 return body
 
@@ -745,8 +751,8 @@
             when(3, store(joint_out.at[0], one, low))
             when(3, store(joint_out.at[1], one, high))
             when(4, store(joint_out.at[2], one, low))
-            when(4, store(mix_out, one, high))
-            when(5, store(mix_out, two, whole))
+            when(4, turn(one, high))
+            when(5, turn(two, whole))
 
     def round_(i):
         stage(i, 0, lambda j: to_y(j).start())
@@ -803,10 +809,10 @@
         land_n[0] = jnp.zeros(land_n.shape[1:], F32)
         land_n[0, 1:2] = jnp.sum(dy * n, axis=0, keepdims=True)
         land_n[0, 3:4] = jnp.sum(dy, axis=0, keepdims=True)
-        dr2 = norm_back(dy * gain_ref[1:2], n, i2_ref[:, :1])
+        dr2 = norm_back(dy * norm_ref[1:2], n, i2_ref[:, :1])
         acc[...] = dr2
         df[...] = dr2.astype(BF)
-        hb[...] = (n1_ref[...].astype(F32) * gain_ref[0:1] + bias_ref[0:1]).astype(BF)
+        hb[...] = (n1_ref[...].astype(F32) * norm_ref[0:1] + norm_ref[2:3]).astype(BF)
 
     @pl.when(step < FIRST_PAIR)
     def _():
@@ -854,7 +860,7 @@
         n = n1_ref[...].astype(F32)
         land_n[0, 0:1] = jnp.sum(dh * n, axis=0, keepdims=True)
         land_n[0, 2:3] = jnp.sum(dh, axis=0, keepdims=True)
-        dr1 = norm_back(dh * gain_ref[0:1], n, i1_ref[:, :1])
+        dr1 = norm_back(dh * norm_ref[0:1], n, i1_ref[:, :1])
         acc[...] = dr1
         df[...] = dr1.astype(BF)
         x_copy.start()
@@ -1045,7 +1051,6 @@
 
 def last_back(x, y, dy, kept, w, norms, cost, sint):
     q, k, v, ko, vo, o, e, l, gu, n1, i1, n2, i2 = kept
-    gains, biases = norms
     rows, width = x.shape
     heads = width // 128
     depth, columns = w.shape[2:]
@@ -1070,17 +1075,17 @@
             once((rows, width)), once((rows, 128)), once((rows, width)), once((rows, 128)),
             pl.BlockSpec((1, 2, rows, 512), lambda i: (jnp.minimum(i, FIRST_PAIR - 1), 0, 0, 0)),
             pl.BlockSpec(group, lambda i: (0, 0, 0, jnp.where(i < FIRST_PAIR, 2 + i, 0))),
-            once((2, width)), once((2, width)),
+            once((4, width)),
             pair, pair, pair, pair, pair,
             by_pair((1, 2, 8, rows)),
             once(cost.shape), once(sint.shape),
             hbm, hbm, hbm, hbm, hbm, hbm,
         ],
         out_specs=[
-            once((3, depth, depth)), once((depth, depth)), once((depth, 2 * units)), once((units, depth)), once(halves), once((8, width)),
+            once((3, depth, depth)), once((depth, depth)), once((depth, 2 * units)), once((depth, units)), once(halves), once((8, width)),
         ],
         out_shape=[
-            sds((3, depth, depth), F32), sds((depth, depth), F32), sds((depth, 2 * units), F32), sds((units, depth), F32),
+            sds((3, depth, depth), F32), sds((depth, depth), F32), sds((depth, 2 * units), F32), sds((depth, units), F32),
             sds(halves, BF), sds((8, width), F32),
         ],
         scratch_shapes=[
@@ -1117,19 +1122,20 @@
         + [dma((FAR,))] * 6,
         compiler_params=pltpu.CompilerParams(collective_id=0, has_side_effects=True, vmem_limit_bytes=63 << 20),
         name="last",
-    )(n1, i1, n2, i2, gu, w, gains, biases, q, k, v, ko, vo, l, cost, sint, dy.reshape(halves), x, y.reshape(halves), e, o, w)
+    )(n1, i1, n2, i2, gu, w, norms, q, k, v, ko, vo, l, cost, sint, dy.reshape(halves), x, y.reshape(halves), e, o, w)
 
 
 LAG = 6
+GATHER = 256
 
 
 def first_kernel(
-    parts, tok_ref, top_ref, shard_ref, gain_ref, bias_ref, len_ref, cos_ref, sin_ref, cost_ref, sint_ref,
+    parts, tok_ref, top_ref, lead_ref, down_ref, pair_ref, gain_ref, bias_ref, len_ref, cos_ref, sin_ref, cost_ref, sint_ref,
     w_out, q_out, k_out, v_out, ko_out, vo_out, y_out, e_out, o_out, gu_out, n1_out, n2_out,
     x_out, dy_out, l_out, i1_out, i2_out, norm_out,
     w, xin, q, kv, land_kv, late_kv, o, hb, acc, relay, land_rows, ext, lens,
     mask, eb, gu, n1, n2, df, do3, dq, keep, oth, got, d,
-    tok_sem, tok_send, tok_recv, shard_sem, back_sem, kv_send, kv_recv, out_sem, row_send, row_recv,
+    tok_sem, tok_send, tok_recv, lead_sem, shard_sem, back_sem, kv_send, kv_recv, out_sem, row_send, row_recv, again_send, again_recv,
     e_sem, gu_sem, oth_send, oth_recv, dz_send, dz_recv,
     small_send, small_recv, rs_sem, rr_sem, ls_sem, lr_sem, ys_sem, yr_sem, cs_sem, cr_sem,
 ):
@@ -1164,8 +1170,18 @@
         for n, src in enumerate((tok_ref, top_ref)):
             pl.when(section == n)(functools.partial(body, src))
 
-    load = pltpu.make_async_copy(shard_ref, w.at[y, c, z], shard_sem)
-    load.start()
+    groups = down_ref.shape[1] // 128
+
+    def load_group(k, m):
+        src = down_ref if m == 0 else pair_ref
+        cols = pl.ds(128 * (k + (m - 1) * groups if m else k), 128)
+        return pltpu.make_async_copy(src.at[:, cols], w.at[y, c, z, :, pl.ds(width + GROUP * k + 128 * m, 128)], shard_sem.at[k, m])
+
+    load_lead = pltpu.make_async_copy(lead_ref, w.at[y, c, z, :, pl.ds(0, width)], lead_sem)
+    load_lead.start()
+    loads = [load_group(k, m) for k in range(groups) for m in range(3)]
+    for load in loads:
+        load.start()
     greet(near)
     greet(across)
     greet(other)
@@ -1200,10 +1216,12 @@
 
     small(0).start()
     small(1).start()
-    load.wait()
+    load_lead.wait()
+    for load in loads:
+        load.wait()
 
     def columns(j):
-        return pl.ds(pl.multiple_of(j * WIDE, WIDE), WIDE)
+        return pl.ds(pl.multiple_of(j * GATHER, GATHER), GATHER)
 
     def go_right(j, h):
         b = jnp.maximum(z - h, 0)
@@ -1281,9 +1299,8 @@
     def rounds(first, end):
         lax.fori_loop(first, end, lambda r, t: (round_(r), t)[1], 0)
 
-    lead_parts = width // WIDE
-    start = 17
-    token_rows = xin.shape[1] // 16
+    start = 9
+    token_rows = xin.shape[1] // 8
     for i in range(2):
 
         @pl.when(at_home(i))
@@ -1318,8 +1335,8 @@
         seg_q = seg_q + jnp.where(end <= at_q, 1, 0)
         seg_k = seg_k + jnp.where(end <= at_k, 1, 0)
     mask[...] = jnp.where(seg_k == seg_q, 0.0, neg_fill).astype(F32)
-    lax.fori_loop(3, 16, early, 0)
-    rounds(16, start)
+    lax.fori_loop(3, 8, early, 0)
+    rounds(8, start)
 
     small(2).wait()
     for k in range(2):
@@ -1379,7 +1396,7 @@
 
     def pair(p, carry):
         heads_of(p, land_kv, lambda h, e, inv: None)
-        round_(start + 1 + p)
+        pl.when(p % 2 == 1)(functools.partial(round_, start + 1 + p // 2))
         return carry
 
     def out_part(p):
@@ -1413,12 +1430,11 @@
     h = n * norm_out[0:1] + norm_out[2:3]
     hb[...] = h.astype(BF)
     acc[...] = h
-    rounds(start + 7, start + 8)
+    rounds(start + 4, start + 5)
 
     def units(k, carry):
-        @pl.when(k != 4)
-        def _():
-            round_(start + 8 + k - k // 5)
+        for at, r in ((2, 5), (4, 6), (4, 7), (5, 8)):
+            pl.when(k == at)(functools.partial(round_, start + r))
 
         unit(k, lambda gate, up: None)
         return carry
@@ -1429,6 +1445,10 @@
 
     def row_copy(b):
         return remote(relay.at[b], land_rows.at[b], row_send.at[b], row_recv.at[b], other)
+
+    def again(b):
+        part = pl.ds(pl.multiple_of(b * piece_rows, piece_rows), piece_rows)
+        return remote(kv.at[:, :, part], late_kv.at[:, :, part], again_send.at[b], again_recv.at[b], near)
 
     kept_out = []
 
@@ -1458,12 +1478,11 @@
             row_copy(b).wait_recv()
             x_out[pl.ds(at, piece_rows)] = land_rows[b]
             project(at, piece_rows, land_rows[b])
+            again(b).start()
             return carry
 
         lax.fori_loop(0, pieces, project_rows, 0)
-        again = remote(kv, late_kv, kv_send.at[1], kv_recv.at[1], near)
-        again.start()
-        again.wait()
+        lax.fori_loop(0, pieces, lambda b, t: (again(b).wait(), t)[1], 0)
 
     for src, dst in ((q, q_out), (kv.at[0], k_out), (kv.at[1], v_out), (late_kv.at[0], ko_out), (late_kv.at[1], vo_out)):
         keep_out(src, dst)
@@ -1646,18 +1665,20 @@
     lax.fori_loop(0, parts, finish, 0)
 
 
-def first_layer(tokens, top, shard, gains, biases, lengths, cos, sin, cost, sint):
+def first_layer(tokens, top, shards, gains, biases, lengths, cos, sin, cost, sint):
     micro, own, width = tokens.shape
-    depth, columns = shard.shape
+    lead_part, down, pair = shards
+    depth = lead_part.shape[0]
+    columns = lead_part.shape[1] + down.shape[1] + pair.shape[1]
     rows = 2 * own
-    parts = columns // WIDE
+    parts = columns // GATHER
     heads = width // 128
     dma = pltpu.SemaphoreType.DMA
     hbm = pl.BlockSpec(memory_space=pl.ANY)
     vm = pl.BlockSpec(memory_space=VM)
     return pl.pallas_call(
         functools.partial(first_kernel, parts),
-        in_specs=[hbm] * 3 + [vm] * 7,
+        in_specs=[hbm] * 5 + [vm] * 7,
         out_specs=[hbm] * 12 + [vm] * 6,
         out_shape=[sds((2, 2, 4, depth, columns), BF)]
         + [sds((heads, rows, 128), BF)] * 5
@@ -1701,7 +1722,7 @@
             VM((heads, 2, 128, rows), BF),
             VM((heads, 2, 128, rows), BF),
             VM((4, rows, 640), BF),
-            dma, dma((2,)), dma((2,)), dma, dma((parts,)), dma((2,)), dma((2,)), dma((9,)), dma((4,)), dma((4,)),
+            dma, dma((2,)), dma((2,)), dma, dma((6, 3)), dma((parts,)), dma((2,)), dma((2,)), dma((9,)), dma((4,)), dma((4,)), dma((4,)), dma((4,)),
             dma((2,)), dma((2,)), dma((6,)), dma((6,)), dma((4,)), dma((4,)),
             dma((3,)), dma((3,)),
             dma((parts, 3)), dma((parts, 3)), dma((parts, 3)), dma((parts, 3)),
@@ -1709,7 +1730,7 @@
         ],
         compiler_params=pltpu.CompilerParams(collective_id=1, has_side_effects=True, vmem_limit_bytes=63 << 20),
         name="first",
-    )(tokens, top, shard, gains, biases, lengths, cos, sin, cost, sint)
+    )(tokens, top, *shards, gains, biases, lengths, cos, sin, cost, sint)
 
 
 def swap_pairs(tp, step, dp_axes):
@@ -1770,8 +1791,12 @@
     first = jnp.concatenate(
         [heads[:, :, :2].reshape(rows, -1), heads[:, :, 2].reshape(rows, -1), mine[:, 2], mine[:, :2].reshape(rows, -1)], axis=1
     )
-    units = jnp.concatenate([w_down.T[:, None], w_gate_up], axis=1)
-    units = units.reshape(rows, 3, -1, 128).transpose(0, 2, 1, 3)
+    return first, w_down.T, w_gate_up.reshape(rows, -1)
+
+
+def join_shard(first, down, pair):
+    rows = first.shape[0]
+    units = jnp.concatenate([down, pair], axis=1).reshape(rows, 3, -1, 128).transpose(0, 2, 1, 3)
     return jnp.concatenate([first, units.reshape(rows, -1)], axis=1)
 
 
@@ -1820,24 +1845,23 @@
     assert micro * 2 == tp
     length = own * tp
     rows = length // 2
-    shard = pack_shard(w_qkv[0], w_out[0], w_gate_up[0], w_down[0])
+    shards = pack_shard(w_qkv[0], w_out[0], w_gate_up[0], w_down[0])
     if dp == 4 and tp == 4:
         wide, signed, cost, sint = host_tables(length)
         (
             weights, q, k, v, ko, vo, y, e, o, gu, n1, n2, inputs, dy, l, i1, i2, small,
-        ) = first_layer(tokens, cotangent, shard, norm_gains, norm_biases, lengths, wide, signed, cost, sint)
+        ) = first_layer(tokens, cotangent, shards, norm_gains, norm_biases, lengths, wide, signed, cost, sint)
         weights = weights.reshape((BLOCKS,) + weights.shape[2:])
-        norms = (small[:2], small[2:])
         kept = (q, k, v, ko, vo, o, e, l, gu, n1, i1, n2, i2)
-        joint, mix, pair, down, ends, total = last_back(inputs, y, dy, kept, weights, norms, cost, sint)
+        joint, mix, pair, down, ends, total = last_back(inputs, y, dy, kept, weights, small, cost, sint)
         small = lax.dynamic_slice_in_dim(total[:4].reshape(2, dp * tp, -1), lax.axis_index(ALL), 1, 1)
         gains, biases = small[0, 0], small[1, 0]
-        joint, mix = joint.transpose(1, 0, 2), mix.T
+        joint, down = joint.transpose(1, 0, 2), down.T
     else:
         near = core * rows + jnp.arange(rows, dtype=jnp.int32)
         far = (1 - core) * rows + jnp.arange(rows, dtype=jnp.int32)
         tabs = rope_tables(near)
-        weights = gather_shard(shard, dp, tp)
+        weights = gather_shard(join_shard(*shards), dp, tp)
         norms = jnp.concatenate([norm_gains, norm_biases])
         norms = lax.all_gather(norms, ("y", "core"), axis=1, tiled=True).astype(F32)
         norms = (norms[0].reshape(2, width), norms[1].reshape(2, width))

time: 379 us -> 382 us (level)
  Pallas kernels: 356 us -> 361 us
    pallas_call x1, Pallas kernels: 128 us -> 140 us  [last_back(): pl.pallas_call(functools.partial(last_kernel, parts), grid=(LAST_STEP + 1...]
    pallas_call x1, Pallas kernels: 228 us -> 221 us  [first_layer(): pl.pallas_call(functools.partial(first_kernel, parts), in_specs=[hbm] * 5...]
    unnamed x18 -> x6, local copies, waits for them, and re-layouts: 6.89 us -> 10.6 us
where the time goes in v9:
time: 382 us; the launch traced here: 379 us
  Pallas kernels  361 us (95%)
  local copies, waits for them, and re-layouts  16.4 us (4%)
    pallas_call x1, Pallas kernels, first_layer(): pl.pallas_call(functools.partial(first_kernel, parts), in_specs=[hbm] * 5...  221 us
    pallas_call x1, Pallas kernels, last_back(): pl.pallas_call(functools.partial(last_kernel, parts), grid=(LAST_STEP + 1...  140 us
    unnamed x6, local copies, waits for them, and re-layouts  10.6 us

profile of v9, /device:TPU:0, one launch (start us, length us, event | category | flops | bytes accessed | tf_op | source)
XLA Modules:
  0.0 379.3 jit_solution(4564135841995806833)
XLA Ops:
  0.7 1.1 copy.26
  1.8 0.1 copy.29
  1.9 0.1 copy.32
  2.0 1.1 copy.25
  3.2 0.1 maximum_select_fusion
  3.3 0.1 copy.30
  3.5 0.1 copy.31
  3.6 0.8 pad_maximum_fusion.lead_ref
  4.4 1.9 copy.33
  6.3 220.8 %first.1 = (bf16[2,2,4,192,3072]{4,3,2,1,0:T(8,128)(2,1)}, bf16[6,512,128]{2,1,0:T(8,128)(2,1)}, bf16[6,512,128]{2,1,0:T(8,128)(2,1)}, bf16[6,512,128]{2,1,0:T(8...) custom-call(bf16[2,256,768]{2,1,0:T(8,128)(2,1)} %tok_ref.1, ...), custom_call_target="tpu_custom_call" | custom-call | tf_op jit(solution)/shard_map/first/pallas_call | solution.py:1679
  227.1 140.2 %last.1 = (f32[3,192,192]{2,1,0:T(8,128)}, f32[192,192]{1,0:T(8,128)}, f32[192,1536]{1,0:T(8,128)}, f32[192,768]{1,0:T(8,128)}, bf16[2,256,768]{2,1,0:T(8,128)(2,1)}, /*index=5*/f32[8,768]{1,0:T(8,128)}) custom-call(bf16[512,768]{1,0:T(8,128)(2,1)} %get-tuple-element.31.n1_ref, f32[512,128]{1,0:T(8,128)} %get-tuple-element.32.i1_ref, ...), custom_call_target="tpu_custom_call" | custom-call | tf_op jit(solution)/shard_map/last/pallas_call | solution.py:1071
  367.3 0.7 slice.45
  368.1 0.1 reshape.41
  368.1 0.5 dynamic-slice_bitcast_fusion
  368.7 3.0 broadcast_in_dim_reshape.3
  371.6 2.1 copy.38
  373.7 1.9 copy.39
  375.6 1.6 copy.40
  377.2 1.9 copy.41
  (9 shorter events, 0.1 us)

commit v10 on v9

--- a/solution.py
+++ b/solution.py
@@ -1896,7 +1896,8 @@
         gains = lax.psum_scatter(ng[0:2].reshape(-1), ALL, scatter_dimension=0, tiled=True)
         biases = lax.psum_scatter(ng[2:4].reshape(-1), ALL, scatter_dimension=0, tiled=True)
     outs = (joint, mix, pair.reshape(pair.shape[0], 2, -1), down, gains, biases)
-    return (ends[None],) + tuple(t[None] for t in outs)
+    here = section >= 0
+    return tuple(jnp.where(here, t, jnp.zeros_like(t))[None] for t in (ends,) + outs)
 
 
 def solution(mesh):

time: 382 us -> 376 us (0.984)
  local copies, waits for them, and re-layouts: 16.4 us -> 5.44 us
  other arithmetic: 0.93 us -> 6.15 us
    unnamed x6 -> x16, local copies, waits for them, and re-layouts: 10.6 us -> 2.89 us
where the time goes in v10:
time: 376 us; the launch traced here: 374 us
  Pallas kernels  361 us (96%)
  other arithmetic  6.15 us (2%)
  local copies, waits for them, and re-layouts  5.44 us (1%)
    pallas_call x1, Pallas kernels, first_layer(): pl.pallas_call(functools.partial(first_kernel, parts), in_specs=[hbm] * 5...  221 us
    pallas_call x1, Pallas kernels, last_back(): pl.pallas_call(functools.partial(last_kernel, parts), grid=(LAST_STEP + 1...  140 us

profile of v10, /device:TPU:0, one launch (start us, length us, event | category | flops | bytes accessed | tf_op | source)
XLA Modules:
  0.0 373.6 jit_solution(11158333365599228028)
XLA Ops:
  0.6 1.1 copy.25
  1.8 0.0 copy-start.5
  1.8 0.1 maximum_select_fusion
  1.9 0.1 copy.30
  2.1 0.0 copy-start.1
  2.1 0.1 copy.31
  2.2 0.5 copy-done.5
  2.7 0.2 copy.26
  2.9 0.1 copy.29
  3.1 0.1 copy.32
  3.2 0.8 pad_maximum_fusion.lead_ref
  4.0 0.0 copy-done.1
  4.0 0.9 copy.33
  4.9 220.7 %first.1 = (bf16[2,2,4,192,3072]{4,3,2,1,0:T(8,128)(2,1)}, bf16[6,512,128]{2,1,0:T(8,128)(2,1)}, bf16[6,512,128]{2,1,0:T(8,128)(2,1)}, bf16[6,512,128]{2,1,0:T(8...) custom-call(bf16[2,256,768]{2,1,0:T(8,128)(2,1)} %tok_ref.1, ...), custom_call_target="tpu_custom_call" | custom-call | tf_op jit(solution)/shard_map/first/pallas_call | solution.py:1679
  225.6 140.3 %last.1 = (f32[3,192,192]{2,1,0:T(8,128)}, f32[192,192]{1,0:T(8,128)}, f32[192,1536]{1,0:T(8,128)}, f32[192,768]{1,0:T(8,128)}, bf16[2,256,768]{2,1,0:T(8,128)(2,1)}, /*index=5*/f32[8,768]{1,0:T(8,128)}) custom-call(bf16[512,768]{1,0:T(8,128)(2,1)} %get-tuple-element.31.n1_ref, f32[512,128]{1,0:T(8,128)} %get-tuple-element.32.i1_ref, ...), custom_call_target="tpu_custom_call" | custom-call | tf_op jit(solution)/shard_map/last/pallas_call | solution.py:1071
  365.9 1.4 broadcast_select_fusion
  367.3 0.0 copy-start
  367.3 1.8 select_n.128
  369.1 0.0 copy-start.3
  369.1 0.0 copy-done
  369.1 0.0 copy-start.2
  369.1 0.9 select_bitcast_fusion
  370.0 0.4 copy-done.3
  370.4 0.0 copy-start.4
  370.4 0.0 copy-start.6
  370.4 0.9 select_bitcast_fusion.1
  371.2 0.0 copy-done.2
  371.2 0.9 select_bitcast_fusion.2
  372.1 0.0 copy-done.4
  372.1 0.7 select_bitcast_fusion.3
  372.8 0.0 copy-done.6
  372.8 0.1 reshape.81
  372.9 0.5 fusion.1
  (10 shorter events, 0.1 us)
Async XLA Ops:
  1.8 0.9 copy-start.5
  2.1 1.9 copy-start.1
  367.3 1.8 copy-start
  369.1 1.3 copy-start.3
  369.1 2.2 copy-start.2
  370.4 1.7 copy-start.4
  370.4 2.4 copy-start.6

commit v11 on v10

--- a/solution.py
+++ b/solution.py
@@ -1706,8 +1706,8 @@
             VM((heads, rows, 128), BF),
             VM((rows, width), BF),
             VM((rows, width), F32),
-            VM((4, rows // 4, width), BF),
-            VM((4, rows // 4, width), BF),
+            VM((8, rows // 8, width), BF),
+            VM((8, rows // 8, width), BF),
             VM((2, 2, 8, gains.shape[1]), F32),
             VM((2,) + lengths.shape, jnp.int32),
             VM((2 * rows, rows), F32),
@@ -1722,8 +1722,8 @@
             VM((heads, 2, 128, rows), BF),
             VM((heads, 2, 128, rows), BF),
             VM((4, rows, 640), BF),
-            dma, dma((2,)), dma((2,)), dma, dma((6, 3)), dma((parts,)), dma((2,)), dma((2,)), dma((9,)), dma((4,)), dma((4,)), dma((4,)), dma((4,)),
-            dma((2,)), dma((2,)), dma((6,)), dma((6,)), dma((4,)), dma((4,)),
+            dma, dma((2,)), dma((2,)), dma, dma((6, 3)), dma((parts,)), dma((2,)), dma((2,)), dma((9,)), dma((8,)), dma((8,)), dma((8,)), dma((8,)),
+            dma((2,)), dma((2,)), dma((6,)), dma((6,)), dma((8,)), dma((8,)),
             dma((3,)), dma((3,)),
             dma((parts, 3)), dma((parts, 3)), dma((parts, 3)), dma((parts, 3)),
             dma((parts,)), dma((parts,)), dma((parts,)), dma((parts,)),

time: 376 us -> 376 us (level)
  no operation moved by 1% of the time
where the time goes in v11:
time: 376 us; the launch traced here: 373 us
  Pallas kernels  361 us (96%)
  other arithmetic  6.15 us (2%)
  local copies, waits for them, and re-layouts  5.44 us (1%)
    pallas_call x1, Pallas kernels, first_layer(): pl.pallas_call(functools.partial(first_kernel, parts), in_specs=[hbm] * 5...  220 us
    pallas_call x1, Pallas kernels, last_back(): pl.pallas_call(functools.partial(last_kernel, parts), grid=(LAST_STEP + 1...  140 us

profile of v11, /device:TPU:0, one launch (start us, length us, event | category | flops | bytes accessed | tf_op | source)
XLA Modules:
  0.0 373.3 jit_solution(3809038797714986805)
XLA Ops:
  0.6 1.1 copy.25
  1.8 0.0 copy-start.5
  1.8 0.1 maximum_select_fusion
  1.9 0.1 copy.30
  2.1 0.0 copy-start.1
  2.1 0.1 copy.31
  2.2 0.5 copy-done.5
  2.7 0.2 copy.26
  2.9 0.1 copy.29
  3.1 0.1 copy.32
  3.2 0.8 pad_maximum_fusion.lead_ref
  4.0 0.0 copy-done.1
  4.0 0.9 copy.33
  4.9 220.5 %first.1 = (bf16[2,2,4,192,3072]{4,3,2,1,0:T(8,128)(2,1)}, bf16[6,512,128]{2,1,0:T(8,128)(2,1)}, bf16[6,512,128]{2,1,0:T(8,128)(2,1)}, bf16[6,512,128]{2,1,0:T(8...) custom-call(bf16[2,256,768]{2,1,0:T(8,128)(2,1)} %tok_ref.1, ...), custom_call_target="tpu_custom_call" | custom-call | tf_op jit(solution)/shard_map/first/pallas_call | solution.py:1679
  225.4 140.3 %last.1 = (f32[3,192,192]{2,1,0:T(8,128)}, f32[192,192]{1,0:T(8,128)}, f32[192,1536]{1,0:T(8,128)}, f32[192,768]{1,0:T(8,128)}, bf16[2,256,768]{2,1,0:T(8,128)(2,1)}, /*index=5*/f32[8,768]{1,0:T(8,128)}) custom-call(bf16[512,768]{1,0:T(8,128)(2,1)} %get-tuple-element.31.n1_ref, f32[512,128]{1,0:T(8,128)} %get-tuple-element.32.i1_ref, ...), custom_call_target="tpu_custom_call" | custom-call | tf_op jit(solution)/shard_map/last/pallas_call | solution.py:1071
  365.6 1.4 broadcast_select_fusion
  367.0 0.0 copy-start
  367.0 1.8 select_n.128
  368.8 0.0 copy-start.3
  368.8 0.0 copy-done
  368.8 0.0 copy-start.2
  368.8 0.9 select_bitcast_fusion
  369.8 0.4 copy-done.3
  370.1 0.0 copy-start.4
  370.1 0.0 copy-start.6
  370.1 0.9 select_bitcast_fusion.1
  371.0 0.0 copy-done.2
  371.0 0.9 select_bitcast_fusion.2
  371.8 0.0 copy-done.4
  371.8 0.7 select_bitcast_fusion.3
  372.5 0.0 copy-done.6
  372.5 0.1 reshape.81
  372.6 0.5 fusion.1
  (10 shorter events, 0.1 us)
Async XLA Ops:
  1.8 0.9 copy-start.5
  2.1 1.9 copy-start.1
  367.0 1.8 copy-start
  368.8 1.3 copy-start.3
  368.8 2.2 copy-start.2
  370.1 1.7 copy-start.4
  370.1 2.4 copy-start.6
